TPU v7x, 32 devices: a whole 2x2x4 slice. The times are simulated.
32 devices in a mesh: cases: 2 (over x), frdm: 16 (over z, y, core).
Axes of the slice: x: 2, y: 2, z: 4, core: 2. Of those that a mesh axis runs over, the one named last changes fastest.
Arguments:
- loads: bfloat16 [32768, 896], P(('cases', 'frdm')), parts along dimension 0, may hold values from -2 to 2
- shapes: bfloat16 [16384, 2048], P('frdm'), may hold values from -0.1875 to 0.1875
- mode_order: int32 [2048], replicated, may hold values from 0 to 2047, each once
- partner: int32 [2048], replicated, may hold values from 0 to 2047, as said below
- taps: float32 [2048, 513], replicated, may hold values from -0.25 to 0.25
- offsets: int32 [2048], replicated, may hold values from 0 to 128
- coef: bfloat16 [2, 2048], P(None, 'frdm'), may hold values from -1.5 to 1.5
Outputs:
- displacement: bfloat16 [32768, 256], P(('cases', 'frdm')), parts along dimension 0
There are 2 independent parts, one for each index of `cases`. A program takes and returns all parts, laid end to end along the dimension named above; an argument that names none is the same for every part. Nothing has to cross between parts.
Inputs may be any that keep to these rules, and one draw needn't show every extreme that they name: `mode_order`: each mode appears once. partner[partner[m]] = m for every mode; exactly two modes are their own partners.
All inputs are finite; a program needn't handle non-finite values.
Results may differ from a plain program's by a relative error of at most 0.0057.
Values may be sent and summed in bfloat16 or wider, within the bound.
No kernel may reach another device: no remote copies, remote signals or barrier semaphores. Data moves between devices by JAX's collectives and lax.ppermute only.
A program may use at most 64 MiB of HBM per device.

v0:
```python
import jax
import jax.numpy as jnp
from jax import lax
from jax.sharding import PartitionSpec as P

W = 256


def convolve(modal_forces, tap_table, offset_table):
    tap_count = tap_table.shape[1]
    delay = modal_forces.shape[1] - W - tap_count + 1
    reversed_taps = tap_table[:, ::-1]
    padded_taps = jnp.pad(reversed_taps, ((0, 0), (delay, delay)))
    spread = jnp.arange(tap_count + delay, dtype=jnp.int32)[None, :] - offset_table[:, None] + delay
    kernel = jnp.take_along_axis(padded_taps, spread, axis=1)
    result = lax.conv_general_dilated(
        modal_forces[None],
        kernel[:, None, :],
        (1,),
        "VALID",
        dimension_numbers=("NCH", "OIH", "NCH"),
        feature_group_count=modal_forces.shape[0],
        precision=lax.Precision.HIGHEST,
    )
    return result[0]


def shards(loads, shapes, mode_order, partner, taps, offsets, coef):
    per_device = coef.shape[1]
    mode_total = shapes.shape[1]
    slot_start = lax.axis_index("frdm") * per_device
    own_taps = lax.dynamic_slice_in_dim(taps, slot_start, per_device, 0)
    own_offsets = lax.dynamic_slice_in_dim(offsets, slot_start, per_device)
    local_modes = lax.dot_general(
        shapes, loads, (((0,), (0,)), ((), ())), preferred_element_type=jnp.float32
    )
    summed_modes = lax.psum(local_modes, "frdm")
    own_modes = lax.dynamic_slice_in_dim(mode_order, slot_start, per_device)
    modal_forces = jnp.take(summed_modes, own_modes, axis=0)
    response = convolve(modal_forces, own_taps, own_offsets).astype(jnp.bfloat16)
    all_responses, all_coef = (
        lax.all_gather(response, "frdm", axis=0, tiled=True),
        lax.all_gather(coef, "frdm", axis=1, tiled=True),
    )
    slot_of = (
        jnp.zeros((mode_total,), jnp.int32)
        .at[mode_order]
        .set(jnp.arange(mode_total, dtype=jnp.int32))
    )
    mate_slot = slot_of[partner]
    both_rows = jnp.take(all_responses, jnp.concatenate([slot_of, mate_slot]), axis=0).astype(
        jnp.float32
    )
    direct = all_coef[0][slot_of].astype(jnp.float32)
    across = all_coef[1][slot_of].astype(jnp.float32)
    paired = (
        direct[:, None] * both_rows[:mode_total] + across[:, None] * both_rows[mode_total:]
    ).astype(jnp.bfloat16)
    return jnp.dot(shapes, paired, preferred_element_type=jnp.float32).astype(jnp.bfloat16)


def solution(mesh):
    in_specs = (P(("cases", "frdm"), None), P("frdm", None), P(), P(), P(), P(), P(None, "frdm"))
    out_specs = P(("cases", "frdm"), None)
    return jax.shard_map(shards, mesh=mesh, in_specs=in_specs, out_specs=out_specs, check_vma=False)
```

profile of v0, /device:TPU:0, one launch (start us, length us, event | category | flops | bytes accessed | tf_op | source)
XLA Modules:
  0.0 667.4 jit_solution(5517696721265598693)
XLA Ops:
  6.5 0.0 copy-start
  6.5 0.0 all-reduce.3.cloned.1.call-start
  6.5 1.5 copy-done
  8.0 8.7 %fusion.17 = f32[2048,896]{1,0:T(8,128)} fusion(bf16[1024,2048]{1,0:T(8,128)(2,1)} %param.8, bf16[1024,896]{1,0:T(8,128)(2,1)S(1)} %copy-done), kind=kOutput, calls=%fused_computation.46 | convolution fusion | flops 3758096384 | bytes 13369344 | tf_op jit(solution)/shard_map/dot_general | solution.py:34
  16.7 0.0 all-reduce.3.cloned.1.call-update
  16.8 0.0 all-gather.3.cloned.1.call-start
  16.8 1.0 constant_dynamic-slice_fusion
  17.8 0.4 rev.3
  18.2 0.8 dynamic_slice.10
  18.9 0.2 fusion.8
  19.1 0.3 reshape.278
  19.5 0.0 copy-start.1
  19.5 491.6 %gather_fusion.5 = f32[82048]{0:T(1024)S(1)} fusion(f32[128,769]{0,1:T(8,128)S(1)} %pad.4, s32[82048]{0:T(1024)S(1)} %reshape.278), kind=kCustom, calls=%fused_computation.5 | custom fusion | bytes 1312768 | tf_op jit(solution)/shard_map/jit(take_along_axis)/gather | solution.py:15
  511.2 0.4 gather.30
  511.5 0.2 fusion.12
  511.7 0.2 copy.12
  511.9 0.0 copy-done.1
  511.9 0.1 compare_and_fusion.1
  512.0 0.0 all-reduce.3.cloned.1.call-done
  512.0 4.1 gather_fusion.2
  516.1 0.1 bitcast_select_fusion
  516.2 0.7 copy.11
  516.9 0.0 copy-start.2
  517.0 46.0 %convolution_convert_fusion.1 = bf16[1,128,256]{1,0,2:T(2,128)(2,1)} fusion(f32[1,128,896]{1,0,2:T(1,128)S(1)} %copy.11, f32[128,1,641]{0,1,2:T(1,128)S(1)} %copy.12), kind=kOutput, calls=%fused_computation.16 | convolution fusion | flops 252084224 | bytes 852480 | tf_op jit(solution)/shard_map/conv_general_dilated | solution.py:16
  562.9 0.0 all-gather.3.cloned.1.call-update
  563.0 8.0 %scatter_custom_fusion = s32[2048]{0:T(1024)S(1)} fusion(s32[2048]{0:T(1024)S(1)} %compare_select_fusion.6, s32[2048]{0:T(1024)S(1)} %iota.12, s32[]{:T(128)} %constant.35.clone.1), kind=kCustom, calls=%fused_computation.40 | custom fusion | bytes 8196 | tf_op jit(solution)/shard_map/scatter | solution.py:48
  571.1 0.0 copy-done.2
  571.1 0.0 copy-start.3
  571.1 11.8 %gather_fusion.1 = s32[2048]{0:T(1024)S(1)} fusion(s32[2048]{0:T(1024)S(1)} %scatter_custom_fusion, s32[2048]{0:T(1024)S(1)} %fusion.14), kind=kCustom, calls=%fused_computation.1 | custom fusion | bytes 24576 | tf_op jit(solution)/shard_map/gather | solution.py:50
  582.9 0.0 copy-done.3
  582.9 23.0 %all_gather.6 = bf16[2,2048]{1,0:T(2,128)(2,1)S(1)} all-gather(bf16[2,128]{1,0:T(2,128)(2,1)S(1)} %copy-done.3), channel_id=1, replica_groups=mesh['cases'=2,'frdm'=16] {'frdm'}, dimensions={1}, use_global_device_ids=true | all-gather | bytes 8704 | tf_op jit(solution)/shard_map/all_gather | solution.py:43
  605.9 0.1 slice_reduce_fusion.1
  606.0 13.1 %gather_fusion.4 = bf16[2048]{0:T(1024)(128)(2,1)S(1)} fusion(bf16[2048]{0:T(1024)(128)(2,1)S(1)} %get-tuple-element.6, s32[2048]{0:T(1024)S(1)} %get-tuple-element.9), kind=kCustom, calls=%fused_computation.4 | custom fusion | bytes 16384 | tf_op jit(solution)/shard_map/gather | solution.py:55
  619.1 13.1 %gather_fusion = bf16[2048]{0:T(1024)(128)(2,1)S(1)} fusion(bf16[2048]{0:T(1024)(128)(2,1)S(1)} %get-tuple-element.5, s32[2048]{0:T(1024)S(1)} %get-tuple-element.9), kind=kCustom, calls=%fused_computation | custom fusion | bytes 16384 | tf_op jit(solution)/shard_map/gather | solution.py:54
  632.3 0.0 all-gather.3.cloned.1.call-done
  632.3 4.5 copy.13
  636.8 16.9 %gather_fusion.3 = bf16[4096,256]{1,0:T(8,128)(2,1)} fusion(bf16[2048,256]{1,0:T(8,128)(2,1)S(1)} %bitcast.16, s32[4096]{0:T(1024)S(1)} %broadcast_clamp_fusion), kind=kCustom, calls=%fused_computation.3 | custom fusion | bytes 4210688 | tf_op jit(solution)/shard_map/jit(_take)/gather | solution.py:51
  653.7 0.0 copy-start.4
  653.7 3.8 select_convert_fusion
  657.5 0.0 copy-done.4
  657.5 2.0 fusion.2
  659.5 1.0 copy.14
  (12 shorter events, 0.1 us)
Async XLA Ops:
  6.5 1.5 copy-start
  6.5 505.5 %all-reduce.3.cloned.1.call-start = ((), (), s32[]{:S(2)}) async-start(), calls=%async_computation | async-start | bytes 14680064 | tf_op jit(solution)/shard_map/psum | solution.py:37
  16.8 615.5 %all-gather.3.cloned.1.call-start = ((), (), s32[]{:S(2)}) async-start(), calls=%async_computation.1 | async-start | bytes 2228224 | tf_op jit(solution)/shard_map/all_gather | solution.py:42
  19.5 492.4 %copy-start.1 = (s32[2048]{0:T(1024)S(1)}, s32[2048]{0:T(1024)}, u32[]{:S(2)}) copy-start(s32[2048]{0:T(1024)} %param.9) | copy-start | bytes 24580
  516.9 54.1 %copy-start.2 = (s32[2048]{0:T(1024)S(1)}, s32[2048]{0:T(1024)}, u32[]{:S(2)}) copy-start(s32[2048]{0:T(1024)} %param.10) | copy-start | bytes 24580
  571.1 11.8 %copy-start.3 = (bf16[2,128]{1,0:T(2,128)(2,1)S(1)}, bf16[2,128]{1,0:T(2,128)(2,1)}, u32[]{:S(2)}) copy-start(bf16[2,128]{1,0:T(2,128)(2,1)} %param.13) | copy-start | bytes 1540
  653.7 3.8 copy-start.4
Sparse Core Ops, SparseCore 0:
  16.9 157.4 all-reduce.2
  563.1 50.2 all-gather.2
where the time goes:
time: 668 us; the launch traced here: 667 us
  local copies, waits for them, and re-layouts  569 us (85%)
  matrix products  56.7 us (8%)
  blocking collectives  23 us (3%)
  between operations  13.7 us (2%)
    gather x3, local copies, waits for them, and re-layouts, convolve(): kernel = jnp.take_along_axis(padded_taps, spread, axis=1)  492 us
    conv_general_dilated x1, matrix products, convolve(): lax.conv_general_dilated(modal_forces[None], kernel[:, None, :], (1,), 'V...  46 us
    all_gather x1, blocking collectives, shards(): lax.all_gather(coef, 'frdm', axis=1, tiled=True)  23 us
    gather x1, local copies, waits for them, and re-layouts, shards(): jnp.take(all_responses, jnp.concatenate([slot_of, mate_slot]), axis=0)  16.9 us
  transfers between devices with their start and end apart: 2, of which 0 were waited for; matrix products, arithmetic and copies ran while one was open for 81% of the time, Pallas kernels for 0%

commit v1 on v0

v1 whole, which is shorter than its diff:
```python
import functools

import jax
import jax.numpy as jnp
import numpy as np
from jax import lax
from jax.experimental import pallas as pl
from jax.experimental.pallas import tpu as pltpu
from jax.sharding import PartitionSpec as P

W = 256
BF = jnp.bfloat16
F32 = jnp.float32
VMEM_BYTES = 56 * 1024 * 1024
NT = (((1,), (1,)), ((), ()))
NN = (((1,), (0,)), ((), ()))


def dot(a, b, dims=NN):
    return lax.dot_general(a, b, dims, preferred_element_type=F32)


def split(table):
    high = table.astype(BF)
    low = (table - high.astype(np.float64)).astype(BF)
    return high, low


def tables(hist, taps):
    half = hist // 2
    odd = 2 * np.arange(half)[:, None] + 1

    def turn(n):
        angle = (odd * n[None, :]) % (2 * hist) * (np.pi / hist)
        return np.cos(angle), np.sin(angle)

    cos, sin = turn(np.arange(hist))
    forward = np.concatenate([cos, -sin])
    cos, sin = turn(np.arange(taps))
    tap_forward = np.concatenate([cos, -sin])
    delay = hist - W - taps + 1
    cos, sin = turn(np.arange(delay + 1))
    phase = np.concatenate([cos, sin])
    cos, sin = turn(np.arange(W) + taps - 1)
    inverse = np.concatenate([cos, -sin]).T * (2.0 / hist)
    return forward, tap_forward, phase, inverse


def params(**kw):
    return pltpu.CompilerParams(vmem_limit_bytes=VMEM_BYTES, **kw)


def once(shape):
    return pl.BlockSpec(shape, lambda *_: (0,) * len(shape), pipeline_mode=pl.Buffered(1))


def project_kernel(place, loads, fhi, flo, shapes, out, lft):
    @pl.when(pl.program_id(0) == 0)
    def _():
        rows = loads.shape[0]
        step = 256
        for r in range(0, rows, step):
            part = loads[r : r + step, :]
            lft[:, r : r + step] = (dot(fhi[...], part, NT) + dot(flo[...], part, NT)).astype(BF)

    out[...] = dot(lft[...], shapes[...]).astype(BF)


def project(place, loads, fhi, flo, shapes, tile=256):
    hist = loads.shape[1]
    rows, modes = shapes.shape
    half = modes // 2
    steps = half // tile
    return pl.pallas_call(
        project_kernel,
        grid_spec=pltpu.PrefetchScalarGridSpec(
            num_scalar_prefetch=1,
            grid=(steps,),
            in_specs=[
                once(loads.shape),
                once(fhi.shape),
                once(flo.shape),
                pl.BlockSpec((rows, tile), lambda i, s: (0, (1 - s[0]) * steps + i)),
            ],
            out_specs=[
                pl.BlockSpec((hist, tile), lambda i, s: (0, i)),
                pl.BlockSpec((hist, rows), lambda i, s: (0, 0)),
            ],
        ),
        out_shape=[
            jax.ShapeDtypeStruct((hist, half), BF),
            jax.ShapeDtypeStruct((hist, rows), BF),
        ],
        compiler_params=params(),
        name="project",
    )(place, loads, fhi, flo, shapes)


def spectrum_kernel(place, slots, offs, taps, thi, tlo, phi, plo, lft, shapes, spec, own, picked):
    tile = shapes.shape[1]
    half = spec.shape[0] // 2
    base = (place[0] * pl.num_programs(0) + pl.program_id(0)) * tile

    def pick(r, _):
        picked[pl.ds(r, 1), :] = taps[pl.ds(slots[base + r], 1), :]
        return _

    lax.fori_loop(0, tile, pick, 0, unroll=8)
    own[...] = dot(lft[...], shapes[...])
    row = picked[...]
    high = row.astype(BF)
    low = (row - high.astype(F32)).astype(BF)
    resp = dot(thi[...], high, NT) + dot(tlo[...], high, NT) + dot(thi[...], low, NT)
    hot = (lax.broadcasted_iota(jnp.int32, (phi.shape[1], tile), 0) == offs[...]).astype(F32).astype(BF)
    turn = dot(phi[...], hot) + dot(plo[...], hot)
    cos, sin = turn[:half], turn[half:]
    re, im = resp[:half], resp[half:]
    spec[:half, :] = cos * re - sin * im
    spec[half:, :] = sin * re + cos * im


def spectrum(place, slots, offs, taps, thi, tlo, phi, plo, lft, shapes, tile=256):
    hist = lft.shape[0]
    rows, modes = shapes.shape
    half = modes // 2
    steps = half // tile
    return pl.pallas_call(
        spectrum_kernel,
        grid_spec=pltpu.PrefetchScalarGridSpec(
            num_scalar_prefetch=2,
            grid=(steps,),
            in_specs=[
                pl.BlockSpec((1, tile), lambda i, s, _: (0, s[0] * steps + i)),
                once(taps.shape),
                once(thi.shape),
                once(tlo.shape),
                once(phi.shape),
                once(plo.shape),
                once(lft.shape),
                pl.BlockSpec((rows, tile), lambda i, s, _: (0, s[0] * steps + i)),
            ],
            out_specs=[
                pl.BlockSpec((hist, tile), lambda i, s, _: (0, i)),
                pl.BlockSpec((hist, tile), lambda i, s, _: (0, i)),
            ],
            scratch_shapes=[pltpu.VMEM((tile, taps.shape[1]), F32)],
        ),
        out_shape=[jax.ShapeDtypeStruct((hist, half), F32)] * 2,
        compiler_params=params(),
        name="spectrum",
    )(place, slots, offs, taps, thi, tlo, phi, plo, lft, shapes)


def respond_kernel(own, other, spec, ihi, ilo, out):
    half = spec.shape[0] // 2
    total = own[...] + other[...].astype(F32)
    re, im = total[:half], total[half:]
    tre, tim = spec[:half, :], spec[half:, :]
    product = jnp.concatenate([re * tre - im * tim, re * tim + im * tre], axis=0).astype(BF)
    out[...] = dot(ihi[...], product) + dot(ilo[...], product)


def respond(own, other, spec, ihi, ilo, tile=256):
    hist, half = own.shape
    block = pl.BlockSpec((hist, tile), lambda i: (0, i))
    return pl.pallas_call(
        respond_kernel,
        grid=(half // tile,),
        in_specs=[block, block, block, once(ihi.shape), once(ilo.shape)],
        out_specs=pl.BlockSpec((W, tile), lambda i: (0, i)),
        out_shape=jax.ShapeDtypeStruct((W, half), F32),
        compiler_params=params(),
        name="respond",
    )(own, other, spec, ihi, ilo)


def expand_kernel(place, resp, mate, coef, shapes, out, acc):
    step = pl.program_id(0)
    modes = resp.shape[1]
    tile = shapes.shape[1]
    hot = (lax.broadcasted_iota(jnp.int32, (modes, tile), 0) == mate[0:1, :]).astype(F32).astype(BF)
    self_hot = (lax.broadcasted_iota(jnp.int32, (modes, tile), 0) == mate[1:2, :]).astype(F32).astype(BF)
    across = dot(resp[...], hot)
    direct = dot(resp[...], self_hot)
    paired = (coef[0:1, :] * direct + coef[1:2, :] * across).astype(BF)
    part = dot(shapes[...], paired, NT)

    @pl.when(step == 0)
    def _():
        acc[...] = part

    @pl.when(step > 0)
    def _():
        acc[...] += part

    @pl.when(step == pl.num_programs(0) - 1)
    def _():
        out[...] = acc[...].astype(BF)


def expand(place, resp, mate, coef, shapes, tile=256):
    rows, modes = shapes.shape
    return pl.pallas_call(
        expand_kernel,
        grid_spec=pltpu.PrefetchScalarGridSpec(
            num_scalar_prefetch=1,
            grid=(modes // tile,),
            in_specs=[
                once(resp.shape),
                pl.BlockSpec((2, tile), lambda i, s: (0, i)),
                pl.BlockSpec((2, tile), lambda i, s: (0, i)),
                pl.BlockSpec((rows, tile), lambda i, s: (0, i)),
            ],
            out_specs=pl.BlockSpec((rows, W), lambda i, s: (0, 0)),
            scratch_shapes=[pltpu.VMEM((rows, W), F32)],
        ),
        out_shape=jax.ShapeDtypeStruct((rows, W), BF),
        compiler_params=params(),
        name="expand",
    )(place, resp, mate, coef, shapes)


def swap(x, devices, bits):
    return lax.ppermute(x, "frdm", [(i, i ^ bits) for i in range(devices)])


def columns(x, start, size):
    return lax.dynamic_slice_in_dim(x, start, size, 1)


def shards(devices, loads, shapes, mode_order, partner, taps, offsets, coef):
    modes = shapes.shape[1]
    half = modes // 2
    me = lax.axis_index("frdm")
    core = me & 1
    forward, tap_forward, phase, inverse = tables(loads.shape[1], taps.shape[1])
    pad = -phase.shape[1] % 128
    phase = np.pad(phase, ((0, 0), (0, pad)))
    place = core.reshape(1).astype(jnp.int32)

    all_coef = lax.all_gather(coef, "frdm", axis=1, tiled=True)
    slot_of = jnp.zeros((modes,), jnp.int32).at[mode_order].set(jnp.arange(modes, dtype=jnp.int32))
    mode_offsets = offsets[slot_of][None]
    mode_coef = all_coef[:, slot_of].astype(F32)

    sent, lft = project(place, loads, *split(forward), shapes)
    got = swap(sent, devices, 1)
    spec, own = spectrum(place, slot_of, mode_offsets, taps, *split(tap_forward), *split(phase), lft, shapes)
    resp = respond(own, got, spec, *split(inverse))
    if devices == 16:
        y, z = (me >> 1) & 1, me >> 2
        quarter, block = half // 2, half // 8
        got = swap(columns(resp, (1 - y) * quarter, quarter).astype(BF), devices, 2)
        resp = columns(resp, y * quarter, quarter) + got.astype(F32)
        parts = [columns(resp, (z ^ d) * block, block) for d in range(4)]
        total = parts[0]
        for d in (1, 2, 3):
            total = total + swap(parts[d].astype(BF), devices, 4 * d).astype(F32)
        total = total.astype(BF)
        resp = jnp.concatenate([total] + [swap(total, devices, 4 * d) for d in (1, 2, 3)], axis=1)
        resp = jnp.concatenate([resp, swap(resp, devices, 2)], axis=1)
        mask = ((core * 8 + y * 4 + z) * block).astype(jnp.int32)
    else:
        groups = [list(range(c, devices, 2)) for c in range(2)]
        resp = lax.psum(resp, "frdm", axis_index_groups=groups).astype(BF)
        mask = (core * half).astype(jnp.int32)
    resp = jnp.concatenate([resp, swap(resp, devices, 1)], axis=1)
    mate = jnp.stack([partner, jnp.arange(modes, dtype=jnp.int32)]) ^ mask
    return expand(place, resp, mate, mode_coef, shapes)


def solution(mesh):
    in_specs = (P(("cases", "frdm"), None), P("frdm", None), P(), P(), P(), P(), P(None, "frdm"))
    out_specs = P(("cases", "frdm"), None)
    body = functools.partial(shards, mesh.shape["frdm"])
    return jax.shard_map(body, mesh=mesh, in_specs=in_specs, out_specs=out_specs, check_vma=False)
```

time: 668 us -> 151 us (0.23)
  local copies, waits for them, and re-layouts: 569 us -> 45 us
  matrix products: 56.7 us -> 0 us
  Pallas kernels: 0 us -> 46.6 us
  waiting for transfers between devices: 0.07 us -> 21.7 us
  starting transfers between devices: 0.04 us -> 13.6 us
  between operations: 13.7 us -> 0.2 us
    gather x8 -> x2, local copies, waits for them, and re-layouts: 551 us -> 26.6 us  [the longest x1 20.5 us: shards(): mode_offsets = offsets[slot_of][None]]
    pallas_call x0 -> x4, Pallas kernels: none -> 46.6 us  [the longest x1 18.3 us: spectrum(): pl.pallas_call(spectrum_kernel, grid_spec=pltpu.PrefetchScalarGridSpec(nu...]
    conv_general_dilated x1 -> x0, matrix products: 46 us -> none  [convolve(): lax.conv_general_dilated(modal_forces[None], kernel[:, None, :], (1,), 'V...]
    ppermute x0 -> x10, waiting for transfers between devices: none -> 21.7 us  [swap(): return lax.ppermute(x, 'frdm', [(i, i ^ bits) for i in range(devices)])]
    ppermute x0 -> x10, starting transfers between devices: none -> 13.6 us  [swap(): return lax.ppermute(x, 'frdm', [(i, i ^ bits) for i in range(devices)])]
    dot_general x2 -> x0, matrix products: 10.7 us -> none  [the longest x1 8.7 us: shards(): lax.dot_general(shapes, loads, (((0,), (0,)), ((), ())), preferred_elemen...]
    unnamed x10 -> x21, local copies, waits for them, and re-layouts: 1.52 us -> 9.05 us
  transfers between devices with their start and end apart: 2 -> 10, of which waited for: 0 -> 6; matrix products, arithmetic and copies ran while one was open for 81% -> 28% of each run, Pallas kernels for 0% -> 12%
where the time goes in v1:
time: 151 us; the launch traced here: 150 us
  Pallas kernels  46.6 us (31%)
  local copies, waits for them, and re-layouts  45 us (30%)
  waiting for transfers between devices  21.7 us (14%)
  blocking collectives  21.6 us (14%)
  starting transfers between devices  13.6 us (9%)
  other arithmetic  1.81 us (1%)
    ppermute x10, waiting for transfers between devices, swap(): return lax.ppermute(x, 'frdm', [(i, i ^ bits) for i in range(devices)])  21.7 us
    all_gather x1, blocking collectives, shards(): all_coef = lax.all_gather(coef, 'frdm', axis=1, tiled=True)  21.6 us
    gather x1, local copies, waits for them, and re-layouts, shards(): mode_offsets = offsets[slot_of][None]  20.5 us
    pallas_call x1, Pallas kernels, spectrum(): pl.pallas_call(spectrum_kernel, grid_spec=pltpu.PrefetchScalarGridSpec(nu...  18.3 us
    ppermute x10, starting transfers between devices, swap(): return lax.ppermute(x, 'frdm', [(i, i ^ bits) for i in range(devices)])  13.6 us
    pallas_call x1, Pallas kernels, expand(): pl.pallas_call(expand_kernel, grid_spec=pltpu.PrefetchScalarGridSpec(num_...  11.2 us
    pallas_call x1, Pallas kernels, project(): pl.pallas_call(project_kernel, grid_spec=pltpu.PrefetchScalarGridSpec(num...  10.7 us
    unnamed x21, local copies, waits for them, and re-layouts  9.05 us
  transfers between devices with their start and end apart: 10, of which 6 were waited for; matrix products, arithmetic and copies ran while one was open for 28% of the time, Pallas kernels for 12%

profile of v1, /device:TPU:0, one launch (start us, length us, event | category | flops | bytes accessed | tf_op | source)
XLA Modules:
  0.0 150.5 jit_solution(4287496891590514886)
XLA Ops:
  0.0 0.0 copy-start
  0.0 10.7 %project.1 = (bf16[896,1024]{1,0:T(8,128)(2,1)}, bf16[896,1024]{1,0:T(8,128)(2,1)}) custom-call(s32[1]{0:T(128)} %bitcast.place, bf16[1024,896]{1,0:T(8,128)(2,1)} %loads.1, bf16[896,896]{1,0:T(8,128)(2,1)} %constant.18.clone.fhi, bf16[896,896]{1,0:T(8,128)(2,1)} %constant.42.clone.flo, bf16[1024,2048]{1,0:T(8,128)(2,1)} %shapes.5), custom_call_target="tpu_custom_call" | custom-call | tf_op jit(solution)/shard_map/project/pallas_call | solution.py:74
  10.7 0.5 collective-permute-start
  11.2 5.7 %copy.19.taps = f32[2048,513]{1,0:T(8,128)} copy(f32[2048,513]{0,1:T(8,128)} %param.19) | data formatting | bytes 8404992 | tf_op args[4]
  16.9 0.0 copy-done.4
  16.9 8.0 %scatter_custom_fusion.slots = s32[2048]{0:T(1024)S(1)} fusion(s32[2048]{0:T(1024)S(1)} %compare_select_fusion.1, s32[2048]{0:T(1024)S(1)} %iota.7, s32[]{:T(128)} %constant.9.clone.1), kind=kCustom, calls=%fused_computation.25 | custom fusion | bytes 8196 | tf_op jit(solution)/shard_map/scatter | solution.py:242
  24.9 0.0 copy-start.3
  24.9 0.0 copy-done
  25.0 20.5 %gather_fusion = s32[2048]{0:T(1024)} fusion(s32[2048]{0:T(1024)S(1)} %copy-done, s32[2048]{0:T(1024)S(1)} %fusion), kind=kCustom, calls=%fused_computation | custom fusion | bytes 24576 | tf_op jit(solution)/shard_map/gather | solution.py:243
  45.4 0.0 copy-done.3
  45.4 18.3 %spectrum.1 = (f32[896,1024]{1,0:T(8,128)}, f32[896,1024]{1,0:T(8,128)}) custom-call(s32[1]{0:T(128)} %bitcast.place, s32[2048]{0:T(1024)} %copy-done.3, s32[1,2048]{1,0:T(1,128)} %bitcast.5, f32[2048,513]{1,0:T(8,128)} %copy.19.taps, bf16[896,513]{1,0:T(8,128)(2,1)} %constant.43.clone.thi, bf16[896,513]{1,0:T(8,128)(2,1)} %constant.44.clone.tlo, ...), custom_call_target="tpu_custom_call" | custom-call | tf_op jit(solution)/shard_map/spectrum/pallas_call | solution.py:127
  63.7 0.0 collective-permute-done.other
  63.7 0.0 copy-start.1
  63.8 1.3 copy-done.1
  65.0 6.4 %respond.1 = f32[256,1024]{1,0:T(8,128)} custom-call(f32[896,1024]{1,0:T(8,128)} %get-tuple-element.10.own, bf16[896,1024]{1,0:T(8,128)(2,1)} %copy-done.1, f32[896,1024]{1,0:T(8,128)} %get-tuple-element.12.spec, bf16[256,896]{1,0:T(8,128)(2,1)} %constant.47.clone.ihi, bf16[256,896]{1,0:T(8,128)(2,1)} %constant.48.clone.ilo), custom_call_target="tpu_custom_call" | custom-call | tf_op jit(solution)/shard_map/respond/pallas_call | solution.py:166
  71.4 1.1 dynamic-slice_convert_fusion
  72.5 2.6 %collective-permute-start.1 = (bf16[256,512]{1,0:T(8,128)(2,1)S(1)}, bf16[256,512]{1,0:T(8,128)(2,1)S(1)}, u32[]{:S(2)}, u32[]{:S(2)}) collective-permute-start(bf16[256,512]{1,0:T(8,128)(2,1)S(1)} %dynamic-slice_convert_fusion), channel_id=1, source_target_pairs={{0,2},{1,3},{2,0},{3,1},{4,6},{5,7},{6,4},{7,5},{8,10},{9,11},{10,... | collective-permute-start | bytes 786440 | tf_op jit(solution)/shard_map/ppermute | solution.py:224
  75.1 0.0 copy-start.6
  75.1 7.0 %collective-permute-done.1 = bf16[256,512]{1,0:T(8,128)(2,1)S(1)} collective-permute-done((bf16[256,512]{1,0:T(8,128)(2,1)S(1)}, bf16[256,512]{1,0:T(8,128)(2,1)S(1)}, u32[]{:S(2)}, u32[]{:S(2)}) %collective-permute-start.1) | collective-permute-done | bytes 262176 | tf_op jit(solution)/shard_map/ppermute | solution.py:224
  82.1 1.1 convert_add_fusion
  83.2 0.1 dynamic-slice_convert_fusion.3
  83.3 1.9 %collective-permute-start.2 = (bf16[256,128]{1,0:T(8,128)(2,1)S(1)}, bf16[256,128]{1,0:T(8,128)(2,1)S(1)}, u32[]{:S(2)}, u32[]{:S(2)}) collective-permute-start(bf16[256,128]{1,0:T(8,128)(2,1)S(1)} %get-tuple-element.15), channel_id=1, source_target_pairs={{0,4},{1,5},{2,6},{3,7},{4,0},{5,1},{6,2},{7,3},{8,12},{9,13},{10,... | collective-permute-start | bytes 196616 | tf_op jit(solution)/shard_map/ppermute | solution.py:224
  85.1 2.6 %collective-permute-start.3 = (bf16[256,128]{1,0:T(8,128)(2,1)S(1)}, bf16[256,128]{1,0:T(8,128)(2,1)S(1)}, u32[]{:S(2)}, u32[]{:S(2)}) collective-permute-start(bf16[256,128]{1,0:T(8,128)(2,1)S(1)} %get-tuple-element.17), channel_id=1, source_target_pairs={{0,8},{1,9},{2,10},{3,11},{4,12},{5,13},{6,14},{7,15},{8,0},{9,1},... | collective-permute-start | bytes 196616 | tf_op jit(solution)/shard_map/ppermute | solution.py:224
  87.7 0.0 collective-permute-start.4
  87.7 0.0 copy-start.5
  87.7 0.0 collective-permute-done.2
  87.7 4.6 %collective-permute-done.3 = bf16[256,128]{1,0:T(8,128)(2,1)S(1)} collective-permute-done((bf16[256,128]{1,0:T(8,128)(2,1)S(1)}, bf16[256,128]{1,0:T(8,128)(2,1)S(1)}, u32[]{:S(2)}, u32[]{:S(2)}) %collective-permute-start.3) | collective-permute-done | bytes 65568 | tf_op jit(solution)/shard_map/ppermute | solution.py:224
  92.3 1.5 collective-permute-done.4
  93.8 0.1 collective-permute-start.5
  93.9 2.2 %collective-permute-start.6 = (bf16[256,128]{1,0:T(8,128)(2,1)S(1)}, bf16[256,128]{1,0:T(8,128)(2,1)S(1)}, u32[]{:S(2)}, u32[]{:S(2)}) collective-permute-start(bf16[256,128]{1,0:T(8,128)(2,1)S(1)} %get-tuple-element.14), channel_id=1, source_target_pairs={{0,8},{1,9},{2,10},{3,11},{4,12},{5,13},{6,14},{7,15},{8,0},{9,1},... | collective-permute-start | bytes 196616 | tf_op jit(solution)/shard_map/ppermute | solution.py:224
  96.1 2.1 %collective-permute-start.7 = (bf16[256,128]{1,0:T(8,128)(2,1)S(1)}, bf16[256,128]{1,0:T(8,128)(2,1)S(1)}, u32[]{:S(2)}, u32[]{:S(2)}) collective-permute-start(bf16[256,128]{1,0:T(8,128)(2,1)S(1)} %get-tuple-element.14), channel_id=1, source_target_pairs={{0,12},{1,13},{2,14},{3,15},{4,8},{5,9},{6,10},{7,11},{8,4},{9,5},... | collective-permute-start | bytes 196616 | tf_op jit(solution)/shard_map/ppermute | solution.py:224
  98.3 0.0 collective-permute-done.5
  98.3 1.3 collective-permute-done.6
  99.6 2.6 %collective-permute-done.7 = bf16[256,128]{1,0:T(8,128)(2,1)S(1)} collective-permute-done((bf16[256,128]{1,0:T(8,128)(2,1)S(1)}, bf16[256,128]{1,0:T(8,128)(2,1)S(1)}, u32[]{:S(2)}, u32[]{:S(2)}) %collective-permute-start.7) | collective-permute-done | bytes 65568 | tf_op jit(solution)/shard_map/ppermute | solution.py:224
  102.2 1.6 %collective-permute-start.8 = (bf16[256,512]{1,0:T(8,128)(2,1)S(1)}, bf16[256,512]{1,0:T(8,128)(2,1)S(1)}, u32[]{:S(2)}, u32[]{:S(2)}) collective-permute-start(bf16[256,512]{1,0:T(8,128)(2,1)S(1)} %pad_maximum_fusion), channel_id=1, source_target_pairs={{0,2},{1,3},{2,0},{3,1},{4,6},{5,7},{6,4},{7,5},{8,10},{9,11},{10,... | collective-permute-start | bytes 786440 | tf_op jit(solution)/shard_map/ppermute | solution.py:224
  103.9 4.7 %collective-permute-done.8 = bf16[256,512]{1,0:T(8,128)(2,1)S(1)} collective-permute-done((bf16[256,512]{1,0:T(8,128)(2,1)S(1)}, bf16[256,512]{1,0:T(8,128)(2,1)S(1)}, u32[]{:S(2)}, u32[]{:S(2)}) %collective-permute-start.8) | collective-permute-done | bytes 262176 | tf_op jit(solution)/shard_map/ppermute | solution.py:224
  108.7 0.1 collective-permute-start.9
  108.8 0.0 copy-done.6
  108.8 0.1 copy.20
  108.9 21.6 %all_gather.3 = bf16[2,2048]{0,1:T(8,128)(2,1)S(1)} all-gather(bf16[2,128]{0,1:T(8,128)(2,1)S(1)} %copy.20), channel_id=1, replica_groups=mesh['cases'=2,'frdm'=16] {'frdm'}, dimensions={1}, use_global_device_ids=true | all-gather | bytes 8704 | tf_op jit(solution)/shard_map/all_gather | solution.py:241
  130.5 6.2 %gather_fusion.1 = bf16[2048,2]{1,0:T(8,128)(2,1)S(1)} fusion(bf16[2,2048]{0,1:T(8,128)(2,1)S(1)} %all_gather.3, s32[2048]{0:T(1024)S(1)} %fusion), kind=kCustom, calls=%fused_computation.1 | custom fusion | bytes 24576 | tf_op jit(solution)/shard_map/gather | solution.py:244
  136.7 0.8 copy.22
  137.6 0.0 copy-done.5
  137.6 0.6 add_xor_fusion.mate
  138.2 0.0 collective-permute-done.9
  138.2 0.0 copy-start.2
  138.2 1.0 copy-done.2
  139.2 11.2 %expand.1 = bf16[1024,256]{1,0:T(8,128)(2,1)} custom-call(s32[1]{0:T(128)} %bitcast.place, bf16[256,2048]{1,0:T(8,128)(2,1)} %copy-done.2, s32[2,2048]{1,0:T(2,128)} %add_xor_fusion.mate, f32[2,2048]{1,0:T(2,128)} %bitcast.4, bf16[1024,2048]{1,0:T(8,128)(2,1)} %shapes.5), custom_call_target="tpu_custom_call" | custom-call | tf_op jit(solution)/shard_map/expand/pallas_call | solution.py:203
  (13 shorter events, 0.3 us)
Async XLA Ops:
  0.0 24.9 %copy-start = (s32[2048]{0:T(1024)S(1)}, s32[2048]{0:T(1024)}, u32[]{:S(2)}) copy-start(s32[2048]{0:T(1024)} %param.20) | copy-start | bytes 24580
  10.7 53.1 %collective-permute-start = (bf16[896,1024]{1,0:T(8,128)(2,1)}, bf16[896,1024]{1,0:T(8,128)(2,1)S(1)}, u32[]{:S(2)}, u32[]{:S(2)}) collective-permute-start(bf16[896,1024]{1,0:T(8,128)(2,1)} %get-tuple-element.11), channel_id=1, source_target_pairs={{0,1},{1,0},{2,3},{3,2},{4,5},{5,4},{6,7},{7,6},{8,9},{9,8},{10,11... | collective-permute-start | bytes 5505032 | tf_op jit(solution)/shard_map/ppermute | solution.py:224
  11.2 5.7 %copy-start.4 = (s32[2048]{0:T(1024)S(1)}, s32[2048]{0:T(1024)}, u32[]{:S(2)}) copy-start(s32[2048]{0:T(1024)} %param.17) | copy-start | bytes 24580
  24.9 20.5 %copy-start.3 = (s32[2048]{0:T(1024)}, s32[2048]{0:T(1024)S(1)}, u32[]{:S(2)}) copy-start(s32[2048]{0:T(1024)S(1)} %scatter_custom_fusion.slots) | copy-start | bytes 24580
  63.7 1.3 copy-start.1
  72.5 9.6 %collective-permute-start.1 = (bf16[256,512]{1,0:T(8,128)(2,1)S(1)}, bf16[256,512]{1,0:T(8,128)(2,1)S(1)}, u32[]{:S(2)}, u32[]{:S(2)}) collective-permute-start(bf16[256,512]{1,0:T(8,128)(2,1)S(1)} %dynamic-slice_convert_fusion), channel_id=1, source_target_pairs={{0,2},{1,3},{2,0},{3,1},{4,6},{5,7},{6,4},{7,5},{8,10},{9,11},{10,... | collective-permute-start | bytes 786440 | tf_op jit(solution)/shard_map/ppermute | solution.py:224
  75.1 33.7 %copy-start.6 = (bf16[2,128]{1,0:T(2,128)(2,1)S(1)}, bf16[2,128]{1,0:T(2,128)(2,1)}, u32[]{:S(2)}) copy-start(bf16[2,128]{1,0:T(2,128)(2,1)} %param.21) | copy-start | bytes 1540
  83.3 4.5 %collective-permute-start.2 = (bf16[256,128]{1,0:T(8,128)(2,1)S(1)}, bf16[256,128]{1,0:T(8,128)(2,1)S(1)}, u32[]{:S(2)}, u32[]{:S(2)}) collective-permute-start(bf16[256,128]{1,0:T(8,128)(2,1)S(1)} %get-tuple-element.15), channel_id=1, source_target_pairs={{0,4},{1,5},{2,6},{3,7},{4,0},{5,1},{6,2},{7,3},{8,12},{9,13},{10,... | collective-permute-start | bytes 196616 | tf_op jit(solution)/shard_map/ppermute | solution.py:224
  85.1 7.2 %collective-permute-start.3 = (bf16[256,128]{1,0:T(8,128)(2,1)S(1)}, bf16[256,128]{1,0:T(8,128)(2,1)S(1)}, u32[]{:S(2)}, u32[]{:S(2)}) collective-permute-start(bf16[256,128]{1,0:T(8,128)(2,1)S(1)} %get-tuple-element.17), channel_id=1, source_target_pairs={{0,8},{1,9},{2,10},{3,11},{4,12},{5,13},{6,14},{7,15},{8,0},{9,1},... | collective-permute-start | bytes 196616 | tf_op jit(solution)/shard_map/ppermute | solution.py:224
  87.7 6.1 %collective-permute-start.4 = (bf16[256,128]{1,0:T(8,128)(2,1)S(1)}, bf16[256,128]{1,0:T(8,128)(2,1)S(1)}, u32[]{:S(2)}, u32[]{:S(2)}) collective-permute-start(bf16[256,128]{1,0:T(8,128)(2,1)S(1)} %get-tuple-element.16), channel_id=1, source_target_pairs={{0,12},{1,13},{2,14},{3,15},{4,8},{5,9},{6,10},{7,11},{8,4},{9,5},... | collective-permute-start | bytes 196616 | tf_op jit(solution)/shard_map/ppermute | solution.py:224
  87.7 49.9 %copy-start.5 = (s32[2048]{0:T(1024)S(1)}, s32[2048]{0:T(1024)}, u32[]{:S(2)}) copy-start(s32[2048]{0:T(1024)} %param.18) | copy-start | bytes 24580
  93.8 4.5 %collective-permute-start.5 = (bf16[256,128]{1,0:T(8,128)(2,1)S(1)}, bf16[256,128]{1,0:T(8,128)(2,1)S(1)}, u32[]{:S(2)}, u32[]{:S(2)}) collective-permute-start(bf16[256,128]{1,0:T(8,128)(2,1)S(1)} %get-tuple-element.14), channel_id=1, source_target_pairs={{0,4},{1,5},{2,6},{3,7},{4,0},{5,1},{6,2},{7,3},{8,12},{9,13},{10,... | collective-permute-start | bytes 196616 | tf_op jit(solution)/shard_map/ppermute | solution.py:224
  93.9 5.7 %collective-permute-start.6 = (bf16[256,128]{1,0:T(8,128)(2,1)S(1)}, bf16[256,128]{1,0:T(8,128)(2,1)S(1)}, u32[]{:S(2)}, u32[]{:S(2)}) collective-permute-start(bf16[256,128]{1,0:T(8,128)(2,1)S(1)} %get-tuple-element.14), channel_id=1, source_target_pairs={{0,8},{1,9},{2,10},{3,11},{4,12},{5,13},{6,14},{7,15},{8,0},{9,1},... | collective-permute-start | bytes 196616 | tf_op jit(solution)/shard_map/ppermute | solution.py:224
  96.1 6.1 %collective-permute-start.7 = (bf16[256,128]{1,0:T(8,128)(2,1)S(1)}, bf16[256,128]{1,0:T(8,128)(2,1)S(1)}, u32[]{:S(2)}, u32[]{:S(2)}) collective-permute-start(bf16[256,128]{1,0:T(8,128)(2,1)S(1)} %get-tuple-element.14), channel_id=1, source_target_pairs={{0,12},{1,13},{2,14},{3,15},{4,8},{5,9},{6,10},{7,11},{8,4},{9,5},... | collective-permute-start | bytes 196616 | tf_op jit(solution)/shard_map/ppermute | solution.py:224
  102.2 6.4 %collective-permute-start.8 = (bf16[256,512]{1,0:T(8,128)(2,1)S(1)}, bf16[256,512]{1,0:T(8,128)(2,1)S(1)}, u32[]{:S(2)}, u32[]{:S(2)}) collective-permute-start(bf16[256,512]{1,0:T(8,128)(2,1)S(1)} %pad_maximum_fusion), channel_id=1, source_target_pairs={{0,2},{1,3},{2,0},{3,1},{4,6},{5,7},{6,4},{7,5},{8,10},{9,11},{10,... | collective-permute-start | bytes 786440 | tf_op jit(solution)/shard_map/ppermute | solution.py:224
  108.7 29.5 %collective-permute-start.9 = (bf16[256,1024]{1,0:T(8,128)(2,1)S(1)}, bf16[256,1024]{1,0:T(8,128)(2,1)S(1)}, u32[]{:S(2)}, u32[]{:S(2)}) collective-permute-start(bf16[256,1024]{1,0:T(8,128)(2,1)S(1)} %get-tuple-element.18), channel_id=1, source_target_pairs={{0,1},{1,0},{2,3},{3,2},{4,5},{5,4},{6,7},{7,6},{8,9},{9,8},{10,11... | collective-permute-start | bytes 1572872 | tf_op jit(solution)/shard_map/ppermute | solution.py:224
  138.2 1.0 copy-start.2

commit v2 on v0

v2 whole, which is shorter than its diff:
```python
import functools

import jax
import jax.numpy as jnp
import numpy as np
from jax import lax
from jax.experimental import pallas as pl
from jax.experimental.pallas import tpu as pltpu
from jax.sharding import PartitionSpec as P

W = 256
LANES = 128
EXTRA = 16
BF = jnp.bfloat16
F32 = jnp.float32
I32 = jnp.int32
NT = (((1,), (1,)), ((), ()))
NN = (((1,), (0,)), ((), ()))


def dot(a, b, dims=NN):
    return lax.dot_general(a, b, dims, preferred_element_type=F32)


def split(table):
    high = table.astype(BF)
    low = (table - high.astype(np.float64)).astype(BF)
    return high, low


def turns(half, n):
    odd = 2 * np.arange(half)[:, None] + 1
    angle = (odd * n[None, :]) % (4 * half) * (np.pi / (2 * half))
    return np.cos(angle), np.sin(angle)


def forward_table(hist):
    cos, sin = turns(hist // 2, np.arange(hist))
    return np.concatenate(split(np.concatenate([cos, -sin])), axis=1)


def tap_table(hist, taps):
    cos, sin = turns(hist // 2, np.arange(taps))
    table = np.concatenate([cos, -sin])
    high, low = split(table[:, :-1])
    last = np.repeat(table[:, -1:], LANES, axis=1).astype(np.float32)
    return np.concatenate([high, low, high], axis=1), last


def phase_table(hist, delay):
    cos, sin = turns(hist // 2, np.arange(1, delay + 1))
    return np.concatenate(split(np.concatenate([cos - 1.0, sin])), axis=1)


def inverse_table(hist, taps):
    cos, sin = turns(hist // 2, np.arange(W) + taps - 1)
    return np.concatenate(split(np.concatenate([cos, -sin]).T * (2.0 / hist)), axis=1)


def call(kernel, name, out_shape, *args, scalars=1, scratch=(), limit=20):
    vmem = pl.BlockSpec(memory_space=pltpu.VMEM)
    smem = pl.BlockSpec(memory_space=pltpu.SMEM)
    return pl.pallas_call(
        kernel,
        in_specs=[smem] * scalars + [vmem] * (len(args) - scalars),
        out_specs=[vmem] * len(out_shape),
        out_shape=out_shape,
        scratch_shapes=list(scratch),
        compiler_params=pltpu.CompilerParams(vmem_limit_bytes=limit * 1024 * 1024),
        name=name,
    )(*args)


def array(*shape, dtype=BF):
    return jax.ShapeDtypeStruct(shape, dtype)


def block(start, size):
    return pl.ds(pl.multiple_of(start, LANES), size)


def hot(mask):
    return mask.astype(F32).astype(BF)


def project_kernel(place, loads, table, shapes, coef, sent, lft):
    rows, half = loads.shape[0], sent.shape[1]
    hist = lft.shape[0]
    for r in range(0, rows, 256):
        part = loads[r : r + 256, :]
        lft[:, r : r + 256] = dot(table[...], jnp.concatenate([part, part], axis=1), NT).astype(BF)
    base = (1 - place[0]) * half
    for c in range(0, half, 256):
        sent[:hist, c : c + 256] = dot(lft[...], shapes[:, block(base + c, 256)]).astype(BF)
    sent[hist:, :] = jnp.zeros((EXTRA, half), BF)
    per = coef.shape[1]
    sent[hist : hist + 2, :per] = coef[...]


def spectrum(base, taps, offsets, order, table, last, phase, stack, put, width):
    count = taps.shape[0] - 1
    half = table.shape[0] // 2
    for r in range(0, count, 64):
        row = taps[r : r + 64, :]
        high = row.astype(BF)
        stack[r : r + 64, :] = high
        stack[count + r : count + r + 64, :] = (row - high.astype(F32)).astype(BF)
    row = taps[count : count + 1, :]
    high = row.astype(BF).astype(F32)
    index = lax.broadcasted_iota(I32, (EXTRA, taps.shape[1]), 0)
    tail = jnp.where(index == 0, high, jnp.where(index == 1, row - high, jnp.where(index == 2, offsets[...].astype(F32), 0.0)))
    stack[2 * count :, :] = tail.astype(BF)
    delay = phase.shape[1] // 2
    for c in range(0, width, 256):
        mode = lax.broadcasted_iota(I32, (256, taps.shape[1]), 0) + (base + c)
        picked = dot(stack[...], hot(mode == order[...]), NT)
        main = picked[: 2 * count].astype(BF)
        tail = picked[2 * count :]
        end = tail[0:1] + tail[1:2]
        offset = tail[2:3].astype(I32)
        resp = dot(table[...], jnp.concatenate([main[:count], main], axis=0))
        resp = resp + jnp.tile(last[...], (1, 2)) * end
        which = hot(lax.broadcasted_iota(I32, (delay, 256), 0) + 1 == offset)
        turn = dot(phase[...], jnp.concatenate([which, which], axis=0))
        cos, sin = turn[:half] + 1.0, turn[half:]
        re, im = resp[:half], resp[half:]
        put(c, cos * re - sin * im, sin * re + cos * im)


def spectrum_kernel(place, taps, offsets, order, table, last, phase, lft, shapes, spec, own, stack):
    width = spec.shape[1]
    half = spec.shape[0] // 2
    base = place[0]
    for c in range(0, width, 256):
        own[:, c : c + 256] = dot(lft[...], shapes[:, block(base + c, 256)])

    def put(c, re, im):
        spec[:half, c : c + 256] = re
        spec[half:, c : c + 256] = im

    spectrum(base, taps, offsets, order, table, last, phase, stack, put, width)


def respond_kernel(place, own, other, spec, inverse, coef, out):
    hist, width = own.shape
    half = hist // 2
    start = place[0]
    for c in range(0, width, 256):
        total = own[:, c : c + 256] + other[:hist, block(start + c, 256)].astype(F32)
        re, im = total[:half], total[half:]
        tre, tim = spec[:half, c : c + 256], spec[half:, c : c + 256]
        product = jnp.concatenate([re * tre - im * tim, re * tim + im * tre], axis=0).astype(BF)
        result = dot(inverse[...], jnp.concatenate([product, product], axis=0))
        out[:W, c : c + 256] = result.astype(out.dtype)
    if out.shape[0] > W:
        out[W:, :] = jnp.zeros((EXTRA, width), BF)
        out[W : W + 2, :LANES] = coef[...]
        out[W + 2 : W + 4, :LANES] = other[hist : hist + 2, :LANES]


def fold_kernel(place, own, got, coef, other, keep, known, first, second, third):
    z = place[0]
    size = keep.shape[1]
    hist = other.shape[0] - EXTRA
    known[...] = jnp.zeros(known.shape, BF)
    known[0:2, :] = coef[...]
    known[2:4, :] = other[hist : hist + 2, :LANES]
    known[4:8, :] = got[W : W + 4, :LANES]
    for d, out in enumerate((keep, first, second, third)):
        where = block((z ^ d) * size, size)
        total = own[:, where] + got[:W, where].astype(F32)
        out[:W, :] = total.astype(out.dtype)
        if d:
            out[W:, :] = known[...]


def settle_kernel(keep, first, second, third, out):
    total = keep[...]
    for got in (first, second, third):
        total = total + got[:W, :].astype(F32)
    out[...] = total.astype(BF)


def mixers_kernel(place, order, partner, known, first, second, third, coef, pick, held):
    me, mask = place[0], place[1]
    modes = order.shape[1]
    held[...] = jnp.zeros(held.shape, F32)
    for z, rows in enumerate((known, first, second, third)):
        top = rows.shape[0] - EXTRA
        for low in range(4):
            where = block((me ^ (4 * z + low)) * LANES, LANES)
            held[0:2, where] = rows[top : top + EXTRA, :].astype(F32)[2 * low : 2 * low + 2]
    mixers(order, partner, mask, held, coef, pick)


def mixers(order, partner, mask, held, coef, pick):
    modes = order.shape[1]
    table = held[...].astype(BF)
    for c in range(0, modes, 256):
        mode = lax.broadcasted_iota(I32, (256, modes), 0) + c
        coef[:, c : c + 256] = dot(table, hot(mode == order[...]), NT)
        mode = lax.broadcasted_iota(I32, (256, modes), 0) + c
        pick[c : c + 256, :] = hot((mode ^ mask) == partner[...])


def plain_mixers_kernel(place, order, partner, every, coef, pick, held):
    held[...] = jnp.zeros(held.shape, F32)
    held[0:2, :] = every[...].astype(F32)
    mixers(order, partner, place[1], held, coef, pick)


def mate_kernel(resp, pick, out):
    for c in range(0, out.shape[1], 256):
        out[:, c : c + 256] = dot(resp[...], pick[: resp.shape[1], c : c + 256])


def expand_kernel(place, resp, other, mates, coef, pick, shapes, out, paired):
    half = resp.shape[1]
    mask = place[1]
    for c in range(0, 2 * half, 256):
        across = mates[:, c : c + 256] + dot(other[...], pick[half:, c : c + 256])
        for k in (c, c + LANES):
            start = mask ^ k
            mine = resp[:, block(start & (half - 1), LANES)].astype(F32)
            theirs = other[:, block(start & (half - 1), LANES)].astype(F32)
            direct = jnp.where(start < half, mine, theirs)
            mixed = coef[0:1, k : k + LANES] * direct + coef[1:2, k : k + LANES] * across[:, k - c : k - c + LANES]
            paired[:, k : k + LANES] = mixed.astype(BF)
    rows = out.shape[0]
    for r in range(0, rows, 256):
        out[r : r + 256, :] = dot(shapes[r : r + 256, :], paired[...], NT).astype(BF)


def swap(x, devices, bits):
    return lax.ppermute(x, "frdm", [(i, i ^ bits) for i in range(devices)])


def scalars(*values):
    return jnp.stack([jnp.asarray(v, I32) for v in values])


def shards(devices, loads, shapes, mode_order, partner, taps, offsets, coef):
    rows, modes = shapes.shape
    hist, count = loads.shape[1], taps.shape[1]
    half, quarter = modes // 2, modes // 4
    me = lax.axis_index("frdm").astype(I32)
    core = me & 1
    forward = forward_table(hist)
    tap_forward, last = tap_table(hist, count)
    phase = phase_table(hist, hist - W - count + 1)
    inverse = inverse_table(hist, count)
    order, mates, offsets, taps = mode_order[None], partner[None], offsets[None], taps.T

    sent, lft = call(
        project_kernel, "project", [array(hist + EXTRA, half), array(hist, rows)],
        scalars(core), loads, forward, shapes, coef,
    )
    got = swap(sent, devices, 1)

    def respond(index, out):
        spec, own = call(
            spectrum_kernel, "spectrum", [array(hist, quarter, dtype=F32)] * 2,
            scalars(core * half + index * quarter), taps, offsets, order, tap_forward, last, phase, lft, shapes,
            scratch=[pltpu.VMEM((2 * (count - 1) + EXTRA, modes), BF)],
        )
        return call(respond_kernel, "respond", [out], scalars(index * quarter), own, got, spec, inverse, coef)[0]

    if devices == 16:
        y, z = (me >> 1) & 1, me >> 2
        size = modes // devices
        away = swap(respond(1 - y, array(W + EXTRA, quarter)), devices, 2)
        mine = respond(y, array(W, quarter, dtype=F32))
        keep, known, *parts = call(
            fold_kernel, "fold", [array(W, size, dtype=F32), array(EXTRA, LANES)] + [array(W + EXTRA, size)] * 3,
            scalars(z), mine, away, coef, got,
        )
        parts = [swap(part, devices, 4 * d) for d, part in zip((1, 2, 3), parts)]
        total = call(settle_kernel, "settle", [array(W, size)], keep, *parts, scalars=0)[0]
        place = scalars(me, (core * 8 + y * 4 + z) * size)
        mode_coef, pick = call(
            mixers_kernel, "mixers", [array(8, modes, dtype=F32), array(modes, modes)],
            place, order, mates, known, *parts, scratch=[pltpu.VMEM((8, modes), F32)],
        )
        resp = jnp.concatenate([total] + [swap(total, devices, 4 * d) for d in (1, 2, 3)], axis=1)
        resp = jnp.concatenate([resp, swap(resp, devices, 2)], axis=1)
    else:
        place = scalars(me, core * half)
        mode_coef, pick = call(
            plain_mixers_kernel, "mixers", [array(8, modes, dtype=F32), array(modes, modes)],
            place, order, mates, lax.all_gather(coef, "frdm", axis=1, tiled=True), scratch=[pltpu.VMEM((8, modes), F32)],
        )
        resp = jnp.concatenate([respond(q, array(W, quarter, dtype=F32)) for q in (0, 1)], axis=1)
        groups = [list(range(c, devices, 2)) for c in range(2)]
        resp = lax.psum(resp, "frdm", axis_index_groups=groups).astype(BF)
    other = swap(resp, devices, 1)
    near = call(mate_kernel, "mate", [array(W, modes, dtype=F32)], resp, pick, scalars=0)[0]
    return call(
        expand_kernel, "expand", [array(rows, W)], place, resp, other, near, mode_coef, pick, shapes,
        scratch=[pltpu.VMEM((W, modes), BF)],
    )[0]


def solution(mesh):
    in_specs = (P(("cases", "frdm"), None), P("frdm", None), P(), P(), P(), P(), P(None, "frdm"))
    out_specs = P(("cases", "frdm"), None)
    body = functools.partial(shards, mesh.shape["frdm"])
    return jax.shard_map(body, mesh=mesh, in_specs=in_specs, out_specs=out_specs, check_vma=False)
```

time: 668 us -> 92.6 us (0.14)
  local copies, waits for them, and re-layouts: 569 us -> 25.9 us
  matrix products: 56.7 us -> 0 us
  Pallas kernels: 0 us -> 36.7 us
  blocking collectives: 23 us -> 0 us
  waiting for transfers between devices: 0.07 us -> 16.5 us
  between operations: 13.7 us -> 0.18 us
  starting transfers between devices: 0.04 us -> 12.6 us
    gather x8 -> x0, local copies, waits for them, and re-layouts: 551 us -> none  [the longest x3 492 us: convolve(): kernel = jnp.take_along_axis(padded_taps, spread, axis=1)]
    conv_general_dilated x1 -> x0, matrix products: 46 us -> none  [convolve(): lax.conv_general_dilated(modal_forces[None], kernel[:, None, :], (1,), 'V...]
    pallas_call x0 -> x10, Pallas kernels: none -> 36.7 us  [call(): pl.pallas_call(kernel, in_specs=[smem] * scalars + [vmem] * (len(args) -...]
    unnamed x10 -> x48, local copies, waits for them, and re-layouts: 1.52 us -> 25.8 us
    all_gather x1 -> x0, blocking collectives: 23 us -> none  [shards(): lax.all_gather(coef, 'frdm', axis=1, tiled=True)]
    ppermute x0 -> x10, waiting for transfers between devices: none -> 16.5 us  [swap(): return lax.ppermute(x, 'frdm', [(i, i ^ bits) for i in range(devices)])]
    ppermute x0 -> x10, starting transfers between devices: none -> 12.6 us  [swap(): return lax.ppermute(x, 'frdm', [(i, i ^ bits) for i in range(devices)])]
    dot_general x2 -> x0, matrix products: 10.7 us -> none  [the longest x1 8.7 us: shards(): lax.dot_general(shapes, loads, (((0,), (0,)), ((), ())), preferred_elemen...]
  transfers between devices with their start and end apart: 2 -> 10, of which waited for: 0 -> 5; matrix products, arithmetic and copies ran while one was open for 81% -> 0% of each run, Pallas kernels for 0% -> 26%
where the time goes in v2:
time: 92.6 us; the launch traced here: 91.9 us
  Pallas kernels  36.7 us (40%)
  local copies, waits for them, and re-layouts  25.9 us (28%)
  waiting for transfers between devices  16.5 us (18%)
  starting transfers between devices  12.6 us (14%)
    pallas_call x10, Pallas kernels, call(): pl.pallas_call(kernel, in_specs=[smem] * scalars + [vmem] * (len(args) -...  36.7 us
    unnamed x48, local copies, waits for them, and re-layouts  25.8 us
    ppermute x10, waiting for transfers between devices, swap(): return lax.ppermute(x, 'frdm', [(i, i ^ bits) for i in range(devices)])  16.5 us
    ppermute x10, starting transfers between devices, swap(): return lax.ppermute(x, 'frdm', [(i, i ^ bits) for i in range(devices)])  12.6 us
  transfers between devices with their start and end apart: 10, of which 5 were waited for; matrix products, arithmetic and copies ran while one was open for 0% of the time, Pallas kernels for 26%

profile of v2, /device:TPU:0, one launch (start us, length us, event | category | flops | bytes accessed | tf_op | source)
XLA Modules:
  0.0 91.9 jit_solution(1605195816105779683)
XLA Ops:
  0.0 2.2 %copy-done = bf16[1024,2048]{1,0:T(8,128)(2,1)S(1)} copy-done((bf16[1024,2048]{1,0:T(8,128)(2,1)S(1)}, bf16[1024,2048]{1,0:T(8,128)(2,1)}, u32[]{:S(2)}) %copy-start) | copy-done | bytes 4194328
  2.2 1.9 %copy-done.12 = bf16[896,1792]{1,0:T(8,128)(2,1)S(1)} copy-done((bf16[896,1792]{1,0:T(8,128)(2,1)S(1)}, bf16[896,1792]{1,0:T(8,128)(2,1)}, u32[]{:S(2)}) %copy-start.12) | copy-done | bytes 3211288
  4.1 1.5 %copy-done.13 = bf16[1024,896]{1,0:T(8,128)(2,1)S(1)} copy-done((bf16[1024,896]{1,0:T(8,128)(2,1)S(1)}, bf16[1024,896]{1,0:T(8,128)(2,1)}, u32[]{:S(2)}) %copy-start.13) | copy-done | bytes 1835032
  5.6 0.7 copy-done.19
  6.3 6.7 %project.1 = (bf16[912,1024]{1,0:T(8,128)(2,1)}, bf16[896,1024]{1,0:T(8,128)(2,1)S(1)}) custom-call(s32[1]{0:T(128)} %bitcast.8.place, bf16[1024,896]{1,0:T(8,128)(2,1)S(1)} %copy-done.13, bf16[896,1792]{1,0:T(8,128)(2,1)S(1)} %copy-done.12, bf16[1024,2048]{1,0:T(8,128)(2,1)S(1)} %copy-done, bf16[2,128]{1,0:T(2,128)(2,1)S(1)} %copy-done.19), custom_call_target="tpu_custom_call" | custom-call | tf_op jit(solution)/shard_map/project/pallas_call | solution.py:63
  12.9 1.2 %copy-done.8 = bf16[896,1024]{1,0:T(8,128)(2,1)} copy-done((bf16[896,1024]{1,0:T(8,128)(2,1)}, bf16[896,1024]{1,0:T(8,128)(2,1)S(1)}, u32[]{:S(2)}) %copy-start.8) | copy-done | bytes 1835032
  14.1 0.5 collective-permute-start
  14.6 0.0 copy-done.18
  14.6 2.2 %copy-done.1 = bf16[1024,2048]{1,0:T(8,128)(2,1)S(1)} copy-done((bf16[1024,2048]{1,0:T(8,128)(2,1)S(1)}, bf16[1024,2048]{1,0:T(8,128)(2,1)}, u32[]{:S(2)}) %copy-start.1) | copy-done | bytes 4194328
  16.8 2.2 %copy-done.4 = f32[2048,513]{0,1:T(8,128)S(1)} copy-done((f32[2048,513]{0,1:T(8,128)S(1)}, f32[2048,513]{0,1:T(8,128)}, u32[]{:S(2)}) %copy-start.4) | copy-done | bytes 4202520
  19.0 1.8 %copy-done.6 = bf16[896,1536]{1,0:T(8,128)(2,1)S(1)} copy-done((bf16[896,1536]{1,0:T(8,128)(2,1)S(1)}, bf16[896,1536]{1,0:T(8,128)(2,1)}, u32[]{:S(2)}) %copy-start.6) | copy-done | bytes 2752536
  20.8 1.5 %copy-done.9 = bf16[896,1024]{1,0:T(8,128)(2,1)S(1)} copy-done((bf16[896,1024]{1,0:T(8,128)(2,1)S(1)}, bf16[896,1024]{1,0:T(8,128)(2,1)}, u32[]{:S(2)}) %copy-start.9) | copy-done | bytes 1835032
  22.3 1.0 %copy-done.15 = f32[896,128]{1,0:T(8,128)S(1)} copy-done((f32[896,128]{1,0:T(8,128)S(1)}, f32[896,128]{1,0:T(8,128)}, u32[]{:S(2)}) %copy-start.15) | copy-done | bytes 458776
  23.3 8.7 %spectrum.3 = (f32[896,512]{1,0:T(8,128)S(1)}, f32[896,512]{1,0:T(8,128)S(1)}) custom-call(s32[1]{0:T(128)} %bitcast.10.place, f32[513,2048]{1,0:T(8,128)S(1)} %bitcast.12, s32[1,2048]{1,0:T(1,128)S(1)} %bitcast.17, s32[1,2048]{1,0:T(1,128)S(1)} %bitcast.14, bf16[896,1536]{1,0:T(8,128)(2,1)S(1)} %copy-done.6, f32[896,128]{1,0:T(8,128)S(1)} %copy-done.15, ...), custom_call_target="tpu_custom_call" | custom-call | tf_op jit(solution)/shard_map/spectrum/pallas_call | solution.py:63
  32.0 0.0 collective-permute-done.other
  32.0 1.7 %respond.3 = bf16[272,512]{1,0:T(8,128)(2,1)} custom-call(s32[1]{0:T(128)} %bitcast.9.place, f32[896,512]{1,0:T(8,128)S(1)} %get-tuple-element.22.own, bf16[912,1024]{1,0:T(8,128)(2,1)S(1)} %collective-permute-done.other, f32[896,512]{1,0:T(8,128)S(1)} %get-tuple-element.23.spec, bf16[256,1792]{1,0:T(8,128)(2,1)S(1)} %copy-done.11, bf16[2,128]{1,0:T(2,128)(2,1)S(1)} %copy-done.20), custom_call_target="tpu_custom_call" | custom-call | tf_op jit(solution)/shard_map/respond/pallas_call | solution.py:63
  33.7 2.5 %collective-permute-start.1 = (bf16[272,512]{1,0:T(8,128)(2,1)}, bf16[272,512]{1,0:T(8,128)(2,1)S(1)}, u32[]{:S(2)}, u32[]{:S(2)}) collective-permute-start(bf16[272,512]{1,0:T(8,128)(2,1)} %respond.3), channel_id=1, source_target_pairs={{0,2},{1,3},{2,0},{3,1},{4,6},{5,7},{6,4},{7,5},{8,10},{9,11},{10,... | collective-permute-start | bytes 835592 | tf_op jit(solution)/shard_map/ppermute | solution.py:235
  36.2 2.2 %copy-done.2 = bf16[1024,2048]{1,0:T(8,128)(2,1)S(1)} copy-done((bf16[1024,2048]{1,0:T(8,128)(2,1)S(1)}, bf16[1024,2048]{1,0:T(8,128)(2,1)}, u32[]{:S(2)}) %copy-start.2) | copy-done | bytes 4194328
  38.4 2.2 %copy-done.5 = f32[2048,513]{0,1:T(8,128)S(1)} copy-done((f32[2048,513]{0,1:T(8,128)S(1)}, f32[2048,513]{0,1:T(8,128)}, u32[]{:S(2)}) %copy-start.5) | copy-done | bytes 4202520
  40.6 1.8 %copy-done.7 = bf16[896,1536]{1,0:T(8,128)(2,1)S(1)} copy-done((bf16[896,1536]{1,0:T(8,128)(2,1)S(1)}, bf16[896,1536]{1,0:T(8,128)(2,1)}, u32[]{:S(2)}) %copy-start.7) | copy-done | bytes 2752536
  42.4 1.5 %copy-done.10 = bf16[896,1024]{1,0:T(8,128)(2,1)S(1)} copy-done((bf16[896,1024]{1,0:T(8,128)(2,1)S(1)}, bf16[896,1024]{1,0:T(8,128)(2,1)}, u32[]{:S(2)}) %copy-start.10) | copy-done | bytes 1835032
  43.9 1.0 %copy-done.16 = f32[896,128]{1,0:T(8,128)S(1)} copy-done((f32[896,128]{1,0:T(8,128)S(1)}, f32[896,128]{1,0:T(8,128)}, u32[]{:S(2)}) %copy-start.16) | copy-done | bytes 458776
  44.9 8.9 %spectrum.2 = (f32[896,512]{1,0:T(8,128)S(1)}, f32[896,512]{1,0:T(8,128)S(1)}) custom-call(s32[1]{0:T(128)} %bitcast.4.place, f32[513,2048]{1,0:T(8,128)S(1)} %bitcast.13, s32[1,2048]{1,0:T(1,128)S(1)} %bitcast.18, s32[1,2048]{1,0:T(1,128)S(1)} %bitcast.15, bf16[896,1536]{1,0:T(8,128)(2,1)S(1)} %copy-done.7, f32[896,128]{1,0:T(8,128)S(1)} %copy-done.16, ...), custom_call_target="tpu_custom_call" | custom-call | tf_op jit(solution)/shard_map/spectrum/pallas_call | solution.py:63
  53.8 1.0 %respond.2.own = f32[256,512]{1,0:T(8,128)S(1)} custom-call(s32[1]{0:T(128)} %bitcast.3.place, f32[896,512]{1,0:T(8,128)S(1)} %get-tuple-element.19.own, bf16[912,1024]{1,0:T(8,128)(2,1)S(1)} %collective-permute-done.other, f32[896,512]{1,0:T(8,128)S(1)} %get-tuple-element.21.spec, bf16[256,1792]{1,0:T(8,128)(2,1)S(1)} %copy-done.11, ...), custom_call_target="tpu_custom_call" | custom-call | tf_op jit(solution)/shard_map/respond/pallas_call | solution.py:63
  54.8 0.0 collective-permute-done.1.got
  54.8 0.0 copy-start.21
  54.8 0.1 fold.1
  54.9 1.6 %collective-permute-start.2 = (bf16[272,128]{1,0:T(8,128)(2,1)S(1)}, bf16[272,128]{1,0:T(8,128)(2,1)S(1)}, u32[]{:S(2)}, u32[]{:S(2)}) collective-permute-start(bf16[272,128]{1,0:T(8,128)(2,1)S(1)} %get-tuple-element.25), channel_id=1, source_target_pairs={{0,4},{1,5},{2,6},{3,7},{4,0},{5,1},{6,2},{7,3},{8,12},{9,13},{10,... | collective-permute-start | bytes 208904 | tf_op jit(solution)/shard_map/ppermute | solution.py:235
  56.5 2.6 %collective-permute-start.3 = (bf16[272,128]{1,0:T(8,128)(2,1)S(1)}, bf16[272,128]{1,0:T(8,128)(2,1)S(1)}, u32[]{:S(2)}, u32[]{:S(2)}) collective-permute-start(bf16[272,128]{1,0:T(8,128)(2,1)S(1)} %get-tuple-element.26), channel_id=1, source_target_pairs={{0,8},{1,9},{2,10},{3,11},{4,12},{5,13},{6,14},{7,15},{8,0},{9,1},... | collective-permute-start | bytes 208904 | tf_op jit(solution)/shard_map/ppermute | solution.py:235
  59.1 0.2 collective-permute-start.4
  59.3 0.0 collective-permute-done.2.first
  59.4 5.0 %collective-permute-done.3.second = bf16[272,128]{1,0:T(8,128)(2,1)S(1)} collective-permute-done((bf16[272,128]{1,0:T(8,128)(2,1)S(1)}, bf16[272,128]{1,0:T(8,128)(2,1)S(1)}, u32[]{:S(2)}, u32[]{:S(2)}) %collective-permute-start.3) | collective-permute-done | bytes 69664 | tf_op jit(solution)/shard_map/ppermute | solution.py:235
  64.4 1.0 %collective-permute-done.4.third = bf16[272,128]{1,0:T(8,128)(2,1)S(1)} collective-permute-done((bf16[272,128]{1,0:T(8,128)(2,1)S(1)}, bf16[272,128]{1,0:T(8,128)(2,1)S(1)}, u32[]{:S(2)}, u32[]{:S(2)}) %collective-permute-start.4) | collective-permute-done | bytes 69664 | tf_op jit(solution)/shard_map/ppermute | solution.py:235
  65.4 2.4 %collective-permute-start.7 = (bf16[256,128]{1,0:T(8,128)(2,1)S(1)}, bf16[256,128]{1,0:T(8,128)(2,1)S(1)}, u32[]{:S(2)}, u32[]{:S(2)}) collective-permute-start(bf16[256,128]{1,0:T(8,128)(2,1)S(1)} %settle.1), channel_id=1, source_target_pairs={{0,12},{1,13},{2,14},{3,15},{4,8},{5,9},{6,10},{7,11},{8,4},{9,5},... | collective-permute-start | bytes 196616 | tf_op jit(solution)/shard_map/ppermute | solution.py:235
  67.8 0.4 collective-permute-start.6
  68.1 1.7 %collective-permute-start.5 = (bf16[256,128]{1,0:T(8,128)(2,1)S(1)}, bf16[256,128]{1,0:T(8,128)(2,1)S(1)}, u32[]{:S(2)}, u32[]{:S(2)}) collective-permute-start(bf16[256,128]{1,0:T(8,128)(2,1)S(1)} %settle.1), channel_id=1, source_target_pairs={{0,4},{1,5},{2,6},{3,7},{4,0},{5,1},{6,2},{7,3},{8,12},{9,13},{10,... | collective-permute-start | bytes 196616 | tf_op jit(solution)/shard_map/ppermute | solution.py:235
  69.9 1.9 %collective-permute-done.7 = bf16[256,128]{1,0:T(8,128)(2,1)S(1)} collective-permute-done((bf16[256,128]{1,0:T(8,128)(2,1)S(1)}, bf16[256,128]{1,0:T(8,128)(2,1)S(1)}, u32[]{:S(2)}, u32[]{:S(2)}) %collective-permute-start.7) | collective-permute-done | bytes 65568 | tf_op jit(solution)/shard_map/ppermute | solution.py:235
  71.7 2.1 %collective-permute-done.6 = bf16[256,128]{1,0:T(8,128)(2,1)S(1)} collective-permute-done((bf16[256,128]{1,0:T(8,128)(2,1)S(1)}, bf16[256,128]{1,0:T(8,128)(2,1)S(1)}, u32[]{:S(2)}, u32[]{:S(2)}) %collective-permute-start.6) | collective-permute-done | bytes 65568 | tf_op jit(solution)/shard_map/ppermute | solution.py:235
  73.8 0.0 collective-permute-done.5
  73.9 0.6 collective-permute-start.8
  74.6 6.6 %collective-permute-done.8 = bf16[256,512]{1,0:T(8,128)(2,1)S(1)} collective-permute-done((bf16[256,512]{1,0:T(8,128)(2,1)S(1)}, bf16[256,512]{1,0:T(8,128)(2,1)S(1)}, u32[]{:S(2)}, u32[]{:S(2)}) %collective-permute-start.8) | collective-permute-done | bytes 262176 | tf_op jit(solution)/shard_map/ppermute | solution.py:235
  81.2 0.1 collective-permute-start.9
  81.3 0.1 pad_add_fusion.place
  81.3 4.0 %mixers.1 = (f32[8,2048]{1,0:T(8,128)S(1)}, bf16[2048,2048]{1,0:T(8,128)(2,1)S(1)}) custom-call(s32[2]{0:T(128)S(1)} %pad_add_fusion.place, s32[1,2048]{1,0:T(1,128)S(1)} %bitcast.16, s32[1,2048]{1,0:T(1,128)S(1)} %bitcast.19, bf16[16,128]{1,0:T(8,128)(2,1)S(1)} %get-tuple-element.28.known, bf16[272,128]{1,0:T(8,128)(2,1)S(1)} %collective-permute-done.2.first, ...), custom_call_target="tpu_custom_call" | custom-call | tf_op jit(solution)/shard_map/mixers/pallas_call | solution.py:63
  85.3 1.3 %mate.1.mates = f32[256,2048]{1,0:T(8,128)S(1)} custom-call(bf16[256,1024]{1,0:T(8,128)(2,1)S(1)} %constant_dynamic-update-slice_fusion.resp, bf16[2048,2048]{1,0:T(8,128)(2,1)S(1)} %get-tuple-element.29.pick), custom_call_target="tpu_custom_call" | custom-call | tf_op jit(solution)/shard_map/mate/pallas_call | solution.py:63
  86.6 0.0 collective-permute-done.9.other
  86.6 0.9 copy-done.3
  87.6 4.4 %expand.1 = bf16[1024,256]{1,0:T(8,128)(2,1)} custom-call(s32[2]{0:T(128)S(1)} %pad_add_fusion.place, bf16[256,1024]{1,0:T(8,128)(2,1)S(1)} %constant_dynamic-update-slice_fusion.resp, bf16[256,1024]{1,0:T(8,128)(2,1)S(1)} %collective-permute-done.9.other, f32[256,2048]{1,0:T(8,128)S(1)} %mate.1.mates, f32[8,2048]{1,0:T(8,128)S(1)} %get-tuple-element.30.coef, ...), custom_call_target="tpu_custom_call" | custom-call | tf_op jit(solution)/shard_map/expand/pallas_call | solution.py:63
  (33 shorter events, 0.2 us)
Async XLA Ops:
  0.0 2.2 %copy-start = (bf16[1024,2048]{1,0:T(8,128)(2,1)S(1)}, bf16[1024,2048]{1,0:T(8,128)(2,1)}, u32[]{:S(2)}) copy-start(bf16[1024,2048]{1,0:T(8,128)(2,1)} %shapes.7) | copy-start | bytes 12582916
  2.2 1.9 %copy-start.12 = (bf16[896,1792]{1,0:T(8,128)(2,1)S(1)}, bf16[896,1792]{1,0:T(8,128)(2,1)}, u32[]{:S(2)}) copy-start(bf16[896,1792]{1,0:T(8,128)(2,1)} %constant.28.clone.table) | copy-start | bytes 9633796
  4.1 1.5 %copy-start.13 = (bf16[1024,896]{1,0:T(8,128)(2,1)S(1)}, bf16[1024,896]{1,0:T(8,128)(2,1)}, u32[]{:S(2)}) copy-start(bf16[1024,896]{1,0:T(8,128)(2,1)} %loads.1) | copy-start | bytes 5505028
  5.6 0.7 copy-start.19
  6.3 8.3 %copy-start.14 = (bf16[896,256]{1,0:T(8,128)(2,1)S(1)}, bf16[896,256]{1,0:T(8,128)(2,1)}, u32[]{:S(2)}) copy-start(bf16[896,256]{1,0:T(8,128)(2,1)} %constant.31.clone.phase) | copy-start | bytes 1376260
  6.3 8.3 %copy-start.17 = (s32[2048]{0:T(1024)S(1)}, s32[2048]{0:T(1024)}, u32[]{:S(2)}) copy-start(s32[2048]{0:T(1024)} %param.14) | copy-start | bytes 24580
  6.3 8.4 %copy-start.18 = (s32[2048]{0:T(1024)S(1)}, s32[2048]{0:T(1024)}, u32[]{:S(2)}) copy-start(s32[2048]{0:T(1024)} %param.17) | copy-start | bytes 24580
  12.9 1.2 %copy-start.8 = (bf16[896,1024]{1,0:T(8,128)(2,1)}, bf16[896,1024]{1,0:T(8,128)(2,1)S(1)}, u32[]{:S(2)}) copy-start(bf16[896,1024]{1,0:T(8,128)(2,1)S(1)} %get-tuple-element.18.lft) | copy-start | bytes 5505028
  14.1 17.8 %collective-permute-start = (bf16[912,1024]{1,0:T(8,128)(2,1)}, bf16[912,1024]{1,0:T(8,128)(2,1)S(1)}, u32[]{:S(2)}, u32[]{:S(2)}) collective-permute-start(bf16[912,1024]{1,0:T(8,128)(2,1)} %get-tuple-element.20), channel_id=1, source_target_pairs={{0,1},{1,0},{2,3},{3,2},{4,5},{5,4},{6,7},{7,6},{8,9},{9,8},{10,11... | collective-permute-start | bytes 5603336 | tf_op jit(solution)/shard_map/ppermute | solution.py:235
  14.6 2.2 %copy-start.1 = (bf16[1024,2048]{1,0:T(8,128)(2,1)S(1)}, bf16[1024,2048]{1,0:T(8,128)(2,1)}, u32[]{:S(2)}) copy-start(bf16[1024,2048]{1,0:T(8,128)(2,1)} %shapes.7) | copy-start | bytes 12582916
  16.8 2.2 %copy-start.4 = (f32[2048,513]{0,1:T(8,128)S(1)}, f32[2048,513]{0,1:T(8,128)}, u32[]{:S(2)}) copy-start(f32[2048,513]{0,1:T(8,128)} %param.16) | copy-start | bytes 12607492
  19.0 1.8 %copy-start.6 = (bf16[896,1536]{1,0:T(8,128)(2,1)S(1)}, bf16[896,1536]{1,0:T(8,128)(2,1)}, u32[]{:S(2)}) copy-start(bf16[896,1536]{1,0:T(8,128)(2,1)} %constant.29.clone.table) | copy-start | bytes 8257540
  20.8 1.5 %copy-start.9 = (bf16[896,1024]{1,0:T(8,128)(2,1)S(1)}, bf16[896,1024]{1,0:T(8,128)(2,1)}, u32[]{:S(2)}) copy-start(bf16[896,1024]{1,0:T(8,128)(2,1)} %copy-done.8) | copy-start | bytes 5505028
  22.3 1.0 %copy-start.15 = (f32[896,128]{1,0:T(8,128)S(1)}, f32[896,128]{1,0:T(8,128)}, u32[]{:S(2)}) copy-start(f32[896,128]{1,0:T(8,128)} %constant.30.clone.last) | copy-start | bytes 1376260
  23.3 8.7 %copy-start.11 = (bf16[256,1792]{1,0:T(8,128)(2,1)S(1)}, bf16[256,1792]{1,0:T(8,128)(2,1)}, u32[]{:S(2)}) copy-start(bf16[256,1792]{1,0:T(8,128)(2,1)} %constant.32.clone.inverse) | copy-start | bytes 2752516
  23.3 8.7 %copy-start.20 = (bf16[2,128]{1,0:T(2,128)(2,1)S(1)}, bf16[2,128]{1,0:T(2,128)(2,1)}, u32[]{:S(2)}) copy-start(bf16[2,128]{1,0:T(2,128)(2,1)} %coef.7) | copy-start | bytes 1540
  33.7 21.0 %collective-permute-start.1 = (bf16[272,512]{1,0:T(8,128)(2,1)}, bf16[272,512]{1,0:T(8,128)(2,1)S(1)}, u32[]{:S(2)}, u32[]{:S(2)}) collective-permute-start(bf16[272,512]{1,0:T(8,128)(2,1)} %respond.3), channel_id=1, source_target_pairs={{0,2},{1,3},{2,0},{3,1},{4,6},{5,7},{6,4},{7,5},{8,10},{9,11},{10,... | collective-permute-start | bytes 835592 | tf_op jit(solution)/shard_map/ppermute | solution.py:235
  36.2 2.2 %copy-start.2 = (bf16[1024,2048]{1,0:T(8,128)(2,1)S(1)}, bf16[1024,2048]{1,0:T(8,128)(2,1)}, u32[]{:S(2)}) copy-start(bf16[1024,2048]{1,0:T(8,128)(2,1)} %shapes.7) | copy-start | bytes 12582916
  38.4 2.2 %copy-start.5 = (f32[2048,513]{0,1:T(8,128)S(1)}, f32[2048,513]{0,1:T(8,128)}, u32[]{:S(2)}) copy-start(f32[2048,513]{0,1:T(8,128)} %param.16) | copy-start | bytes 12607492
  40.6 1.8 %copy-start.7 = (bf16[896,1536]{1,0:T(8,128)(2,1)S(1)}, bf16[896,1536]{1,0:T(8,128)(2,1)}, u32[]{:S(2)}) copy-start(bf16[896,1536]{1,0:T(8,128)(2,1)} %constant.29.clone.table) | copy-start | bytes 8257540
  42.4 1.5 %copy-start.10 = (bf16[896,1024]{1,0:T(8,128)(2,1)S(1)}, bf16[896,1024]{1,0:T(8,128)(2,1)}, u32[]{:S(2)}) copy-start(bf16[896,1024]{1,0:T(8,128)(2,1)} %copy-done.8) | copy-start | bytes 5505028
  43.9 1.0 %copy-start.16 = (f32[896,128]{1,0:T(8,128)S(1)}, f32[896,128]{1,0:T(8,128)}, u32[]{:S(2)}) copy-start(f32[896,128]{1,0:T(8,128)} %constant.30.clone.last) | copy-start | bytes 1376260
  54.8 26.6 %copy-start.21 = (s32[2048]{0:T(1024)S(1)}, s32[2048]{0:T(1024)}, u32[]{:S(2)}) copy-start(s32[2048]{0:T(1024)} %param.15) | copy-start | bytes 24580
  54.9 4.5 %collective-permute-start.2 = (bf16[272,128]{1,0:T(8,128)(2,1)S(1)}, bf16[272,128]{1,0:T(8,128)(2,1)S(1)}, u32[]{:S(2)}, u32[]{:S(2)}) collective-permute-start(bf16[272,128]{1,0:T(8,128)(2,1)S(1)} %get-tuple-element.25), channel_id=1, source_target_pairs={{0,4},{1,5},{2,6},{3,7},{4,0},{5,1},{6,2},{7,3},{8,12},{9,13},{10,... | collective-permute-start | bytes 208904 | tf_op jit(solution)/shard_map/ppermute | solution.py:235
  56.5 7.8 %collective-permute-start.3 = (bf16[272,128]{1,0:T(8,128)(2,1)S(1)}, bf16[272,128]{1,0:T(8,128)(2,1)S(1)}, u32[]{:S(2)}, u32[]{:S(2)}) collective-permute-start(bf16[272,128]{1,0:T(8,128)(2,1)S(1)} %get-tuple-element.26), channel_id=1, source_target_pairs={{0,8},{1,9},{2,10},{3,11},{4,12},{5,13},{6,14},{7,15},{8,0},{9,1},... | collective-permute-start | bytes 208904 | tf_op jit(solution)/shard_map/ppermute | solution.py:235
  59.1 6.2 %collective-permute-start.4 = (bf16[272,128]{1,0:T(8,128)(2,1)S(1)}, bf16[272,128]{1,0:T(8,128)(2,1)S(1)}, u32[]{:S(2)}, u32[]{:S(2)}) collective-permute-start(bf16[272,128]{1,0:T(8,128)(2,1)S(1)} %get-tuple-element.27), channel_id=1, source_target_pairs={{0,12},{1,13},{2,14},{3,15},{4,8},{5,9},{6,10},{7,11},{8,4},{9,5},... | collective-permute-start | bytes 208904 | tf_op jit(solution)/shard_map/ppermute | solution.py:235
  65.4 6.4 %collective-permute-start.7 = (bf16[256,128]{1,0:T(8,128)(2,1)S(1)}, bf16[256,128]{1,0:T(8,128)(2,1)S(1)}, u32[]{:S(2)}, u32[]{:S(2)}) collective-permute-start(bf16[256,128]{1,0:T(8,128)(2,1)S(1)} %settle.1), channel_id=1, source_target_pairs={{0,12},{1,13},{2,14},{3,15},{4,8},{5,9},{6,10},{7,11},{8,4},{9,5},... | collective-permute-start | bytes 196616 | tf_op jit(solution)/shard_map/ppermute | solution.py:235
  67.8 6.0 %collective-permute-start.6 = (bf16[256,128]{1,0:T(8,128)(2,1)S(1)}, bf16[256,128]{1,0:T(8,128)(2,1)S(1)}, u32[]{:S(2)}, u32[]{:S(2)}) collective-permute-start(bf16[256,128]{1,0:T(8,128)(2,1)S(1)} %settle.1), channel_id=1, source_target_pairs={{0,8},{1,9},{2,10},{3,11},{4,12},{5,13},{6,14},{7,15},{8,0},{9,1},... | collective-permute-start | bytes 196616 | tf_op jit(solution)/shard_map/ppermute | solution.py:235
  68.1 5.7 %collective-permute-start.5 = (bf16[256,128]{1,0:T(8,128)(2,1)S(1)}, bf16[256,128]{1,0:T(8,128)(2,1)S(1)}, u32[]{:S(2)}, u32[]{:S(2)}) collective-permute-start(bf16[256,128]{1,0:T(8,128)(2,1)S(1)} %settle.1), channel_id=1, source_target_pairs={{0,4},{1,5},{2,6},{3,7},{4,0},{5,1},{6,2},{7,3},{8,12},{9,13},{10,... | collective-permute-start | bytes 196616 | tf_op jit(solution)/shard_map/ppermute | solution.py:235
  73.9 7.3 %collective-permute-start.8 = (bf16[256,512]{1,0:T(8,128)(2,1)S(1)}, bf16[256,512]{1,0:T(8,128)(2,1)S(1)}, u32[]{:S(2)}, u32[]{:S(2)}) collective-permute-start(bf16[256,512]{1,0:T(8,128)(2,1)S(1)} %pad_maximum_fusion), channel_id=1, source_target_pairs={{0,2},{1,3},{2,0},{3,1},{4,6},{5,7},{6,4},{7,5},{8,10},{9,11},{10,... | collective-permute-start | bytes 786440 | tf_op jit(solution)/shard_map/ppermute | solution.py:235
  81.2 5.5 %collective-permute-start.9 = (bf16[256,1024]{1,0:T(8,128)(2,1)S(1)}, bf16[256,1024]{1,0:T(8,128)(2,1)S(1)}, u32[]{:S(2)}, u32[]{:S(2)}) collective-permute-start(bf16[256,1024]{1,0:T(8,128)(2,1)S(1)} %constant_dynamic-update-slice_fusion.resp), channel_id=1, source_target_pairs={{0,1},{1,0},{2,3},{3,2},{4,5},{5,4},{6,7},{7,6},{8,9},{9,8},{10,11... | collective-permute-start | bytes 1572872 | tf_op jit(solution)/shard_map/ppermute | solution.py:235
  85.3 2.2 %copy-start.3 = (bf16[1024,2048]{1,0:T(8,128)(2,1)S(1)}, bf16[1024,2048]{1,0:T(8,128)(2,1)}, u32[]{:S(2)}) copy-start(bf16[1024,2048]{1,0:T(8,128)(2,1)} %shapes.7) | copy-start | bytes 12582916

commit v3 on v2

--- a/solution.py
+++ b/solution.py
@@ -42,9 +42,8 @@
 def tap_table(hist, taps):
     cos, sin = turns(hist // 2, np.arange(taps))
     table = np.concatenate([cos, -sin])
-    high, low = split(table[:, :-1])
     last = np.repeat(table[:, -1:], LANES, axis=1).astype(np.float32)
-    return np.concatenate([high, low, high], axis=1), last
+    return np.concatenate(split(table[:, :-1]), axis=1), last
 
 
 def phase_table(hist, delay):
@@ -57,12 +56,18 @@
     return np.concatenate(split(np.concatenate([cos, -sin]).T * (2.0 / hist)), axis=1)
 
 
-def call(kernel, name, out_shape, *args, scalars=1, scratch=(), limit=20):
+def call(kernel, name, out_shape, *args, scalars=1, far=(), scratch=(), limit=16):
     vmem = pl.BlockSpec(memory_space=pltpu.VMEM)
     smem = pl.BlockSpec(memory_space=pltpu.SMEM)
+    hbm = pl.BlockSpec(memory_space=pltpu.HBM)
+    places = [smem] * scalars + [vmem] * (len(args) - scalars)
+    args = list(args)
+    for i in far:
+        places[i] = hbm
+        args[i] = pltpu.with_memory_space_constraint(jnp.asarray(args[i]), pltpu.HBM)
     return pl.pallas_call(
         kernel,
-        in_specs=[smem] * scalars + [vmem] * (len(args) - scalars),
+        in_specs=places,
         out_specs=[vmem] * len(out_shape),
         out_shape=out_shape,
         scratch_shapes=list(scratch),
@@ -75,6 +80,10 @@
     return jax.ShapeDtypeStruct(shape, dtype)
 
 
+def near(*shape, dtype=BF):
+    return pltpu.VMEM(shape, dtype)
+
+
 def block(start, size):
     return pl.ds(pl.multiple_of(start, LANES), size)
 
@@ -83,42 +92,62 @@
     return mask.astype(F32).astype(BF)
 
 
-def project_kernel(place, loads, table, shapes, coef, sent, lft):
+def project_kernel(
+    place, loads_far, forward_far, shapes_far, taps_far, table_far, last_far, phase_far, inverse_far, offsets, coef,
+    sent, lft, shapes, stack, table, last, phase, inverse, loads, forward, taps, sems,
+):
     rows, half = loads.shape[0], sent.shape[1]
     hist = lft.shape[0]
+    core = place[0]
+    far, own = block((1 - core) * half, half), block(core * half, half)
+    pairs = [
+        (forward_far, forward),
+        (loads_far, loads),
+        (shapes_far.at[:, far], shapes.at[:, far]),
+        (taps_far, taps),
+        (table_far, table),
+        (shapes_far.at[:, own], shapes.at[:, own]),
+        (last_far, last),
+        (phase_far, phase),
+        (inverse_far, inverse),
+    ]
+    copies = [pltpu.make_async_copy(a, b, sems.at[i]) for i, (a, b) in enumerate(pairs)]
+    for copy in copies:
+        copy.start()
+    copies[0].wait()
+    copies[1].wait()
     for r in range(0, rows, 256):
         part = loads[r : r + 256, :]
-        lft[:, r : r + 256] = dot(table[...], jnp.concatenate([part, part], axis=1), NT).astype(BF)
-    base = (1 - place[0]) * half
+        lft[:, r : r + 256] = dot(forward[...], jnp.concatenate([part, part], axis=1), NT).astype(BF)
+    copies[2].wait()
+    copies[3].wait()
+    count = taps.shape[0] - 1
     for c in range(0, half, 256):
-        sent[:hist, c : c + 256] = dot(lft[...], shapes[:, block(base + c, 256)]).astype(BF)
+        sent[:hist, c : c + 256] = dot(lft[...], shapes[:, block((1 - core) * half + c, 256)]).astype(BF)
     sent[hist:, :] = jnp.zeros((EXTRA, half), BF)
     per = coef.shape[1]
     sent[hist : hist + 2, :per] = coef[...]
-
-
-def spectrum(base, taps, offsets, order, table, last, phase, stack, put, width):
-    count = taps.shape[0] - 1
+    for r in range(0, count, 64):
+        stack[r : r + 64, :] = taps[r : r + 64, :].astype(BF)
+    index = lax.broadcasted_iota(I32, (EXTRA, taps.shape[1]), 0)
+    end = taps[count : count + 1, :]
+    tail = jnp.where(index == 0, end, jnp.where(index == 1, offsets[...].astype(F32), 0.0))
+    stack[count:, :] = tail.astype(BF)
+    for copy in copies[4:]:
+        copy.wait()
+
+
+def spectrum(base, stack, order, table, last, phase, put, width):
+    count = stack.shape[0] - EXTRA
     half = table.shape[0] // 2
-    for r in range(0, count, 64):
-        row = taps[r : r + 64, :]
-        high = row.astype(BF)
-        stack[r : r + 64, :] = high
-        stack[count + r : count + r + 64, :] = (row - high.astype(F32)).astype(BF)
-    row = taps[count : count + 1, :]
-    high = row.astype(BF).astype(F32)
-    index = lax.broadcasted_iota(I32, (EXTRA, taps.shape[1]), 0)
-    tail = jnp.where(index == 0, high, jnp.where(index == 1, row - high, jnp.where(index == 2, offsets[...].astype(F32), 0.0)))
-    stack[2 * count :, :] = tail.astype(BF)
     delay = phase.shape[1] // 2
     for c in range(0, width, 256):
-        mode = lax.broadcasted_iota(I32, (256, taps.shape[1]), 0) + (base + c)
+        mode = lax.broadcasted_iota(I32, (256, stack.shape[1]), 0) + (base + c)
         picked = dot(stack[...], hot(mode == order[...]), NT)
-        main = picked[: 2 * count].astype(BF)
-        tail = picked[2 * count :]
-        end = tail[0:1] + tail[1:2]
-        offset = tail[2:3].astype(I32)
-        resp = dot(table[...], jnp.concatenate([main[:count], main], axis=0))
+        main = picked[:count].astype(BF)
+        tail = picked[count:]
+        end, offset = tail[0:1], tail[1:2].astype(I32)
+        resp = dot(table[...], jnp.concatenate([main, main], axis=0))
         resp = resp + jnp.tile(last[...], (1, 2)) * end
         which = hot(lax.broadcasted_iota(I32, (delay, 256), 0) + 1 == offset)
         turn = dot(phase[...], jnp.concatenate([which, which], axis=0))
@@ -127,7 +156,7 @@
         put(c, cos * re - sin * im, sin * re + cos * im)
 
 
-def spectrum_kernel(place, taps, offsets, order, table, last, phase, lft, shapes, spec, own, stack):
+def spectrum_kernel(place, stack, order, table, last, phase, lft, shapes, spec, own):
     width = spec.shape[1]
     half = spec.shape[0] // 2
     base = place[0]
@@ -138,24 +167,38 @@
         spec[:half, c : c + 256] = re
         spec[half:, c : c + 256] = im
 
-    spectrum(base, taps, offsets, order, table, last, phase, stack, put, width)
+    spectrum(base, stack, order, table, last, phase, put, width)
+
+
+def impose(total, tre, tim, inverse):
+    half = tre.shape[0]
+    re, im = total[:half], total[half:]
+    product = jnp.concatenate([re * tre - im * tim, re * tim + im * tre], axis=0).astype(BF)
+    return dot(inverse[...], jnp.concatenate([product, product], axis=0))
+
+
+def whole_kernel(place, stack, order, table, last, phase, lft, shapes, other, inverse, out):
+    hist = lft.shape[0]
+    base, start = place[0], place[1]
+
+    def put(c, re, im):
+        total = dot(lft[...], shapes[:, block(base + c, 256)]) + other[:hist, block(start + c, 256)].astype(F32)
+        out[:, c : c + 256] = impose(total, re, im, inverse)
+
+    spectrum(base, stack, order, table, last, phase, put, out.shape[1])
 
 
 def respond_kernel(place, own, other, spec, inverse, coef, out):
     hist, width = own.shape
     half = hist // 2
-    start = place[0]
+    start = place[1]
     for c in range(0, width, 256):
         total = own[:, c : c + 256] + other[:hist, block(start + c, 256)].astype(F32)
-        re, im = total[:half], total[half:]
-        tre, tim = spec[:half, c : c + 256], spec[half:, c : c + 256]
-        product = jnp.concatenate([re * tre - im * tim, re * tim + im * tre], axis=0).astype(BF)
-        result = dot(inverse[...], jnp.concatenate([product, product], axis=0))
-        out[:W, c : c + 256] = result.astype(out.dtype)
-    if out.shape[0] > W:
-        out[W:, :] = jnp.zeros((EXTRA, width), BF)
-        out[W : W + 2, :LANES] = coef[...]
-        out[W + 2 : W + 4, :LANES] = other[hist : hist + 2, :LANES]
+        result = impose(total, spec[:half, c : c + 256], spec[half:, c : c + 256], inverse)
+        out[:W, c : c + 256] = result.astype(BF)
+    out[W:, :] = jnp.zeros((EXTRA, width), BF)
+    out[W : W + 2, :LANES] = coef[...]
+    out[W + 2 : W + 4, :LANES] = other[hist : hist + 2, :LANES]
 
 
 def fold_kernel(place, own, got, coef, other, keep, known, first, second, third):
@@ -181,7 +224,7 @@
     out[...] = total.astype(BF)
 
 
-def mixers_kernel(place, order, partner, known, first, second, third, coef, pick, held):
+def mixers_kernel(place, order, partner, known, first, second, third, after, coef, pick, held):
     me, mask = place[0], place[1]
     modes = order.shape[1]
     held[...] = jnp.zeros(held.shape, F32)
@@ -207,6 +250,12 @@
     held[...] = jnp.zeros(held.shape, F32)
     held[0:2, :] = every[...].astype(F32)
     mixers(order, partner, place[1], held, coef, pick)
+
+
+def join_kernel(quarter, got, before, out):
+    width = quarter.shape[1]
+    out[:, :width] = quarter[...]
+    out[:, width:] = got[...]
 
 
 def mate_kernel(resp, pick, out):
@@ -251,51 +300,63 @@
     inverse = inverse_table(hist, count)
     order, mates, offsets, taps = mode_order[None], partner[None], offsets[None], taps.T
 
-    sent, lft = call(
-        project_kernel, "project", [array(hist + EXTRA, half), array(hist, rows)],
-        scalars(core), loads, forward, shapes, coef,
+    sent, lft, shapes, stack, tap_forward, last, phase, inverse = call(
+        project_kernel, "project",
+        [near(hist + EXTRA, half), near(hist, rows), near(rows, modes), near(count - 1 + EXTRA, modes)]
+        + [near(*tap_forward.shape), near(*last.shape, dtype=F32), near(*phase.shape), near(*inverse.shape)],
+        scalars(core), loads, forward, shapes, taps, tap_forward, last, phase, inverse, offsets, coef,
+        far=range(1, 9),
+        scratch=[
+            pltpu.VMEM(loads.shape, BF), pltpu.VMEM(forward.shape, BF), pltpu.VMEM(taps.shape, F32),
+            pltpu.SemaphoreType.DMA((9,)),
+        ],
+        limit=24,
     )
     got = swap(sent, devices, 1)
-
-    def respond(index, out):
-        spec, own = call(
-            spectrum_kernel, "spectrum", [array(hist, quarter, dtype=F32)] * 2,
-            scalars(core * half + index * quarter), taps, offsets, order, tap_forward, last, phase, lft, shapes,
-            scratch=[pltpu.VMEM((2 * (count - 1) + EXTRA, modes), BF)],
-        )
-        return call(respond_kernel, "respond", [out], scalars(index * quarter), own, got, spec, inverse, coef)[0]
+    common = (stack, order, tap_forward, last, phase, lft, shapes)
+
+    def quarter_of(index):
+        return scalars(core * half + index * quarter, index * quarter)
+
+    def respond(index):
+        return call(whole_kernel, "whole", [array(W, quarter, dtype=F32)], quarter_of(index), *common, got, inverse)[0]
 
     if devices == 16:
         y, z = (me >> 1) & 1, me >> 2
         size = modes // devices
-        away = swap(respond(1 - y, array(W + EXTRA, quarter)), devices, 2)
-        mine = respond(y, array(W, quarter, dtype=F32))
+        spec, own = call(
+            spectrum_kernel, "spectrum", [near(hist, quarter, dtype=F32)] * 2, quarter_of(1 - y), *common
+        )
+        away = call(
+            respond_kernel, "respond", [array(W + EXTRA, quarter)], quarter_of(1 - y), own, got, spec, inverse, coef
+        )[0]
+        away = swap(away, devices, 2)
         keep, known, *parts = call(
             fold_kernel, "fold", [array(W, size, dtype=F32), array(EXTRA, LANES)] + [array(W + EXTRA, size)] * 3,
-            scalars(z), mine, away, coef, got,
+            scalars(z), respond(y), away, coef, got,
         )
         parts = [swap(part, devices, 4 * d) for d, part in zip((1, 2, 3), parts)]
         total = call(settle_kernel, "settle", [array(W, size)], keep, *parts, scalars=0)[0]
+        resp = jnp.concatenate([total] + [swap(total, devices, 4 * d) for d in (1, 2, 3)], axis=1)
         place = scalars(me, (core * 8 + y * 4 + z) * size)
         mode_coef, pick = call(
-            mixers_kernel, "mixers", [array(8, modes, dtype=F32), array(modes, modes)],
-            place, order, mates, known, *parts, scratch=[pltpu.VMEM((8, modes), F32)],
+            mixers_kernel, "mixers", [array(8, modes, dtype=F32), near(modes, modes)],
+            place, order, mates, known, *parts, resp, scratch=[pltpu.VMEM((8, modes), F32)],
         )
-        resp = jnp.concatenate([total] + [swap(total, devices, 4 * d) for d in (1, 2, 3)], axis=1)
-        resp = jnp.concatenate([resp, swap(resp, devices, 2)], axis=1)
+        resp = call(join_kernel, "join", [array(W, half)], resp, swap(resp, devices, 2), mode_coef, scalars=0)[0]
     else:
         place = scalars(me, core * half)
         mode_coef, pick = call(
-            plain_mixers_kernel, "mixers", [array(8, modes, dtype=F32), array(modes, modes)],
+            plain_mixers_kernel, "mixers", [array(8, modes, dtype=F32), near(modes, modes)],
             place, order, mates, lax.all_gather(coef, "frdm", axis=1, tiled=True), scratch=[pltpu.VMEM((8, modes), F32)],
         )
-        resp = jnp.concatenate([respond(q, array(W, quarter, dtype=F32)) for q in (0, 1)], axis=1)
+        resp = jnp.concatenate([respond(q) for q in (0, 1)], axis=1)
         groups = [list(range(c, devices, 2)) for c in range(2)]
         resp = lax.psum(resp, "frdm", axis_index_groups=groups).astype(BF)
     other = swap(resp, devices, 1)
-    near = call(mate_kernel, "mate", [array(W, modes, dtype=F32)], resp, pick, scalars=0)[0]
+    mine = call(mate_kernel, "mate", [array(W, modes, dtype=F32)], resp, pick, scalars=0)[0]
     return call(
-        expand_kernel, "expand", [array(rows, W)], place, resp, other, near, mode_coef, pick, shapes,
+        expand_kernel, "expand", [array(rows, W)], place, resp, other, mine, mode_coef, pick, shapes,
         scratch=[pltpu.VMEM((W, modes), BF)],
     )[0]
 

time: 92.6 us -> 84.5 us (0.913)
  waiting for transfers between devices: 16.5 us -> 13.2 us
  Pallas kernels: 36.7 us -> 33.9 us
  local copies, waits for them, and re-layouts: 25.9 us -> 23.9 us
    ppermute x10, waiting for transfers between devices: 16.5 us -> 13.2 us  [swap(): return lax.ppermute(x, 'frdm', [(i, i ^ bits) for i in range(devices)])]
    pallas_call x10, Pallas kernels: 36.7 us -> 33.9 us  [call(): pl.pallas_call(kernel, in_specs=places, out_specs=[vmem] * len(out_shape)...]
    unnamed x48 -> x42, local copies, waits for them, and re-layouts: 25.8 us -> 23.9 us
  transfers between devices with their start and end apart: 10 -> 10, of which waited for: 5 -> 6; matrix products, arithmetic and copies ran while one was open for 0% -> 0% of each run, Pallas kernels for 26% -> 21%
where the time goes in v3:
time: 84.5 us; the launch traced here: 84 us
  Pallas kernels  33.9 us (40%)
  local copies, waits for them, and re-layouts  23.9 us (28%)
  waiting for transfers between devices  13.2 us (16%)
  starting transfers between devices  12.6 us (15%)
    pallas_call x10, Pallas kernels, call(): pl.pallas_call(kernel, in_specs=places, out_specs=[vmem] * len(out_shape)...  33.9 us
    unnamed x42, local copies, waits for them, and re-layouts  23.9 us
    ppermute x10, waiting for transfers between devices, swap(): return lax.ppermute(x, 'frdm', [(i, i ^ bits) for i in range(devices)])  13.2 us
    ppermute x10, starting transfers between devices, swap(): return lax.ppermute(x, 'frdm', [(i, i ^ bits) for i in range(devices)])  12.6 us
  transfers between devices with their start and end apart: 10, of which 6 were waited for; matrix products, arithmetic and copies ran while one was open for 0% of the time, Pallas kernels for 21%

profile of v3, /device:TPU:0, one launch (start us, length us, event | category | flops | bytes accessed | tf_op | source)
XLA Modules:
  0.0 84.0 jit_solution(5793318826462870095)
XLA Ops:
  0.0 0.7 copy-done.17
  0.7 0.7 copy-done.19
  1.4 9.7 %project.1 = (bf16[912,1024]{1,0:T(8,128)(2,1)}, bf16[896,1024]{1,0:T(8,128)(2,1)S(1)}, bf16[1024,2048]{1,0:T(8,128)(2,1)S(1)}, bf16[528,2048]{1,0:T(8,128)(2,1)...) custom-call(s32[1]{0:T(128)} %bitcast.5.place, ...), custom_call_target="tpu_custom_call" | custom-call | tf_op jit(solution)/shard_map/project/pallas_call | solution.py:68
  11.0 1.9 %copy-done = bf16[1024,2048]{1,0:T(8,128)(2,1)} copy-done((bf16[1024,2048]{1,0:T(8,128)(2,1)}, bf16[1024,2048]{1,0:T(8,128)(2,1)S(1)}, u32[]{:S(2)}) %copy-start) | copy-done | bytes 4194328
  13.0 1.4 %copy-done.4 = bf16[528,2048]{1,0:T(8,128)(2,1)} copy-done((bf16[528,2048]{1,0:T(8,128)(2,1)}, bf16[528,2048]{1,0:T(8,128)(2,1)S(1)}, u32[]{:S(2)}) %copy-start.4) | copy-done | bytes 2162712
  14.4 1.2 %copy-done.7 = bf16[896,1024]{1,0:T(8,128)(2,1)} copy-done((bf16[896,1024]{1,0:T(8,128)(2,1)}, bf16[896,1024]{1,0:T(8,128)(2,1)S(1)}, u32[]{:S(2)}) %copy-start.7) | copy-done | bytes 1835032
  15.6 1.3 %copy-done.10 = bf16[896,1024]{1,0:T(8,128)(2,1)} copy-done((bf16[896,1024]{1,0:T(8,128)(2,1)}, bf16[896,1024]{1,0:T(8,128)(2,1)S(1)}, u32[]{:S(2)}) %copy-start.10) | copy-done | bytes 1835032
  16.9 0.8 copy-done.13
  17.6 0.5 collective-permute-start
  18.1 0.1 pad_add_fusion.2.place
  18.2 2.2 %copy-done.1 = bf16[1024,2048]{1,0:T(8,128)(2,1)S(1)} copy-done((bf16[1024,2048]{1,0:T(8,128)(2,1)S(1)}, bf16[1024,2048]{1,0:T(8,128)(2,1)}, u32[]{:S(2)}) %copy-start.1) | copy-done | bytes 4194328
  20.4 1.6 %copy-done.5 = bf16[528,2048]{1,0:T(8,128)(2,1)S(1)} copy-done((bf16[528,2048]{1,0:T(8,128)(2,1)S(1)}, bf16[528,2048]{1,0:T(8,128)(2,1)}, u32[]{:S(2)}) %copy-start.5) | copy-done | bytes 2162712
  22.0 1.5 %copy-done.8 = bf16[896,1024]{1,0:T(8,128)(2,1)S(1)} copy-done((bf16[896,1024]{1,0:T(8,128)(2,1)S(1)}, bf16[896,1024]{1,0:T(8,128)(2,1)}, u32[]{:S(2)}) %copy-start.8) | copy-done | bytes 1835032
  23.5 1.5 %copy-done.11 = bf16[896,1024]{1,0:T(8,128)(2,1)S(1)} copy-done((bf16[896,1024]{1,0:T(8,128)(2,1)S(1)}, bf16[896,1024]{1,0:T(8,128)(2,1)}, u32[]{:S(2)}) %copy-start.11) | copy-done | bytes 1835032
  25.0 1.0 %copy-done.14 = bf16[896,256]{1,0:T(8,128)(2,1)S(1)} copy-done((bf16[896,256]{1,0:T(8,128)(2,1)S(1)}, bf16[896,256]{1,0:T(8,128)(2,1)}, u32[]{:S(2)}) %copy-start.14) | copy-done | bytes 458776
  26.0 5.3 %spectrum.1 = (f32[896,512]{1,0:T(8,128)S(1)}, f32[896,512]{1,0:T(8,128)S(1)}) custom-call(s32[2]{0:T(128)S(1)} %pad_add_fusion.2.place, bf16[528,2048]{1,0:T(8,128)(2,1)S(1)} %copy-done.5, s32[1,2048]{1,0:T(1,128)S(1)} %bitcast.12, bf16[896,1024]{1,0:T(8,128)(2,1)S(1)} %copy-done.11, f32[896,128]{1,0:T(8,128)S(1)} %get-tuple-element.24.last, ...), custom_call_target="tpu_custom_call" | custom-call | tf_op jit(solution)/shard_map/spectrum/pallas_call | solution.py:68
  31.3 2.2 %respond.1 = bf16[272,512]{1,0:T(8,128)(2,1)} custom-call(s32[2]{0:T(128)S(1)} %pad_add_fusion.2.place, f32[896,512]{1,0:T(8,128)S(1)} %get-tuple-element.30.own, bf16[912,1024]{1,0:T(8,128)(2,1)S(1)} %collective-permute-done.other, f32[896,512]{1,0:T(8,128)S(1)} %get-tuple-element.31.spec, bf16[256,1792]{1,0:T(8,128)(2,1)S(1)} %get-tuple-element.29.inverse, ...), custom_call_target="tpu_custom_call" | custom-call | tf_op jit(solution)/shard_map/respond/pallas_call | solution.py:68
  33.5 2.5 %collective-permute-start.1 = (bf16[272,512]{1,0:T(8,128)(2,1)}, bf16[272,512]{1,0:T(8,128)(2,1)S(1)}, u32[]{:S(2)}, u32[]{:S(2)}) collective-permute-start(bf16[272,512]{1,0:T(8,128)(2,1)} %respond.1), channel_id=1, source_target_pairs={{0,2},{1,3},{2,0},{3,1},{4,6},{5,7},{6,4},{7,5},{8,10},{9,11},{10,... | collective-permute-start | bytes 835592 | tf_op jit(solution)/shard_map/ppermute | solution.py:284
  36.0 0.1 pad_add_fusion.1.place
  36.1 2.2 %copy-done.2 = bf16[1024,2048]{1,0:T(8,128)(2,1)S(1)} copy-done((bf16[1024,2048]{1,0:T(8,128)(2,1)S(1)}, bf16[1024,2048]{1,0:T(8,128)(2,1)}, u32[]{:S(2)}) %copy-start.2) | copy-done | bytes 4194328
  38.3 1.6 %copy-done.6 = bf16[528,2048]{1,0:T(8,128)(2,1)S(1)} copy-done((bf16[528,2048]{1,0:T(8,128)(2,1)S(1)}, bf16[528,2048]{1,0:T(8,128)(2,1)}, u32[]{:S(2)}) %copy-start.6) | copy-done | bytes 2162712
  39.9 1.5 %copy-done.9 = bf16[896,1024]{1,0:T(8,128)(2,1)S(1)} copy-done((bf16[896,1024]{1,0:T(8,128)(2,1)S(1)}, bf16[896,1024]{1,0:T(8,128)(2,1)}, u32[]{:S(2)}) %copy-start.9) | copy-done | bytes 1835032
  41.4 1.5 %copy-done.12 = bf16[896,1024]{1,0:T(8,128)(2,1)S(1)} copy-done((bf16[896,1024]{1,0:T(8,128)(2,1)S(1)}, bf16[896,1024]{1,0:T(8,128)(2,1)}, u32[]{:S(2)}) %copy-start.12) | copy-done | bytes 1835032
  42.9 1.0 %copy-done.15 = bf16[896,256]{1,0:T(8,128)(2,1)S(1)} copy-done((bf16[896,256]{1,0:T(8,128)(2,1)S(1)}, bf16[896,256]{1,0:T(8,128)(2,1)}, u32[]{:S(2)}) %copy-start.15) | copy-done | bytes 458776
  43.9 6.9 %whole.1.own = f32[256,512]{1,0:T(8,128)S(1)} custom-call(s32[2]{0:T(128)S(1)} %pad_add_fusion.1.place, bf16[528,2048]{1,0:T(8,128)(2,1)S(1)} %copy-done.6, s32[1,2048]{1,0:T(1,128)S(1)} %bitcast.13, bf16[896,1024]{1,0:T(8,128)(2,1)S(1)} %copy-done.12, f32[896,128]{1,0:T(8,128)S(1)} %get-tuple-element.24.last, bf16[896,256]{1,0:T(8,128)(2,1)S(1)} %copy-done.15, ...), custom_call_target="tpu_custom_call" | custom-call | tf_op jit(solution)/shard_map/whole/pallas_call | solution.py:68
  50.9 0.0 copy-start.18
  50.9 0.1 fold.1
  51.0 1.7 %collective-permute-start.2 = (bf16[272,128]{1,0:T(8,128)(2,1)S(1)}, bf16[272,128]{1,0:T(8,128)(2,1)S(1)}, u32[]{:S(2)}, u32[]{:S(2)}) collective-permute-start(bf16[272,128]{1,0:T(8,128)(2,1)S(1)} %get-tuple-element.33), channel_id=1, source_target_pairs={{0,4},{1,5},{2,6},{3,7},{4,0},{5,1},{6,2},{7,3},{8,12},{9,13},{10,... | collective-permute-start | bytes 208904 | tf_op jit(solution)/shard_map/ppermute | solution.py:284
  52.7 2.6 %collective-permute-start.3 = (bf16[272,128]{1,0:T(8,128)(2,1)S(1)}, bf16[272,128]{1,0:T(8,128)(2,1)S(1)}, u32[]{:S(2)}, u32[]{:S(2)}) collective-permute-start(bf16[272,128]{1,0:T(8,128)(2,1)S(1)} %get-tuple-element.34), channel_id=1, source_target_pairs={{0,8},{1,9},{2,10},{3,11},{4,12},{5,13},{6,14},{7,15},{8,0},{9,1},... | collective-permute-start | bytes 208904 | tf_op jit(solution)/shard_map/ppermute | solution.py:284
  55.3 0.2 collective-permute-start.4
  55.5 0.0 collective-permute-done.2.first
  55.5 5.0 %collective-permute-done.3.second = bf16[272,128]{1,0:T(8,128)(2,1)S(1)} collective-permute-done((bf16[272,128]{1,0:T(8,128)(2,1)S(1)}, bf16[272,128]{1,0:T(8,128)(2,1)S(1)}, u32[]{:S(2)}, u32[]{:S(2)}) %collective-permute-start.3) | collective-permute-done | bytes 69664 | tf_op jit(solution)/shard_map/ppermute | solution.py:284
  60.5 0.9 %collective-permute-done.4.third = bf16[272,128]{1,0:T(8,128)(2,1)S(1)} collective-permute-done((bf16[272,128]{1,0:T(8,128)(2,1)S(1)}, bf16[272,128]{1,0:T(8,128)(2,1)S(1)}, u32[]{:S(2)}, u32[]{:S(2)}) %collective-permute-start.4) | collective-permute-done | bytes 69664 | tf_op jit(solution)/shard_map/ppermute | solution.py:284
  61.5 2.4 %collective-permute-start.7 = (bf16[256,128]{1,0:T(8,128)(2,1)S(1)}, bf16[256,128]{1,0:T(8,128)(2,1)S(1)}, u32[]{:S(2)}, u32[]{:S(2)}) collective-permute-start(bf16[256,128]{1,0:T(8,128)(2,1)S(1)} %settle.1), channel_id=1, source_target_pairs={{0,12},{1,13},{2,14},{3,15},{4,8},{5,9},{6,10},{7,11},{8,4},{9,5},... | collective-permute-start | bytes 196616 | tf_op jit(solution)/shard_map/ppermute | solution.py:284
  63.9 0.4 collective-permute-start.6
  64.3 1.7 %collective-permute-start.5 = (bf16[256,128]{1,0:T(8,128)(2,1)S(1)}, bf16[256,128]{1,0:T(8,128)(2,1)S(1)}, u32[]{:S(2)}, u32[]{:S(2)}) collective-permute-start(bf16[256,128]{1,0:T(8,128)(2,1)S(1)} %settle.1), channel_id=1, source_target_pairs={{0,4},{1,5},{2,6},{3,7},{4,0},{5,1},{6,2},{7,3},{8,12},{9,13},{10,... | collective-permute-start | bytes 196616 | tf_op jit(solution)/shard_map/ppermute | solution.py:284
  66.0 1.9 %collective-permute-done.7 = bf16[256,128]{1,0:T(8,128)(2,1)S(1)} collective-permute-done((bf16[256,128]{1,0:T(8,128)(2,1)S(1)}, bf16[256,128]{1,0:T(8,128)(2,1)S(1)}, u32[]{:S(2)}, u32[]{:S(2)}) %collective-permute-start.7) | collective-permute-done | bytes 65568 | tf_op jit(solution)/shard_map/ppermute | solution.py:284
  67.9 2.1 %collective-permute-done.6 = bf16[256,128]{1,0:T(8,128)(2,1)S(1)} collective-permute-done((bf16[256,128]{1,0:T(8,128)(2,1)S(1)}, bf16[256,128]{1,0:T(8,128)(2,1)S(1)}, u32[]{:S(2)}, u32[]{:S(2)}) %collective-permute-start.6) | collective-permute-done | bytes 65568 | tf_op jit(solution)/shard_map/ppermute | solution.py:284
  70.0 0.0 collective-permute-done.5
  70.0 0.6 collective-permute-start.8
  70.6 0.1 pad_add_fusion.place
  70.7 4.0 %mixers.1 = (f32[8,2048]{1,0:T(8,128)S(1)}, bf16[2048,2048]{1,0:T(8,128)(2,1)S(1)}) custom-call(s32[2]{0:T(128)S(1)} %pad_add_fusion.place, s32[1,2048]{1,0:T(1,128)S(1)} %bitcast.14, s32[1,2048]{1,0:T(1,128)S(1)} %bitcast.16, bf16[16,128]{1,0:T(8,128)(2,1)S(1)} %get-tuple-element.36.known, bf16[272,128]{1,0:T(8,128)(2,1)S(1)} %collective-permute-done.2.first, ...), custom_call_target="tpu_custom_call" | custom-call | tf_op jit(solution)/shard_map/mixers/pallas_call | solution.py:68
  74.7 2.6 %collective-permute-done.8.got = bf16[256,512]{1,0:T(8,128)(2,1)S(1)} collective-permute-done((bf16[256,512]{1,0:T(8,128)(2,1)S(1)}, bf16[256,512]{1,0:T(8,128)(2,1)S(1)}, u32[]{:S(2)}, u32[]{:S(2)}) %collective-permute-start.8) | collective-permute-done | bytes 262176 | tf_op jit(solution)/shard_map/ppermute | solution.py:284
  77.3 0.1 collective-permute-start.9
  77.4 1.3 %mate.1.mates = f32[256,2048]{1,0:T(8,128)S(1)} custom-call(bf16[256,1024]{1,0:T(8,128)(2,1)S(1)} %join.1.resp, bf16[2048,2048]{1,0:T(8,128)(2,1)S(1)} %get-tuple-element.38.pick), custom_call_target="tpu_custom_call" | custom-call | tf_op jit(solution)/shard_map/mate/pallas_call | solution.py:68
  78.7 0.6 collective-permute-done.9.other
  79.3 0.3 copy-done.3
  79.6 4.4 %expand.1 = bf16[1024,256]{1,0:T(8,128)(2,1)} custom-call(s32[2]{0:T(128)S(1)} %pad_add_fusion.place, bf16[256,1024]{1,0:T(8,128)(2,1)S(1)} %join.1.resp, bf16[256,1024]{1,0:T(8,128)(2,1)S(1)} %collective-permute-done.9.other, f32[256,2048]{1,0:T(8,128)S(1)} %mate.1.mates, f32[8,2048]{1,0:T(8,128)S(1)} %get-tuple-element.37.before.coef, ...), custom_call_target="tpu_custom_call" | custom-call | tf_op jit(solution)/shard_map/expand/pallas_call | solution.py:68
  (28 shorter events, 0.1 us)
Async XLA Ops:
  0.0 0.7 copy-start.17
  0.7 0.7 copy-start.19
  1.4 16.8 %copy-start.16 = (s32[2048]{0:T(1024)S(1)}, s32[2048]{0:T(1024)}, u32[]{:S(2)}) copy-start(s32[2048]{0:T(1024)} %param.14) | copy-start | bytes 24580
  11.0 2.0 %copy-start = (bf16[1024,2048]{1,0:T(8,128)(2,1)}, bf16[1024,2048]{1,0:T(8,128)(2,1)S(1)}, u32[]{:S(2)}) copy-start(bf16[1024,2048]{1,0:T(8,128)(2,1)S(1)} %get-tuple-element.27.shapes) | copy-start | bytes 12582916
  13.0 1.4 %copy-start.4 = (bf16[528,2048]{1,0:T(8,128)(2,1)}, bf16[528,2048]{1,0:T(8,128)(2,1)S(1)}, u32[]{:S(2)}) copy-start(bf16[528,2048]{1,0:T(8,128)(2,1)S(1)} %get-tuple-element.22.stack) | copy-start | bytes 6488068
  14.4 1.2 %copy-start.7 = (bf16[896,1024]{1,0:T(8,128)(2,1)}, bf16[896,1024]{1,0:T(8,128)(2,1)S(1)}, u32[]{:S(2)}) copy-start(bf16[896,1024]{1,0:T(8,128)(2,1)S(1)} %get-tuple-element.26.lft) | copy-start | bytes 5505028
  15.6 1.3 %copy-start.10 = (bf16[896,1024]{1,0:T(8,128)(2,1)}, bf16[896,1024]{1,0:T(8,128)(2,1)S(1)}, u32[]{:S(2)}) copy-start(bf16[896,1024]{1,0:T(8,128)(2,1)S(1)} %get-tuple-element.23.table) | copy-start | bytes 5505028
  16.9 0.8 copy-start.13
  17.6 13.6 %collective-permute-start = (bf16[912,1024]{1,0:T(8,128)(2,1)}, bf16[912,1024]{1,0:T(8,128)(2,1)S(1)}, u32[]{:S(2)}, u32[]{:S(2)}) collective-permute-start(bf16[912,1024]{1,0:T(8,128)(2,1)} %get-tuple-element.28), channel_id=1, source_target_pairs={{0,1},{1,0},{2,3},{3,2},{4,5},{5,4},{6,7},{7,6},{8,9},{9,8},{10,11... | collective-permute-start | bytes 5603336 | tf_op jit(solution)/shard_map/ppermute | solution.py:284
  18.2 2.2 %copy-start.1 = (bf16[1024,2048]{1,0:T(8,128)(2,1)S(1)}, bf16[1024,2048]{1,0:T(8,128)(2,1)}, u32[]{:S(2)}) copy-start(bf16[1024,2048]{1,0:T(8,128)(2,1)} %copy-done) | copy-start | bytes 12582916
  20.4 1.6 %copy-start.5 = (bf16[528,2048]{1,0:T(8,128)(2,1)S(1)}, bf16[528,2048]{1,0:T(8,128)(2,1)}, u32[]{:S(2)}) copy-start(bf16[528,2048]{1,0:T(8,128)(2,1)} %copy-done.4) | copy-start | bytes 6488068
  22.0 1.5 %copy-start.8 = (bf16[896,1024]{1,0:T(8,128)(2,1)S(1)}, bf16[896,1024]{1,0:T(8,128)(2,1)}, u32[]{:S(2)}) copy-start(bf16[896,1024]{1,0:T(8,128)(2,1)} %copy-done.7) | copy-start | bytes 5505028
  23.5 1.5 %copy-start.11 = (bf16[896,1024]{1,0:T(8,128)(2,1)S(1)}, bf16[896,1024]{1,0:T(8,128)(2,1)}, u32[]{:S(2)}) copy-start(bf16[896,1024]{1,0:T(8,128)(2,1)} %copy-done.10) | copy-start | bytes 5505028
  25.0 1.0 %copy-start.14 = (bf16[896,256]{1,0:T(8,128)(2,1)S(1)}, bf16[896,256]{1,0:T(8,128)(2,1)}, u32[]{:S(2)}) copy-start(bf16[896,256]{1,0:T(8,128)(2,1)} %copy-done.13) | copy-start | bytes 1376260
  26.0 5.3 %copy-start.20 = (bf16[2,128]{1,0:T(2,128)(2,1)S(1)}, bf16[2,128]{1,0:T(2,128)(2,1)}, u32[]{:S(2)}) copy-start(bf16[2,128]{1,0:T(2,128)(2,1)} %coef.5) | copy-start | bytes 1540
  33.5 17.4 %collective-permute-start.1 = (bf16[272,512]{1,0:T(8,128)(2,1)}, bf16[272,512]{1,0:T(8,128)(2,1)S(1)}, u32[]{:S(2)}, u32[]{:S(2)}) collective-permute-start(bf16[272,512]{1,0:T(8,128)(2,1)} %respond.1), channel_id=1, source_target_pairs={{0,2},{1,3},{2,0},{3,1},{4,6},{5,7},{6,4},{7,5},{8,10},{9,11},{10,... | collective-permute-start | bytes 835592 | tf_op jit(solution)/shard_map/ppermute | solution.py:284
  36.1 2.2 %copy-start.2 = (bf16[1024,2048]{1,0:T(8,128)(2,1)S(1)}, bf16[1024,2048]{1,0:T(8,128)(2,1)}, u32[]{:S(2)}) copy-start(bf16[1024,2048]{1,0:T(8,128)(2,1)} %copy-done) | copy-start | bytes 12582916
  38.3 1.6 %copy-start.6 = (bf16[528,2048]{1,0:T(8,128)(2,1)S(1)}, bf16[528,2048]{1,0:T(8,128)(2,1)}, u32[]{:S(2)}) copy-start(bf16[528,2048]{1,0:T(8,128)(2,1)} %copy-done.4) | copy-start | bytes 6488068
  39.9 1.5 %copy-start.9 = (bf16[896,1024]{1,0:T(8,128)(2,1)S(1)}, bf16[896,1024]{1,0:T(8,128)(2,1)}, u32[]{:S(2)}) copy-start(bf16[896,1024]{1,0:T(8,128)(2,1)} %copy-done.7) | copy-start | bytes 5505028
  41.4 1.5 %copy-start.12 = (bf16[896,1024]{1,0:T(8,128)(2,1)S(1)}, bf16[896,1024]{1,0:T(8,128)(2,1)}, u32[]{:S(2)}) copy-start(bf16[896,1024]{1,0:T(8,128)(2,1)} %copy-done.10) | copy-start | bytes 5505028
  42.9 1.0 %copy-start.15 = (bf16[896,256]{1,0:T(8,128)(2,1)S(1)}, bf16[896,256]{1,0:T(8,128)(2,1)}, u32[]{:S(2)}) copy-start(bf16[896,256]{1,0:T(8,128)(2,1)} %copy-done.13) | copy-start | bytes 1376260
  50.9 19.8 %copy-start.18 = (s32[2048]{0:T(1024)S(1)}, s32[2048]{0:T(1024)}, u32[]{:S(2)}) copy-start(s32[2048]{0:T(1024)} %param.15) | copy-start | bytes 24580
  51.0 4.5 %collective-permute-start.2 = (bf16[272,128]{1,0:T(8,128)(2,1)S(1)}, bf16[272,128]{1,0:T(8,128)(2,1)S(1)}, u32[]{:S(2)}, u32[]{:S(2)}) collective-permute-start(bf16[272,128]{1,0:T(8,128)(2,1)S(1)} %get-tuple-element.33), channel_id=1, source_target_pairs={{0,4},{1,5},{2,6},{3,7},{4,0},{5,1},{6,2},{7,3},{8,12},{9,13},{10,... | collective-permute-start | bytes 208904 | tf_op jit(solution)/shard_map/ppermute | solution.py:284
  52.7 7.9 %collective-permute-start.3 = (bf16[272,128]{1,0:T(8,128)(2,1)S(1)}, bf16[272,128]{1,0:T(8,128)(2,1)S(1)}, u32[]{:S(2)}, u32[]{:S(2)}) collective-permute-start(bf16[272,128]{1,0:T(8,128)(2,1)S(1)} %get-tuple-element.34), channel_id=1, source_target_pairs={{0,8},{1,9},{2,10},{3,11},{4,12},{5,13},{6,14},{7,15},{8,0},{9,1},... | collective-permute-start | bytes 208904 | tf_op jit(solution)/shard_map/ppermute | solution.py:284
  55.3 6.2 %collective-permute-start.4 = (bf16[272,128]{1,0:T(8,128)(2,1)S(1)}, bf16[272,128]{1,0:T(8,128)(2,1)S(1)}, u32[]{:S(2)}, u32[]{:S(2)}) collective-permute-start(bf16[272,128]{1,0:T(8,128)(2,1)S(1)} %get-tuple-element.35), channel_id=1, source_target_pairs={{0,12},{1,13},{2,14},{3,15},{4,8},{5,9},{6,10},{7,11},{8,4},{9,5},... | collective-permute-start | bytes 208904 | tf_op jit(solution)/shard_map/ppermute | solution.py:284
  61.5 6.4 %collective-permute-start.7 = (bf16[256,128]{1,0:T(8,128)(2,1)S(1)}, bf16[256,128]{1,0:T(8,128)(2,1)S(1)}, u32[]{:S(2)}, u32[]{:S(2)}) collective-permute-start(bf16[256,128]{1,0:T(8,128)(2,1)S(1)} %settle.1), channel_id=1, source_target_pairs={{0,12},{1,13},{2,14},{3,15},{4,8},{5,9},{6,10},{7,11},{8,4},{9,5},... | collective-permute-start | bytes 196616 | tf_op jit(solution)/shard_map/ppermute | solution.py:284
  63.9 6.1 %collective-permute-start.6 = (bf16[256,128]{1,0:T(8,128)(2,1)S(1)}, bf16[256,128]{1,0:T(8,128)(2,1)S(1)}, u32[]{:S(2)}, u32[]{:S(2)}) collective-permute-start(bf16[256,128]{1,0:T(8,128)(2,1)S(1)} %settle.1), channel_id=1, source_target_pairs={{0,8},{1,9},{2,10},{3,11},{4,12},{5,13},{6,14},{7,15},{8,0},{9,1},... | collective-permute-start | bytes 196616 | tf_op jit(solution)/shard_map/ppermute | solution.py:284
  64.3 5.7 %collective-permute-start.5 = (bf16[256,128]{1,0:T(8,128)(2,1)S(1)}, bf16[256,128]{1,0:T(8,128)(2,1)S(1)}, u32[]{:S(2)}, u32[]{:S(2)}) collective-permute-start(bf16[256,128]{1,0:T(8,128)(2,1)S(1)} %settle.1), channel_id=1, source_target_pairs={{0,4},{1,5},{2,6},{3,7},{4,0},{5,1},{6,2},{7,3},{8,12},{9,13},{10,... | collective-permute-start | bytes 196616 | tf_op jit(solution)/shard_map/ppermute | solution.py:284
  70.0 7.3 %collective-permute-start.8 = (bf16[256,512]{1,0:T(8,128)(2,1)S(1)}, bf16[256,512]{1,0:T(8,128)(2,1)S(1)}, u32[]{:S(2)}, u32[]{:S(2)}) collective-permute-start(bf16[256,512]{1,0:T(8,128)(2,1)S(1)} %pad_maximum_fusion.after.quarter), channel_id=1, source_target_pairs={{0,2},{1,3},{2,0},{3,1},{4,6},{5,7},{6,4},{7,5},{8,10},{9,11},{10,... | collective-permute-start | bytes 786440 | tf_op jit(solution)/shard_map/ppermute | solution.py:284
  77.3 2.0 %collective-permute-start.9 = (bf16[256,1024]{1,0:T(8,128)(2,1)S(1)}, bf16[256,1024]{1,0:T(8,128)(2,1)S(1)}, u32[]{:S(2)}, u32[]{:S(2)}) collective-permute-start(bf16[256,1024]{1,0:T(8,128)(2,1)S(1)} %join.1.resp), channel_id=1, source_target_pairs={{0,1},{1,0},{2,3},{3,2},{4,5},{5,4},{6,7},{7,6},{8,9},{9,8},{10,11... | collective-permute-start | bytes 1572872 | tf_op jit(solution)/shard_map/ppermute | solution.py:284
  77.4 2.2 %copy-start.3 = (bf16[1024,2048]{1,0:T(8,128)(2,1)S(1)}, bf16[1024,2048]{1,0:T(8,128)(2,1)}, u32[]{:S(2)}) copy-start(bf16[1024,2048]{1,0:T(8,128)(2,1)} %copy-done) | copy-start | bytes 12582916

commit v4 on v3

--- a/solution.py
+++ b/solution.py
@@ -98,7 +98,7 @@
 ):
     rows, half = loads.shape[0], sent.shape[1]
     hist = lft.shape[0]
-    core = place[0]
+    core = place[0] & 1
     far, own = block((1 - core) * half, half), block(core * half, half)
     pairs = [
         (forward_far, forward),
@@ -137,6 +137,13 @@
         copy.wait()
 
 
+def quarter_base(place, which, modes):
+    me = place[0]
+    index = which - 2 if which > 1 else ((me >> 1) & 1) ^ which
+    start = index * (modes // 4)
+    return (me & 1) * (modes // 2) + start, start
+
+
 def spectrum(base, stack, order, table, last, phase, put, width):
     count = stack.shape[0] - EXTRA
     half = table.shape[0] // 2
@@ -159,7 +166,7 @@
 def spectrum_kernel(place, stack, order, table, last, phase, lft, shapes, spec, own):
     width = spec.shape[1]
     half = spec.shape[0] // 2
-    base = place[0]
+    base = quarter_base(place, 1, shapes.shape[1])[0]
     for c in range(0, width, 256):
         own[:, c : c + 256] = dot(lft[...], shapes[:, block(base + c, 256)])
 
@@ -177,9 +184,9 @@
     return dot(inverse[...], jnp.concatenate([product, product], axis=0))
 
 
-def whole_kernel(place, stack, order, table, last, phase, lft, shapes, other, inverse, out):
+def whole_kernel(which, place, stack, order, table, last, phase, lft, shapes, other, inverse, out):
     hist = lft.shape[0]
-    base, start = place[0], place[1]
+    base, start = quarter_base(place, which, shapes.shape[1])
 
     def put(c, re, im):
         total = dot(lft[...], shapes[:, block(base + c, 256)]) + other[:hist, block(start + c, 256)].astype(F32)
@@ -191,7 +198,7 @@
 def respond_kernel(place, own, other, spec, inverse, coef, out):
     hist, width = own.shape
     half = hist // 2
-    start = place[1]
+    start = quarter_base(place, 1, 4 * width)[1]
     for c in range(0, width, 256):
         total = own[:, c : c + 256] + other[:hist, block(start + c, 256)].astype(F32)
         result = impose(total, spec[:half, c : c + 256], spec[half:, c : c + 256], inverse)
@@ -202,7 +209,7 @@
 
 
 def fold_kernel(place, own, got, coef, other, keep, known, first, second, third):
-    z = place[0]
+    z = place[0] >> 2
     size = keep.shape[1]
     hist = other.shape[0] - EXTRA
     known[...] = jnp.zeros(known.shape, BF)
@@ -224,9 +231,15 @@
     out[...] = total.astype(BF)
 
 
+def mask_of(place, devices, modes):
+    me = place[0]
+    if devices == 16:
+        return ((me & 1) * 8 + (me & 2) * 2 + (me >> 2)) * (modes // 16)
+    return (me & 1) * (modes // 2)
+
+
 def mixers_kernel(place, order, partner, known, first, second, third, after, coef, pick, held):
-    me, mask = place[0], place[1]
-    modes = order.shape[1]
+    me, mask = place[0], mask_of(place, 16, order.shape[1])
     held[...] = jnp.zeros(held.shape, F32)
     for z, rows in enumerate((known, first, second, third)):
         top = rows.shape[0] - EXTRA
@@ -246,10 +259,10 @@
         pick[c : c + 256, :] = hot((mode ^ mask) == partner[...])
 
 
-def plain_mixers_kernel(place, order, partner, every, coef, pick, held):
+def plain_mixers_kernel(devices, place, order, partner, every, coef, pick, held):
     held[...] = jnp.zeros(held.shape, F32)
     held[0:2, :] = every[...].astype(F32)
-    mixers(order, partner, place[1], held, coef, pick)
+    mixers(order, partner, mask_of(place, devices, order.shape[1]), held, coef, pick)
 
 
 def join_kernel(quarter, got, before, out):
@@ -263,9 +276,9 @@
         out[:, c : c + 256] = dot(resp[...], pick[: resp.shape[1], c : c + 256])
 
 
-def expand_kernel(place, resp, other, mates, coef, pick, shapes, out, paired):
+def expand_kernel(devices, place, resp, other, mates, coef, pick, shapes, out, paired):
     half = resp.shape[1]
-    mask = place[1]
+    mask = mask_of(place, devices, shapes.shape[1])
     for c in range(0, 2 * half, 256):
         across = mates[:, c : c + 256] + dot(other[...], pick[half:, c : c + 256])
         for k in (c, c + LANES):
@@ -284,16 +297,11 @@
     return lax.ppermute(x, "frdm", [(i, i ^ bits) for i in range(devices)])
 
 
-def scalars(*values):
-    return jnp.stack([jnp.asarray(v, I32) for v in values])
-
-
 def shards(devices, loads, shapes, mode_order, partner, taps, offsets, coef):
     rows, modes = shapes.shape
     hist, count = loads.shape[1], taps.shape[1]
     half, quarter = modes // 2, modes // 4
-    me = lax.axis_index("frdm").astype(I32)
-    core = me & 1
+    place = lax.axis_index("frdm").astype(I32).reshape(1)
     forward = forward_table(hist)
     tap_forward, last = tap_table(hist, count)
     phase = phase_table(hist, hist - W - count + 1)
@@ -304,7 +312,7 @@
         project_kernel, "project",
         [near(hist + EXTRA, half), near(hist, rows), near(rows, modes), near(count - 1 + EXTRA, modes)]
         + [near(*tap_forward.shape), near(*last.shape, dtype=F32), near(*phase.shape), near(*inverse.shape)],
-        scalars(core), loads, forward, shapes, taps, tap_forward, last, phase, inverse, offsets, coef,
+        place, loads, forward, shapes, taps, tap_forward, last, phase, inverse, offsets, coef,
         far=range(1, 9),
         scratch=[
             pltpu.VMEM(loads.shape, BF), pltpu.VMEM(forward.shape, BF), pltpu.VMEM(taps.shape, F32),
@@ -315,48 +323,43 @@
     got = swap(sent, devices, 1)
     common = (stack, order, tap_forward, last, phase, lft, shapes)
 
-    def quarter_of(index):
-        return scalars(core * half + index * quarter, index * quarter)
-
-    def respond(index):
-        return call(whole_kernel, "whole", [array(W, quarter, dtype=F32)], quarter_of(index), *common, got, inverse)[0]
+    def respond(which):
+        kernel = functools.partial(whole_kernel, which)
+        return call(kernel, "whole", [array(W, quarter, dtype=F32)], place, *common, got, inverse)[0]
 
     if devices == 16:
-        y, z = (me >> 1) & 1, me >> 2
         size = modes // devices
         spec, own = call(
-            spectrum_kernel, "spectrum", [near(hist, quarter, dtype=F32)] * 2, quarter_of(1 - y), *common
+            spectrum_kernel, "spectrum", [near(hist, quarter, dtype=F32)] * 2, place, *common
         )
         away = call(
-            respond_kernel, "respond", [array(W + EXTRA, quarter)], quarter_of(1 - y), own, got, spec, inverse, coef
+            respond_kernel, "respond", [array(W + EXTRA, quarter)], place, own, got, spec, inverse, coef
         )[0]
         away = swap(away, devices, 2)
         keep, known, *parts = call(
             fold_kernel, "fold", [array(W, size, dtype=F32), array(EXTRA, LANES)] + [array(W + EXTRA, size)] * 3,
-            scalars(z), respond(y), away, coef, got,
+            place, respond(0), away, coef, got,
         )
         parts = [swap(part, devices, 4 * d) for d, part in zip((1, 2, 3), parts)]
         total = call(settle_kernel, "settle", [array(W, size)], keep, *parts, scalars=0)[0]
         resp = jnp.concatenate([total] + [swap(total, devices, 4 * d) for d in (1, 2, 3)], axis=1)
-        place = scalars(me, (core * 8 + y * 4 + z) * size)
         mode_coef, pick = call(
             mixers_kernel, "mixers", [array(8, modes, dtype=F32), near(modes, modes)],
             place, order, mates, known, *parts, resp, scratch=[pltpu.VMEM((8, modes), F32)],
         )
         resp = call(join_kernel, "join", [array(W, half)], resp, swap(resp, devices, 2), mode_coef, scalars=0)[0]
     else:
-        place = scalars(me, core * half)
         mode_coef, pick = call(
-            plain_mixers_kernel, "mixers", [array(8, modes, dtype=F32), near(modes, modes)],
+            functools.partial(plain_mixers_kernel, devices), "mixers", [array(8, modes, dtype=F32), near(modes, modes)],
             place, order, mates, lax.all_gather(coef, "frdm", axis=1, tiled=True), scratch=[pltpu.VMEM((8, modes), F32)],
         )
-        resp = jnp.concatenate([respond(q) for q in (0, 1)], axis=1)
+        resp = jnp.concatenate([respond(q) for q in (2, 3)], axis=1)
         groups = [list(range(c, devices, 2)) for c in range(2)]
         resp = lax.psum(resp, "frdm", axis_index_groups=groups).astype(BF)
     other = swap(resp, devices, 1)
     mine = call(mate_kernel, "mate", [array(W, modes, dtype=F32)], resp, pick, scalars=0)[0]
     return call(
-        expand_kernel, "expand", [array(rows, W)], place, resp, other, mine, mode_coef, pick, shapes,
+        functools.partial(expand_kernel, devices), "expand", [array(rows, W)], place, resp, other, mine, mode_coef, pick, shapes,
         scratch=[pltpu.VMEM((W, modes), BF)],
     )[0]
 

time: 84.5 us -> 56.8 us (0.67)
  local copies, waits for them, and re-layouts: 23.9 us -> 1.36 us
  Pallas kernels: 33.9 us -> 29.3 us
  starting transfers between devices: 12.6 us -> 13.7 us
  waiting for transfers between devices: 13.2 us -> 12.1 us
    unnamed x42 -> x8, local copies, waits for them, and re-layouts: 23.9 us -> 1.36 us
    pallas_call x10, Pallas kernels: 33.9 us -> 29.3 us  [call(): pl.pallas_call(kernel, in_specs=places, out_specs=[vmem] * len(out_shape)...]
    ppermute x10, starting transfers between devices: 12.6 us -> 13.7 us  [swap(): return lax.ppermute(x, 'frdm', [(i, i ^ bits) for i in range(devices)])]
    ppermute x10, waiting for transfers between devices: 13.2 us -> 12.1 us  [swap(): return lax.ppermute(x, 'frdm', [(i, i ^ bits) for i in range(devices)])]
  transfers between devices with their start and end apart: 10 -> 10, of which waited for: 6 -> 7; matrix products, arithmetic and copies ran while one was open for 0% -> 0% of each run, Pallas kernels for 21% -> 28%
where the time goes in v4:
time: 56.8 us; the launch traced here: 56.5 us
  Pallas kernels  29.3 us (52%)
  starting transfers between devices  13.7 us (24%)
  waiting for transfers between devices  12.1 us (21%)
  local copies, waits for them, and re-layouts  1.36 us (2%)
    pallas_call x10, Pallas kernels, call(): pl.pallas_call(kernel, in_specs=places, out_specs=[vmem] * len(out_shape)...  29.3 us
    ppermute x10, starting transfers between devices, swap(): return lax.ppermute(x, 'frdm', [(i, i ^ bits) for i in range(devices)])  13.7 us
    ppermute x10, waiting for transfers between devices, swap(): return lax.ppermute(x, 'frdm', [(i, i ^ bits) for i in range(devices)])  12.1 us
    unnamed x8, local copies, waits for them, and re-layouts  1.36 us
  transfers between devices with their start and end apart: 10, of which 7 were waited for; matrix products, arithmetic and copies ran while one was open for 0% of the time, Pallas kernels for 28%

profile of v4, /device:TPU:0, one launch (start us, length us, event | category | flops | bytes accessed | tf_op | source)
XLA Modules:
  0.0 56.5 jit_solution(15381225634417785523)
XLA Ops:
  0.0 0.0 copy-start.1
  0.0 0.7 %copy-done.1 = s32[2048]{0:T(1024)S(1)} copy-done((s32[2048]{0:T(1024)S(1)}, s32[2048]{0:T(1024)}, u32[]{:S(2)}) %copy-start.1) | copy-done | bytes 8216
  0.7 0.0 copy-start.3
  0.7 0.7 %copy-done.3 = bf16[2,128]{1,0:T(2,128)(2,1)S(1)} copy-done((bf16[2,128]{1,0:T(2,128)(2,1)S(1)}, bf16[2,128]{1,0:T(2,128)(2,1)}, u32[]{:S(2)}) %copy-start.3) | copy-done | bytes 536
  1.4 0.0 copy-start
  1.4 8.4 %project.1 = (bf16[912,1024]{1,0:T(8,128)(2,1)S(1)}, bf16[896,1024]{1,0:T(8,128)(2,1)S(1)}, bf16[1024,2048]{1,0:T(8,128)(2,1)S(1)}, bf16[528,2048]{1,0:T(8,128)(...) custom-call(s32[1]{0:T(128)} %bitcast.place, ...), custom_call_target="tpu_custom_call" | custom-call | tf_op jit(solution)/shard_map/project/pallas_call | solution.py:68
  9.7 0.5 collective-permute-start
  10.3 0.0 copy-done
  10.3 4.7 %spectrum.1 = (f32[896,512]{1,0:T(8,128)S(1)}, f32[896,512]{1,0:T(8,128)S(1)}) custom-call(s32[1]{0:T(128)} %bitcast.place, bf16[528,2048]{1,0:T(8,128)(2,1)S(1)} %get-tuple-element.22.stack, s32[1,2048]{1,0:T(1,128)S(1)} %bitcast.5, bf16[896,1024]{1,0:T(8,128)(2,1)S(1)} %get-tuple-element.23.table, f32[896,128]{1,0:T(8,128)S(1)} %get-tuple-element.24.last, ...), custom_call_target="tpu_custom_call" | custom-call | tf_op jit(solution)/shard_map/spectrum/pallas_call | solution.py:68
  15.0 0.0 collective-permute-done.other
  15.0 1.0 %respond.1 = bf16[272,512]{1,0:T(8,128)(2,1)S(1)} custom-call(s32[1]{0:T(128)} %bitcast.place, f32[896,512]{1,0:T(8,128)S(1)} %get-tuple-element.30.own, bf16[912,1024]{1,0:T(8,128)(2,1)S(1)} %collective-permute-done.other, f32[896,512]{1,0:T(8,128)S(1)} %get-tuple-element.31.spec, bf16[256,1792]{1,0:T(8,128)(2,1)S(1)} %get-tuple-element.29.inverse, ...), custom_call_target="tpu_custom_call" | custom-call | tf_op jit(solution)/shard_map/respond/pallas_call | solution.py:68
  16.1 2.6 %collective-permute-start.1 = (bf16[272,512]{1,0:T(8,128)(2,1)S(1)}, bf16[272,512]{1,0:T(8,128)(2,1)S(1)}, u32[]{:S(2)}, u32[]{:S(2)}) collective-permute-start(bf16[272,512]{1,0:T(8,128)(2,1)S(1)} %respond.1), channel_id=1, source_target_pairs={{0,2},{1,3},{2,0},{3,1},{4,6},{5,7},{6,4},{7,5},{8,10},{9,11},{10,... | collective-permute-start | bytes 835592 | tf_op jit(solution)/shard_map/ppermute | solution.py:297
  18.6 6.5 %whole.1.own = f32[256,512]{1,0:T(8,128)S(1)} custom-call(s32[1]{0:T(128)} %bitcast.place, bf16[528,2048]{1,0:T(8,128)(2,1)S(1)} %get-tuple-element.22.stack, s32[1,2048]{1,0:T(1,128)S(1)} %bitcast.6, bf16[896,1024]{1,0:T(8,128)(2,1)S(1)} %get-tuple-element.23.table, f32[896,128]{1,0:T(8,128)S(1)} %get-tuple-element.24.last, ...), custom_call_target="tpu_custom_call" | custom-call | tf_op jit(solution)/shard_map/whole/pallas_call | solution.py:68
  25.1 0.0 copy-start.2
  25.1 0.8 %collective-permute-done.1.got = bf16[272,512]{1,0:T(8,128)(2,1)S(1)} collective-permute-done((bf16[272,512]{1,0:T(8,128)(2,1)S(1)}, bf16[272,512]{1,0:T(8,128)(2,1)S(1)}, u32[]{:S(2)}, u32[]{:S(2)}) %collective-permute-start.1) | collective-permute-done | bytes 278560 | tf_op jit(solution)/shard_map/ppermute | solution.py:297
  25.9 0.1 fold.1
  26.0 1.9 %collective-permute-start.2 = (bf16[272,128]{1,0:T(8,128)(2,1)S(1)}, bf16[272,128]{1,0:T(8,128)(2,1)S(1)}, u32[]{:S(2)}, u32[]{:S(2)}) collective-permute-start(bf16[272,128]{1,0:T(8,128)(2,1)S(1)} %get-tuple-element.33), channel_id=1, source_target_pairs={{0,4},{1,5},{2,6},{3,7},{4,0},{5,1},{6,2},{7,3},{8,12},{9,13},{10,... | collective-permute-start | bytes 208904 | tf_op jit(solution)/shard_map/ppermute | solution.py:297
  27.9 2.6 %collective-permute-start.3 = (bf16[272,128]{1,0:T(8,128)(2,1)S(1)}, bf16[272,128]{1,0:T(8,128)(2,1)S(1)}, u32[]{:S(2)}, u32[]{:S(2)}) collective-permute-start(bf16[272,128]{1,0:T(8,128)(2,1)S(1)} %get-tuple-element.34), channel_id=1, source_target_pairs={{0,8},{1,9},{2,10},{3,11},{4,12},{5,13},{6,14},{7,15},{8,0},{9,1},... | collective-permute-start | bytes 208904 | tf_op jit(solution)/shard_map/ppermute | solution.py:297
  30.5 0.0 collective-permute-start.4
  30.5 0.0 collective-permute-done.2.first
  30.5 4.8 %collective-permute-done.3.second = bf16[272,128]{1,0:T(8,128)(2,1)S(1)} collective-permute-done((bf16[272,128]{1,0:T(8,128)(2,1)S(1)}, bf16[272,128]{1,0:T(8,128)(2,1)S(1)}, u32[]{:S(2)}, u32[]{:S(2)}) %collective-permute-start.3) | collective-permute-done | bytes 69664 | tf_op jit(solution)/shard_map/ppermute | solution.py:297
  35.3 1.4 %collective-permute-done.4.third = bf16[272,128]{1,0:T(8,128)(2,1)S(1)} collective-permute-done((bf16[272,128]{1,0:T(8,128)(2,1)S(1)}, bf16[272,128]{1,0:T(8,128)(2,1)S(1)}, u32[]{:S(2)}, u32[]{:S(2)}) %collective-permute-start.4) | collective-permute-done | bytes 69664 | tf_op jit(solution)/shard_map/ppermute | solution.py:297
  36.8 1.9 %collective-permute-start.7 = (bf16[256,128]{1,0:T(8,128)(2,1)S(1)}, bf16[256,128]{1,0:T(8,128)(2,1)S(1)}, u32[]{:S(2)}, u32[]{:S(2)}) collective-permute-start(bf16[256,128]{1,0:T(8,128)(2,1)S(1)} %settle.1), channel_id=1, source_target_pairs={{0,12},{1,13},{2,14},{3,15},{4,8},{5,9},{6,10},{7,11},{8,4},{9,5},... | collective-permute-start | bytes 196616 | tf_op jit(solution)/shard_map/ppermute | solution.py:297
  38.7 0.3 collective-permute-start.6
  38.9 2.3 %collective-permute-start.5 = (bf16[256,128]{1,0:T(8,128)(2,1)S(1)}, bf16[256,128]{1,0:T(8,128)(2,1)S(1)}, u32[]{:S(2)}, u32[]{:S(2)}) collective-permute-start(bf16[256,128]{1,0:T(8,128)(2,1)S(1)} %settle.1), channel_id=1, source_target_pairs={{0,4},{1,5},{2,6},{3,7},{4,0},{5,1},{6,2},{7,3},{8,12},{9,13},{10,... | collective-permute-start | bytes 196616 | tf_op jit(solution)/shard_map/ppermute | solution.py:297
  41.2 1.7 %collective-permute-done.7 = bf16[256,128]{1,0:T(8,128)(2,1)S(1)} collective-permute-done((bf16[256,128]{1,0:T(8,128)(2,1)S(1)}, bf16[256,128]{1,0:T(8,128)(2,1)S(1)}, u32[]{:S(2)}, u32[]{:S(2)}) %collective-permute-start.7) | collective-permute-done | bytes 65568 | tf_op jit(solution)/shard_map/ppermute | solution.py:297
  42.9 1.4 %collective-permute-done.6 = bf16[256,128]{1,0:T(8,128)(2,1)S(1)} collective-permute-done((bf16[256,128]{1,0:T(8,128)(2,1)S(1)}, bf16[256,128]{1,0:T(8,128)(2,1)S(1)}, u32[]{:S(2)}, u32[]{:S(2)}) %collective-permute-start.6) | collective-permute-done | bytes 65568 | tf_op jit(solution)/shard_map/ppermute | solution.py:297
  44.4 0.0 collective-permute-done.5
  44.4 1.5 %collective-permute-start.8 = (bf16[256,512]{1,0:T(8,128)(2,1)S(1)}, bf16[256,512]{1,0:T(8,128)(2,1)S(1)}, u32[]{:S(2)}, u32[]{:S(2)}) collective-permute-start(bf16[256,512]{1,0:T(8,128)(2,1)S(1)} %pad_maximum_fusion.after.quarter), channel_id=1, source_target_pairs={{0,2},{1,3},{2,0},{3,1},{4,6},{5,7},{6,4},{7,5},{8,10},{9,11},{10,... | collective-permute-start | bytes 786440 | tf_op jit(solution)/shard_map/ppermute | solution.py:297
  46.0 0.0 copy-done.2
  46.0 3.6 %mixers.1 = (f32[8,2048]{1,0:T(8,128)S(1)}, bf16[2048,2048]{1,0:T(8,128)(2,1)S(1)}) custom-call(s32[1]{0:T(128)} %bitcast.place, s32[1,2048]{1,0:T(1,128)S(1)} %bitcast.7, s32[1,2048]{1,0:T(1,128)S(1)} %bitcast.9, bf16[16,128]{1,0:T(8,128)(2,1)S(1)} %get-tuple-element.36.known, bf16[272,128]{1,0:T(8,128)(2,1)S(1)} %collective-permute-done.2.first, ...), custom_call_target="tpu_custom_call" | custom-call | tf_op jit(solution)/shard_map/mixers/pallas_call | solution.py:68
  49.5 1.3 %collective-permute-done.8.got = bf16[256,512]{1,0:T(8,128)(2,1)S(1)} collective-permute-done((bf16[256,512]{1,0:T(8,128)(2,1)S(1)}, bf16[256,512]{1,0:T(8,128)(2,1)S(1)}, u32[]{:S(2)}, u32[]{:S(2)}) %collective-permute-start.8) | collective-permute-done | bytes 262176 | tf_op jit(solution)/shard_map/ppermute | solution.py:297
  50.9 0.1 collective-permute-start.9
  51.0 1.2 %mate.1.mates = f32[256,2048]{1,0:T(8,128)S(1)} custom-call(bf16[256,1024]{1,0:T(8,128)(2,1)S(1)} %join.1.resp, bf16[2048,2048]{1,0:T(8,128)(2,1)S(1)} %get-tuple-element.38.pick), custom_call_target="tpu_custom_call" | custom-call | tf_op jit(solution)/shard_map/mate/pallas_call | solution.py:68
  52.2 0.6 %collective-permute-done.9.other = bf16[256,1024]{1,0:T(8,128)(2,1)S(1)} collective-permute-done((bf16[256,1024]{1,0:T(8,128)(2,1)S(1)}, bf16[256,1024]{1,0:T(8,128)(2,1)S(1)}, u32[]{:S(2)}, u32[]{:S(2)}) %collective-permute-start.9) | collective-permute-done | bytes 524320 | tf_op jit(solution)/shard_map/ppermute | solution.py:297
  52.9 3.7 %expand.1 = bf16[1024,256]{1,0:T(8,128)(2,1)} custom-call(s32[1]{0:T(128)} %bitcast.place, bf16[256,1024]{1,0:T(8,128)(2,1)S(1)} %join.1.resp, bf16[256,1024]{1,0:T(8,128)(2,1)S(1)} %collective-permute-done.9.other, f32[256,2048]{1,0:T(8,128)S(1)} %mate.1.mates, f32[8,2048]{1,0:T(8,128)S(1)} %get-tuple-element.37.before.coef, ...), custom_call_target="tpu_custom_call" | custom-call | tf_op jit(solution)/shard_map/expand/pallas_call | solution.py:68
  (3 shorter events, 0.1 us)
Async XLA Ops:
  0.0 0.7 %copy-start.1 = (s32[2048]{0:T(1024)S(1)}, s32[2048]{0:T(1024)}, u32[]{:S(2)}) copy-start(s32[2048]{0:T(1024)} %param.17) | copy-start | bytes 24580
  0.7 0.7 %copy-start.3 = (bf16[2,128]{1,0:T(2,128)(2,1)S(1)}, bf16[2,128]{1,0:T(2,128)(2,1)}, u32[]{:S(2)}) copy-start(bf16[2,128]{1,0:T(2,128)(2,1)} %coef.5) | copy-start | bytes 1540
  1.4 8.9 %copy-start = (s32[2048]{0:T(1024)S(1)}, s32[2048]{0:T(1024)}, u32[]{:S(2)}) copy-start(s32[2048]{0:T(1024)} %param.14) | copy-start | bytes 24580
  9.7 5.3 %collective-permute-start = (bf16[912,1024]{1,0:T(8,128)(2,1)S(1)}, bf16[912,1024]{1,0:T(8,128)(2,1)S(1)}, u32[]{:S(2)}, u32[]{:S(2)}) collective-permute-start(bf16[912,1024]{1,0:T(8,128)(2,1)S(1)} %get-tuple-element.28), channel_id=1, source_target_pairs={{0,1},{1,0},{2,3},{3,2},{4,5},{5,4},{6,7},{7,6},{8,9},{9,8},{10,11... | collective-permute-start | bytes 5603336 | tf_op jit(solution)/shard_map/ppermute | solution.py:297
  16.1 9.9 %collective-permute-start.1 = (bf16[272,512]{1,0:T(8,128)(2,1)S(1)}, bf16[272,512]{1,0:T(8,128)(2,1)S(1)}, u32[]{:S(2)}, u32[]{:S(2)}) collective-permute-start(bf16[272,512]{1,0:T(8,128)(2,1)S(1)} %respond.1), channel_id=1, source_target_pairs={{0,2},{1,3},{2,0},{3,1},{4,6},{5,7},{6,4},{7,5},{8,10},{9,11},{10,... | collective-permute-start | bytes 835592 | tf_op jit(solution)/shard_map/ppermute | solution.py:297
  25.1 20.9 %copy-start.2 = (s32[2048]{0:T(1024)S(1)}, s32[2048]{0:T(1024)}, u32[]{:S(2)}) copy-start(s32[2048]{0:T(1024)} %param.15) | copy-start | bytes 24580
  26.0 4.5 %collective-permute-start.2 = (bf16[272,128]{1,0:T(8,128)(2,1)S(1)}, bf16[272,128]{1,0:T(8,128)(2,1)S(1)}, u32[]{:S(2)}, u32[]{:S(2)}) collective-permute-start(bf16[272,128]{1,0:T(8,128)(2,1)S(1)} %get-tuple-element.33), channel_id=1, source_target_pairs={{0,4},{1,5},{2,6},{3,7},{4,0},{5,1},{6,2},{7,3},{8,12},{9,13},{10,... | collective-permute-start | bytes 208904 | tf_op jit(solution)/shard_map/ppermute | solution.py:297
  27.9 7.4 %collective-permute-start.3 = (bf16[272,128]{1,0:T(8,128)(2,1)S(1)}, bf16[272,128]{1,0:T(8,128)(2,1)S(1)}, u32[]{:S(2)}, u32[]{:S(2)}) collective-permute-start(bf16[272,128]{1,0:T(8,128)(2,1)S(1)} %get-tuple-element.34), channel_id=1, source_target_pairs={{0,8},{1,9},{2,10},{3,11},{4,12},{5,13},{6,14},{7,15},{8,0},{9,1},... | collective-permute-start | bytes 208904 | tf_op jit(solution)/shard_map/ppermute | solution.py:297
  30.5 6.2 %collective-permute-start.4 = (bf16[272,128]{1,0:T(8,128)(2,1)S(1)}, bf16[272,128]{1,0:T(8,128)(2,1)S(1)}, u32[]{:S(2)}, u32[]{:S(2)}) collective-permute-start(bf16[272,128]{1,0:T(8,128)(2,1)S(1)} %get-tuple-element.35), channel_id=1, source_target_pairs={{0,12},{1,13},{2,14},{3,15},{4,8},{5,9},{6,10},{7,11},{8,4},{9,5},... | collective-permute-start | bytes 208904 | tf_op jit(solution)/shard_map/ppermute | solution.py:297
  36.8 6.1 %collective-permute-start.7 = (bf16[256,128]{1,0:T(8,128)(2,1)S(1)}, bf16[256,128]{1,0:T(8,128)(2,1)S(1)}, u32[]{:S(2)}, u32[]{:S(2)}) collective-permute-start(bf16[256,128]{1,0:T(8,128)(2,1)S(1)} %settle.1), channel_id=1, source_target_pairs={{0,12},{1,13},{2,14},{3,15},{4,8},{5,9},{6,10},{7,11},{8,4},{9,5},... | collective-permute-start | bytes 196616 | tf_op jit(solution)/shard_map/ppermute | solution.py:297
  38.7 5.7 %collective-permute-start.6 = (bf16[256,128]{1,0:T(8,128)(2,1)S(1)}, bf16[256,128]{1,0:T(8,128)(2,1)S(1)}, u32[]{:S(2)}, u32[]{:S(2)}) collective-permute-start(bf16[256,128]{1,0:T(8,128)(2,1)S(1)} %settle.1), channel_id=1, source_target_pairs={{0,8},{1,9},{2,10},{3,11},{4,12},{5,13},{6,14},{7,15},{8,0},{9,1},... | collective-permute-start | bytes 196616 | tf_op jit(solution)/shard_map/ppermute | solution.py:297
  38.9 5.4 %collective-permute-start.5 = (bf16[256,128]{1,0:T(8,128)(2,1)S(1)}, bf16[256,128]{1,0:T(8,128)(2,1)S(1)}, u32[]{:S(2)}, u32[]{:S(2)}) collective-permute-start(bf16[256,128]{1,0:T(8,128)(2,1)S(1)} %settle.1), channel_id=1, source_target_pairs={{0,4},{1,5},{2,6},{3,7},{4,0},{5,1},{6,2},{7,3},{8,12},{9,13},{10,... | collective-permute-start | bytes 196616 | tf_op jit(solution)/shard_map/ppermute | solution.py:297
  44.4 6.4 %collective-permute-start.8 = (bf16[256,512]{1,0:T(8,128)(2,1)S(1)}, bf16[256,512]{1,0:T(8,128)(2,1)S(1)}, u32[]{:S(2)}, u32[]{:S(2)}) collective-permute-start(bf16[256,512]{1,0:T(8,128)(2,1)S(1)} %pad_maximum_fusion.after.quarter), channel_id=1, source_target_pairs={{0,2},{1,3},{2,0},{3,1},{4,6},{5,7},{6,4},{7,5},{8,10},{9,11},{10,... | collective-permute-start | bytes 786440 | tf_op jit(solution)/shard_map/ppermute | solution.py:297
  50.9 2.0 %collective-permute-start.9 = (bf16[256,1024]{1,0:T(8,128)(2,1)S(1)}, bf16[256,1024]{1,0:T(8,128)(2,1)S(1)}, u32[]{:S(2)}, u32[]{:S(2)}) collective-permute-start(bf16[256,1024]{1,0:T(8,128)(2,1)S(1)} %join.1.resp), channel_id=1, source_target_pairs={{0,1},{1,0},{2,3},{3,2},{4,5},{5,4},{6,7},{7,6},{8,9},{9,8},{10,11... | collective-permute-start | bytes 1572872 | tf_op jit(solution)/shard_map/ppermute | solution.py:297

commit v5 on v4

--- a/solution.py
+++ b/solution.py
@@ -36,7 +36,7 @@
 
 def forward_table(hist):
     cos, sin = turns(hist // 2, np.arange(hist))
-    return np.concatenate(split(np.concatenate([cos, -sin])), axis=1)
+    return np.concatenate([cos, -sin]).astype(BF)
 
 
 def tap_table(hist, taps):
@@ -53,7 +53,8 @@
 
 def inverse_table(hist, taps):
     cos, sin = turns(hist // 2, np.arange(W) + taps - 1)
-    return np.concatenate(split(np.concatenate([cos, -sin]).T * (2.0 / hist)), axis=1)
+    high, low = split(np.concatenate([cos, -sin]).T * (2.0 / hist))
+    return np.concatenate([high, high, low], axis=1)
 
 
 def call(kernel, name, out_shape, *args, scalars=1, far=(), scratch=(), limit=16):
@@ -93,16 +94,20 @@
 
 
 def project_kernel(
-    place, loads_far, forward_far, shapes_far, taps_far, table_far, last_far, phase_far, inverse_far, offsets, coef,
-    sent, lft, shapes, stack, table, last, phase, inverse, loads, forward, taps, sems,
+    place, loads_far, forward_far, shapes_far, taps_far, table_far, last_far, phase_far, inverse_far, offsets_far, coef_far,
+    sent, lft, shapes, stack, table, last, phase, inverse, coef, loads, forward, taps, offsets, sems,
 ):
     rows, half = loads.shape[0], sent.shape[1]
     hist = lft.shape[0]
     core = place[0] & 1
     far, own = block((1 - core) * half, half), block(core * half, half)
-    pairs = [
-        (forward_far, forward),
-        (loads_far, loads),
+    step = 256
+    chunks = [pl.ds(r, step) for r in range(0, rows, step)]
+    pairs = [(forward_far, forward)] + [(loads_far.at[r, :], loads.at[r, :]) for r in chunks]
+    first = len(pairs)
+    pairs += [
+        (coef_far, coef),
+        (offsets_far, offsets),
         (shapes_far.at[:, far], shapes.at[:, far]),
         (taps_far, taps),
         (table_far, table),
@@ -112,15 +117,18 @@
         (inverse_far, inverse),
     ]
     copies = [pltpu.make_async_copy(a, b, sems.at[i]) for i, (a, b) in enumerate(pairs)]
-    for copy in copies:
+    for copy in copies[:first]:
         copy.start()
     copies[0].wait()
     copies[1].wait()
-    for r in range(0, rows, 256):
-        part = loads[r : r + 256, :]
-        lft[:, r : r + 256] = dot(forward[...], jnp.concatenate([part, part], axis=1), NT).astype(BF)
-    copies[2].wait()
-    copies[3].wait()
+    for copy in copies[first:]:
+        copy.start()
+    for i, r in enumerate(chunks):
+        if i:
+            copies[1 + i].wait()
+        lft[:, i * step : (i + 1) * step] = dot(forward[...], loads[r, :], NT).astype(BF)
+    for copy in copies[first : first + 4]:
+        copy.wait()
     count = taps.shape[0] - 1
     for c in range(0, half, 256):
         sent[:hist, c : c + 256] = dot(lft[...], shapes[:, block((1 - core) * half + c, 256)]).astype(BF)
@@ -133,7 +141,7 @@
     end = taps[count : count + 1, :]
     tail = jnp.where(index == 0, end, jnp.where(index == 1, offsets[...].astype(F32), 0.0))
     stack[count:, :] = tail.astype(BF)
-    for copy in copies[4:]:
+    for copy in copies[first + 4 :]:
         copy.wait()
 
 
@@ -180,8 +188,10 @@
 def impose(total, tre, tim, inverse):
     half = tre.shape[0]
     re, im = total[:half], total[half:]
-    product = jnp.concatenate([re * tre - im * tim, re * tim + im * tre], axis=0).astype(BF)
-    return dot(inverse[...], jnp.concatenate([product, product], axis=0))
+    product = jnp.concatenate([re * tre - im * tim, re * tim + im * tre], axis=0)
+    high = product.astype(BF)
+    low = (product - high.astype(F32)).astype(BF)
+    return dot(inverse[...], jnp.concatenate([high, low, high], axis=0))
 
 
 def whole_kernel(which, place, stack, order, table, last, phase, lft, shapes, other, inverse, out):
@@ -224,7 +234,7 @@
             out[W:, :] = known[...]
 
 
-def settle_kernel(keep, first, second, third, out):
+def settle_kernel(after, keep, first, second, third, out):
     total = keep[...]
     for got in (first, second, third):
         total = total + got[:W, :].astype(F32)
@@ -238,37 +248,52 @@
     return (me & 1) * (modes // 2)
 
 
-def mixers_kernel(place, order, partner, known, first, second, third, after, coef, pick, held):
-    me, mask = place[0], mask_of(place, 16, order.shape[1])
+def pick_kernel(devices, place, partner, after, pick):
+    modes = partner.shape[1]
+    mask = mask_of(place, devices, modes)
+    for c in range(0, modes, 256):
+        mode = lax.broadcasted_iota(I32, (256, modes), 0) + c
+        pick[c : c + 256, :] = hot((mode ^ mask) == partner[...])
+
+
+def mixers_kernel(place, order, known, third, second, first, after, coef, held):
+    me = place[0]
     held[...] = jnp.zeros(held.shape, F32)
     for z, rows in enumerate((known, first, second, third)):
         top = rows.shape[0] - EXTRA
         for low in range(4):
             where = block((me ^ (4 * z + low)) * LANES, LANES)
             held[0:2, where] = rows[top : top + EXTRA, :].astype(F32)[2 * low : 2 * low + 2]
-    mixers(order, partner, mask, held, coef, pick)
-
-
-def mixers(order, partner, mask, held, coef, pick):
+    mixers(order, held, coef)
+
+
+def mixers(order, held, coef):
     modes = order.shape[1]
     table = held[...].astype(BF)
     for c in range(0, modes, 256):
         mode = lax.broadcasted_iota(I32, (256, modes), 0) + c
         coef[:, c : c + 256] = dot(table, hot(mode == order[...]), NT)
-        mode = lax.broadcasted_iota(I32, (256, modes), 0) + c
-        pick[c : c + 256, :] = hot((mode ^ mask) == partner[...])
-
-
-def plain_mixers_kernel(devices, place, order, partner, every, coef, pick, held):
+
+
+def plain_mixers_kernel(order, every, coef, held):
     held[...] = jnp.zeros(held.shape, F32)
     held[0:2, :] = every[...].astype(F32)
-    mixers(order, partner, mask_of(place, devices, order.shape[1]), held, coef, pick)
-
-
-def join_kernel(quarter, got, before, out):
-    width = quarter.shape[1]
-    out[:, :width] = quarter[...]
-    out[:, width:] = got[...]
+    mixers(order, held, coef)
+
+
+def join_kernel(*refs):
+    *parts, out = refs
+    start = 0
+    for part in parts:
+        out[:, start : start + part.shape[1]] = part[...]
+        start += part.shape[1]
+
+
+def join(*parts, after=None):
+    width = sum(part.shape[1] for part in parts)
+    kernel = join_kernel if after is None else lambda _, *refs: join_kernel(*refs)
+    first = () if after is None else (after,)
+    return call(kernel, "join", [array(parts[0].shape[0], width)], *first, *parts, scalars=0)[0]
 
 
 def mate_kernel(resp, pick, out):
@@ -308,15 +333,15 @@
     inverse = inverse_table(hist, count)
     order, mates, offsets, taps = mode_order[None], partner[None], offsets[None], taps.T
 
-    sent, lft, shapes, stack, tap_forward, last, phase, inverse = call(
+    sent, lft, shapes, stack, tap_forward, last, phase, inverse, coef_near = call(
         project_kernel, "project",
         [near(hist + EXTRA, half), near(hist, rows), near(rows, modes), near(count - 1 + EXTRA, modes)]
-        + [near(*tap_forward.shape), near(*last.shape, dtype=F32), near(*phase.shape), near(*inverse.shape)],
+        + [near(*tap_forward.shape), near(*last.shape, dtype=F32), near(*phase.shape), near(*inverse.shape), near(*coef.shape)],
         place, loads, forward, shapes, taps, tap_forward, last, phase, inverse, offsets, coef,
-        far=range(1, 9),
+        far=range(1, 11),
         scratch=[
             pltpu.VMEM(loads.shape, BF), pltpu.VMEM(forward.shape, BF), pltpu.VMEM(taps.shape, F32),
-            pltpu.SemaphoreType.DMA((9,)),
+            pltpu.VMEM(offsets.shape, I32), pltpu.SemaphoreType.DMA((10 + rows // 256,)),
         ],
         limit=24,
     )
@@ -333,26 +358,31 @@
             spectrum_kernel, "spectrum", [near(hist, quarter, dtype=F32)] * 2, place, *common
         )
         away = call(
-            respond_kernel, "respond", [array(W + EXTRA, quarter)], place, own, got, spec, inverse, coef
+            respond_kernel, "respond", [array(W + EXTRA, quarter)], place, own, got, spec, inverse, coef_near
         )[0]
         away = swap(away, devices, 2)
         keep, known, *parts = call(
             fold_kernel, "fold", [array(W, size, dtype=F32), array(EXTRA, LANES)] + [array(W + EXTRA, size)] * 3,
-            place, respond(0), away, coef, got,
+            place, respond(0), away, coef_near, got,
         )
-        parts = [swap(part, devices, 4 * d) for d, part in zip((1, 2, 3), parts)]
-        total = call(settle_kernel, "settle", [array(W, size)], keep, *parts, scalars=0)[0]
-        resp = jnp.concatenate([total] + [swap(total, devices, 4 * d) for d in (1, 2, 3)], axis=1)
-        mode_coef, pick = call(
-            mixers_kernel, "mixers", [array(8, modes, dtype=F32), near(modes, modes)],
-            place, order, mates, known, *parts, resp, scratch=[pltpu.VMEM((8, modes), F32)],
-        )
-        resp = call(join_kernel, "join", [array(W, half)], resp, swap(resp, devices, 2), mode_coef, scalars=0)[0]
+        parts = [swap(part, devices, 4 * d) for d, part in reversed(list(zip((1, 2, 3), parts)))]
+        pick = call(functools.partial(pick_kernel, devices), "pick", [near(modes, modes)], place, mates, keep)[0]
+        total = call(settle_kernel, "settle", [array(W, size)], pick, keep, *parts, scalars=0)[0]
+        spread = [swap(total, devices, 4 * d) for d in (1, 2, 3)]
+        ends = join(total, spread[0])
+        mode_coef = call(
+            mixers_kernel, "mixers", [array(8, modes, dtype=F32)],
+            place, order, known, *parts, ends, scratch=[pltpu.VMEM((8, modes), F32)],
+        )[0]
+        halves = [swap(ends, devices, 2), join(*spread[1:], after=mode_coef)]
+        halves = [ends, halves[1], halves[0], swap(halves[1], devices, 2)]
+        resp = join(*halves)
     else:
-        mode_coef, pick = call(
-            functools.partial(plain_mixers_kernel, devices), "mixers", [array(8, modes, dtype=F32), near(modes, modes)],
-            place, order, mates, lax.all_gather(coef, "frdm", axis=1, tiled=True), scratch=[pltpu.VMEM((8, modes), F32)],
-        )
+        pick = call(functools.partial(pick_kernel, devices), "pick", [near(modes, modes)], place, mates, mates)[0]
+        mode_coef = call(
+            plain_mixers_kernel, "mixers", [array(8, modes, dtype=F32)],
+            order, lax.all_gather(coef, "frdm", axis=1, tiled=True), scalars=0, scratch=[pltpu.VMEM((8, modes), F32)],
+        )[0]
         resp = jnp.concatenate([respond(q) for q in (2, 3)], axis=1)
         groups = [list(range(c, devices, 2)) for c in range(2)]
         resp = lax.psum(resp, "frdm", axis_index_groups=groups).astype(BF)

time: 56.8 us -> 56.9 us (level)
  Pallas kernels: 29.3 us -> 30.8 us
  local copies, waits for them, and re-layouts: 1.36 us -> 0.01 us
    pallas_call x10 -> x13, Pallas kernels: 29.3 us -> 30.8 us  [call(): pl.pallas_call(kernel, in_specs=places, out_specs=[vmem] * len(out_shape)...]
    unnamed x8 -> x4, local copies, waits for them, and re-layouts: 1.36 us -> 0.01 us
    ppermute x10 -> x11, waiting for transfers between devices: 12.1 us -> 12.4 us  [swap(): return lax.ppermute(x, 'frdm', [(i, i ^ bits) for i in range(devices)])]
    ppermute x10 -> x11, starting transfers between devices: 13.7 us -> 13.4 us  [swap(): return lax.ppermute(x, 'frdm', [(i, i ^ bits) for i in range(devices)])]
  transfers between devices with their start and end apart: 10 -> 11, of which waited for: 7 -> 8; matrix products, arithmetic and copies ran while one was open for 0% -> 0% of each run, Pallas kernels for 28% -> 30%
where the time goes in v5:
time: 56.9 us; the launch traced here: 56.7 us
  Pallas kernels  30.8 us (54%)
  starting transfers between devices  13.4 us (24%)
  waiting for transfers between devices  12.4 us (22%)
    pallas_call x13, Pallas kernels, call(): pl.pallas_call(kernel, in_specs=places, out_specs=[vmem] * len(out_shape)...  30.8 us
    ppermute x11, starting transfers between devices, swap(): return lax.ppermute(x, 'frdm', [(i, i ^ bits) for i in range(devices)])  13.4 us
    ppermute x11, waiting for transfers between devices, swap(): return lax.ppermute(x, 'frdm', [(i, i ^ bits) for i in range(devices)])  12.4 us
  transfers between devices with their start and end apart: 11, of which 8 were waited for; matrix products, arithmetic and copies ran while one was open for 0% of the time, Pallas kernels for 30%

profile of v5, /device:TPU:0, one launch (start us, length us, event | category | flops | bytes accessed | tf_op | source)
XLA Modules:
  0.0 56.7 jit_solution(6758817977042261712)
XLA Ops:
  0.0 0.0 copy-start
  0.0 8.5 %project.1 = (bf16[912,1024]{1,0:T(8,128)(2,1)S(1)}, bf16[896,1024]{1,0:T(8,128)(2,1)S(1)}, bf16[1024,2048]{1,0:T(8,128)(2,1)S(1)}, bf16[528,2048]{1,0:T(8,128)(...) custom-call(s32[1]{0:T(128)} %bitcast.place, ...), custom_call_target="tpu_custom_call" | custom-call | tf_op jit(solution)/shard_map/project/pallas_call | solution.py:69
  8.5 0.5 collective-permute-start
  9.0 0.0 copy-done
  9.0 4.8 %spectrum.1 = (f32[896,512]{1,0:T(8,128)S(1)}, f32[896,512]{1,0:T(8,128)S(1)}) custom-call(s32[1]{0:T(128)} %bitcast.place, bf16[528,2048]{1,0:T(8,128)(2,1)S(1)} %get-tuple-element.21.stack, s32[1,2048]{1,0:T(1,128)S(1)} %bitcast.5, bf16[896,1024]{1,0:T(8,128)(2,1)S(1)} %get-tuple-element.22.table, f32[896,128]{1,0:T(8,128)S(1)} %get-tuple-element.23.last, ...), custom_call_target="tpu_custom_call" | custom-call | tf_op jit(solution)/shard_map/spectrum/pallas_call | solution.py:69
  13.8 0.0 collective-permute-done.other
  13.8 1.4 %respond.1 = bf16[272,512]{1,0:T(8,128)(2,1)S(1)} custom-call(s32[1]{0:T(128)} %bitcast.place, f32[896,512]{1,0:T(8,128)S(1)} %get-tuple-element.29.own, bf16[912,1024]{1,0:T(8,128)(2,1)S(1)} %collective-permute-done.other, f32[896,512]{1,0:T(8,128)S(1)} %get-tuple-element.30.spec, bf16[256,2688]{1,0:T(8,128)(2,1)S(1)} %get-tuple-element.28.inverse, ...), custom_call_target="tpu_custom_call" | custom-call | tf_op jit(solution)/shard_map/respond/pallas_call | solution.py:69
  15.2 2.6 %collective-permute-start.1 = (bf16[272,512]{1,0:T(8,128)(2,1)S(1)}, bf16[272,512]{1,0:T(8,128)(2,1)S(1)}, u32[]{:S(2)}, u32[]{:S(2)}) collective-permute-start(bf16[272,512]{1,0:T(8,128)(2,1)S(1)} %respond.1), channel_id=1, source_target_pairs={{0,2},{1,3},{2,0},{3,1},{4,6},{5,7},{6,4},{7,5},{8,10},{9,11},{10,... | collective-permute-start | bytes 835592 | tf_op jit(solution)/shard_map/ppermute | solution.py:322
  17.8 7.2 %whole.1.own = f32[256,512]{1,0:T(8,128)S(1)} custom-call(s32[1]{0:T(128)} %bitcast.place, bf16[528,2048]{1,0:T(8,128)(2,1)S(1)} %get-tuple-element.21.stack, s32[1,2048]{1,0:T(1,128)S(1)} %bitcast.6, bf16[896,1024]{1,0:T(8,128)(2,1)S(1)} %get-tuple-element.22.table, f32[896,128]{1,0:T(8,128)S(1)} %get-tuple-element.23.last, ...), custom_call_target="tpu_custom_call" | custom-call | tf_op jit(solution)/shard_map/whole/pallas_call | solution.py:69
  24.9 0.0 copy-start.1
  24.9 0.1 collective-permute-done.1.got
  25.1 0.1 fold.1
  25.2 3.9 %collective-permute-start.2 = (bf16[272,128]{1,0:T(8,128)(2,1)S(1)}, bf16[272,128]{1,0:T(8,128)(2,1)S(1)}, u32[]{:S(2)}, u32[]{:S(2)}) collective-permute-start(bf16[272,128]{1,0:T(8,128)(2,1)S(1)} %get-tuple-element.33), channel_id=1, source_target_pairs={{0,12},{1,13},{2,14},{3,15},{4,8},{5,9},{6,10},{7,11},{8,4},{9,5},... | collective-permute-start | bytes 208904 | tf_op jit(solution)/shard_map/ppermute | solution.py:322
  29.1 0.0 collective-permute-start.3
  29.1 0.6 %collective-permute-start.4 = (bf16[272,128]{1,0:T(8,128)(2,1)S(1)}, bf16[272,128]{1,0:T(8,128)(2,1)S(1)}, u32[]{:S(2)}, u32[]{:S(2)}) collective-permute-start(bf16[272,128]{1,0:T(8,128)(2,1)S(1)} %get-tuple-element.35), channel_id=1, source_target_pairs={{0,4},{1,5},{2,6},{3,7},{4,0},{5,1},{6,2},{7,3},{8,12},{9,13},{10,... | collective-permute-start | bytes 208904 | tf_op jit(solution)/shard_map/ppermute | solution.py:322
  29.8 0.0 copy-done.1
  29.8 1.4 %pick.1.after = bf16[2048,2048]{1,0:T(8,128)(2,1)S(1)} custom-call(s32[1]{0:T(128)} %bitcast.place, s32[1,2048]{1,0:T(1,128)S(1)} %bitcast.8, f32[256,128]{1,0:T(8,128)S(1)} %get-tuple-element.32.after.keep), custom_call_target="tpu_custom_call" | custom-call | tf_op jit(solution)/shard_map/pick/pallas_call | solution.py:69
  31.2 0.6 %collective-permute-done.2.first.third = bf16[272,128]{1,0:T(8,128)(2,1)S(1)} collective-permute-done((bf16[272,128]{1,0:T(8,128)(2,1)S(1)}, bf16[272,128]{1,0:T(8,128)(2,1)S(1)}, u32[]{:S(2)}, u32[]{:S(2)}) %collective-permute-start.2) | collective-permute-done | bytes 69664 | tf_op jit(solution)/shard_map/ppermute | solution.py:322
  31.8 3.2 %collective-permute-done.3.second = bf16[272,128]{1,0:T(8,128)(2,1)S(1)} collective-permute-done((bf16[272,128]{1,0:T(8,128)(2,1)S(1)}, bf16[272,128]{1,0:T(8,128)(2,1)S(1)}, u32[]{:S(2)}, u32[]{:S(2)}) %collective-permute-start.3) | collective-permute-done | bytes 69664 | tf_op jit(solution)/shard_map/ppermute | solution.py:322
  35.0 0.0 collective-permute-done.4.third.first
  35.1 1.1 %collective-permute-start.5 = (bf16[256,128]{1,0:T(8,128)(2,1)S(1)}, bf16[256,128]{1,0:T(8,128)(2,1)S(1)}, u32[]{:S(2)}, u32[]{:S(2)}) collective-permute-start(bf16[256,128]{1,0:T(8,128)(2,1)S(1)} %settle.1.refs_0_), channel_id=1, source_target_pairs={{0,4},{1,5},{2,6},{3,7},{4,0},{5,1},{6,2},{7,3},{8,12},{9,13},{10,... | collective-permute-start | bytes 196616 | tf_op jit(solution)/shard_map/ppermute | solution.py:322
  36.2 1.8 %collective-permute-start.7 = (bf16[256,128]{1,0:T(8,128)(2,1)S(1)}, bf16[256,128]{1,0:T(8,128)(2,1)S(1)}, u32[]{:S(2)}, u32[]{:S(2)}) collective-permute-start(bf16[256,128]{1,0:T(8,128)(2,1)S(1)} %settle.1.refs_0_), channel_id=1, source_target_pairs={{0,12},{1,13},{2,14},{3,15},{4,8},{5,9},{6,10},{7,11},{8,4},{9,5},... | collective-permute-start | bytes 196616 | tf_op jit(solution)/shard_map/ppermute | solution.py:322
  37.9 0.7 %collective-permute-start.6 = (bf16[256,128]{1,0:T(8,128)(2,1)S(1)}, bf16[256,128]{1,0:T(8,128)(2,1)S(1)}, u32[]{:S(2)}, u32[]{:S(2)}) collective-permute-start(bf16[256,128]{1,0:T(8,128)(2,1)S(1)} %settle.1.refs_0_), channel_id=1, source_target_pairs={{0,8},{1,9},{2,10},{3,11},{4,12},{5,13},{6,14},{7,15},{8,0},{9,1},... | collective-permute-start | bytes 196616 | tf_op jit(solution)/shard_map/ppermute | solution.py:322
  38.6 1.8 %collective-permute-done.5.refs_1_ = bf16[256,128]{1,0:T(8,128)(2,1)S(1)} collective-permute-done((bf16[256,128]{1,0:T(8,128)(2,1)S(1)}, bf16[256,128]{1,0:T(8,128)(2,1)S(1)}, u32[]{:S(2)}, u32[]{:S(2)}) %collective-permute-start.5) | collective-permute-done | bytes 65568 | tf_op jit(solution)/shard_map/ppermute | solution.py:322
  40.5 2.3 %mixers.1._.coef = f32[8,2048]{1,0:T(8,128)S(1)} custom-call(s32[1]{0:T(128)} %bitcast.place, s32[1,2048]{1,0:T(1,128)S(1)} %bitcast.7, bf16[16,128]{1,0:T(8,128)(2,1)S(1)} %get-tuple-element.36.known, bf16[272,128]{1,0:T(8,128)(2,1)S(1)} %collective-permute-done.2.first.third, bf16[272,128]{1,0:T(8,128)(2,1)S(1)} %collective-permute-done.3.second, ...), custom_call_target="tpu_custom_call" | custom-call | tf_op jit(solution)/shard_map/mixers/pallas_call | solution.py:69
  42.7 0.0 collective-permute-done.7.refs_1_
  42.7 1.4 %collective-permute-done.6.refs_0_ = bf16[256,128]{1,0:T(8,128)(2,1)S(1)} collective-permute-done((bf16[256,128]{1,0:T(8,128)(2,1)S(1)}, bf16[256,128]{1,0:T(8,128)(2,1)S(1)}, u32[]{:S(2)}, u32[]{:S(2)}) %collective-permute-start.6) | collective-permute-done | bytes 65568 | tf_op jit(solution)/shard_map/ppermute | solution.py:322
  44.1 1.8 %collective-permute-start.9 = (bf16[256,256]{1,0:T(8,128)(2,1)S(1)}, bf16[256,256]{1,0:T(8,128)(2,1)S(1)}, u32[]{:S(2)}, u32[]{:S(2)}) collective-permute-start(bf16[256,256]{1,0:T(8,128)(2,1)S(1)} %join.4.refs_1_), channel_id=1, source_target_pairs={{0,2},{1,3},{2,0},{3,1},{4,6},{5,7},{6,4},{7,5},{8,10},{9,11},{10,... | collective-permute-start | bytes 393224 | tf_op jit(solution)/shard_map/ppermute | solution.py:322
  45.9 0.3 collective-permute-start.8
  46.2 3.0 %collective-permute-done.9.refs_3_ = bf16[256,256]{1,0:T(8,128)(2,1)S(1)} collective-permute-done((bf16[256,256]{1,0:T(8,128)(2,1)S(1)}, bf16[256,256]{1,0:T(8,128)(2,1)S(1)}, u32[]{:S(2)}, u32[]{:S(2)}) %collective-permute-start.9) | collective-permute-done | bytes 131104 | tf_op jit(solution)/shard_map/ppermute | solution.py:322
  49.2 1.6 %collective-permute-done.8.refs_2_ = bf16[256,256]{1,0:T(8,128)(2,1)S(1)} collective-permute-done((bf16[256,256]{1,0:T(8,128)(2,1)S(1)}, bf16[256,256]{1,0:T(8,128)(2,1)S(1)}, u32[]{:S(2)}, u32[]{:S(2)}) %collective-permute-start.8) | collective-permute-done | bytes 131104 | tf_op jit(solution)/shard_map/ppermute | solution.py:322
  50.9 0.1 join.5.resp
  50.9 0.1 collective-permute-start.10
  51.0 1.3 %mate.1.mates = f32[256,2048]{1,0:T(8,128)S(1)} custom-call(bf16[256,1024]{1,0:T(8,128)(2,1)S(1)} %join.5.resp, bf16[2048,2048]{1,0:T(8,128)(2,1)S(1)} %pick.1.after), custom_call_target="tpu_custom_call" | custom-call | tf_op jit(solution)/shard_map/mate/pallas_call | solution.py:69
  52.3 0.6 %collective-permute-done.10.other = bf16[256,1024]{1,0:T(8,128)(2,1)S(1)} collective-permute-done((bf16[256,1024]{1,0:T(8,128)(2,1)S(1)}, bf16[256,1024]{1,0:T(8,128)(2,1)S(1)}, u32[]{:S(2)}, u32[]{:S(2)}) %collective-permute-start.10) | collective-permute-done | bytes 524320 | tf_op jit(solution)/shard_map/ppermute | solution.py:322
  52.9 3.8 %expand.1 = bf16[1024,256]{1,0:T(8,128)(2,1)} custom-call(s32[1]{0:T(128)} %bitcast.place, bf16[256,1024]{1,0:T(8,128)(2,1)S(1)} %join.5.resp, bf16[256,1024]{1,0:T(8,128)(2,1)S(1)} %collective-permute-done.10.other, f32[256,2048]{1,0:T(8,128)S(1)} %mate.1.mates, f32[8,2048]{1,0:T(8,128)S(1)} %mixers.1._.coef, bf16[2048,2048]{1,0:T(8,128)(2,1)S(1)} %pick.1.after, ...), custom_call_target="tpu_custom_call" | custom-call | tf_op jit(solution)/shard_map/expand/pallas_call | solution.py:69
  (3 shorter events, 0.1 us)
Async XLA Ops:
  0.0 9.0 %copy-start = (s32[2048]{0:T(1024)S(1)}, s32[2048]{0:T(1024)}, u32[]{:S(2)}) copy-start(s32[2048]{0:T(1024)} %param.14) | copy-start | bytes 24580
  8.5 5.3 %collective-permute-start = (bf16[912,1024]{1,0:T(8,128)(2,1)S(1)}, bf16[912,1024]{1,0:T(8,128)(2,1)S(1)}, u32[]{:S(2)}, u32[]{:S(2)}) collective-permute-start(bf16[912,1024]{1,0:T(8,128)(2,1)S(1)} %get-tuple-element.27), channel_id=1, source_target_pairs={{0,1},{1,0},{2,3},{3,2},{4,5},{5,4},{6,7},{7,6},{8,9},{9,8},{10,11... | collective-permute-start | bytes 5603336 | tf_op jit(solution)/shard_map/ppermute | solution.py:322
  15.2 9.9 %collective-permute-start.1 = (bf16[272,512]{1,0:T(8,128)(2,1)S(1)}, bf16[272,512]{1,0:T(8,128)(2,1)S(1)}, u32[]{:S(2)}, u32[]{:S(2)}) collective-permute-start(bf16[272,512]{1,0:T(8,128)(2,1)S(1)} %respond.1), channel_id=1, source_target_pairs={{0,2},{1,3},{2,0},{3,1},{4,6},{5,7},{6,4},{7,5},{8,10},{9,11},{10,... | collective-permute-start | bytes 835592 | tf_op jit(solution)/shard_map/ppermute | solution.py:322
  24.9 4.8 %copy-start.1 = (s32[2048]{0:T(1024)S(1)}, s32[2048]{0:T(1024)}, u32[]{:S(2)}) copy-start(s32[2048]{0:T(1024)} %param.15) | copy-start | bytes 24580
  25.2 6.6 %collective-permute-start.2 = (bf16[272,128]{1,0:T(8,128)(2,1)S(1)}, bf16[272,128]{1,0:T(8,128)(2,1)S(1)}, u32[]{:S(2)}, u32[]{:S(2)}) collective-permute-start(bf16[272,128]{1,0:T(8,128)(2,1)S(1)} %get-tuple-element.33), channel_id=1, source_target_pairs={{0,12},{1,13},{2,14},{3,15},{4,8},{5,9},{6,10},{7,11},{8,4},{9,5},... | collective-permute-start | bytes 208904 | tf_op jit(solution)/shard_map/ppermute | solution.py:322
  29.1 5.9 %collective-permute-start.3 = (bf16[272,128]{1,0:T(8,128)(2,1)S(1)}, bf16[272,128]{1,0:T(8,128)(2,1)S(1)}, u32[]{:S(2)}, u32[]{:S(2)}) collective-permute-start(bf16[272,128]{1,0:T(8,128)(2,1)S(1)} %get-tuple-element.34), channel_id=1, source_target_pairs={{0,8},{1,9},{2,10},{3,11},{4,12},{5,13},{6,14},{7,15},{8,0},{9,1},... | collective-permute-start | bytes 208904 | tf_op jit(solution)/shard_map/ppermute | solution.py:322
  29.1 5.9 %collective-permute-start.4 = (bf16[272,128]{1,0:T(8,128)(2,1)S(1)}, bf16[272,128]{1,0:T(8,128)(2,1)S(1)}, u32[]{:S(2)}, u32[]{:S(2)}) collective-permute-start(bf16[272,128]{1,0:T(8,128)(2,1)S(1)} %get-tuple-element.35), channel_id=1, source_target_pairs={{0,4},{1,5},{2,6},{3,7},{4,0},{5,1},{6,2},{7,3},{8,12},{9,13},{10,... | collective-permute-start | bytes 208904 | tf_op jit(solution)/shard_map/ppermute | solution.py:322
  35.1 5.4 %collective-permute-start.5 = (bf16[256,128]{1,0:T(8,128)(2,1)S(1)}, bf16[256,128]{1,0:T(8,128)(2,1)S(1)}, u32[]{:S(2)}, u32[]{:S(2)}) collective-permute-start(bf16[256,128]{1,0:T(8,128)(2,1)S(1)} %settle.1.refs_0_), channel_id=1, source_target_pairs={{0,4},{1,5},{2,6},{3,7},{4,0},{5,1},{6,2},{7,3},{8,12},{9,13},{10,... | collective-permute-start | bytes 196616 | tf_op jit(solution)/shard_map/ppermute | solution.py:322
  36.2 6.6 %collective-permute-start.7 = (bf16[256,128]{1,0:T(8,128)(2,1)S(1)}, bf16[256,128]{1,0:T(8,128)(2,1)S(1)}, u32[]{:S(2)}, u32[]{:S(2)}) collective-permute-start(bf16[256,128]{1,0:T(8,128)(2,1)S(1)} %settle.1.refs_0_), channel_id=1, source_target_pairs={{0,12},{1,13},{2,14},{3,15},{4,8},{5,9},{6,10},{7,11},{8,4},{9,5},... | collective-permute-start | bytes 196616 | tf_op jit(solution)/shard_map/ppermute | solution.py:322
  37.9 6.2 %collective-permute-start.6 = (bf16[256,128]{1,0:T(8,128)(2,1)S(1)}, bf16[256,128]{1,0:T(8,128)(2,1)S(1)}, u32[]{:S(2)}, u32[]{:S(2)}) collective-permute-start(bf16[256,128]{1,0:T(8,128)(2,1)S(1)} %settle.1.refs_0_), channel_id=1, source_target_pairs={{0,8},{1,9},{2,10},{3,11},{4,12},{5,13},{6,14},{7,15},{8,0},{9,1},... | collective-permute-start | bytes 196616 | tf_op jit(solution)/shard_map/ppermute | solution.py:322
  44.1 5.1 %collective-permute-start.9 = (bf16[256,256]{1,0:T(8,128)(2,1)S(1)}, bf16[256,256]{1,0:T(8,128)(2,1)S(1)}, u32[]{:S(2)}, u32[]{:S(2)}) collective-permute-start(bf16[256,256]{1,0:T(8,128)(2,1)S(1)} %join.4.refs_1_), channel_id=1, source_target_pairs={{0,2},{1,3},{2,0},{3,1},{4,6},{5,7},{6,4},{7,5},{8,10},{9,11},{10,... | collective-permute-start | bytes 393224 | tf_op jit(solution)/shard_map/ppermute | solution.py:322
  45.9 5.0 %collective-permute-start.8 = (bf16[256,256]{1,0:T(8,128)(2,1)S(1)}, bf16[256,256]{1,0:T(8,128)(2,1)S(1)}, u32[]{:S(2)}, u32[]{:S(2)}) collective-permute-start(bf16[256,256]{1,0:T(8,128)(2,1)S(1)} %join.3.after.refs_0_), channel_id=1, source_target_pairs={{0,2},{1,3},{2,0},{3,1},{4,6},{5,7},{6,4},{7,5},{8,10},{9,11},{10,... | collective-permute-start | bytes 393224 | tf_op jit(solution)/shard_map/ppermute | solution.py:322
  50.9 2.0 %collective-permute-start.10 = (bf16[256,1024]{1,0:T(8,128)(2,1)S(1)}, bf16[256,1024]{1,0:T(8,128)(2,1)S(1)}, u32[]{:S(2)}, u32[]{:S(2)}) collective-permute-start(bf16[256,1024]{1,0:T(8,128)(2,1)S(1)} %join.5.resp), channel_id=1, source_target_pairs={{0,1},{1,0},{2,3},{3,2},{4,5},{5,4},{6,7},{7,6},{8,9},{9,8},{10,11... | collective-permute-start | bytes 1572872 | tf_op jit(solution)/shard_map/ppermute | solution.py:322

commit v6 on v5

v6 whole, which is shorter than its diff:
```python
import functools

import jax
import jax.numpy as jnp
import numpy as np
from jax import lax
from jax.experimental import pallas as pl
from jax.experimental.pallas import tpu as pltpu
from jax.sharding import PartitionSpec as P

W = 256
LANES = 128
EXTRA = 16
BF = jnp.bfloat16
F32 = jnp.float32
I32 = jnp.int32
NT = (((1,), (1,)), ((), ()))
NN = (((1,), (0,)), ((), ()))


def dot(a, b, dims=NN):
    return lax.dot_general(a, b, dims, preferred_element_type=F32)


def split(table):
    high = table.astype(BF)
    low = (table - high.astype(np.float64)).astype(BF)
    return high, low


def turns(half, n):
    odd = 2 * np.arange(half)[:, None] + 1
    angle = (odd * n[None, :]) % (4 * half) * (np.pi / (2 * half))
    return np.cos(angle), np.sin(angle)


def forward_table(hist):
    cos, sin = turns(hist // 2, np.arange(hist))
    return np.concatenate([cos, -sin]).astype(BF)


def tap_table(hist, taps):
    cos, sin = turns(hist // 2, np.arange(taps))
    table = np.concatenate([cos, -sin])
    last = np.repeat(table[:, -1:], LANES, axis=1).astype(BF)
    return np.concatenate(split(table[:, :-1]), axis=1), last


def phase_table(hist, delay):
    cos, sin = turns(hist // 2, np.arange(1, delay + 1))
    return np.concatenate(split(np.concatenate([cos - 1.0, sin])), axis=1)


def inverse_table(hist, taps):
    cos, sin = turns(hist // 2, np.arange(W) + taps - 1)
    return np.concatenate(split(np.concatenate([cos, -sin]).T * (2.0 / hist)), axis=1)


def call(kernel, name, out_shape, *args, scalars=1, far=(), scratch=(), limit=16):
    vmem = pl.BlockSpec(memory_space=pltpu.VMEM)
    smem = pl.BlockSpec(memory_space=pltpu.SMEM)
    hbm = pl.BlockSpec(memory_space=pltpu.HBM)
    places = [smem] * scalars + [vmem] * (len(args) - scalars)
    args = list(args)
    for i in far:
        places[i] = hbm
        args[i] = pltpu.with_memory_space_constraint(jnp.asarray(args[i]), pltpu.HBM)
    return pl.pallas_call(
        kernel,
        in_specs=places,
        out_specs=[vmem] * len(out_shape),
        out_shape=out_shape,
        scratch_shapes=list(scratch),
        compiler_params=pltpu.CompilerParams(vmem_limit_bytes=limit * 1024 * 1024),
        name=name,
    )(*args)


def array(*shape, dtype=BF):
    return jax.ShapeDtypeStruct(shape, dtype)


def near(*shape, dtype=BF):
    return pltpu.VMEM(shape, dtype)


def block(start, size):
    return pl.ds(pl.multiple_of(start, LANES), size)


def hot(mask):
    return mask.astype(F32).astype(BF)


def fetch(pairs, sems):
    return [pltpu.make_async_copy(a, b, sems.at[i]) for i, (a, b) in enumerate(pairs)]


def project_kernel(
    place, loads_far, forward_far, shapes_far, taps_far, offsets_far, coef_far,
    sent, lft, shapes, stack, coef, loads, forward, taps, offsets, sems,
):
    rows, half = loads.shape[0], sent.shape[1]
    hist = lft.shape[0]
    start = (1 - (place[0] & 1)) * half
    step = 256
    chunks = [pl.ds(r, step) for r in range(0, rows, step)]
    pairs = [(forward_far, forward)] + [(loads_far.at[r, :], loads.at[r, :]) for r in chunks]
    first = len(pairs)
    pairs += [
        (coef_far, coef),
        (offsets_far, offsets),
        (shapes_far.at[:, block(start, half)], shapes),
        (taps_far, taps),
    ]
    copies = fetch(pairs, sems)
    for copy in copies:
        copy.start()
    copies[0].wait()
    for i, r in enumerate(chunks):
        copies[1 + i].wait()
        lft[:, i * step : (i + 1) * step] = dot(forward[...], loads[r, :], NT).astype(BF)
    for copy in copies[first : first + 3]:
        copy.wait()
    count = taps.shape[0] - 1
    for c in range(0, half, step):
        sent[:hist, c : c + step] = dot(lft[...], shapes[:, c : c + step]).astype(BF)
    sent[hist:, :] = jnp.zeros((EXTRA, half), BF)
    sent[hist : hist + 2, : coef.shape[1]] = coef[...]
    copies[first + 3].wait()
    for r in range(0, count, 64):
        stack[r : r + 64, :] = taps[r : r + 64, :].astype(BF)
    index = lax.broadcasted_iota(I32, (EXTRA, taps.shape[1]), 0)
    end = taps[count : count + 1, :]
    tail = jnp.where(index == 0, end, jnp.where(index == 1, offsets[...].astype(F32), 0.0))
    stack[count:, :] = tail.astype(BF)


def quarter_start(place, which, modes):
    return (((place[0] >> 1) & 1) ^ which) * (modes // 4)


def gather_taps(base, stack, order):
    count = stack.shape[0] - EXTRA
    mode = lax.broadcasted_iota(I32, (256, stack.shape[1]), 0) + base
    picked = dot(stack[...], hot(mode == order[...]), NT)
    tail = picked[count:]
    return picked[:count].astype(BF), tail[0:1], tail[1:2].astype(I32)


def spectrum_of(main, end, offset, table, last, phase):
    half = table.shape[0] // 2
    delay = phase.shape[1] // 2
    resp = dot(table[...], jnp.concatenate([main, main], axis=0))
    resp = resp + jnp.tile(last[...].astype(F32), (1, 2)) * end
    which = hot(lax.broadcasted_iota(I32, (delay, 256), 0) + 1 == offset)
    turn = dot(phase[...], jnp.concatenate([which, which], axis=0))
    cos, sin = turn[:half] + 1.0, turn[half:]
    re, im = resp[:half], resp[half:]
    return cos * re - sin * im, sin * re + cos * im


def spectrum_kernel(
    place, stack, order, lft, shapes_far, table_far, last_far, phase_far, inverse_far,
    spec, own, shapes, table, last, phase, inverse, sems,
):
    width = spec.shape[1]
    half = spec.shape[0] // 2
    modes = shapes_far.shape[1]
    core = place[0] & 1
    start, later = quarter_start(place, 1, modes), quarter_start(place, 0, modes)
    near = core * 2 * width
    copies = fetch(
        [
            (shapes_far.at[:, block(near + start, width)], shapes.at[:, block(start, width)]),
            (table_far, table),
            (last_far, last),
            (phase_far, phase),
            (inverse_far, inverse),
            (shapes_far.at[:, block(near + later, width)], shapes.at[:, block(later, width)]),
        ],
        sems,
    )
    for copy in copies:
        copy.start()
    tiles = range(0, width, 256)
    picked = [gather_taps(near + start + c, stack, order) for c in tiles]
    copies[0].wait()
    for c in tiles:
        own[:, c : c + 256] = dot(lft[...], shapes[:, block(start + c, 256)])
    for copy in copies[1:4]:
        copy.wait()
    for c, parts in zip(tiles, picked):
        spec[:half, c : c + 256], spec[half:, c : c + 256] = spectrum_of(*parts, table, last, phase)
    for copy in copies[4:]:
        copy.wait()


def impose(total, tre, tim, inverse):
    half = tre.shape[0]
    re, im = total[:half], total[half:]
    product = jnp.concatenate([re * tre - im * tim, re * tim + im * tre], axis=0)
    high = product.astype(BF)
    low = (product - high.astype(F32)).astype(BF)
    both = dot(inverse[...], jnp.concatenate([high, high], axis=0))
    return both + dot(inverse[:, : 2 * half], low)


def whole_kernel(place, stack, order, lft, other, shapes, table, last, phase, inverse, out):
    hist, modes = lft.shape[0], order.shape[1]
    start = quarter_start(place, 0, modes)
    near = (place[0] & 1) * (modes // 2) + start
    for c in range(0, out.shape[1], 256):
        spec = spectrum_of(*gather_taps(near + c, stack, order), table, last, phase)
        here = block(start + c, 256)
        total = dot(lft[...], shapes[:, here]) + other[:hist, here].astype(F32)
        out[:, c : c + 256] = impose(total, *spec, inverse)


def respond_kernel(place, own, other, spec, inverse, coef, out):
    hist, width = own.shape
    half = hist // 2
    start = quarter_start(place, 1, 4 * width)
    for c in range(0, width, 256):
        total = own[:, c : c + 256] + other[:hist, block(start + c, 256)].astype(F32)
        result = impose(total, spec[:half, c : c + 256], spec[half:, c : c + 256], inverse)
        out[:W, c : c + 256] = result.astype(BF)
    out[W:, :] = jnp.zeros((EXTRA, width), BF)
    out[W : W + 2, : coef.shape[1]] = coef[...]
    out[W + 2 : W + 4, :LANES] = other[hist : hist + 2, :LANES]


def fold_kernel(place, own, got, coef, other, keep, known, first, second, third):
    z = place[0] >> 2
    size = keep.shape[1]
    hist = other.shape[0] - EXTRA
    known[...] = jnp.zeros(known.shape, BF)
    known[0:2, :] = coef[...]
    known[2:4, :] = other[hist : hist + 2, :LANES]
    known[4:8, :] = got[W : W + 4, :LANES]
    for d, out in enumerate((keep, first, second, third)):
        where = block((z ^ d) * size, size)
        total = own[:, where] + got[:W, where].astype(F32)
        out[:W, :] = total.astype(out.dtype)
        if d:
            out[W:, :] = known[...]


def settle_kernel(after, keep, first, second, third, out):
    total = keep[...]
    for got in (first, second, third):
        total = total + got[:W, :].astype(F32)
    out[...] = total.astype(BF)


def mask_of(place, devices, modes):
    me = place[0]
    if devices == 16:
        return ((me & 1) * 8 + (me & 2) * 2 + (me >> 2)) * (modes // 16)
    return (me & 1) * (modes // 2)


def pick_kernel(devices, place, partner, after, pick):
    modes = partner.shape[1]
    mask = mask_of(place, devices, modes)
    mates = [partner[:, block(c ^ mask, LANES)] ^ mask for c in range(0, modes, LANES)]
    mates = jnp.concatenate(mates, axis=1)
    for c in range(0, modes, 256):
        pick[c : c + 256, :] = hot(lax.broadcasted_iota(I32, (256, modes), 0) + c == mates)


def mixers_kernel(place, order, known, third, second, first, after, coef, held):
    me = place[0]
    held[...] = jnp.zeros(held.shape, F32)
    for z, rows in enumerate((known, first, second, third)):
        top = rows.shape[0] - EXTRA
        for low in range(4):
            where = block((me ^ (4 * z + low)) * LANES, LANES)
            held[0:2, where] = rows[top : top + EXTRA, :].astype(F32)[2 * low : 2 * low + 2]
    mixers(order, mask_of(place, 16, order.shape[1]), held, coef)


def mixers(order, mask, held, coef):
    modes = order.shape[1]
    table = held[...].astype(BF)
    slots = order[...] ^ mask
    for c in range(0, modes, 256):
        coef[:, c : c + 256] = dot(table, hot(lax.broadcasted_iota(I32, (256, modes), 0) + c == slots), NT)


def plain_mixers_kernel(devices, place, order, every, coef, held):
    held[...] = jnp.zeros(held.shape, F32)
    held[0:2, :] = every[...].astype(F32)
    mixers(order, mask_of(place, devices, order.shape[1]), held, coef)


def join_kernel(*refs):
    *parts, out = refs
    start = 0
    for part in parts:
        out[:, start : start + part.shape[1]] = part[...]
        start += part.shape[1]


def join(*parts, after=None):
    width = sum(part.shape[1] for part in parts)
    kernel = join_kernel if after is None else lambda _, *refs: join_kernel(*refs)
    first = () if after is None else (after,)
    return call(kernel, "join", [array(parts[0].shape[0], width)], *first, *parts, scalars=0)[0]


def mate_kernel(mine, theirs, pick, out):
    width = mine.shape[1]
    resp = jnp.concatenate([mine[...], theirs[...]], axis=1)
    for c in range(0, out.shape[1], 256):
        here = slice(c, c + 256)
        out[:, here] = dot(resp, jnp.concatenate([pick[:width, here], pick[2 * width : 3 * width, here]], axis=0))


def more_kernel(mates, got, pick, out):
    width = got.shape[1]
    for c in range(0, out.shape[1], 256):
        out[:, c : c + 256] = mates[:, c : c + 256] + dot(got[...], pick[width : 2 * width, c : c + 256])


def expand_kernel(devices, place, mine, got, theirs, other, mates, pick, coef, near, far, out, near_pair, far_pair):
    width = mine.shape[1]
    half = 2 * width
    mask = mask_of(place, devices, 2 * half)
    for q, direct in enumerate((mine, got, theirs, other)):
        pair = near_pair if q < 2 else far_pair
        for c in range(0, width, 256):
            k = q * width + c
            across = mates[:, k : k + 256] + dot(other[...], pick[3 * width :, k : k + 256])
            mixed = coef[0:1, k : k + 256] * direct[:, c : c + 256].astype(F32) + coef[1:2, k : k + 256] * across
            for d in (0, LANES):
                pair[:, block((mask ^ (k + d)) & (half - 1), LANES)] = mixed[:, d : d + LANES].astype(BF)
    rows = out.shape[0]
    for r in range(0, rows, 256):
        total = dot(near[r : r + 256, :], near_pair[...], NT) + dot(far[r : r + 256, :], far_pair[...], NT)
        out[r : r + 256, :] = total.astype(BF)


def swap(x, devices, bits):
    return lax.ppermute(x, "frdm", [(i, i ^ bits) for i in range(devices)])


def shards(devices, loads, shapes, mode_order, partner, taps, offsets, coef):
    rows, modes = shapes.shape
    hist, count = loads.shape[1], taps.shape[1]
    half, quarter = modes // 2, modes // 4
    place = lax.axis_index("frdm").astype(I32).reshape(1)
    forward = forward_table(hist)
    tap_forward, last = tap_table(hist, count)
    phase = phase_table(hist, hist - W - count + 1)
    inverse = inverse_table(hist, count)
    order, mates, offsets, taps = mode_order[None], partner[None], offsets[None], taps.T

    sent, lft, far, stack, coef_near = call(
        project_kernel, "project",
        [near(hist + EXTRA, half), near(hist, rows), near(rows, half), near(count - 1 + EXTRA, modes), near(*coef.shape)],
        place, loads, forward, shapes, taps, offsets, coef, far=range(1, 7),
        scratch=[
            pltpu.VMEM(loads.shape, BF), pltpu.VMEM(forward.shape, BF), pltpu.VMEM(taps.shape, F32),
            pltpu.VMEM(offsets.shape, I32), pltpu.SemaphoreType.DMA((5 + rows // 256,)),
        ],
        limit=24,
    )
    got = swap(sent, devices, 1)
    spec, own, shapes, *held = call(
        spectrum_kernel, "spectrum",
        [near(hist, quarter, dtype=F32)] * 2 + [near(rows, half)]
        + [near(*t.shape) for t in (tap_forward, last, phase, inverse)],
        place, stack, order, lft, shapes, tap_forward, last, phase, inverse, far=range(4, 9),
        scratch=[pltpu.SemaphoreType.DMA((6,))],
    )
    inverse = held[-1]
    away = call(respond_kernel, "respond", [array(W + EXTRA, quarter)], place, own, got, spec, inverse, coef_near)[0]

    def respond_own():
        return call(
            whole_kernel, "whole", [array(W, quarter, dtype=F32)], place, stack, order, lft, got, shapes, *held
        )[0]

    pair = functools.partial(pick_kernel, devices)
    if devices == 16:
        size = modes // devices
        away = swap(away, devices, 2)
        keep, known, *parts = call(
            fold_kernel, "fold", [array(W, size, dtype=F32), array(EXTRA, LANES)] + [array(W + EXTRA, size)] * 3,
            place, respond_own(), away, coef_near, got,
        )
        parts = [swap(part, devices, 4 * d) for d, part in reversed(list(zip((1, 2, 3), parts)))]
        pick = call(pair, "pick", [near(modes, modes)], place, mates, keep)[0]
        total = call(settle_kernel, "settle", [array(W, size)], pick, keep, *parts, scalars=0)[0]
        spread = [swap(total, devices, 4 * d) for d in (3, 2, 1)]
        mode_coef = call(
            mixers_kernel, "mixers", [array(8, modes, dtype=F32)],
            place, order, known, *parts, total, scratch=[pltpu.VMEM((8, modes), F32)],
        )[0]
        mine = join(total, *reversed(spread), after=mode_coef)
        resp = swap(mine, devices, 2)
        theirs = swap(mine, devices, 1)
        first = call(mate_kernel, "mate", [array(W, modes, dtype=F32)], mine, theirs, pick, scalars=0)[0]
        resp = join(resp, after=first)
    else:
        pick = call(pair, "pick", [near(modes, modes)], place, mates, mates)[0]
        mode_coef = call(
            functools.partial(plain_mixers_kernel, devices), "mixers", [array(8, modes, dtype=F32)],
            place, order, lax.all_gather(coef, "frdm", axis=1, tiled=True), scratch=[pltpu.VMEM((8, modes), F32)],
        )[0]
        away, resp = away[:W].astype(F32), respond_own()
        resp = jnp.where(place[0] & 2, jnp.concatenate([away, resp], axis=1), jnp.concatenate([resp, away], axis=1))
        groups = [list(range(c, devices, 2)) for c in range(2)]
        resp = lax.psum(resp, "frdm", axis_index_groups=groups).astype(BF)
        mine, resp = resp[:, :quarter], resp[:, quarter:]
        theirs = swap(mine, devices, 1)
        first = call(mate_kernel, "mate", [array(W, modes, dtype=F32)], mine, theirs, pick, scalars=0)[0]
    other = swap(resp, devices, 1)
    most = call(more_kernel, "more", [array(W, modes, dtype=F32)], first, resp, pick, scalars=0)[0]
    return call(
        functools.partial(expand_kernel, devices), "expand", [array(rows, W)],
        place, mine, resp, theirs, other, most, pick, mode_coef, shapes, far,
        scratch=[pltpu.VMEM((W, half), BF)] * 2,
    )[0]


def solution(mesh):
    in_specs = (P(("cases", "frdm"), None), P("frdm", None), P(), P(), P(), P(), P(None, "frdm"))
    out_specs = P(("cases", "frdm"), None)
    body = functools.partial(shards, mesh.shape["frdm"])
    return jax.shard_map(body, mesh=mesh, in_specs=in_specs, out_specs=out_specs, check_vma=False)
```

time: 56.9 us -> 57.6 us (1.012)
  transfers between devices with their start and end apart: 11 -> 11, of which waited for: 8 -> 6; matrix products, arithmetic and copies ran while one was open for 0% -> 0% of each run, Pallas kernels for 30% -> 31%
where the time goes in v6:
time: 57.6 us; the launch traced here: 57.5 us
  Pallas kernels  30.7 us (53%)
  starting transfers between devices  13.8 us (24%)
  waiting for transfers between devices  12.9 us (22%)
    pallas_call x13, Pallas kernels, call(): pl.pallas_call(kernel, in_specs=places, out_specs=[vmem] * len(out_shape)...  30.7 us
    ppermute x11, starting transfers between devices, swap(): return lax.ppermute(x, 'frdm', [(i, i ^ bits) for i in range(devices)])  13.8 us
    ppermute x11, waiting for transfers between devices, swap(): return lax.ppermute(x, 'frdm', [(i, i ^ bits) for i in range(devices)])  12.9 us
  transfers between devices with their start and end apart: 11, of which 6 were waited for; matrix products, arithmetic and copies ran while one was open for 0% of the time, Pallas kernels for 31%

profile of v6, /device:TPU:0, one launch (start us, length us, event | category | flops | bytes accessed | tf_op | source)
XLA Modules:
  0.0 57.5 jit_solution(7523245186122728625)
XLA Ops:
  0.0 0.0 copy-start
  0.0 8.4 %project.1 = (bf16[912,1024]{1,0:T(8,128)(2,1)S(1)}, bf16[896,1024]{1,0:T(8,128)(2,1)S(1)}, bf16[1024,1024]{1,0:T(8,128)(2,1)S(1)}, bf16[528,2048]{1,0:T(8,128)(2,1)S(1)}, bf16[2,128]{1,0:T(2,128)(2,1)S(1)}) custom-call(s32[1]{0:T(128)} %bitcast.place, bf16[1024,896]{1,0:T(8,128)(2,1)} %loads_far.1, bf16[896,896]{1,0:T(8,128)(2,1)} %constant.14.clone.forward_far, ...), custom_call_target="tpu_custom_call" | custom-call | tf_op jit(solution)/shard_map/project/pallas_call | solution.py:68
  8.4 0.5 collective-permute-start
  8.9 0.0 copy-done
  8.9 5.0 %spectrum.1 = (f32[896,512]{1,0:T(8,128)S(1)}, f32[896,512]{1,0:T(8,128)S(1)}, bf16[1024,1024]{1,0:T(8,128)(2,1)S(1)}, bf16[896,1024]{1,0:T(8,128)(2,1)S(1)}, bf...) custom-call(s32[1]{0:T(128)} %bitcast.place, ...), custom_call_target="tpu_custom_call" | custom-call | tf_op jit(solution)/shard_map/spectrum/pallas_call | solution.py:68
  14.0 0.0 collective-permute-done.other
  14.0 1.3 %respond.1 = bf16[272,512]{1,0:T(8,128)(2,1)S(1)} custom-call(s32[1]{0:T(128)} %bitcast.place, f32[896,512]{1,0:T(8,128)S(1)} %get-tuple-element.30.own, bf16[912,1024]{1,0:T(8,128)(2,1)S(1)} %collective-permute-done.other, f32[896,512]{1,0:T(8,128)S(1)} %get-tuple-element.31.spec, bf16[256,1792]{1,0:T(8,128)(2,1)S(1)} %get-tuple-element.29.inverse, ...), custom_call_target="tpu_custom_call" | custom-call | tf_op jit(solution)/shard_map/respond/pallas_call | solution.py:68
  15.3 2.6 %collective-permute-start.1 = (bf16[272,512]{1,0:T(8,128)(2,1)S(1)}, bf16[272,512]{1,0:T(8,128)(2,1)S(1)}, u32[]{:S(2)}, u32[]{:S(2)}) collective-permute-start(bf16[272,512]{1,0:T(8,128)(2,1)S(1)} %respond.1), channel_id=1, source_target_pairs={{0,2},{1,3},{2,0},{3,1},{4,6},{5,7},{6,4},{7,5},{8,10},{9,11},{10,... | collective-permute-start | bytes 835592 | tf_op jit(solution)/shard_map/ppermute | solution.py:345
  17.9 7.1 %whole.1.own = f32[256,512]{1,0:T(8,128)S(1)} custom-call(s32[1]{0:T(128)} %bitcast.place, bf16[528,2048]{1,0:T(8,128)(2,1)S(1)} %get-tuple-element.22.stack, s32[1,2048]{1,0:T(1,128)S(1)} %bitcast.6, bf16[896,1024]{1,0:T(8,128)(2,1)S(1)} %get-tuple-element.23.lft, bf16[912,1024]{1,0:T(8,128)(2,1)S(1)} %collective-permute-done.other, ...), custom_call_target="tpu_custom_call" | custom-call | tf_op jit(solution)/shard_map/whole/pallas_call | solution.py:68
  25.0 0.0 copy-start.1
  25.1 0.2 collective-permute-done.1.got
  25.2 0.1 fold.1
  25.3 3.9 %collective-permute-start.2 = (bf16[272,128]{1,0:T(8,128)(2,1)S(1)}, bf16[272,128]{1,0:T(8,128)(2,1)S(1)}, u32[]{:S(2)}, u32[]{:S(2)}) collective-permute-start(bf16[272,128]{1,0:T(8,128)(2,1)S(1)} %get-tuple-element.34), channel_id=1, source_target_pairs={{0,12},{1,13},{2,14},{3,15},{4,8},{5,9},{6,10},{7,11},{8,4},{9,5},... | collective-permute-start | bytes 208904 | tf_op jit(solution)/shard_map/ppermute | solution.py:345
  29.2 0.0 collective-permute-start.3
  29.2 0.6 %collective-permute-start.4 = (bf16[272,128]{1,0:T(8,128)(2,1)S(1)}, bf16[272,128]{1,0:T(8,128)(2,1)S(1)}, u32[]{:S(2)}, u32[]{:S(2)}) collective-permute-start(bf16[272,128]{1,0:T(8,128)(2,1)S(1)} %get-tuple-element.36), channel_id=1, source_target_pairs={{0,4},{1,5},{2,6},{3,7},{4,0},{5,1},{6,2},{7,3},{8,12},{9,13},{10,... | collective-permute-start | bytes 208904 | tf_op jit(solution)/shard_map/ppermute | solution.py:345
  29.8 0.0 copy-done.1
  29.8 1.4 %pick.1.after = bf16[2048,2048]{1,0:T(8,128)(2,1)S(1)} custom-call(s32[1]{0:T(128)} %bitcast.place, s32[1,2048]{1,0:T(1,128)S(1)} %bitcast.8, f32[256,128]{1,0:T(8,128)S(1)} %get-tuple-element.37.after.keep), custom_call_target="tpu_custom_call" | custom-call | tf_op jit(solution)/shard_map/pick/pallas_call | solution.py:68
  31.2 0.6 %collective-permute-done.2.first.third = bf16[272,128]{1,0:T(8,128)(2,1)S(1)} collective-permute-done((bf16[272,128]{1,0:T(8,128)(2,1)S(1)}, bf16[272,128]{1,0:T(8,128)(2,1)S(1)}, u32[]{:S(2)}, u32[]{:S(2)}) %collective-permute-start.2) | collective-permute-done | bytes 69664 | tf_op jit(solution)/shard_map/ppermute | solution.py:345
  31.9 3.2 %collective-permute-done.3.second = bf16[272,128]{1,0:T(8,128)(2,1)S(1)} collective-permute-done((bf16[272,128]{1,0:T(8,128)(2,1)S(1)}, bf16[272,128]{1,0:T(8,128)(2,1)S(1)}, u32[]{:S(2)}, u32[]{:S(2)}) %collective-permute-start.3) | collective-permute-done | bytes 69664 | tf_op jit(solution)/shard_map/ppermute | solution.py:345
  35.1 0.0 collective-permute-done.4.third.first
  35.2 2.8 %collective-permute-start.7 = (bf16[256,128]{1,0:T(8,128)(2,1)S(1)}, bf16[256,128]{1,0:T(8,128)(2,1)S(1)}, u32[]{:S(2)}, u32[]{:S(2)}) collective-permute-start(bf16[256,128]{1,0:T(8,128)(2,1)S(1)} %settle.1.after.refs_0_), channel_id=1, source_target_pairs={{0,12},{1,13},{2,14},{3,15},{4,8},{5,9},{6,10},{7,11},{8,4},{9,5},... | collective-permute-start | bytes 196616 | tf_op jit(solution)/shard_map/ppermute | solution.py:345
  38.0 0.0 collective-permute-start.6
  38.0 1.7 %collective-permute-start.5 = (bf16[256,128]{1,0:T(8,128)(2,1)S(1)}, bf16[256,128]{1,0:T(8,128)(2,1)S(1)}, u32[]{:S(2)}, u32[]{:S(2)}) collective-permute-start(bf16[256,128]{1,0:T(8,128)(2,1)S(1)} %settle.1.after.refs_0_), channel_id=1, source_target_pairs={{0,4},{1,5},{2,6},{3,7},{4,0},{5,1},{6,2},{7,3},{8,12},{9,13},{10,... | collective-permute-start | bytes 196616 | tf_op jit(solution)/shard_map/ppermute | solution.py:345
  39.6 2.3 %mixers.1._.coef = f32[8,2048]{1,0:T(8,128)S(1)} custom-call(s32[1]{0:T(128)} %bitcast.place, s32[1,2048]{1,0:T(1,128)S(1)} %bitcast.7, bf16[16,128]{1,0:T(8,128)(2,1)S(1)} %get-tuple-element.33.known, bf16[272,128]{1,0:T(8,128)(2,1)S(1)} %collective-permute-done.2.first.third, bf16[272,128]{1,0:T(8,128)(2,1)S(1)} %collective-permute-done.3.second, ...), custom_call_target="tpu_custom_call" | custom-call | tf_op jit(solution)/shard_map/mixers/pallas_call | solution.py:68
  41.9 0.0 collective-permute-done.7.refs_3_
  41.9 2.2 %collective-permute-done.6.refs_2_ = bf16[256,128]{1,0:T(8,128)(2,1)S(1)} collective-permute-done((bf16[256,128]{1,0:T(8,128)(2,1)S(1)}, bf16[256,128]{1,0:T(8,128)(2,1)S(1)}, u32[]{:S(2)}, u32[]{:S(2)}) %collective-permute-start.6) | collective-permute-done | bytes 65568 | tf_op jit(solution)/shard_map/ppermute | solution.py:345
  44.1 0.0 collective-permute-done.5.refs_1_
  44.1 0.1 collective-permute-start.8
  44.2 1.6 %collective-permute-start.9 = (bf16[256,512]{1,0:T(8,128)(2,1)S(1)}, bf16[256,512]{1,0:T(8,128)(2,1)S(1)}, u32[]{:S(2)}, u32[]{:S(2)}) collective-permute-start(bf16[256,512]{1,0:T(8,128)(2,1)S(1)} %join.2.mine), channel_id=1, source_target_pairs={{0,2},{1,3},{2,0},{3,1},{4,6},{5,7},{6,4},{7,5},{8,10},{9,11},{10,... | collective-permute-start | bytes 786440 | tf_op jit(solution)/shard_map/ppermute | solution.py:345
  45.8 0.0 collective-permute-done.8.theirs
  45.8 1.2 %mate.1._.mates = f32[256,2048]{1,0:T(8,128)S(1)} custom-call(bf16[256,512]{1,0:T(8,128)(2,1)S(1)} %join.2.mine, bf16[256,512]{1,0:T(8,128)(2,1)S(1)} %collective-permute-done.8.theirs, bf16[2048,2048]{1,0:T(8,128)(2,1)S(1)} %pick.1.after), custom_call_target="tpu_custom_call" | custom-call | tf_op jit(solution)/shard_map/mate/pallas_call | solution.py:68
  47.0 5.9 %collective-permute-done.9.refs_0_ = bf16[256,512]{1,0:T(8,128)(2,1)S(1)} collective-permute-done((bf16[256,512]{1,0:T(8,128)(2,1)S(1)}, bf16[256,512]{1,0:T(8,128)(2,1)S(1)}, u32[]{:S(2)}, u32[]{:S(2)}) %collective-permute-start.9) | collective-permute-done | bytes 262176 | tf_op jit(solution)/shard_map/ppermute | solution.py:345
  52.9 0.1 collective-permute-start.10
  53.0 0.8 %more.1.mates = f32[256,2048]{1,0:T(8,128)S(1)} custom-call(f32[256,2048]{1,0:T(8,128)S(1)} %mate.1._.mates, bf16[256,512]{1,0:T(8,128)(2,1)S(1)} %join.3.got, bf16[2048,2048]{1,0:T(8,128)(2,1)S(1)} %pick.1.after), custom_call_target="tpu_custom_call" | custom-call | tf_op jit(solution)/shard_map/more/pallas_call | solution.py:68
  53.8 0.8 %collective-permute-done.10.other = bf16[256,512]{1,0:T(8,128)(2,1)S(1)} collective-permute-done((bf16[256,512]{1,0:T(8,128)(2,1)S(1)}, bf16[256,512]{1,0:T(8,128)(2,1)S(1)}, u32[]{:S(2)}, u32[]{:S(2)}) %collective-permute-start.10) | collective-permute-done | bytes 262176 | tf_op jit(solution)/shard_map/ppermute | solution.py:345
  54.5 3.0 %expand.1 = bf16[1024,256]{1,0:T(8,128)(2,1)} custom-call(s32[1]{0:T(128)} %bitcast.place, bf16[256,512]{1,0:T(8,128)(2,1)S(1)} %join.2.mine, bf16[256,512]{1,0:T(8,128)(2,1)S(1)} %join.3.got, bf16[256,512]{1,0:T(8,128)(2,1)S(1)} %collective-permute-done.8.theirs, bf16[256,512]{1,0:T(8,128)(2,1)S(1)} %collective-permute-done.10.other, ...), custom_call_target="tpu_custom_call" | custom-call | tf_op jit(solution)/shard_map/expand/pallas_call | solution.py:68
  (3 shorter events, 0.1 us)
Async XLA Ops:
  0.0 8.9 %copy-start = (s32[2048]{0:T(1024)S(1)}, s32[2048]{0:T(1024)}, u32[]{:S(2)}) copy-start(s32[2048]{0:T(1024)} %param.14) | copy-start | bytes 24580
  8.4 5.5 %collective-permute-start = (bf16[912,1024]{1,0:T(8,128)(2,1)S(1)}, bf16[912,1024]{1,0:T(8,128)(2,1)S(1)}, u32[]{:S(2)}, u32[]{:S(2)}) collective-permute-start(bf16[912,1024]{1,0:T(8,128)(2,1)S(1)} %get-tuple-element.24), channel_id=1, source_target_pairs={{0,1},{1,0},{2,3},{3,2},{4,5},{5,4},{6,7},{7,6},{8,9},{9,8},{10,11... | collective-permute-start | bytes 5603336 | tf_op jit(solution)/shard_map/ppermute | solution.py:345
  15.3 9.9 %collective-permute-start.1 = (bf16[272,512]{1,0:T(8,128)(2,1)S(1)}, bf16[272,512]{1,0:T(8,128)(2,1)S(1)}, u32[]{:S(2)}, u32[]{:S(2)}) collective-permute-start(bf16[272,512]{1,0:T(8,128)(2,1)S(1)} %respond.1), channel_id=1, source_target_pairs={{0,2},{1,3},{2,0},{3,1},{4,6},{5,7},{6,4},{7,5},{8,10},{9,11},{10,... | collective-permute-start | bytes 835592 | tf_op jit(solution)/shard_map/ppermute | solution.py:345
  25.0 4.8 %copy-start.1 = (s32[2048]{0:T(1024)S(1)}, s32[2048]{0:T(1024)}, u32[]{:S(2)}) copy-start(s32[2048]{0:T(1024)} %param.15) | copy-start | bytes 24580
  25.3 6.5 %collective-permute-start.2 = (bf16[272,128]{1,0:T(8,128)(2,1)S(1)}, bf16[272,128]{1,0:T(8,128)(2,1)S(1)}, u32[]{:S(2)}, u32[]{:S(2)}) collective-permute-start(bf16[272,128]{1,0:T(8,128)(2,1)S(1)} %get-tuple-element.34), channel_id=1, source_target_pairs={{0,12},{1,13},{2,14},{3,15},{4,8},{5,9},{6,10},{7,11},{8,4},{9,5},... | collective-permute-start | bytes 208904 | tf_op jit(solution)/shard_map/ppermute | solution.py:345
  29.2 5.9 %collective-permute-start.3 = (bf16[272,128]{1,0:T(8,128)(2,1)S(1)}, bf16[272,128]{1,0:T(8,128)(2,1)S(1)}, u32[]{:S(2)}, u32[]{:S(2)}) collective-permute-start(bf16[272,128]{1,0:T(8,128)(2,1)S(1)} %get-tuple-element.35), channel_id=1, source_target_pairs={{0,8},{1,9},{2,10},{3,11},{4,12},{5,13},{6,14},{7,15},{8,0},{9,1},... | collective-permute-start | bytes 208904 | tf_op jit(solution)/shard_map/ppermute | solution.py:345
  29.2 5.9 %collective-permute-start.4 = (bf16[272,128]{1,0:T(8,128)(2,1)S(1)}, bf16[272,128]{1,0:T(8,128)(2,1)S(1)}, u32[]{:S(2)}, u32[]{:S(2)}) collective-permute-start(bf16[272,128]{1,0:T(8,128)(2,1)S(1)} %get-tuple-element.36), channel_id=1, source_target_pairs={{0,4},{1,5},{2,6},{3,7},{4,0},{5,1},{6,2},{7,3},{8,12},{9,13},{10,... | collective-permute-start | bytes 208904 | tf_op jit(solution)/shard_map/ppermute | solution.py:345
  35.2 6.7 %collective-permute-start.7 = (bf16[256,128]{1,0:T(8,128)(2,1)S(1)}, bf16[256,128]{1,0:T(8,128)(2,1)S(1)}, u32[]{:S(2)}, u32[]{:S(2)}) collective-permute-start(bf16[256,128]{1,0:T(8,128)(2,1)S(1)} %settle.1.after.refs_0_), channel_id=1, source_target_pairs={{0,12},{1,13},{2,14},{3,15},{4,8},{5,9},{6,10},{7,11},{8,4},{9,5},... | collective-permute-start | bytes 196616 | tf_op jit(solution)/shard_map/ppermute | solution.py:345
  38.0 6.1 %collective-permute-start.6 = (bf16[256,128]{1,0:T(8,128)(2,1)S(1)}, bf16[256,128]{1,0:T(8,128)(2,1)S(1)}, u32[]{:S(2)}, u32[]{:S(2)}) collective-permute-start(bf16[256,128]{1,0:T(8,128)(2,1)S(1)} %settle.1.after.refs_0_), channel_id=1, source_target_pairs={{0,8},{1,9},{2,10},{3,11},{4,12},{5,13},{6,14},{7,15},{8,0},{9,1},... | collective-permute-start | bytes 196616 | tf_op jit(solution)/shard_map/ppermute | solution.py:345
  38.0 6.1 %collective-permute-start.5 = (bf16[256,128]{1,0:T(8,128)(2,1)S(1)}, bf16[256,128]{1,0:T(8,128)(2,1)S(1)}, u32[]{:S(2)}, u32[]{:S(2)}) collective-permute-start(bf16[256,128]{1,0:T(8,128)(2,1)S(1)} %settle.1.after.refs_0_), channel_id=1, source_target_pairs={{0,4},{1,5},{2,6},{3,7},{4,0},{5,1},{6,2},{7,3},{8,12},{9,13},{10,... | collective-permute-start | bytes 196616 | tf_op jit(solution)/shard_map/ppermute | solution.py:345
  44.1 1.7 %collective-permute-start.8 = (bf16[256,512]{1,0:T(8,128)(2,1)S(1)}, bf16[256,512]{1,0:T(8,128)(2,1)S(1)}, u32[]{:S(2)}, u32[]{:S(2)}) collective-permute-start(bf16[256,512]{1,0:T(8,128)(2,1)S(1)} %join.2.mine), channel_id=1, source_target_pairs={{0,1},{1,0},{2,3},{3,2},{4,5},{5,4},{6,7},{7,6},{8,9},{9,8},{10,11... | collective-permute-start | bytes 786440 | tf_op jit(solution)/shard_map/ppermute | solution.py:345
  44.2 8.7 %collective-permute-start.9 = (bf16[256,512]{1,0:T(8,128)(2,1)S(1)}, bf16[256,512]{1,0:T(8,128)(2,1)S(1)}, u32[]{:S(2)}, u32[]{:S(2)}) collective-permute-start(bf16[256,512]{1,0:T(8,128)(2,1)S(1)} %join.2.mine), channel_id=1, source_target_pairs={{0,2},{1,3},{2,0},{3,1},{4,6},{5,7},{6,4},{7,5},{8,10},{9,11},{10,... | collective-permute-start | bytes 786440 | tf_op jit(solution)/shard_map/ppermute | solution.py:345
  52.9 1.6 %collective-permute-start.10 = (bf16[256,512]{1,0:T(8,128)(2,1)S(1)}, bf16[256,512]{1,0:T(8,128)(2,1)S(1)}, u32[]{:S(2)}, u32[]{:S(2)}) collective-permute-start(bf16[256,512]{1,0:T(8,128)(2,1)S(1)} %join.3.got), channel_id=1, source_target_pairs={{0,1},{1,0},{2,3},{3,2},{4,5},{5,4},{6,7},{7,6},{8,9},{9,8},{10,11... | collective-permute-start | bytes 786440 | tf_op jit(solution)/shard_map/ppermute | solution.py:345

commit v7 on v6

--- a/solution.py
+++ b/solution.py
@@ -114,11 +114,14 @@
         (taps_far, taps),
     ]
     copies = fetch(pairs, sems)
-    for copy in copies:
+    for copy in copies[:first]:
         copy.start()
     copies[0].wait()
     for i, r in enumerate(chunks):
         copies[1 + i].wait()
+        if i == 0:
+            for copy in copies[first:]:
+                copy.start()
         lft[:, i * step : (i + 1) * step] = dot(forward[...], loads[r, :], NT).astype(BF)
     for copy in copies[first : first + 3]:
         copy.wait()
@@ -309,29 +312,19 @@
     return call(kernel, "join", [array(parts[0].shape[0], width)], *first, *parts, scalars=0)[0]
 
 
-def mate_kernel(mine, theirs, pick, out):
-    width = mine.shape[1]
-    resp = jnp.concatenate([mine[...], theirs[...]], axis=1)
-    for c in range(0, out.shape[1], 256):
-        here = slice(c, c + 256)
-        out[:, here] = dot(resp, jnp.concatenate([pick[:width, here], pick[2 * width : 3 * width, here]], axis=0))
-
-
-def more_kernel(mates, got, pick, out):
-    width = got.shape[1]
-    for c in range(0, out.shape[1], 256):
-        out[:, c : c + 256] = mates[:, c : c + 256] + dot(got[...], pick[width : 2 * width, c : c + 256])
-
-
-def expand_kernel(devices, place, mine, got, theirs, other, mates, pick, coef, near, far, out, near_pair, far_pair):
-    width = mine.shape[1]
-    half = 2 * width
+def mate_kernel(mine, pick, out):
+    half = mine.shape[1]
+    for c in range(0, 2 * half, 256):
+        out[:, c : c + 256] = dot(mine[...], pick[:half, c : c + 256])
+
+
+def expand_kernel(devices, place, mine, theirs, mates, pick, coef, near, far, out, near_pair, far_pair):
+    half = mine.shape[1]
     mask = mask_of(place, devices, 2 * half)
-    for q, direct in enumerate((mine, got, theirs, other)):
-        pair = near_pair if q < 2 else far_pair
-        for c in range(0, width, 256):
-            k = q * width + c
-            across = mates[:, k : k + 256] + dot(other[...], pick[3 * width :, k : k + 256])
+    for q, (direct, pair) in enumerate(((mine, near_pair), (theirs, far_pair))):
+        for c in range(0, half, 256):
+            k = q * half + c
+            across = mates[:, k : k + 256] + dot(theirs[...], pick[half:, k : k + 256])
             mixed = coef[0:1, k : k + 256] * direct[:, c : c + 256].astype(F32) + coef[1:2, k : k + 256] * across
             for d in (0, LANES):
                 pair[:, block((mask ^ (k + d)) & (half - 1), LANES)] = mixed[:, d : d + LANES].astype(BF)
@@ -398,11 +391,8 @@
             mixers_kernel, "mixers", [array(8, modes, dtype=F32)],
             place, order, known, *parts, total, scratch=[pltpu.VMEM((8, modes), F32)],
         )[0]
-        mine = join(total, *reversed(spread), after=mode_coef)
-        resp = swap(mine, devices, 2)
-        theirs = swap(mine, devices, 1)
-        first = call(mate_kernel, "mate", [array(W, modes, dtype=F32)], mine, theirs, pick, scalars=0)[0]
-        resp = join(resp, after=first)
+        resp = join(total, *reversed(spread), after=mode_coef)
+        mine = join(resp, swap(resp, devices, 2))
     else:
         pick = call(pair, "pick", [near(modes, modes)], place, mates, mates)[0]
         mode_coef = call(
@@ -412,15 +402,12 @@
         away, resp = away[:W].astype(F32), respond_own()
         resp = jnp.where(place[0] & 2, jnp.concatenate([away, resp], axis=1), jnp.concatenate([resp, away], axis=1))
         groups = [list(range(c, devices, 2)) for c in range(2)]
-        resp = lax.psum(resp, "frdm", axis_index_groups=groups).astype(BF)
-        mine, resp = resp[:, :quarter], resp[:, quarter:]
-        theirs = swap(mine, devices, 1)
-        first = call(mate_kernel, "mate", [array(W, modes, dtype=F32)], mine, theirs, pick, scalars=0)[0]
-    other = swap(resp, devices, 1)
-    most = call(more_kernel, "more", [array(W, modes, dtype=F32)], first, resp, pick, scalars=0)[0]
+        mine = lax.psum(resp, "frdm", axis_index_groups=groups).astype(BF)
+    theirs = swap(mine, devices, 1)
+    first = call(mate_kernel, "mate", [array(W, modes, dtype=F32)], mine, pick, scalars=0)[0]
     return call(
         functools.partial(expand_kernel, devices), "expand", [array(rows, W)],
-        place, mine, resp, theirs, other, most, pick, mode_coef, shapes, far,
+        place, mine, theirs, first, pick, mode_coef, shapes, far,
         scratch=[pltpu.VMEM((W, half), BF)] * 2,
     )[0]
 

time: 57.6 us -> 57.5 us (level)
    pallas_call x13 -> x12, Pallas kernels: 30.7 us -> 30.5 us  [call(): pl.pallas_call(kernel, in_specs=places, out_specs=[vmem] * len(out_shape)...]
    ppermute x11 -> x10, waiting for transfers between devices: 12.9 us -> 13 us  [swap(): return lax.ppermute(x, 'frdm', [(i, i ^ bits) for i in range(devices)])]
    ppermute x11 -> x10, starting transfers between devices: 13.8 us -> 13.8 us  [swap(): return lax.ppermute(x, 'frdm', [(i, i ^ bits) for i in range(devices)])]
  transfers between devices with their start and end apart: 11 -> 10, of which waited for: 6 -> 6; matrix products, arithmetic and copies ran while one was open for 0% -> 0% of each run, Pallas kernels for 31% -> 30%
where the time goes in v7:
time: 57.5 us; the launch traced here: 57.4 us
  Pallas kernels  30.5 us (53%)
  starting transfers between devices  13.8 us (24%)
  waiting for transfers between devices  13 us (23%)
    pallas_call x12, Pallas kernels, call(): pl.pallas_call(kernel, in_specs=places, out_specs=[vmem] * len(out_shape)...  30.5 us
    ppermute x10, starting transfers between devices, swap(): return lax.ppermute(x, 'frdm', [(i, i ^ bits) for i in range(devices)])  13.8 us
    ppermute x10, waiting for transfers between devices, swap(): return lax.ppermute(x, 'frdm', [(i, i ^ bits) for i in range(devices)])  13 us
  transfers between devices with their start and end apart: 10, of which 6 were waited for; matrix products, arithmetic and copies ran while one was open for 0% of the time, Pallas kernels for 30%

profile of v7, /device:TPU:0, one launch (start us, length us, event | category | flops | bytes accessed | tf_op | source)
XLA Modules:
  0.0 57.4 jit_solution(3934403012177647174)
XLA Ops:
  0.0 0.0 copy-start
  0.0 8.4 %project.1 = (bf16[912,1024]{1,0:T(8,128)(2,1)S(1)}, bf16[896,1024]{1,0:T(8,128)(2,1)S(1)}, bf16[1024,1024]{1,0:T(8,128)(2,1)S(1)}, bf16[528,2048]{1,0:T(8,128)(2,1)S(1)}, bf16[2,128]{1,0:T(2,128)(2,1)S(1)}) custom-call(s32[1]{0:T(128)} %bitcast.place, bf16[1024,896]{1,0:T(8,128)(2,1)} %loads_far.1, bf16[896,896]{1,0:T(8,128)(2,1)} %constant.14.clone.forward_far, ...), custom_call_target="tpu_custom_call" | custom-call | tf_op jit(solution)/shard_map/project/pallas_call | solution.py:68
  8.4 0.5 collective-permute-start
  8.9 0.0 copy-done
  8.9 5.0 %spectrum.1 = (f32[896,512]{1,0:T(8,128)S(1)}, f32[896,512]{1,0:T(8,128)S(1)}, bf16[1024,1024]{1,0:T(8,128)(2,1)S(1)}, bf16[896,1024]{1,0:T(8,128)(2,1)S(1)}, bf...) custom-call(s32[1]{0:T(128)} %bitcast.place, ...), custom_call_target="tpu_custom_call" | custom-call | tf_op jit(solution)/shard_map/spectrum/pallas_call | solution.py:68
  14.0 0.0 collective-permute-done.other
  14.0 1.3 %respond.1 = bf16[272,512]{1,0:T(8,128)(2,1)S(1)} custom-call(s32[1]{0:T(128)} %bitcast.place, f32[896,512]{1,0:T(8,128)S(1)} %get-tuple-element.30.own, bf16[912,1024]{1,0:T(8,128)(2,1)S(1)} %collective-permute-done.other, f32[896,512]{1,0:T(8,128)S(1)} %get-tuple-element.31.spec, bf16[256,1792]{1,0:T(8,128)(2,1)S(1)} %get-tuple-element.29.inverse, ...), custom_call_target="tpu_custom_call" | custom-call | tf_op jit(solution)/shard_map/respond/pallas_call | solution.py:68
  15.3 2.6 %collective-permute-start.1 = (bf16[272,512]{1,0:T(8,128)(2,1)S(1)}, bf16[272,512]{1,0:T(8,128)(2,1)S(1)}, u32[]{:S(2)}, u32[]{:S(2)}) collective-permute-start(bf16[272,512]{1,0:T(8,128)(2,1)S(1)} %respond.1), channel_id=1, source_target_pairs={{0,2},{1,3},{2,0},{3,1},{4,6},{5,7},{6,4},{7,5},{8,10},{9,11},{10,... | collective-permute-start | bytes 835592 | tf_op jit(solution)/shard_map/ppermute | solution.py:338
  17.9 7.1 %whole.1.own = f32[256,512]{1,0:T(8,128)S(1)} custom-call(s32[1]{0:T(128)} %bitcast.place, bf16[528,2048]{1,0:T(8,128)(2,1)S(1)} %get-tuple-element.22.stack, s32[1,2048]{1,0:T(1,128)S(1)} %bitcast.6, bf16[896,1024]{1,0:T(8,128)(2,1)S(1)} %get-tuple-element.23.lft, bf16[912,1024]{1,0:T(8,128)(2,1)S(1)} %collective-permute-done.other, ...), custom_call_target="tpu_custom_call" | custom-call | tf_op jit(solution)/shard_map/whole/pallas_call | solution.py:68
  25.0 0.0 copy-start.1
  25.1 0.2 collective-permute-done.1.got
  25.2 0.1 fold.1
  25.3 3.9 %collective-permute-start.2 = (bf16[272,128]{1,0:T(8,128)(2,1)S(1)}, bf16[272,128]{1,0:T(8,128)(2,1)S(1)}, u32[]{:S(2)}, u32[]{:S(2)}) collective-permute-start(bf16[272,128]{1,0:T(8,128)(2,1)S(1)} %get-tuple-element.34), channel_id=1, source_target_pairs={{0,12},{1,13},{2,14},{3,15},{4,8},{5,9},{6,10},{7,11},{8,4},{9,5},... | collective-permute-start | bytes 208904 | tf_op jit(solution)/shard_map/ppermute | solution.py:338
  29.2 0.0 collective-permute-start.3
  29.2 0.6 %collective-permute-start.4 = (bf16[272,128]{1,0:T(8,128)(2,1)S(1)}, bf16[272,128]{1,0:T(8,128)(2,1)S(1)}, u32[]{:S(2)}, u32[]{:S(2)}) collective-permute-start(bf16[272,128]{1,0:T(8,128)(2,1)S(1)} %get-tuple-element.36), channel_id=1, source_target_pairs={{0,4},{1,5},{2,6},{3,7},{4,0},{5,1},{6,2},{7,3},{8,12},{9,13},{10,... | collective-permute-start | bytes 208904 | tf_op jit(solution)/shard_map/ppermute | solution.py:338
  29.8 0.0 copy-done.1
  29.8 1.4 %pick.1.after = bf16[2048,2048]{1,0:T(8,128)(2,1)S(1)} custom-call(s32[1]{0:T(128)} %bitcast.place, s32[1,2048]{1,0:T(1,128)S(1)} %bitcast.8, f32[256,128]{1,0:T(8,128)S(1)} %get-tuple-element.37.after.keep), custom_call_target="tpu_custom_call" | custom-call | tf_op jit(solution)/shard_map/pick/pallas_call | solution.py:68
  31.2 0.6 %collective-permute-done.2.first.third = bf16[272,128]{1,0:T(8,128)(2,1)S(1)} collective-permute-done((bf16[272,128]{1,0:T(8,128)(2,1)S(1)}, bf16[272,128]{1,0:T(8,128)(2,1)S(1)}, u32[]{:S(2)}, u32[]{:S(2)}) %collective-permute-start.2) | collective-permute-done | bytes 69664 | tf_op jit(solution)/shard_map/ppermute | solution.py:338
  31.9 3.2 %collective-permute-done.3.second = bf16[272,128]{1,0:T(8,128)(2,1)S(1)} collective-permute-done((bf16[272,128]{1,0:T(8,128)(2,1)S(1)}, bf16[272,128]{1,0:T(8,128)(2,1)S(1)}, u32[]{:S(2)}, u32[]{:S(2)}) %collective-permute-start.3) | collective-permute-done | bytes 69664 | tf_op jit(solution)/shard_map/ppermute | solution.py:338
  35.1 0.0 collective-permute-done.4.third.first
  35.2 2.8 %collective-permute-start.7 = (bf16[256,128]{1,0:T(8,128)(2,1)S(1)}, bf16[256,128]{1,0:T(8,128)(2,1)S(1)}, u32[]{:S(2)}, u32[]{:S(2)}) collective-permute-start(bf16[256,128]{1,0:T(8,128)(2,1)S(1)} %settle.1.after.refs_0_), channel_id=1, source_target_pairs={{0,12},{1,13},{2,14},{3,15},{4,8},{5,9},{6,10},{7,11},{8,4},{9,5},... | collective-permute-start | bytes 196616 | tf_op jit(solution)/shard_map/ppermute | solution.py:338
  38.0 0.0 collective-permute-start.6
  38.0 1.7 %collective-permute-start.5 = (bf16[256,128]{1,0:T(8,128)(2,1)S(1)}, bf16[256,128]{1,0:T(8,128)(2,1)S(1)}, u32[]{:S(2)}, u32[]{:S(2)}) collective-permute-start(bf16[256,128]{1,0:T(8,128)(2,1)S(1)} %settle.1.after.refs_0_), channel_id=1, source_target_pairs={{0,4},{1,5},{2,6},{3,7},{4,0},{5,1},{6,2},{7,3},{8,12},{9,13},{10,... | collective-permute-start | bytes 196616 | tf_op jit(solution)/shard_map/ppermute | solution.py:338
  39.6 2.3 %mixers.1._.coef = f32[8,2048]{1,0:T(8,128)S(1)} custom-call(s32[1]{0:T(128)} %bitcast.place, s32[1,2048]{1,0:T(1,128)S(1)} %bitcast.7, bf16[16,128]{1,0:T(8,128)(2,1)S(1)} %get-tuple-element.33.known, bf16[272,128]{1,0:T(8,128)(2,1)S(1)} %collective-permute-done.2.first.third, bf16[272,128]{1,0:T(8,128)(2,1)S(1)} %collective-permute-done.3.second, ...), custom_call_target="tpu_custom_call" | custom-call | tf_op jit(solution)/shard_map/mixers/pallas_call | solution.py:68
  41.9 0.0 collective-permute-done.7.refs_3_
  41.9 2.2 %collective-permute-done.6.refs_2_ = bf16[256,128]{1,0:T(8,128)(2,1)S(1)} collective-permute-done((bf16[256,128]{1,0:T(8,128)(2,1)S(1)}, bf16[256,128]{1,0:T(8,128)(2,1)S(1)}, u32[]{:S(2)}, u32[]{:S(2)}) %collective-permute-start.6) | collective-permute-done | bytes 65568 | tf_op jit(solution)/shard_map/ppermute | solution.py:338
  44.1 0.0 collective-permute-done.5.refs_1_
  44.1 1.6 %collective-permute-start.8 = (bf16[256,512]{1,0:T(8,128)(2,1)S(1)}, bf16[256,512]{1,0:T(8,128)(2,1)S(1)}, u32[]{:S(2)}, u32[]{:S(2)}) collective-permute-start(bf16[256,512]{1,0:T(8,128)(2,1)S(1)} %join.2.refs_0_), channel_id=1, source_target_pairs={{0,2},{1,3},{2,0},{3,1},{4,6},{5,7},{6,4},{7,5},{8,10},{9,11},{10,... | collective-permute-start | bytes 786440 | tf_op jit(solution)/shard_map/ppermute | solution.py:338
  45.7 6.2 %collective-permute-done.8.refs_1_ = bf16[256,512]{1,0:T(8,128)(2,1)S(1)} collective-permute-done((bf16[256,512]{1,0:T(8,128)(2,1)S(1)}, bf16[256,512]{1,0:T(8,128)(2,1)S(1)}, u32[]{:S(2)}, u32[]{:S(2)}) %collective-permute-start.8) | collective-permute-done | bytes 262176 | tf_op jit(solution)/shard_map/ppermute | solution.py:338
  51.9 0.1 collective-permute-start.9
  52.0 1.3 %mate.1.mates = f32[256,2048]{1,0:T(8,128)S(1)} custom-call(bf16[256,1024]{1,0:T(8,128)(2,1)S(1)} %join.3.mine, bf16[2048,2048]{1,0:T(8,128)(2,1)S(1)} %pick.1.after), custom_call_target="tpu_custom_call" | custom-call | tf_op jit(solution)/shard_map/mate/pallas_call | solution.py:68
  53.2 0.6 %collective-permute-done.9.theirs = bf16[256,1024]{1,0:T(8,128)(2,1)S(1)} collective-permute-done((bf16[256,1024]{1,0:T(8,128)(2,1)S(1)}, bf16[256,1024]{1,0:T(8,128)(2,1)S(1)}, u32[]{:S(2)}, u32[]{:S(2)}) %collective-permute-start.9) | collective-permute-done | bytes 524320 | tf_op jit(solution)/shard_map/ppermute | solution.py:338
  53.9 3.5 %expand.1 = bf16[1024,256]{1,0:T(8,128)(2,1)} custom-call(s32[1]{0:T(128)} %bitcast.place, bf16[256,1024]{1,0:T(8,128)(2,1)S(1)} %join.3.mine, bf16[256,1024]{1,0:T(8,128)(2,1)S(1)} %collective-permute-done.9.theirs, f32[256,2048]{1,0:T(8,128)S(1)} %mate.1.mates, bf16[2048,2048]{1,0:T(8,128)(2,1)S(1)} %pick.1.after, f32[8,2048]{1,0:T(8,128)S(1)} %mixers.1._.coef, ...), custom_call_target="tpu_custom_call" | custom-call | tf_op jit(solution)/shard_map/expand/pallas_call | solution.py:68
  (3 shorter events, 0.1 us)
Async XLA Ops:
  0.0 8.9 %copy-start = (s32[2048]{0:T(1024)S(1)}, s32[2048]{0:T(1024)}, u32[]{:S(2)}) copy-start(s32[2048]{0:T(1024)} %param.14) | copy-start | bytes 24580
  8.4 5.5 %collective-permute-start = (bf16[912,1024]{1,0:T(8,128)(2,1)S(1)}, bf16[912,1024]{1,0:T(8,128)(2,1)S(1)}, u32[]{:S(2)}, u32[]{:S(2)}) collective-permute-start(bf16[912,1024]{1,0:T(8,128)(2,1)S(1)} %get-tuple-element.24), channel_id=1, source_target_pairs={{0,1},{1,0},{2,3},{3,2},{4,5},{5,4},{6,7},{7,6},{8,9},{9,8},{10,11... | collective-permute-start | bytes 5603336 | tf_op jit(solution)/shard_map/ppermute | solution.py:338
  15.3 9.9 %collective-permute-start.1 = (bf16[272,512]{1,0:T(8,128)(2,1)S(1)}, bf16[272,512]{1,0:T(8,128)(2,1)S(1)}, u32[]{:S(2)}, u32[]{:S(2)}) collective-permute-start(bf16[272,512]{1,0:T(8,128)(2,1)S(1)} %respond.1), channel_id=1, source_target_pairs={{0,2},{1,3},{2,0},{3,1},{4,6},{5,7},{6,4},{7,5},{8,10},{9,11},{10,... | collective-permute-start | bytes 835592 | tf_op jit(solution)/shard_map/ppermute | solution.py:338
  25.0 4.8 %copy-start.1 = (s32[2048]{0:T(1024)S(1)}, s32[2048]{0:T(1024)}, u32[]{:S(2)}) copy-start(s32[2048]{0:T(1024)} %param.15) | copy-start | bytes 24580
  25.3 6.5 %collective-permute-start.2 = (bf16[272,128]{1,0:T(8,128)(2,1)S(1)}, bf16[272,128]{1,0:T(8,128)(2,1)S(1)}, u32[]{:S(2)}, u32[]{:S(2)}) collective-permute-start(bf16[272,128]{1,0:T(8,128)(2,1)S(1)} %get-tuple-element.34), channel_id=1, source_target_pairs={{0,12},{1,13},{2,14},{3,15},{4,8},{5,9},{6,10},{7,11},{8,4},{9,5},... | collective-permute-start | bytes 208904 | tf_op jit(solution)/shard_map/ppermute | solution.py:338
  29.2 5.9 %collective-permute-start.3 = (bf16[272,128]{1,0:T(8,128)(2,1)S(1)}, bf16[272,128]{1,0:T(8,128)(2,1)S(1)}, u32[]{:S(2)}, u32[]{:S(2)}) collective-permute-start(bf16[272,128]{1,0:T(8,128)(2,1)S(1)} %get-tuple-element.35), channel_id=1, source_target_pairs={{0,8},{1,9},{2,10},{3,11},{4,12},{5,13},{6,14},{7,15},{8,0},{9,1},... | collective-permute-start | bytes 208904 | tf_op jit(solution)/shard_map/ppermute | solution.py:338
  29.2 5.9 %collective-permute-start.4 = (bf16[272,128]{1,0:T(8,128)(2,1)S(1)}, bf16[272,128]{1,0:T(8,128)(2,1)S(1)}, u32[]{:S(2)}, u32[]{:S(2)}) collective-permute-start(bf16[272,128]{1,0:T(8,128)(2,1)S(1)} %get-tuple-element.36), channel_id=1, source_target_pairs={{0,4},{1,5},{2,6},{3,7},{4,0},{5,1},{6,2},{7,3},{8,12},{9,13},{10,... | collective-permute-start | bytes 208904 | tf_op jit(solution)/shard_map/ppermute | solution.py:338
  35.2 6.7 %collective-permute-start.7 = (bf16[256,128]{1,0:T(8,128)(2,1)S(1)}, bf16[256,128]{1,0:T(8,128)(2,1)S(1)}, u32[]{:S(2)}, u32[]{:S(2)}) collective-permute-start(bf16[256,128]{1,0:T(8,128)(2,1)S(1)} %settle.1.after.refs_0_), channel_id=1, source_target_pairs={{0,12},{1,13},{2,14},{3,15},{4,8},{5,9},{6,10},{7,11},{8,4},{9,5},... | collective-permute-start | bytes 196616 | tf_op jit(solution)/shard_map/ppermute | solution.py:338
  38.0 6.1 %collective-permute-start.6 = (bf16[256,128]{1,0:T(8,128)(2,1)S(1)}, bf16[256,128]{1,0:T(8,128)(2,1)S(1)}, u32[]{:S(2)}, u32[]{:S(2)}) collective-permute-start(bf16[256,128]{1,0:T(8,128)(2,1)S(1)} %settle.1.after.refs_0_), channel_id=1, source_target_pairs={{0,8},{1,9},{2,10},{3,11},{4,12},{5,13},{6,14},{7,15},{8,0},{9,1},... | collective-permute-start | bytes 196616 | tf_op jit(solution)/shard_map/ppermute | solution.py:338
  38.0 6.1 %collective-permute-start.5 = (bf16[256,128]{1,0:T(8,128)(2,1)S(1)}, bf16[256,128]{1,0:T(8,128)(2,1)S(1)}, u32[]{:S(2)}, u32[]{:S(2)}) collective-permute-start(bf16[256,128]{1,0:T(8,128)(2,1)S(1)} %settle.1.after.refs_0_), channel_id=1, source_target_pairs={{0,4},{1,5},{2,6},{3,7},{4,0},{5,1},{6,2},{7,3},{8,12},{9,13},{10,... | collective-permute-start | bytes 196616 | tf_op jit(solution)/shard_map/ppermute | solution.py:338
  44.1 7.7 %collective-permute-start.8 = (bf16[256,512]{1,0:T(8,128)(2,1)S(1)}, bf16[256,512]{1,0:T(8,128)(2,1)S(1)}, u32[]{:S(2)}, u32[]{:S(2)}) collective-permute-start(bf16[256,512]{1,0:T(8,128)(2,1)S(1)} %join.2.refs_0_), channel_id=1, source_target_pairs={{0,2},{1,3},{2,0},{3,1},{4,6},{5,7},{6,4},{7,5},{8,10},{9,11},{10,... | collective-permute-start | bytes 786440 | tf_op jit(solution)/shard_map/ppermute | solution.py:338
  51.9 2.0 %collective-permute-start.9 = (bf16[256,1024]{1,0:T(8,128)(2,1)S(1)}, bf16[256,1024]{1,0:T(8,128)(2,1)S(1)}, u32[]{:S(2)}, u32[]{:S(2)}) collective-permute-start(bf16[256,1024]{1,0:T(8,128)(2,1)S(1)} %join.3.mine), channel_id=1, source_target_pairs={{0,1},{1,0},{2,3},{3,2},{4,5},{5,4},{6,7},{7,6},{8,9},{9,8},{10,11... | collective-permute-start | bytes 1572872 | tf_op jit(solution)/shard_map/ppermute | solution.py:338

commit v8 on v7

--- a/solution.py
+++ b/solution.py
@@ -10,6 +10,7 @@
 
 W = 256
 LANES = 128
+TILE = 512
 EXTRA = 16
 BF = jnp.bfloat16
 F32 = jnp.float32
@@ -103,9 +104,8 @@
     rows, half = loads.shape[0], sent.shape[1]
     hist = lft.shape[0]
     start = (1 - (place[0] & 1)) * half
-    step = 256
-    chunks = [pl.ds(r, step) for r in range(0, rows, step)]
-    pairs = [(forward_far, forward)] + [(loads_far.at[r, :], loads.at[r, :]) for r in chunks]
+    step = TILE
+    pairs = [(forward_far, forward), (loads_far, loads)]
     first = len(pairs)
     pairs += [
         (coef_far, coef),
@@ -117,12 +117,16 @@
     for copy in copies[:first]:
         copy.start()
     copies[0].wait()
-    for i, r in enumerate(chunks):
-        copies[1 + i].wait()
-        if i == 0:
-            for copy in copies[first:]:
-                copy.start()
-        lft[:, i * step : (i + 1) * step] = dot(forward[...], loads[r, :], NT).astype(BF)
+    for copy in copies[1:first]:
+        copy.wait()
+    for copy in copies[first:]:
+        copy.start()
+
+    @pl.loop(0, rows // step)
+    def _(j):
+        here = block(j * step, step)
+        lft[:, here] = dot(forward[...], loads[here, :], NT).astype(BF)
+
     for copy in copies[first : first + 3]:
         copy.wait()
     count = taps.shape[0] - 1
@@ -145,7 +149,7 @@
 
 def gather_taps(base, stack, order):
     count = stack.shape[0] - EXTRA
-    mode = lax.broadcasted_iota(I32, (256, stack.shape[1]), 0) + base
+    mode = lax.broadcasted_iota(I32, (TILE, stack.shape[1]), 0) + base
     picked = dot(stack[...], hot(mode == order[...]), NT)
     tail = picked[count:]
     return picked[:count].astype(BF), tail[0:1], tail[1:2].astype(I32)
@@ -155,8 +159,8 @@
     half = table.shape[0] // 2
     delay = phase.shape[1] // 2
     resp = dot(table[...], jnp.concatenate([main, main], axis=0))
-    resp = resp + jnp.tile(last[...].astype(F32), (1, 2)) * end
-    which = hot(lax.broadcasted_iota(I32, (delay, 256), 0) + 1 == offset)
+    resp = resp + jnp.tile(last[...].astype(F32), (1, TILE // LANES)) * end
+    which = hot(lax.broadcasted_iota(I32, (delay, TILE), 0) + 1 == offset)
     turn = dot(phase[...], jnp.concatenate([which, which], axis=0))
     cos, sin = turn[:half] + 1.0, turn[half:]
     re, im = resp[:half], resp[half:]
@@ -186,15 +190,15 @@
     )
     for copy in copies:
         copy.start()
-    tiles = range(0, width, 256)
+    tiles = range(0, width, TILE)
     picked = [gather_taps(near + start + c, stack, order) for c in tiles]
     copies[0].wait()
     for c in tiles:
-        own[:, c : c + 256] = dot(lft[...], shapes[:, block(start + c, 256)])
+        own[:, c : c + TILE] = dot(lft[...], shapes[:, block(start + c, TILE)])
     for copy in copies[1:4]:
         copy.wait()
     for c, parts in zip(tiles, picked):
-        spec[:half, c : c + 256], spec[half:, c : c + 256] = spectrum_of(*parts, table, last, phase)
+        spec[:half, c : c + TILE], spec[half:, c : c + TILE] = spectrum_of(*parts, table, last, phase)
     for copy in copies[4:]:
         copy.wait()
 
@@ -213,27 +217,27 @@
     hist, modes = lft.shape[0], order.shape[1]
     start = quarter_start(place, 0, modes)
     near = (place[0] & 1) * (modes // 2) + start
-    for c in range(0, out.shape[1], 256):
+    for c in range(0, out.shape[1], TILE):
         spec = spectrum_of(*gather_taps(near + c, stack, order), table, last, phase)
-        here = block(start + c, 256)
+        here = block(start + c, TILE)
         total = dot(lft[...], shapes[:, here]) + other[:hist, here].astype(F32)
-        out[:, c : c + 256] = impose(total, *spec, inverse)
+        out[:, c : c + TILE] = impose(total, *spec, inverse)
 
 
 def respond_kernel(place, own, other, spec, inverse, coef, out):
     hist, width = own.shape
     half = hist // 2
     start = quarter_start(place, 1, 4 * width)
-    for c in range(0, width, 256):
-        total = own[:, c : c + 256] + other[:hist, block(start + c, 256)].astype(F32)
-        result = impose(total, spec[:half, c : c + 256], spec[half:, c : c + 256], inverse)
-        out[:W, c : c + 256] = result.astype(BF)
+    for c in range(0, width, TILE):
+        total = own[:, c : c + TILE] + other[:hist, block(start + c, TILE)].astype(F32)
+        result = impose(total, spec[:half, c : c + TILE], spec[half:, c : c + TILE], inverse)
+        out[:W, c : c + TILE] = result.astype(BF)
     out[W:, :] = jnp.zeros((EXTRA, width), BF)
     out[W : W + 2, : coef.shape[1]] = coef[...]
     out[W + 2 : W + 4, :LANES] = other[hist : hist + 2, :LANES]
 
 
-def fold_kernel(place, own, got, coef, other, keep, known, first, second, third):
+def fold_kernel(place, own, got, coef, other, before, keep, known, first, second, third):
     z = place[0] >> 2
     size = keep.shape[1]
     hist = other.shape[0] - EXTRA
@@ -249,7 +253,7 @@
             out[W:, :] = known[...]
 
 
-def settle_kernel(after, keep, first, second, third, out):
+def settle_kernel(keep, first, second, third, out):
     total = keep[...]
     for got in (first, second, third):
         total = total + got[:W, :].astype(F32)
@@ -287,8 +291,8 @@
     modes = order.shape[1]
     table = held[...].astype(BF)
     slots = order[...] ^ mask
-    for c in range(0, modes, 256):
-        coef[:, c : c + 256] = dot(table, hot(lax.broadcasted_iota(I32, (256, modes), 0) + c == slots), NT)
+    for c in range(0, modes, TILE):
+        coef[:, c : c + TILE] = dot(table, hot(lax.broadcasted_iota(I32, (TILE, modes), 0) + c == slots), NT)
 
 
 def plain_mixers_kernel(devices, place, order, every, coef, held):
@@ -314,24 +318,25 @@
 
 def mate_kernel(mine, pick, out):
     half = mine.shape[1]
-    for c in range(0, 2 * half, 256):
-        out[:, c : c + 256] = dot(mine[...], pick[:half, c : c + 256])
+    for c in range(0, 2 * half, TILE):
+        out[:, c : c + TILE] = dot(mine[...], pick[:half, c : c + TILE])
 
 
 def expand_kernel(devices, place, mine, theirs, mates, pick, coef, near, far, out, near_pair, far_pair):
     half = mine.shape[1]
     mask = mask_of(place, devices, 2 * half)
     for q, (direct, pair) in enumerate(((mine, near_pair), (theirs, far_pair))):
-        for c in range(0, half, 256):
+        for c in range(0, half, TILE):
             k = q * half + c
-            across = mates[:, k : k + 256] + dot(theirs[...], pick[half:, k : k + 256])
-            mixed = coef[0:1, k : k + 256] * direct[:, c : c + 256].astype(F32) + coef[1:2, k : k + 256] * across
-            for d in (0, LANES):
+            here = slice(k, k + TILE)
+            across = mates[:, here] + dot(theirs[...], pick[half:, here])
+            mixed = coef[0:1, here] * direct[:, c : c + TILE].astype(F32) + coef[1:2, here] * across
+            for d in range(0, TILE, LANES):
                 pair[:, block((mask ^ (k + d)) & (half - 1), LANES)] = mixed[:, d : d + LANES].astype(BF)
     rows = out.shape[0]
-    for r in range(0, rows, 256):
-        total = dot(near[r : r + 256, :], near_pair[...], NT) + dot(far[r : r + 256, :], far_pair[...], NT)
-        out[r : r + 256, :] = total.astype(BF)
+    for r in range(0, rows, TILE):
+        total = dot(near[r : r + TILE, :], near_pair[...], NT) + dot(far[r : r + TILE, :], far_pair[...], NT)
+        out[r : r + TILE, :] = total.astype(BF)
 
 
 def swap(x, devices, bits):
@@ -355,7 +360,7 @@
         place, loads, forward, shapes, taps, offsets, coef, far=range(1, 7),
         scratch=[
             pltpu.VMEM(loads.shape, BF), pltpu.VMEM(forward.shape, BF), pltpu.VMEM(taps.shape, F32),
-            pltpu.VMEM(offsets.shape, I32), pltpu.SemaphoreType.DMA((5 + rows // 256,)),
+            pltpu.VMEM(offsets.shape, I32), pltpu.SemaphoreType.DMA((6,)),
         ],
         limit=24,
     )
@@ -378,21 +383,21 @@
     pair = functools.partial(pick_kernel, devices)
     if devices == 16:
         size = modes // devices
+        pick = call(pair, "pick", [near(modes, modes)], place, mates, away)[0]
         away = swap(away, devices, 2)
         keep, known, *parts = call(
             fold_kernel, "fold", [array(W, size, dtype=F32), array(EXTRA, LANES)] + [array(W + EXTRA, size)] * 3,
-            place, respond_own(), away, coef_near, got,
+            place, respond_own(), away, coef_near, got, pick,
         )
         parts = [swap(part, devices, 4 * d) for d, part in reversed(list(zip((1, 2, 3), parts)))]
-        pick = call(pair, "pick", [near(modes, modes)], place, mates, keep)[0]
-        total = call(settle_kernel, "settle", [array(W, size)], pick, keep, *parts, scalars=0)[0]
-        spread = [swap(total, devices, 4 * d) for d in (3, 2, 1)]
+        total = call(settle_kernel, "settle", [array(W, size)], keep, *parts, scalars=0)[0]
+        spread = [swap(total, devices, 4 * d) for d in (1, 2, 3)]
+        resp = join(total, *spread)
         mode_coef = call(
             mixers_kernel, "mixers", [array(8, modes, dtype=F32)],
-            place, order, known, *parts, total, scratch=[pltpu.VMEM((8, modes), F32)],
+            place, order, known, *parts, resp, scratch=[pltpu.VMEM((8, modes), F32)],
         )[0]
-        resp = join(total, *reversed(spread), after=mode_coef)
-        mine = join(resp, swap(resp, devices, 2))
+        mine = join(resp, swap(resp, devices, 2), after=mode_coef)
     else:
         pick = call(pair, "pick", [near(modes, modes)], place, mates, mates)[0]
         mode_coef = call(

time: 57.5 us -> 56 us (0.974)
  Pallas kernels: 30.5 us -> 27 us
  waiting for transfers between devices: 13 us -> 15 us
    pallas_call x12, Pallas kernels: 30.5 us -> 27 us  [call(): pl.pallas_call(kernel, in_specs=places, out_specs=[vmem] * len(out_shape)...]
    ppermute x10, waiting for transfers between devices: 13 us -> 15 us  [swap(): return lax.ppermute(x, 'frdm', [(i, i ^ bits) for i in range(devices)])]
  transfers between devices with their start and end apart: 10 -> 10, of which waited for: 6 -> 7; matrix products, arithmetic and copies ran while one was open for 0% -> 0% of each run, Pallas kernels for 30% -> 27%
where the time goes in v8:
time: 56 us; the launch traced here: 55.8 us
  Pallas kernels  27 us (48%)
  waiting for transfers between devices  15 us (27%)
  starting transfers between devices  13.8 us (25%)
    pallas_call x12, Pallas kernels, call(): pl.pallas_call(kernel, in_specs=places, out_specs=[vmem] * len(out_shape)...  27 us
    ppermute x10, waiting for transfers between devices, swap(): return lax.ppermute(x, 'frdm', [(i, i ^ bits) for i in range(devices)])  15 us
    ppermute x10, starting transfers between devices, swap(): return lax.ppermute(x, 'frdm', [(i, i ^ bits) for i in range(devices)])  13.8 us
  transfers between devices with their start and end apart: 10, of which 7 were waited for; matrix products, arithmetic and copies ran while one was open for 0% of the time, Pallas kernels for 27%

profile of v8, /device:TPU:0, one launch (start us, length us, event | category | flops | bytes accessed | tf_op | source)
XLA Modules:
  0.0 55.8 jit_solution(18052005728589841447)
XLA Ops:
  0.0 0.0 copy-start
  0.0 6.6 %project.1 = (bf16[912,1024]{1,0:T(8,128)(2,1)S(1)}, bf16[896,1024]{1,0:T(8,128)(2,1)S(1)}, bf16[1024,1024]{1,0:T(8,128)(2,1)S(1)}, bf16[528,2048]{1,0:T(8,128)(2,1)S(1)}, bf16[2,128]{1,0:T(2,128)(2,1)S(1)}) custom-call(s32[1]{0:T(128)} %bitcast.place, bf16[1024,896]{1,0:T(8,128)(2,1)} %loads_far.1, bf16[896,896]{1,0:T(8,128)(2,1)} %constant.14.clone.forward_far, ...), custom_call_target="tpu_custom_call" | custom-call | tf_op jit(solution)/shard_map/project/pallas_call | solution.py:69
  6.6 0.5 collective-permute-start
  7.2 0.0 copy-done
  7.2 5.2 %spectrum.1 = (f32[896,512]{1,0:T(8,128)S(1)}, f32[896,512]{1,0:T(8,128)S(1)}, bf16[1024,1024]{1,0:T(8,128)(2,1)S(1)}, bf16[896,1024]{1,0:T(8,128)(2,1)S(1)}, bf...) custom-call(s32[1]{0:T(128)} %bitcast.place, ...), custom_call_target="tpu_custom_call" | custom-call | tf_op jit(solution)/shard_map/spectrum/pallas_call | solution.py:69
  12.3 0.0 collective-permute-done.other
  12.4 0.0 copy-start.1
  12.4 1.3 %respond.1.after = bf16[272,512]{1,0:T(8,128)(2,1)S(1)} custom-call(s32[1]{0:T(128)} %bitcast.place, f32[896,512]{1,0:T(8,128)S(1)} %get-tuple-element.30.own, bf16[912,1024]{1,0:T(8,128)(2,1)S(1)} %collective-permute-done.other, f32[896,512]{1,0:T(8,128)S(1)} %get-tuple-element.31.spec, bf16[256,1792]{1,0:T(8,128)(2,1)S(1)} %get-tuple-element.29.inverse, ...), custom_call_target="tpu_custom_call" | custom-call | tf_op jit(solution)/shard_map/respond/pallas_call | solution.py:69
  13.7 2.6 %collective-permute-start.1 = (bf16[272,512]{1,0:T(8,128)(2,1)S(1)}, bf16[272,512]{1,0:T(8,128)(2,1)S(1)}, u32[]{:S(2)}, u32[]{:S(2)}) collective-permute-start(bf16[272,512]{1,0:T(8,128)(2,1)S(1)} %respond.1.after), channel_id=1, source_target_pairs={{0,2},{1,3},{2,0},{3,1},{4,6},{5,7},{6,4},{7,5},{8,10},{9,11},{10,... | collective-permute-start | bytes 835592 | tf_op jit(solution)/shard_map/ppermute | solution.py:343
  16.3 0.0 copy-done.1
  16.3 1.4 %pick.1.before = bf16[2048,2048]{1,0:T(8,128)(2,1)S(1)} custom-call(s32[1]{0:T(128)} %bitcast.place, s32[1,2048]{1,0:T(1,128)S(1)} %bitcast.8, bf16[272,512]{1,0:T(8,128)(2,1)S(1)} %respond.1.after), custom_call_target="tpu_custom_call" | custom-call | tf_op jit(solution)/shard_map/pick/pallas_call | solution.py:69
  17.7 5.1 %whole.1.own = f32[256,512]{1,0:T(8,128)S(1)} custom-call(s32[1]{0:T(128)} %bitcast.place, bf16[528,2048]{1,0:T(8,128)(2,1)S(1)} %get-tuple-element.22.stack, s32[1,2048]{1,0:T(1,128)S(1)} %bitcast.6, bf16[896,1024]{1,0:T(8,128)(2,1)S(1)} %get-tuple-element.23.lft, bf16[912,1024]{1,0:T(8,128)(2,1)S(1)} %collective-permute-done.other, ...), custom_call_target="tpu_custom_call" | custom-call | tf_op jit(solution)/shard_map/whole/pallas_call | solution.py:69
  22.8 0.8 %collective-permute-done.1.got = bf16[272,512]{1,0:T(8,128)(2,1)S(1)} collective-permute-done((bf16[272,512]{1,0:T(8,128)(2,1)S(1)}, bf16[272,512]{1,0:T(8,128)(2,1)S(1)}, u32[]{:S(2)}, u32[]{:S(2)}) %collective-permute-start.1) | collective-permute-done | bytes 278560 | tf_op jit(solution)/shard_map/ppermute | solution.py:343
  23.6 0.1 fold.1
  23.7 3.9 %collective-permute-start.2 = (bf16[272,128]{1,0:T(8,128)(2,1)S(1)}, bf16[272,128]{1,0:T(8,128)(2,1)S(1)}, u32[]{:S(2)}, u32[]{:S(2)}) collective-permute-start(bf16[272,128]{1,0:T(8,128)(2,1)S(1)} %get-tuple-element.34), channel_id=1, source_target_pairs={{0,12},{1,13},{2,14},{3,15},{4,8},{5,9},{6,10},{7,11},{8,4},{9,5},... | collective-permute-start | bytes 208904 | tf_op jit(solution)/shard_map/ppermute | solution.py:343
  27.6 0.0 collective-permute-start.3
  27.6 0.6 %collective-permute-start.4 = (bf16[272,128]{1,0:T(8,128)(2,1)S(1)}, bf16[272,128]{1,0:T(8,128)(2,1)S(1)}, u32[]{:S(2)}, u32[]{:S(2)}) collective-permute-start(bf16[272,128]{1,0:T(8,128)(2,1)S(1)} %get-tuple-element.36), channel_id=1, source_target_pairs={{0,4},{1,5},{2,6},{3,7},{4,0},{5,1},{6,2},{7,3},{8,12},{9,13},{10,... | collective-permute-start | bytes 208904 | tf_op jit(solution)/shard_map/ppermute | solution.py:343
  28.3 2.2 %collective-permute-done.2.first.third = bf16[272,128]{1,0:T(8,128)(2,1)S(1)} collective-permute-done((bf16[272,128]{1,0:T(8,128)(2,1)S(1)}, bf16[272,128]{1,0:T(8,128)(2,1)S(1)}, u32[]{:S(2)}, u32[]{:S(2)}) %collective-permute-start.2) | collective-permute-done | bytes 69664 | tf_op jit(solution)/shard_map/ppermute | solution.py:343
  30.4 3.0 %collective-permute-done.3.second = bf16[272,128]{1,0:T(8,128)(2,1)S(1)} collective-permute-done((bf16[272,128]{1,0:T(8,128)(2,1)S(1)}, bf16[272,128]{1,0:T(8,128)(2,1)S(1)}, u32[]{:S(2)}, u32[]{:S(2)}) %collective-permute-start.3) | collective-permute-done | bytes 69664 | tf_op jit(solution)/shard_map/ppermute | solution.py:343
  33.4 0.0 collective-permute-done.4.third.first
  33.4 2.8 %collective-permute-start.7 = (bf16[256,128]{1,0:T(8,128)(2,1)S(1)}, bf16[256,128]{1,0:T(8,128)(2,1)S(1)}, u32[]{:S(2)}, u32[]{:S(2)}) collective-permute-start(bf16[256,128]{1,0:T(8,128)(2,1)S(1)} %settle.1.refs_0_), channel_id=1, source_target_pairs={{0,12},{1,13},{2,14},{3,15},{4,8},{5,9},{6,10},{7,11},{8,4},{9,5},... | collective-permute-start | bytes 196616 | tf_op jit(solution)/shard_map/ppermute | solution.py:343
  36.2 0.0 collective-permute-start.6
  36.2 1.7 %collective-permute-start.5 = (bf16[256,128]{1,0:T(8,128)(2,1)S(1)}, bf16[256,128]{1,0:T(8,128)(2,1)S(1)}, u32[]{:S(2)}, u32[]{:S(2)}) collective-permute-start(bf16[256,128]{1,0:T(8,128)(2,1)S(1)} %settle.1.refs_0_), channel_id=1, source_target_pairs={{0,4},{1,5},{2,6},{3,7},{4,0},{5,1},{6,2},{7,3},{8,12},{9,13},{10,... | collective-permute-start | bytes 196616 | tf_op jit(solution)/shard_map/ppermute | solution.py:343
  37.9 2.4 %collective-permute-done.7.refs_3_ = bf16[256,128]{1,0:T(8,128)(2,1)S(1)} collective-permute-done((bf16[256,128]{1,0:T(8,128)(2,1)S(1)}, bf16[256,128]{1,0:T(8,128)(2,1)S(1)}, u32[]{:S(2)}, u32[]{:S(2)}) %collective-permute-start.7) | collective-permute-done | bytes 65568 | tf_op jit(solution)/shard_map/ppermute | solution.py:343
  40.3 2.1 %collective-permute-done.6.refs_2_ = bf16[256,128]{1,0:T(8,128)(2,1)S(1)} collective-permute-done((bf16[256,128]{1,0:T(8,128)(2,1)S(1)}, bf16[256,128]{1,0:T(8,128)(2,1)S(1)}, u32[]{:S(2)}, u32[]{:S(2)}) %collective-permute-start.6) | collective-permute-done | bytes 65568 | tf_op jit(solution)/shard_map/ppermute | solution.py:343
  42.5 0.0 collective-permute-done.5.refs_1_
  42.5 1.6 %collective-permute-start.8 = (bf16[256,512]{1,0:T(8,128)(2,1)S(1)}, bf16[256,512]{1,0:T(8,128)(2,1)S(1)}, u32[]{:S(2)}, u32[]{:S(2)}) collective-permute-start(bf16[256,512]{1,0:T(8,128)(2,1)S(1)} %join.2.after.refs_0_), channel_id=1, source_target_pairs={{0,2},{1,3},{2,0},{3,1},{4,6},{5,7},{6,4},{7,5},{8,10},{9,11},{10,... | collective-permute-start | bytes 786440 | tf_op jit(solution)/shard_map/ppermute | solution.py:343
  44.1 2.4 %mixers.1._.coef = f32[8,2048]{1,0:T(8,128)S(1)} custom-call(s32[1]{0:T(128)} %bitcast.place, s32[1,2048]{1,0:T(1,128)S(1)} %bitcast.7, bf16[16,128]{1,0:T(8,128)(2,1)S(1)} %get-tuple-element.33.known, bf16[272,128]{1,0:T(8,128)(2,1)S(1)} %collective-permute-done.2.first.third, bf16[272,128]{1,0:T(8,128)(2,1)S(1)} %collective-permute-done.3.second, ...), custom_call_target="tpu_custom_call" | custom-call | tf_op jit(solution)/shard_map/mixers/pallas_call | solution.py:69
  46.5 3.8 %collective-permute-done.8.refs_1_ = bf16[256,512]{1,0:T(8,128)(2,1)S(1)} collective-permute-done((bf16[256,512]{1,0:T(8,128)(2,1)S(1)}, bf16[256,512]{1,0:T(8,128)(2,1)S(1)}, u32[]{:S(2)}, u32[]{:S(2)}) %collective-permute-start.8) | collective-permute-done | bytes 262176 | tf_op jit(solution)/shard_map/ppermute | solution.py:343
  50.3 0.1 collective-permute-start.9
  50.4 1.2 %mate.1.mates = f32[256,2048]{1,0:T(8,128)S(1)} custom-call(bf16[256,1024]{1,0:T(8,128)(2,1)S(1)} %join.3.mine, bf16[2048,2048]{1,0:T(8,128)(2,1)S(1)} %pick.1.before), custom_call_target="tpu_custom_call" | custom-call | tf_op jit(solution)/shard_map/mate/pallas_call | solution.py:69
  51.7 0.6 %collective-permute-done.9.theirs = bf16[256,1024]{1,0:T(8,128)(2,1)S(1)} collective-permute-done((bf16[256,1024]{1,0:T(8,128)(2,1)S(1)}, bf16[256,1024]{1,0:T(8,128)(2,1)S(1)}, u32[]{:S(2)}, u32[]{:S(2)}) %collective-permute-start.9) | collective-permute-done | bytes 524320 | tf_op jit(solution)/shard_map/ppermute | solution.py:343
  52.3 3.5 %expand.1 = bf16[1024,256]{1,0:T(8,128)(2,1)} custom-call(s32[1]{0:T(128)} %bitcast.place, bf16[256,1024]{1,0:T(8,128)(2,1)S(1)} %join.3.mine, bf16[256,1024]{1,0:T(8,128)(2,1)S(1)} %collective-permute-done.9.theirs, f32[256,2048]{1,0:T(8,128)S(1)} %mate.1.mates, bf16[2048,2048]{1,0:T(8,128)(2,1)S(1)} %pick.1.before, f32[8,2048]{1,0:T(8,128)S(1)} %mixers.1._.coef, ...), custom_call_target="tpu_custom_call" | custom-call | tf_op jit(solution)/shard_map/expand/pallas_call | solution.py:69
  (3 shorter events, 0.1 us)
Async XLA Ops:
  0.0 7.2 %copy-start = (s32[2048]{0:T(1024)S(1)}, s32[2048]{0:T(1024)}, u32[]{:S(2)}) copy-start(s32[2048]{0:T(1024)} %param.14) | copy-start | bytes 24580
  6.6 5.7 %collective-permute-start = (bf16[912,1024]{1,0:T(8,128)(2,1)S(1)}, bf16[912,1024]{1,0:T(8,128)(2,1)S(1)}, u32[]{:S(2)}, u32[]{:S(2)}) collective-permute-start(bf16[912,1024]{1,0:T(8,128)(2,1)S(1)} %get-tuple-element.24), channel_id=1, source_target_pairs={{0,1},{1,0},{2,3},{3,2},{4,5},{5,4},{6,7},{7,6},{8,9},{9,8},{10,11... | collective-permute-start | bytes 5603336 | tf_op jit(solution)/shard_map/ppermute | solution.py:343
  12.4 4.0 %copy-start.1 = (s32[2048]{0:T(1024)S(1)}, s32[2048]{0:T(1024)}, u32[]{:S(2)}) copy-start(s32[2048]{0:T(1024)} %param.15) | copy-start | bytes 24580
  13.7 9.9 %collective-permute-start.1 = (bf16[272,512]{1,0:T(8,128)(2,1)S(1)}, bf16[272,512]{1,0:T(8,128)(2,1)S(1)}, u32[]{:S(2)}, u32[]{:S(2)}) collective-permute-start(bf16[272,512]{1,0:T(8,128)(2,1)S(1)} %respond.1.after), channel_id=1, source_target_pairs={{0,2},{1,3},{2,0},{3,1},{4,6},{5,7},{6,4},{7,5},{8,10},{9,11},{10,... | collective-permute-start | bytes 835592 | tf_op jit(solution)/shard_map/ppermute | solution.py:343
  23.7 6.7 %collective-permute-start.2 = (bf16[272,128]{1,0:T(8,128)(2,1)S(1)}, bf16[272,128]{1,0:T(8,128)(2,1)S(1)}, u32[]{:S(2)}, u32[]{:S(2)}) collective-permute-start(bf16[272,128]{1,0:T(8,128)(2,1)S(1)} %get-tuple-element.34), channel_id=1, source_target_pairs={{0,12},{1,13},{2,14},{3,15},{4,8},{5,9},{6,10},{7,11},{8,4},{9,5},... | collective-permute-start | bytes 208904 | tf_op jit(solution)/shard_map/ppermute | solution.py:343
  27.6 5.8 %collective-permute-start.3 = (bf16[272,128]{1,0:T(8,128)(2,1)S(1)}, bf16[272,128]{1,0:T(8,128)(2,1)S(1)}, u32[]{:S(2)}, u32[]{:S(2)}) collective-permute-start(bf16[272,128]{1,0:T(8,128)(2,1)S(1)} %get-tuple-element.35), channel_id=1, source_target_pairs={{0,8},{1,9},{2,10},{3,11},{4,12},{5,13},{6,14},{7,15},{8,0},{9,1},... | collective-permute-start | bytes 208904 | tf_op jit(solution)/shard_map/ppermute | solution.py:343
  27.6 5.8 %collective-permute-start.4 = (bf16[272,128]{1,0:T(8,128)(2,1)S(1)}, bf16[272,128]{1,0:T(8,128)(2,1)S(1)}, u32[]{:S(2)}, u32[]{:S(2)}) collective-permute-start(bf16[272,128]{1,0:T(8,128)(2,1)S(1)} %get-tuple-element.36), channel_id=1, source_target_pairs={{0,4},{1,5},{2,6},{3,7},{4,0},{5,1},{6,2},{7,3},{8,12},{9,13},{10,... | collective-permute-start | bytes 208904 | tf_op jit(solution)/shard_map/ppermute | solution.py:343
  33.4 6.9 %collective-permute-start.7 = (bf16[256,128]{1,0:T(8,128)(2,1)S(1)}, bf16[256,128]{1,0:T(8,128)(2,1)S(1)}, u32[]{:S(2)}, u32[]{:S(2)}) collective-permute-start(bf16[256,128]{1,0:T(8,128)(2,1)S(1)} %settle.1.refs_0_), channel_id=1, source_target_pairs={{0,12},{1,13},{2,14},{3,15},{4,8},{5,9},{6,10},{7,11},{8,4},{9,5},... | collective-permute-start | bytes 196616 | tf_op jit(solution)/shard_map/ppermute | solution.py:343
  36.2 6.2 %collective-permute-start.6 = (bf16[256,128]{1,0:T(8,128)(2,1)S(1)}, bf16[256,128]{1,0:T(8,128)(2,1)S(1)}, u32[]{:S(2)}, u32[]{:S(2)}) collective-permute-start(bf16[256,128]{1,0:T(8,128)(2,1)S(1)} %settle.1.refs_0_), channel_id=1, source_target_pairs={{0,8},{1,9},{2,10},{3,11},{4,12},{5,13},{6,14},{7,15},{8,0},{9,1},... | collective-permute-start | bytes 196616 | tf_op jit(solution)/shard_map/ppermute | solution.py:343
  36.2 6.2 %collective-permute-start.5 = (bf16[256,128]{1,0:T(8,128)(2,1)S(1)}, bf16[256,128]{1,0:T(8,128)(2,1)S(1)}, u32[]{:S(2)}, u32[]{:S(2)}) collective-permute-start(bf16[256,128]{1,0:T(8,128)(2,1)S(1)} %settle.1.refs_0_), channel_id=1, source_target_pairs={{0,4},{1,5},{2,6},{3,7},{4,0},{5,1},{6,2},{7,3},{8,12},{9,13},{10,... | collective-permute-start | bytes 196616 | tf_op jit(solution)/shard_map/ppermute | solution.py:343
  42.5 7.8 %collective-permute-start.8 = (bf16[256,512]{1,0:T(8,128)(2,1)S(1)}, bf16[256,512]{1,0:T(8,128)(2,1)S(1)}, u32[]{:S(2)}, u32[]{:S(2)}) collective-permute-start(bf16[256,512]{1,0:T(8,128)(2,1)S(1)} %join.2.after.refs_0_), channel_id=1, source_target_pairs={{0,2},{1,3},{2,0},{3,1},{4,6},{5,7},{6,4},{7,5},{8,10},{9,11},{10,... | collective-permute-start | bytes 786440 | tf_op jit(solution)/shard_map/ppermute | solution.py:343
  50.3 2.0 %collective-permute-start.9 = (bf16[256,1024]{1,0:T(8,128)(2,1)S(1)}, bf16[256,1024]{1,0:T(8,128)(2,1)S(1)}, u32[]{:S(2)}, u32[]{:S(2)}) collective-permute-start(bf16[256,1024]{1,0:T(8,128)(2,1)S(1)} %join.3.mine), channel_id=1, source_target_pairs={{0,1},{1,0},{2,3},{3,2},{4,5},{5,4},{6,7},{7,6},{8,9},{9,8},{10,11... | collective-permute-start | bytes 1572872 | tf_op jit(solution)/shard_map/ppermute | solution.py:343

commit v9 on v8

--- a/solution.py
+++ b/solution.py
@@ -57,7 +57,7 @@
     return np.concatenate(split(np.concatenate([cos, -sin]).T * (2.0 / hist)), axis=1)
 
 
-def call(kernel, name, out_shape, *args, scalars=1, far=(), scratch=(), limit=16):
+def call(kernel, name, out_shape, *args, scalars=1, far=(), scratch=(), limit=16, alias=None):
     vmem = pl.BlockSpec(memory_space=pltpu.VMEM)
     smem = pl.BlockSpec(memory_space=pltpu.SMEM)
     hbm = pl.BlockSpec(memory_space=pltpu.HBM)
@@ -71,6 +71,7 @@
         in_specs=places,
         out_specs=[vmem] * len(out_shape),
         out_shape=out_shape,
+        input_output_aliases=alias or {},
         scratch_shapes=list(scratch),
         compiler_params=pltpu.CompilerParams(vmem_limit_bytes=limit * 1024 * 1024),
         name=name,
@@ -224,7 +225,7 @@
         out[:, c : c + TILE] = impose(total, *spec, inverse)
 
 
-def respond_kernel(place, own, other, spec, inverse, coef, out):
+def respond_kernel(place, own, other, spec, inverse, coef, before, out):
     hist, width = own.shape
     half = hist // 2
     start = quarter_start(place, 1, 4 * width)
@@ -237,7 +238,7 @@
     out[W + 2 : W + 4, :LANES] = other[hist : hist + 2, :LANES]
 
 
-def fold_kernel(place, own, got, coef, other, before, keep, known, first, second, third):
+def fold_kernel(place, own, got, coef, other, keep, known, first, second, third):
     z = place[0] >> 2
     size = keep.shape[1]
     hist = other.shape[0] - EXTRA
@@ -267,16 +268,20 @@
     return (me & 1) * (modes // 2)
 
 
-def pick_kernel(devices, place, partner, after, pick):
+def pick_kernel(devices, turn, place, partner, after, *refs):
+    pick = refs[-1]
     modes = partner.shape[1]
     mask = mask_of(place, devices, modes)
-    mates = [partner[:, block(c ^ mask, LANES)] ^ mask for c in range(0, modes, LANES)]
-    mates = jnp.concatenate(mates, axis=1)
-    for c in range(0, modes, 256):
-        pick[c : c + 256, :] = hot(lax.broadcasted_iota(I32, (256, modes), 0) + c == mates)
-
-
-def mixers_kernel(place, order, known, third, second, first, after, coef, held):
+
+    @pl.when(place[0] & 1 == turn)
+    def _():
+        mates = [partner[:, block(c ^ mask, LANES)] ^ mask for c in range(0, modes, LANES)]
+        mates = jnp.concatenate(mates, axis=1)
+        for c in range(0, modes, 256):
+            pick[c : c + 256, :] = hot(lax.broadcasted_iota(I32, (256, modes), 0) + c == mates)
+
+
+def mixers_kernel(place, order, known, first, second, third, after, coef, held):
     me = place[0]
     held[...] = jnp.zeros(held.shape, F32)
     for z, rows in enumerate((known, first, second, third)):
@@ -373,23 +378,30 @@
         scratch=[pltpu.SemaphoreType.DMA((6,))],
     )
     inverse = held[-1]
-    away = call(respond_kernel, "respond", [array(W + EXTRA, quarter)], place, own, got, spec, inverse, coef_near)[0]
+    def pair(turn, after, *pick):
+        return call(
+            functools.partial(pick_kernel, devices, turn), "pick", [near(modes, modes)], place, mates, after, *pick,
+            alias={3: 0} if pick else None,
+        )[0]
+
+    pick = pair(0, spec)
+    away = call(
+        respond_kernel, "respond", [array(W + EXTRA, quarter)], place, own, got, spec, inverse, coef_near, pick
+    )[0]
 
     def respond_own():
         return call(
             whole_kernel, "whole", [array(W, quarter, dtype=F32)], place, stack, order, lft, got, shapes, *held
         )[0]
 
-    pair = functools.partial(pick_kernel, devices)
     if devices == 16:
         size = modes // devices
-        pick = call(pair, "pick", [near(modes, modes)], place, mates, away)[0]
         away = swap(away, devices, 2)
         keep, known, *parts = call(
             fold_kernel, "fold", [array(W, size, dtype=F32), array(EXTRA, LANES)] + [array(W + EXTRA, size)] * 3,
-            place, respond_own(), away, coef_near, got, pick,
+            place, respond_own(), away, coef_near, got,
         )
-        parts = [swap(part, devices, 4 * d) for d, part in reversed(list(zip((1, 2, 3), parts)))]
+        parts = [swap(part, devices, 4 * d) for d, part in zip((1, 2, 3), parts)]
         total = call(settle_kernel, "settle", [array(W, size)], keep, *parts, scalars=0)[0]
         spread = [swap(total, devices, 4 * d) for d in (1, 2, 3)]
         resp = join(total, *spread)
@@ -397,9 +409,10 @@
             mixers_kernel, "mixers", [array(8, modes, dtype=F32)],
             place, order, known, *parts, resp, scratch=[pltpu.VMEM((8, modes), F32)],
         )[0]
-        mine = join(resp, swap(resp, devices, 2), after=mode_coef)
+        pick = pair(1, mode_coef, pick)
+        mine = join(resp, swap(resp, devices, 2), after=pick)
     else:
-        pick = call(pair, "pick", [near(modes, modes)], place, mates, mates)[0]
+        pick = pair(1, mates, pick)
         mode_coef = call(
             functools.partial(plain_mixers_kernel, devices), "mixers", [array(8, modes, dtype=F32)],
             place, order, lax.all_gather(coef, "frdm", axis=1, tiled=True), scratch=[pltpu.VMEM((8, modes), F32)],

time: 56 us -> 54.2 us (0.968)
  waiting for transfers between devices: 15 us -> 13 us
    ppermute x10, waiting for transfers between devices: 15 us -> 13 us  [swap(): return lax.ppermute(x, 'frdm', [(i, i ^ bits) for i in range(devices)])]
    pallas_call x12 -> x13, Pallas kernels: 27 us -> 27.1 us  [call(): pl.pallas_call(kernel, in_specs=places, out_specs=[vmem] * len(out_shape)...]
  transfers between devices with their start and end apart: 10 -> 10, of which waited for: 7 -> 8; matrix products, arithmetic and copies ran while one was open for 0% -> 0% of each run, Pallas kernels for 27% -> 29%
where the time goes in v9:
time: 54.2 us; the launch traced here: 54 us
  Pallas kernels  27.1 us (50%)
  starting transfers between devices  13.8 us (25%)
  waiting for transfers between devices  13 us (24%)
    pallas_call x13, Pallas kernels, call(): pl.pallas_call(kernel, in_specs=places, out_specs=[vmem] * len(out_shape)...  27.1 us
    ppermute x10, starting transfers between devices, swap(): return lax.ppermute(x, 'frdm', [(i, i ^ bits) for i in range(devices)])  13.8 us
    ppermute x10, waiting for transfers between devices, swap(): return lax.ppermute(x, 'frdm', [(i, i ^ bits) for i in range(devices)])  13 us
  transfers between devices with their start and end apart: 10, of which 8 were waited for; matrix products, arithmetic and copies ran while one was open for 0% of the time, Pallas kernels for 29%

profile of v9, /device:TPU:0, one launch (start us, length us, event | category | flops | bytes accessed | tf_op | source)
XLA Modules:
  0.0 54.0 jit_solution(8783119182601609713)
XLA Ops:
  0.0 0.0 copy-start
  0.0 6.6 %project.1 = (bf16[912,1024]{1,0:T(8,128)(2,1)S(1)}, bf16[896,1024]{1,0:T(8,128)(2,1)S(1)}, bf16[1024,1024]{1,0:T(8,128)(2,1)S(1)}, bf16[528,2048]{1,0:T(8,128)(2,1)S(1)}, bf16[2,128]{1,0:T(2,128)(2,1)S(1)}) custom-call(s32[1]{0:T(128)} %bitcast.place, bf16[1024,896]{1,0:T(8,128)(2,1)} %loads_far.1, bf16[896,896]{1,0:T(8,128)(2,1)} %constant.14.clone.forward_far, ...), custom_call_target="tpu_custom_call" | custom-call | tf_op jit(solution)/shard_map/project/pallas_call | solution.py:69
  6.6 0.5 collective-permute-start
  7.2 0.0 copy-done
  7.2 0.0 copy-start.1
  7.2 5.2 %spectrum.1 = (f32[896,512]{1,0:T(8,128)S(1)}, f32[896,512]{1,0:T(8,128)S(1)}, bf16[1024,1024]{1,0:T(8,128)(2,1)S(1)}, bf16[896,1024]{1,0:T(8,128)(2,1)S(1)}, bf...) custom-call(s32[1]{0:T(128)} %bitcast.place, ...), custom_call_target="tpu_custom_call" | custom-call | tf_op jit(solution)/shard_map/spectrum/pallas_call | solution.py:69
  12.4 0.0 copy-done.1
  12.4 1.6 %pick.2.before.refs_0_ = bf16[2048,2048]{1,0:T(8,128)(2,1)S(1)} custom-call(s32[1]{0:T(128)} %bitcast.place, s32[1,2048]{1,0:T(1,128)S(1)} %bitcast.8, f32[896,512]{1,0:T(8,128)S(1)} %get-tuple-element.31.after.spec), custom_call_target="tpu_custom_call" | custom-call | tf_op jit(solution)/shard_map/pick/pallas_call | solution.py:69
  14.0 0.0 collective-permute-done.other
  14.0 1.3 %respond.1 = bf16[272,512]{1,0:T(8,128)(2,1)S(1)} custom-call(s32[1]{0:T(128)} %bitcast.place, f32[896,512]{1,0:T(8,128)S(1)} %get-tuple-element.30.own, bf16[912,1024]{1,0:T(8,128)(2,1)S(1)} %collective-permute-done.other, f32[896,512]{1,0:T(8,128)S(1)} %get-tuple-element.31.after.spec, bf16[256,1792]{1,0:T(8,128)(2,1)S(1)} %get-tuple-element.29.inverse, ...), custom_call_target="tpu_custom_call" | custom-call | tf_op jit(solution)/shard_map/respond/pallas_call | solution.py:69
  15.3 2.7 %collective-permute-start.1 = (bf16[272,512]{1,0:T(8,128)(2,1)S(1)}, bf16[272,512]{1,0:T(8,128)(2,1)S(1)}, u32[]{:S(2)}, u32[]{:S(2)}) collective-permute-start(bf16[272,512]{1,0:T(8,128)(2,1)S(1)} %respond.1), channel_id=1, source_target_pairs={{0,2},{1,3},{2,0},{3,1},{4,6},{5,7},{6,4},{7,5},{8,10},{9,11},{10,... | collective-permute-start | bytes 835592 | tf_op jit(solution)/shard_map/ppermute | solution.py:348
  18.0 5.1 %whole.1.own = f32[256,512]{1,0:T(8,128)S(1)} custom-call(s32[1]{0:T(128)} %bitcast.place, bf16[528,2048]{1,0:T(8,128)(2,1)S(1)} %get-tuple-element.22.stack, s32[1,2048]{1,0:T(1,128)S(1)} %bitcast.6, bf16[896,1024]{1,0:T(8,128)(2,1)S(1)} %get-tuple-element.23.lft, bf16[912,1024]{1,0:T(8,128)(2,1)S(1)} %collective-permute-done.other, ...), custom_call_target="tpu_custom_call" | custom-call | tf_op jit(solution)/shard_map/whole/pallas_call | solution.py:69
  23.1 0.8 %collective-permute-done.1.got = bf16[272,512]{1,0:T(8,128)(2,1)S(1)} collective-permute-done((bf16[272,512]{1,0:T(8,128)(2,1)S(1)}, bf16[272,512]{1,0:T(8,128)(2,1)S(1)}, u32[]{:S(2)}, u32[]{:S(2)}) %collective-permute-start.1) | collective-permute-done | bytes 278560 | tf_op jit(solution)/shard_map/ppermute | solution.py:348
  23.9 0.1 fold.1
  24.0 1.8 %collective-permute-start.2 = (bf16[272,128]{1,0:T(8,128)(2,1)S(1)}, bf16[272,128]{1,0:T(8,128)(2,1)S(1)}, u32[]{:S(2)}, u32[]{:S(2)}) collective-permute-start(bf16[272,128]{1,0:T(8,128)(2,1)S(1)} %get-tuple-element.34), channel_id=1, source_target_pairs={{0,4},{1,5},{2,6},{3,7},{4,0},{5,1},{6,2},{7,3},{8,12},{9,13},{10,... | collective-permute-start | bytes 208904 | tf_op jit(solution)/shard_map/ppermute | solution.py:348
  25.8 2.6 %collective-permute-start.3 = (bf16[272,128]{1,0:T(8,128)(2,1)S(1)}, bf16[272,128]{1,0:T(8,128)(2,1)S(1)}, u32[]{:S(2)}, u32[]{:S(2)}) collective-permute-start(bf16[272,128]{1,0:T(8,128)(2,1)S(1)} %get-tuple-element.35), channel_id=1, source_target_pairs={{0,8},{1,9},{2,10},{3,11},{4,12},{5,13},{6,14},{7,15},{8,0},{9,1},... | collective-permute-start | bytes 208904 | tf_op jit(solution)/shard_map/ppermute | solution.py:348
  28.4 0.1 collective-permute-start.4
  28.5 0.1 collective-permute-done.2.first
  28.6 4.1 %collective-permute-done.3.second = bf16[272,128]{1,0:T(8,128)(2,1)S(1)} collective-permute-done((bf16[272,128]{1,0:T(8,128)(2,1)S(1)}, bf16[272,128]{1,0:T(8,128)(2,1)S(1)}, u32[]{:S(2)}, u32[]{:S(2)}) %collective-permute-start.3) | collective-permute-done | bytes 69664 | tf_op jit(solution)/shard_map/ppermute | solution.py:348
  32.7 1.9 %collective-permute-done.4.third = bf16[272,128]{1,0:T(8,128)(2,1)S(1)} collective-permute-done((bf16[272,128]{1,0:T(8,128)(2,1)S(1)}, bf16[272,128]{1,0:T(8,128)(2,1)S(1)}, u32[]{:S(2)}, u32[]{:S(2)}) %collective-permute-start.4) | collective-permute-done | bytes 69664 | tf_op jit(solution)/shard_map/ppermute | solution.py:348
  34.7 0.8 %collective-permute-start.7 = (bf16[256,128]{1,0:T(8,128)(2,1)S(1)}, bf16[256,128]{1,0:T(8,128)(2,1)S(1)}, u32[]{:S(2)}, u32[]{:S(2)}) collective-permute-start(bf16[256,128]{1,0:T(8,128)(2,1)S(1)} %settle.1.refs_0_), channel_id=1, source_target_pairs={{0,12},{1,13},{2,14},{3,15},{4,8},{5,9},{6,10},{7,11},{8,4},{9,5},... | collective-permute-start | bytes 196616 | tf_op jit(solution)/shard_map/ppermute | solution.py:348
  35.5 1.4 %collective-permute-start.6 = (bf16[256,128]{1,0:T(8,128)(2,1)S(1)}, bf16[256,128]{1,0:T(8,128)(2,1)S(1)}, u32[]{:S(2)}, u32[]{:S(2)}) collective-permute-start(bf16[256,128]{1,0:T(8,128)(2,1)S(1)} %settle.1.refs_0_), channel_id=1, source_target_pairs={{0,8},{1,9},{2,10},{3,11},{4,12},{5,13},{6,14},{7,15},{8,0},{9,1},... | collective-permute-start | bytes 196616 | tf_op jit(solution)/shard_map/ppermute | solution.py:348
  36.8 2.3 %collective-permute-start.5 = (bf16[256,128]{1,0:T(8,128)(2,1)S(1)}, bf16[256,128]{1,0:T(8,128)(2,1)S(1)}, u32[]{:S(2)}, u32[]{:S(2)}) collective-permute-start(bf16[256,128]{1,0:T(8,128)(2,1)S(1)} %settle.1.refs_0_), channel_id=1, source_target_pairs={{0,4},{1,5},{2,6},{3,7},{4,0},{5,1},{6,2},{7,3},{8,12},{9,13},{10,... | collective-permute-start | bytes 196616 | tf_op jit(solution)/shard_map/ppermute | solution.py:348
  39.1 1.8 %collective-permute-done.7.refs_3_ = bf16[256,128]{1,0:T(8,128)(2,1)S(1)} collective-permute-done((bf16[256,128]{1,0:T(8,128)(2,1)S(1)}, bf16[256,128]{1,0:T(8,128)(2,1)S(1)}, u32[]{:S(2)}, u32[]{:S(2)}) %collective-permute-start.7) | collective-permute-done | bytes 65568 | tf_op jit(solution)/shard_map/ppermute | solution.py:348
  40.9 1.1 %collective-permute-done.6.refs_2_ = bf16[256,128]{1,0:T(8,128)(2,1)S(1)} collective-permute-done((bf16[256,128]{1,0:T(8,128)(2,1)S(1)}, bf16[256,128]{1,0:T(8,128)(2,1)S(1)}, u32[]{:S(2)}, u32[]{:S(2)}) %collective-permute-start.6) | collective-permute-done | bytes 65568 | tf_op jit(solution)/shard_map/ppermute | solution.py:348
  42.0 0.0 collective-permute-done.5.refs_1_
  42.1 1.7 %collective-permute-start.8 = (bf16[256,512]{1,0:T(8,128)(2,1)S(1)}, bf16[256,512]{1,0:T(8,128)(2,1)S(1)}, u32[]{:S(2)}, u32[]{:S(2)}) collective-permute-start(bf16[256,512]{1,0:T(8,128)(2,1)S(1)} %join.2.after.refs_0_), channel_id=1, source_target_pairs={{0,2},{1,3},{2,0},{3,1},{4,6},{5,7},{6,4},{7,5},{8,10},{9,11},{10,... | collective-permute-start | bytes 786440 | tf_op jit(solution)/shard_map/ppermute | solution.py:348
  43.8 2.3 %mixers.1.after.coef = f32[8,2048]{1,0:T(8,128)S(1)} custom-call(s32[1]{0:T(128)} %bitcast.place, s32[1,2048]{1,0:T(1,128)S(1)} %bitcast.7, bf16[16,128]{1,0:T(8,128)(2,1)S(1)} %get-tuple-element.33.known, bf16[272,128]{1,0:T(8,128)(2,1)S(1)} %collective-permute-done.2.first, bf16[272,128]{1,0:T(8,128)(2,1)S(1)} %collective-permute-done.3.second, ...), custom_call_target="tpu_custom_call" | custom-call | tf_op jit(solution)/shard_map/mixers/pallas_call | solution.py:69
  46.0 2.5 %collective-permute-done.8.refs_1_ = bf16[256,512]{1,0:T(8,128)(2,1)S(1)} collective-permute-done((bf16[256,512]{1,0:T(8,128)(2,1)S(1)}, bf16[256,512]{1,0:T(8,128)(2,1)S(1)}, u32[]{:S(2)}, u32[]{:S(2)}) %collective-permute-start.8) | collective-permute-done | bytes 262176 | tf_op jit(solution)/shard_map/ppermute | solution.py:348
  48.6 0.1 collective-permute-start.9
  48.7 1.3 %mate.1.mates = f32[256,2048]{1,0:T(8,128)S(1)} custom-call(bf16[256,1024]{1,0:T(8,128)(2,1)S(1)} %join.3.mine, bf16[2048,2048]{1,0:T(8,128)(2,1)S(1)} %pick.3._), custom_call_target="tpu_custom_call" | custom-call | tf_op jit(solution)/shard_map/mate/pallas_call | solution.py:69
  49.9 0.6 %collective-permute-done.9.theirs = bf16[256,1024]{1,0:T(8,128)(2,1)S(1)} collective-permute-done((bf16[256,1024]{1,0:T(8,128)(2,1)S(1)}, bf16[256,1024]{1,0:T(8,128)(2,1)S(1)}, u32[]{:S(2)}, u32[]{:S(2)}) %collective-permute-start.9) | collective-permute-done | bytes 524320 | tf_op jit(solution)/shard_map/ppermute | solution.py:348
  50.6 3.5 %expand.1 = bf16[1024,256]{1,0:T(8,128)(2,1)} custom-call(s32[1]{0:T(128)} %bitcast.place, bf16[256,1024]{1,0:T(8,128)(2,1)S(1)} %join.3.mine, bf16[256,1024]{1,0:T(8,128)(2,1)S(1)} %collective-permute-done.9.theirs, f32[256,2048]{1,0:T(8,128)S(1)} %mate.1.mates, bf16[2048,2048]{1,0:T(8,128)(2,1)S(1)} %pick.3._, f32[8,2048]{1,0:T(8,128)S(1)} %mixers.1.after.coef, ...), custom_call_target="tpu_custom_call" | custom-call | tf_op jit(solution)/shard_map/expand/pallas_call | solution.py:69
  (4 shorter events, 0.1 us)
Async XLA Ops:
  0.0 7.2 %copy-start = (s32[2048]{0:T(1024)S(1)}, s32[2048]{0:T(1024)}, u32[]{:S(2)}) copy-start(s32[2048]{0:T(1024)} %param.14) | copy-start | bytes 24580
  6.6 7.3 %collective-permute-start = (bf16[912,1024]{1,0:T(8,128)(2,1)S(1)}, bf16[912,1024]{1,0:T(8,128)(2,1)S(1)}, u32[]{:S(2)}, u32[]{:S(2)}) collective-permute-start(bf16[912,1024]{1,0:T(8,128)(2,1)S(1)} %get-tuple-element.24), channel_id=1, source_target_pairs={{0,1},{1,0},{2,3},{3,2},{4,5},{5,4},{6,7},{7,6},{8,9},{9,8},{10,11... | collective-permute-start | bytes 5603336 | tf_op jit(solution)/shard_map/ppermute | solution.py:348
  7.2 5.2 %copy-start.1 = (s32[2048]{0:T(1024)S(1)}, s32[2048]{0:T(1024)}, u32[]{:S(2)}) copy-start(s32[2048]{0:T(1024)} %param.15) | copy-start | bytes 24580
  15.3 8.6 %collective-permute-start.1 = (bf16[272,512]{1,0:T(8,128)(2,1)S(1)}, bf16[272,512]{1,0:T(8,128)(2,1)S(1)}, u32[]{:S(2)}, u32[]{:S(2)}) collective-permute-start(bf16[272,512]{1,0:T(8,128)(2,1)S(1)} %respond.1), channel_id=1, source_target_pairs={{0,2},{1,3},{2,0},{3,1},{4,6},{5,7},{6,4},{7,5},{8,10},{9,11},{10,... | collective-permute-start | bytes 835592 | tf_op jit(solution)/shard_map/ppermute | solution.py:348
  24.0 4.6 %collective-permute-start.2 = (bf16[272,128]{1,0:T(8,128)(2,1)S(1)}, bf16[272,128]{1,0:T(8,128)(2,1)S(1)}, u32[]{:S(2)}, u32[]{:S(2)}) collective-permute-start(bf16[272,128]{1,0:T(8,128)(2,1)S(1)} %get-tuple-element.34), channel_id=1, source_target_pairs={{0,4},{1,5},{2,6},{3,7},{4,0},{5,1},{6,2},{7,3},{8,12},{9,13},{10,... | collective-permute-start | bytes 208904 | tf_op jit(solution)/shard_map/ppermute | solution.py:348
  25.8 6.9 %collective-permute-start.3 = (bf16[272,128]{1,0:T(8,128)(2,1)S(1)}, bf16[272,128]{1,0:T(8,128)(2,1)S(1)}, u32[]{:S(2)}, u32[]{:S(2)}) collective-permute-start(bf16[272,128]{1,0:T(8,128)(2,1)S(1)} %get-tuple-element.35), channel_id=1, source_target_pairs={{0,8},{1,9},{2,10},{3,11},{4,12},{5,13},{6,14},{7,15},{8,0},{9,1},... | collective-permute-start | bytes 208904 | tf_op jit(solution)/shard_map/ppermute | solution.py:348
  28.4 6.2 %collective-permute-start.4 = (bf16[272,128]{1,0:T(8,128)(2,1)S(1)}, bf16[272,128]{1,0:T(8,128)(2,1)S(1)}, u32[]{:S(2)}, u32[]{:S(2)}) collective-permute-start(bf16[272,128]{1,0:T(8,128)(2,1)S(1)} %get-tuple-element.36), channel_id=1, source_target_pairs={{0,12},{1,13},{2,14},{3,15},{4,8},{5,9},{6,10},{7,11},{8,4},{9,5},... | collective-permute-start | bytes 208904 | tf_op jit(solution)/shard_map/ppermute | solution.py:348
  34.7 6.3 %collective-permute-start.7 = (bf16[256,128]{1,0:T(8,128)(2,1)S(1)}, bf16[256,128]{1,0:T(8,128)(2,1)S(1)}, u32[]{:S(2)}, u32[]{:S(2)}) collective-permute-start(bf16[256,128]{1,0:T(8,128)(2,1)S(1)} %settle.1.refs_0_), channel_id=1, source_target_pairs={{0,12},{1,13},{2,14},{3,15},{4,8},{5,9},{6,10},{7,11},{8,4},{9,5},... | collective-permute-start | bytes 196616 | tf_op jit(solution)/shard_map/ppermute | solution.py:348
  35.5 6.6 %collective-permute-start.6 = (bf16[256,128]{1,0:T(8,128)(2,1)S(1)}, bf16[256,128]{1,0:T(8,128)(2,1)S(1)}, u32[]{:S(2)}, u32[]{:S(2)}) collective-permute-start(bf16[256,128]{1,0:T(8,128)(2,1)S(1)} %settle.1.refs_0_), channel_id=1, source_target_pairs={{0,8},{1,9},{2,10},{3,11},{4,12},{5,13},{6,14},{7,15},{8,0},{9,1},... | collective-permute-start | bytes 196616 | tf_op jit(solution)/shard_map/ppermute | solution.py:348
  36.8 5.2 %collective-permute-start.5 = (bf16[256,128]{1,0:T(8,128)(2,1)S(1)}, bf16[256,128]{1,0:T(8,128)(2,1)S(1)}, u32[]{:S(2)}, u32[]{:S(2)}) collective-permute-start(bf16[256,128]{1,0:T(8,128)(2,1)S(1)} %settle.1.refs_0_), channel_id=1, source_target_pairs={{0,4},{1,5},{2,6},{3,7},{4,0},{5,1},{6,2},{7,3},{8,12},{9,13},{10,... | collective-permute-start | bytes 196616 | tf_op jit(solution)/shard_map/ppermute | solution.py:348
  42.1 6.4 %collective-permute-start.8 = (bf16[256,512]{1,0:T(8,128)(2,1)S(1)}, bf16[256,512]{1,0:T(8,128)(2,1)S(1)}, u32[]{:S(2)}, u32[]{:S(2)}) collective-permute-start(bf16[256,512]{1,0:T(8,128)(2,1)S(1)} %join.2.after.refs_0_), channel_id=1, source_target_pairs={{0,2},{1,3},{2,0},{3,1},{4,6},{5,7},{6,4},{7,5},{8,10},{9,11},{10,... | collective-permute-start | bytes 786440 | tf_op jit(solution)/shard_map/ppermute | solution.py:348
  48.6 2.0 %collective-permute-start.9 = (bf16[256,1024]{1,0:T(8,128)(2,1)S(1)}, bf16[256,1024]{1,0:T(8,128)(2,1)S(1)}, u32[]{:S(2)}, u32[]{:S(2)}) collective-permute-start(bf16[256,1024]{1,0:T(8,128)(2,1)S(1)} %join.3.mine), channel_id=1, source_target_pairs={{0,1},{1,0},{2,3},{3,2},{4,5},{5,4},{6,7},{7,6},{8,9},{9,8},{10,11... | collective-permute-start | bytes 1572872 | tf_op jit(solution)/shard_map/ppermute | solution.py:348

commit v10 on v8

--- a/solution.py
+++ b/solution.py
@@ -57,7 +57,7 @@
     return np.concatenate(split(np.concatenate([cos, -sin]).T * (2.0 / hist)), axis=1)
 
 
-def call(kernel, name, out_shape, *args, scalars=1, far=(), scratch=(), limit=16):
+def call(kernel, name, out_shape, *args, scalars=1, far=(), scratch=(), limit=16, products=0):
     vmem = pl.BlockSpec(memory_space=pltpu.VMEM)
     smem = pl.BlockSpec(memory_space=pltpu.SMEM)
     hbm = pl.BlockSpec(memory_space=pltpu.HBM)
@@ -72,6 +72,7 @@
         out_specs=[vmem] * len(out_shape),
         out_shape=out_shape,
         scratch_shapes=list(scratch),
+        cost_estimate=pl.CostEstimate(flops=2 * products, bytes_accessed=0, transcendentals=0) if products else None,
         compiler_params=pltpu.CompilerParams(vmem_limit_bytes=limit * 1024 * 1024),
         name=name,
     )(*args)
@@ -101,17 +102,19 @@
     place, loads_far, forward_far, shapes_far, taps_far, offsets_far, coef_far,
     sent, lft, shapes, stack, coef, loads, forward, taps, offsets, sems,
 ):
-    rows, half = loads.shape[0], sent.shape[1]
-    hist = lft.shape[0]
-    start = (1 - (place[0] & 1)) * half
+    rows, half = shapes.shape
+    hist, width = lft.shape[0], sent.shape[1]
+    start, later = quarter_start(place, 1, 2 * half), quarter_start(place, 0, 2 * half)
+    base = (1 - (place[0] & 1)) * half
     step = TILE
     pairs = [(forward_far, forward), (loads_far, loads)]
     first = len(pairs)
     pairs += [
         (coef_far, coef),
         (offsets_far, offsets),
-        (shapes_far.at[:, block(start, half)], shapes),
+        (shapes_far.at[:, block(base + start, width)], shapes.at[:, block(start, width)]),
         (taps_far, taps),
+        (shapes_far.at[:, block(base + later, width)], shapes.at[:, block(later, width)]),
     ]
     copies = fetch(pairs, sems)
     for copy in copies[:first]:
@@ -130,9 +133,9 @@
     for copy in copies[first : first + 3]:
         copy.wait()
     count = taps.shape[0] - 1
-    for c in range(0, half, step):
-        sent[:hist, c : c + step] = dot(lft[...], shapes[:, c : c + step]).astype(BF)
-    sent[hist:, :] = jnp.zeros((EXTRA, half), BF)
+    for c in range(0, width, step):
+        sent[:hist, c : c + step] = dot(lft[...], shapes[:, block(start + c, step)]).astype(BF)
+    sent[hist:, :] = jnp.zeros((EXTRA, width), BF)
     sent[hist : hist + 2, : coef.shape[1]] = coef[...]
     copies[first + 3].wait()
     for r in range(0, count, 64):
@@ -141,6 +144,14 @@
     end = taps[count : count + 1, :]
     tail = jnp.where(index == 0, end, jnp.where(index == 1, offsets[...].astype(F32), 0.0))
     stack[count:, :] = tail.astype(BF)
+    copies[first + 4].wait()
+
+
+def project_rest_kernel(place, lft, shapes, after, sent):
+    width = sent.shape[1]
+    later = quarter_start(place, 0, 4 * width)
+    for c in range(0, width, TILE):
+        sent[:, c : c + TILE] = dot(lft[...], shapes[:, block(later + c, TILE)]).astype(BF)
 
 
 def quarter_start(place, which, modes):
@@ -167,40 +178,48 @@
     return cos * re - sin * im, sin * re + cos * im
 
 
+def spectrum_tiles(base, stack, order, table, last, phase, spec):
+    half = spec.shape[0] // 2
+    for c in range(0, spec.shape[1], TILE):
+        parts = spectrum_of(*gather_taps(base + c, stack, order), table, last, phase)
+        spec[:half, c : c + TILE], spec[half:, c : c + TILE] = parts
+
+
 def spectrum_kernel(
-    place, stack, order, lft, shapes_far, table_far, last_far, phase_far, inverse_far,
-    spec, own, shapes, table, last, phase, inverse, sems,
+    place, stack, order, shapes_far, table_far, last_far, phase_far, inverse_far,
+    spec, shapes, table, last, phase, inverse, sems,
 ):
-    width = spec.shape[1]
-    half = spec.shape[0] // 2
-    modes = shapes_far.shape[1]
-    core = place[0] & 1
-    start, later = quarter_start(place, 1, modes), quarter_start(place, 0, modes)
-    near = core * 2 * width
+    half, modes = shapes.shape[1], shapes_far.shape[1]
+    near = (place[0] & 1) * half
     copies = fetch(
         [
-            (shapes_far.at[:, block(near + start, width)], shapes.at[:, block(start, width)]),
             (table_far, table),
             (last_far, last),
             (phase_far, phase),
+            (shapes_far.at[:, block(near, half)], shapes),
             (inverse_far, inverse),
-            (shapes_far.at[:, block(near + later, width)], shapes.at[:, block(later, width)]),
         ],
         sems,
     )
     for copy in copies:
         copy.start()
+    width = spec.shape[1]
+    start = near + quarter_start(place, 1, modes)
     tiles = range(0, width, TILE)
-    picked = [gather_taps(near + start + c, stack, order) for c in tiles]
-    copies[0].wait()
-    for c in tiles:
-        own[:, c : c + TILE] = dot(lft[...], shapes[:, block(start + c, TILE)])
-    for copy in copies[1:4]:
+    picked = [gather_taps(start + c, stack, order) for c in tiles]
+    for copy in copies[:3]:
         copy.wait()
+    top = spec.shape[0] // 2
     for c, parts in zip(tiles, picked):
-        spec[:half, c : c + TILE], spec[half:, c : c + TILE] = spectrum_of(*parts, table, last, phase)
-    for copy in copies[4:]:
+        spec[:top, c : c + TILE], spec[top:, c : c + TILE] = spectrum_of(*parts, table, last, phase)
+    for copy in copies[3:]:
         copy.wait()
+
+
+def spectrum_rest_kernel(place, stack, order, table, last, phase, after, spec):
+    modes = order.shape[1]
+    start = (place[0] & 1) * (modes // 2) + quarter_start(place, 0, modes)
+    spectrum_tiles(start, stack, order, table, last, phase, spec)
 
 
 def impose(total, tre, tim, inverse):
@@ -213,31 +232,21 @@
     return both + dot(inverse[:, : 2 * half], low)
 
 
-def whole_kernel(place, stack, order, lft, other, shapes, table, last, phase, inverse, out):
-    hist, modes = lft.shape[0], order.shape[1]
-    start = quarter_start(place, 0, modes)
-    near = (place[0] & 1) * (modes // 2) + start
-    for c in range(0, out.shape[1], TILE):
-        spec = spectrum_of(*gather_taps(near + c, stack, order), table, last, phase)
-        here = block(start + c, TILE)
-        total = dot(lft[...], shapes[:, here]) + other[:hist, here].astype(F32)
-        out[:, c : c + TILE] = impose(total, *spec, inverse)
-
-
-def respond_kernel(place, own, other, spec, inverse, coef, out):
-    hist, width = own.shape
+def respond_kernel(which, place, lft, shapes, other, spec, inverse, coef, out):
+    hist, width = spec.shape
     half = hist // 2
-    start = quarter_start(place, 1, 4 * width)
+    start = quarter_start(place, which, 4 * width)
     for c in range(0, width, TILE):
-        total = own[:, c : c + TILE] + other[:hist, block(start + c, TILE)].astype(F32)
+        total = dot(lft[...], shapes[:, block(start + c, TILE)]) + other[:hist, c : c + TILE].astype(F32)
         result = impose(total, spec[:half, c : c + TILE], spec[half:, c : c + TILE], inverse)
-        out[:W, c : c + TILE] = result.astype(BF)
-    out[W:, :] = jnp.zeros((EXTRA, width), BF)
-    out[W : W + 2, : coef.shape[1]] = coef[...]
-    out[W + 2 : W + 4, :LANES] = other[hist : hist + 2, :LANES]
-
-
-def fold_kernel(place, own, got, coef, other, before, keep, known, first, second, third):
+        out[:W, c : c + TILE] = result.astype(out.dtype)
+    if out.shape[0] > W:
+        out[W:, :] = jnp.zeros((EXTRA, width), BF)
+        out[W : W + 2, : coef.shape[1]] = coef[...]
+        out[W + 2 : W + 4, :LANES] = other[hist : hist + 2, :LANES]
+
+
+def fold_kernel(place, own, got, coef, other, keep, known, first, second, third):
     z = place[0] >> 2
     size = keep.shape[1]
     hist = other.shape[0] - EXTRA
@@ -276,7 +285,7 @@
         pick[c : c + 256, :] = hot(lax.broadcasted_iota(I32, (256, modes), 0) + c == mates)
 
 
-def mixers_kernel(place, order, known, third, second, first, after, coef, held):
+def mixers_kernel(place, order, known, first, second, third, after, coef, held):
     me = place[0]
     held[...] = jnp.zeros(held.shape, F32)
     for z, rows in enumerate((known, first, second, third)):
@@ -356,40 +365,47 @@
 
     sent, lft, far, stack, coef_near = call(
         project_kernel, "project",
-        [near(hist + EXTRA, half), near(hist, rows), near(rows, half), near(count - 1 + EXTRA, modes), near(*coef.shape)],
+        [near(hist + EXTRA, quarter), near(hist, rows), near(rows, half), near(count - 1 + EXTRA, modes), near(*coef.shape)],
         place, loads, forward, shapes, taps, offsets, coef, far=range(1, 7),
         scratch=[
             pltpu.VMEM(loads.shape, BF), pltpu.VMEM(forward.shape, BF), pltpu.VMEM(taps.shape, F32),
-            pltpu.VMEM(offsets.shape, I32), pltpu.SemaphoreType.DMA((6,)),
+            pltpu.VMEM(offsets.shape, I32), pltpu.SemaphoreType.DMA((7,)),
         ],
         limit=24,
     )
     got = swap(sent, devices, 1)
-    spec, own, shapes, *held = call(
+    spec, shapes, *held = call(
         spectrum_kernel, "spectrum",
-        [near(hist, quarter, dtype=F32)] * 2 + [near(rows, half)]
-        + [near(*t.shape) for t in (tap_forward, last, phase, inverse)],
-        place, stack, order, lft, shapes, tap_forward, last, phase, inverse, far=range(4, 9),
-        scratch=[pltpu.SemaphoreType.DMA((6,))],
+        [near(hist, quarter, dtype=F32), near(rows, half)] + [near(*t.shape) for t in (tap_forward, last, phase, inverse)],
+        place, stack, order, shapes, tap_forward, last, phase, inverse, far=range(3, 8),
+        scratch=[pltpu.SemaphoreType.DMA((5,))],
     )
-    inverse = held[-1]
-    away = call(respond_kernel, "respond", [array(W + EXTRA, quarter)], place, own, got, spec, inverse, coef_near)[0]
-
-    def respond_own():
-        return call(
-            whole_kernel, "whole", [array(W, quarter, dtype=F32)], place, stack, order, lft, got, shapes, *held
-        )[0]
-
-    pair = functools.partial(pick_kernel, devices)
+    inverse = held.pop()
+
+    def respond(which, got, spec, out):
+        kernel = functools.partial(respond_kernel, which)
+        return call(kernel, "respond", [out], place, lft, shapes, got, spec, inverse, coef_near)[0]
+
+    away = respond(1, got, spec, array(W + EXTRA, quarter))
+    sent = call(project_rest_kernel, "project_rest", [array(hist, quarter)], place, lft, far, away, products=4 * hist * rows * quarter)[0]
+    rest = swap(sent, devices, 1)
+    spec = call(
+        spectrum_rest_kernel, "spectrum_rest", [array(hist, quarter, dtype=F32)], place, stack, order, *held, sent
+    )[0]
+    own = respond(0, rest, spec, array(W, quarter, dtype=F32))
+
+    def pair(after):
+        kernel = functools.partial(pick_kernel, devices)
+        return call(kernel, "pick", [near(modes, modes)], place, mates, after)[0]
+
     if devices == 16:
         size = modes // devices
-        pick = call(pair, "pick", [near(modes, modes)], place, mates, away)[0]
         away = swap(away, devices, 2)
         keep, known, *parts = call(
             fold_kernel, "fold", [array(W, size, dtype=F32), array(EXTRA, LANES)] + [array(W + EXTRA, size)] * 3,
-            place, respond_own(), away, coef_near, got, pick,
+            place, own, away, coef_near, got,
         )
-        parts = [swap(part, devices, 4 * d) for d, part in reversed(list(zip((1, 2, 3), parts)))]
+        parts = [swap(part, devices, 4 * d) for d, part in zip((1, 2, 3), parts)]
         total = call(settle_kernel, "settle", [array(W, size)], keep, *parts, scalars=0)[0]
         spread = [swap(total, devices, 4 * d) for d in (1, 2, 3)]
         resp = join(total, *spread)
@@ -397,15 +413,16 @@
             mixers_kernel, "mixers", [array(8, modes, dtype=F32)],
             place, order, known, *parts, resp, scratch=[pltpu.VMEM((8, modes), F32)],
         )[0]
-        mine = join(resp, swap(resp, devices, 2), after=mode_coef)
+        pick = pair(mode_coef)
+        mine = join(resp, swap(resp, devices, 2), after=pick)
     else:
-        pick = call(pair, "pick", [near(modes, modes)], place, mates, mates)[0]
+        pick = pair(mates)
         mode_coef = call(
             functools.partial(plain_mixers_kernel, devices), "mixers", [array(8, modes, dtype=F32)],
             place, order, lax.all_gather(coef, "frdm", axis=1, tiled=True), scratch=[pltpu.VMEM((8, modes), F32)],
         )[0]
-        away, resp = away[:W].astype(F32), respond_own()
-        resp = jnp.where(place[0] & 2, jnp.concatenate([away, resp], axis=1), jnp.concatenate([resp, away], axis=1))
+        away = away[:W].astype(F32)
+        resp = jnp.where(place[0] & 2, jnp.concatenate([away, own], axis=1), jnp.concatenate([own, away], axis=1))
         groups = [list(range(c, devices, 2)) for c in range(2)]
         mine = lax.psum(resp, "frdm", axis_index_groups=groups).astype(BF)
     theirs = swap(mine, devices, 1)

time: 56 us -> 53.4 us (0.954)
  waiting for transfers between devices: 15 us -> 12.5 us
    ppermute x10 -> x11, waiting for transfers between devices: 15 us -> 12.5 us  [swap(): return lax.ppermute(x, 'frdm', [(i, i ^ bits) for i in range(devices)])]
    pallas_call x12 -> x14, Pallas kernels: 27 us -> 26.5 us  [call(): pl.pallas_call(kernel, in_specs=places, out_specs=[vmem] * len(out_shape)...]
    ppermute x10 -> x11, starting transfers between devices: 13.8 us -> 14.2 us  [swap(): return lax.ppermute(x, 'frdm', [(i, i ^ bits) for i in range(devices)])]
  transfers between devices with their start and end apart: 10 -> 11, of which waited for: 7 -> 7; matrix products, arithmetic and copies ran while one was open for 0% -> 0% of each run, Pallas kernels for 27% -> 25%
where the time goes in v10:
time: 53.4 us; the launch traced here: 53.3 us
  Pallas kernels  26.5 us (50%)
  starting transfers between devices  14.2 us (27%)
  waiting for transfers between devices  12.5 us (23%)
    pallas_call x14, Pallas kernels, call(): pl.pallas_call(kernel, in_specs=places, out_specs=[vmem] * len(out_shape)...  26.5 us
    ppermute x11, starting transfers between devices, swap(): return lax.ppermute(x, 'frdm', [(i, i ^ bits) for i in range(devices)])  14.2 us
    ppermute x11, waiting for transfers between devices, swap(): return lax.ppermute(x, 'frdm', [(i, i ^ bits) for i in range(devices)])  12.5 us
  transfers between devices with their start and end apart: 11, of which 7 were waited for; matrix products, arithmetic and copies ran while one was open for 0% of the time, Pallas kernels for 25%

profile of v10, /device:TPU:0, one launch (start us, length us, event | category | flops | bytes accessed | tf_op | source)
XLA Modules:
  0.0 53.3 jit_solution(8190612151156232282)
XLA Ops:
  0.0 0.0 copy-start
  0.0 5.7 %project.1 = (bf16[912,512]{1,0:T(8,128)(2,1)S(1)}, bf16[896,1024]{1,0:T(8,128)(2,1)S(1)}, bf16[1024,1024]{1,0:T(8,128)(2,1)S(1)}, bf16[528,2048]{1,0:T(8,128)(2,1)S(1)}, bf16[2,128]{1,0:T(2,128)(2,1)S(1)}) custom-call(s32[1]{0:T(128)} %bitcast.place, bf16[1024,896]{1,0:T(8,128)(2,1)} %loads_far.1, bf16[896,896]{1,0:T(8,128)(2,1)} %constant.14.clone.forward_far, ...), custom_call_target="tpu_custom_call" | custom-call | tf_op jit(solution)/shard_map/project/pallas_call | solution.py:69
  5.7 0.5 collective-permute-start
  6.2 0.0 copy-done
  6.2 3.3 %spectrum.1 = (f32[896,512]{1,0:T(8,128)S(1)}, bf16[1024,1024]{1,0:T(8,128)(2,1)S(1)}, bf16[896,1024]{1,0:T(8,128)(2,1)S(1)}, bf16[896,128]{1,0:T(8,128)(2,1)S(1...) custom-call(s32[1]{0:T(128)} %bitcast.place, bf16[528,2048]{1,0:T(8,128)(2,1)S(1)} %get-tuple-element.22.stack, ...), custom_call_target="tpu_custom_call" | custom-call | tf_op jit(solution)/shard_map/spectrum/pallas_call | solution.py:69
  9.5 0.0 collective-permute-done.other
  9.5 2.4 %respond.2.after = bf16[272,512]{1,0:T(8,128)(2,1)S(1)} custom-call(s32[1]{0:T(128)} %bitcast.place, bf16[896,1024]{1,0:T(8,128)(2,1)S(1)} %get-tuple-element.21.lft, bf16[1024,1024]{1,0:T(8,128)(2,1)S(1)} %get-tuple-element.23.shapes.near, bf16[912,512]{1,0:T(8,128)(2,1)S(1)} %collective-permute-done.other, f32[896,512]{1,0:T(8,128)S(1)} %get-tuple-element.26.spec, ...), custom_call_target="tpu_custom_call" | custom-call | tf_op jit(solution)/shard_map/respond/pallas_call | solution.py:69
  11.9 1.1 %project_rest.1.after = bf16[896,512]{1,0:T(8,128)(2,1)S(1)} custom-call(s32[1]{0:T(128)} %bitcast.place, bf16[896,1024]{1,0:T(8,128)(2,1)S(1)} %get-tuple-element.21.lft, bf16[1024,1024]{1,0:T(8,128)(2,1)S(1)} %get-tuple-element.24.shapes.far, bf16[272,512]{1,0:T(8,128)(2,1)S(1)} %respond.2.after), custom_call_target="tpu_custom_call" | custom-call | flops 3758096384 | tf_op jit(solution)/shard_map/project_rest/pallas_call | solution.py:69
  13.0 0.1 collective-permute-start.1
  13.1 3.0 %collective-permute-start.2 = (bf16[272,512]{1,0:T(8,128)(2,1)S(1)}, bf16[272,512]{1,0:T(8,128)(2,1)S(1)}, u32[]{:S(2)}, u32[]{:S(2)}) collective-permute-start(bf16[272,512]{1,0:T(8,128)(2,1)S(1)} %respond.2.after), channel_id=1, source_target_pairs={{0,2},{1,3},{2,0},{3,1},{4,6},{5,7},{6,4},{7,5},{8,10},{9,11},{10,... | collective-permute-start | bytes 835592 | tf_op jit(solution)/shard_map/ppermute | solution.py:352
  16.1 2.9 %spectrum_rest.1.spec = f32[896,512]{1,0:T(8,128)S(1)} custom-call(s32[1]{0:T(128)} %bitcast.place, bf16[528,2048]{1,0:T(8,128)(2,1)S(1)} %get-tuple-element.22.stack, s32[1,2048]{1,0:T(1,128)S(1)} %bitcast.6, bf16[896,1024]{1,0:T(8,128)(2,1)S(1)} %get-tuple-element.29.table, bf16[896,128]{1,0:T(8,128)(2,1)S(1)} %get-tuple-element.30.last, ...), custom_call_target="tpu_custom_call" | custom-call | tf_op jit(solution)/shard_map/spectrum_rest/pallas_call | solution.py:69
  19.0 0.0 collective-permute-done.1.other
  19.0 2.3 %respond.3.own = f32[256,512]{1,0:T(8,128)S(1)} custom-call(s32[1]{0:T(128)} %bitcast.place, bf16[896,1024]{1,0:T(8,128)(2,1)S(1)} %get-tuple-element.21.lft, bf16[1024,1024]{1,0:T(8,128)(2,1)S(1)} %get-tuple-element.23.shapes.near, bf16[896,512]{1,0:T(8,128)(2,1)S(1)} %collective-permute-done.1.other, f32[896,512]{1,0:T(8,128)S(1)} %spectrum_rest.1.spec, ...), custom_call_target="tpu_custom_call" | custom-call | tf_op jit(solution)/shard_map/respond/pallas_call | solution.py:69
  21.3 0.0 copy-start.1
  21.4 1.6 %collective-permute-done.2.got = bf16[272,512]{1,0:T(8,128)(2,1)S(1)} collective-permute-done((bf16[272,512]{1,0:T(8,128)(2,1)S(1)}, bf16[272,512]{1,0:T(8,128)(2,1)S(1)}, u32[]{:S(2)}, u32[]{:S(2)}) %collective-permute-start.2) | collective-permute-done | bytes 278560 | tf_op jit(solution)/shard_map/ppermute | solution.py:352
  23.0 0.1 fold.1
  23.1 1.9 %collective-permute-start.3 = (bf16[272,128]{1,0:T(8,128)(2,1)S(1)}, bf16[272,128]{1,0:T(8,128)(2,1)S(1)}, u32[]{:S(2)}, u32[]{:S(2)}) collective-permute-start(bf16[272,128]{1,0:T(8,128)(2,1)S(1)} %get-tuple-element.33), channel_id=1, source_target_pairs={{0,4},{1,5},{2,6},{3,7},{4,0},{5,1},{6,2},{7,3},{8,12},{9,13},{10,... | collective-permute-start | bytes 208904 | tf_op jit(solution)/shard_map/ppermute | solution.py:352
  25.0 2.6 %collective-permute-start.4 = (bf16[272,128]{1,0:T(8,128)(2,1)S(1)}, bf16[272,128]{1,0:T(8,128)(2,1)S(1)}, u32[]{:S(2)}, u32[]{:S(2)}) collective-permute-start(bf16[272,128]{1,0:T(8,128)(2,1)S(1)} %get-tuple-element.34), channel_id=1, source_target_pairs={{0,8},{1,9},{2,10},{3,11},{4,12},{5,13},{6,14},{7,15},{8,0},{9,1},... | collective-permute-start | bytes 208904 | tf_op jit(solution)/shard_map/ppermute | solution.py:352
  27.6 0.0 collective-permute-start.5
  27.6 0.0 collective-permute-done.3.first
  27.6 4.3 %collective-permute-done.4.second = bf16[272,128]{1,0:T(8,128)(2,1)S(1)} collective-permute-done((bf16[272,128]{1,0:T(8,128)(2,1)S(1)}, bf16[272,128]{1,0:T(8,128)(2,1)S(1)}, u32[]{:S(2)}, u32[]{:S(2)}) %collective-permute-start.4) | collective-permute-done | bytes 69664 | tf_op jit(solution)/shard_map/ppermute | solution.py:352
  31.9 1.8 %collective-permute-done.5.third = bf16[272,128]{1,0:T(8,128)(2,1)S(1)} collective-permute-done((bf16[272,128]{1,0:T(8,128)(2,1)S(1)}, bf16[272,128]{1,0:T(8,128)(2,1)S(1)}, u32[]{:S(2)}, u32[]{:S(2)}) %collective-permute-start.5) | collective-permute-done | bytes 69664 | tf_op jit(solution)/shard_map/ppermute | solution.py:352
  33.7 1.5 %collective-permute-start.8 = (bf16[256,128]{1,0:T(8,128)(2,1)S(1)}, bf16[256,128]{1,0:T(8,128)(2,1)S(1)}, u32[]{:S(2)}, u32[]{:S(2)}) collective-permute-start(bf16[256,128]{1,0:T(8,128)(2,1)S(1)} %settle.1.refs_0_), channel_id=1, source_target_pairs={{0,12},{1,13},{2,14},{3,15},{4,8},{5,9},{6,10},{7,11},{8,4},{9,5},... | collective-permute-start | bytes 196616 | tf_op jit(solution)/shard_map/ppermute | solution.py:352
  35.2 0.0 collective-permute-start.7
  35.3 2.9 %collective-permute-start.6 = (bf16[256,128]{1,0:T(8,128)(2,1)S(1)}, bf16[256,128]{1,0:T(8,128)(2,1)S(1)}, u32[]{:S(2)}, u32[]{:S(2)}) collective-permute-start(bf16[256,128]{1,0:T(8,128)(2,1)S(1)} %settle.1.refs_0_), channel_id=1, source_target_pairs={{0,4},{1,5},{2,6},{3,7},{4,0},{5,1},{6,2},{7,3},{8,12},{9,13},{10,... | collective-permute-start | bytes 196616 | tf_op jit(solution)/shard_map/ppermute | solution.py:352
  38.2 1.7 %collective-permute-done.8.refs_3_ = bf16[256,128]{1,0:T(8,128)(2,1)S(1)} collective-permute-done((bf16[256,128]{1,0:T(8,128)(2,1)S(1)}, bf16[256,128]{1,0:T(8,128)(2,1)S(1)}, u32[]{:S(2)}, u32[]{:S(2)}) %collective-permute-start.8) | collective-permute-done | bytes 65568 | tf_op jit(solution)/shard_map/ppermute | solution.py:352
  39.9 1.4 %collective-permute-done.7.refs_2_ = bf16[256,128]{1,0:T(8,128)(2,1)S(1)} collective-permute-done((bf16[256,128]{1,0:T(8,128)(2,1)S(1)}, bf16[256,128]{1,0:T(8,128)(2,1)S(1)}, u32[]{:S(2)}, u32[]{:S(2)}) %collective-permute-start.7) | collective-permute-done | bytes 65568 | tf_op jit(solution)/shard_map/ppermute | solution.py:352
  41.3 0.0 collective-permute-done.6.refs_1_
  41.3 1.6 %collective-permute-start.9 = (bf16[256,512]{1,0:T(8,128)(2,1)S(1)}, bf16[256,512]{1,0:T(8,128)(2,1)S(1)}, u32[]{:S(2)}, u32[]{:S(2)}) collective-permute-start(bf16[256,512]{1,0:T(8,128)(2,1)S(1)} %join.2.after.refs_0_), channel_id=1, source_target_pairs={{0,2},{1,3},{2,0},{3,1},{4,6},{5,7},{6,4},{7,5},{8,10},{9,11},{10,... | collective-permute-start | bytes 786440 | tf_op jit(solution)/shard_map/ppermute | solution.py:352
  42.9 2.3 %mixers.1.after.coef = f32[8,2048]{1,0:T(8,128)S(1)} custom-call(s32[1]{0:T(128)} %bitcast.place, s32[1,2048]{1,0:T(1,128)S(1)} %bitcast.7, bf16[16,128]{1,0:T(8,128)(2,1)S(1)} %get-tuple-element.32.known, bf16[272,128]{1,0:T(8,128)(2,1)S(1)} %collective-permute-done.3.first, bf16[272,128]{1,0:T(8,128)(2,1)S(1)} %collective-permute-done.4.second, ...), custom_call_target="tpu_custom_call" | custom-call | tf_op jit(solution)/shard_map/mixers/pallas_call | solution.py:69
  45.2 0.0 copy-done.1
  45.2 1.6 %pick.1._ = bf16[2048,2048]{1,0:T(8,128)(2,1)S(1)} custom-call(s32[1]{0:T(128)} %bitcast.place, s32[1,2048]{1,0:T(1,128)S(1)} %bitcast.8, f32[8,2048]{1,0:T(8,128)S(1)} %mixers.1.after.coef), custom_call_target="tpu_custom_call" | custom-call | tf_op jit(solution)/shard_map/pick/pallas_call | solution.py:69
  46.8 1.0 %collective-permute-done.9.refs_1_ = bf16[256,512]{1,0:T(8,128)(2,1)S(1)} collective-permute-done((bf16[256,512]{1,0:T(8,128)(2,1)S(1)}, bf16[256,512]{1,0:T(8,128)(2,1)S(1)}, u32[]{:S(2)}, u32[]{:S(2)}) %collective-permute-start.9) | collective-permute-done | bytes 262176 | tf_op jit(solution)/shard_map/ppermute | solution.py:352
  47.8 0.1 collective-permute-start.10
  47.9 1.2 %mate.1.mates = f32[256,2048]{1,0:T(8,128)S(1)} custom-call(bf16[256,1024]{1,0:T(8,128)(2,1)S(1)} %join.3.mine, bf16[2048,2048]{1,0:T(8,128)(2,1)S(1)} %pick.1._), custom_call_target="tpu_custom_call" | custom-call | tf_op jit(solution)/shard_map/mate/pallas_call | solution.py:69
  49.1 0.6 %collective-permute-done.10.theirs = bf16[256,1024]{1,0:T(8,128)(2,1)S(1)} collective-permute-done((bf16[256,1024]{1,0:T(8,128)(2,1)S(1)}, bf16[256,1024]{1,0:T(8,128)(2,1)S(1)}, u32[]{:S(2)}, u32[]{:S(2)}) %collective-permute-start.10) | collective-permute-done | bytes 524320 | tf_op jit(solution)/shard_map/ppermute | solution.py:352
  49.8 3.5 %expand.1 = bf16[1024,256]{1,0:T(8,128)(2,1)} custom-call(s32[1]{0:T(128)} %bitcast.place, bf16[256,1024]{1,0:T(8,128)(2,1)S(1)} %join.3.mine, bf16[256,1024]{1,0:T(8,128)(2,1)S(1)} %collective-permute-done.10.theirs, f32[256,2048]{1,0:T(8,128)S(1)} %mate.1.mates, bf16[2048,2048]{1,0:T(8,128)(2,1)S(1)} %pick.1._, f32[8,2048]{1,0:T(8,128)S(1)} %mixers.1.after.coef, ...), custom_call_target="tpu_custom_call" | custom-call | tf_op jit(solution)/shard_map/expand/pallas_call | solution.py:69
  (3 shorter events, 0.1 us)
Async XLA Ops:
  0.0 6.2 %copy-start = (s32[2048]{0:T(1024)S(1)}, s32[2048]{0:T(1024)}, u32[]{:S(2)}) copy-start(s32[2048]{0:T(1024)} %param.14) | copy-start | bytes 24580
  5.7 3.8 %collective-permute-start = (bf16[912,512]{1,0:T(8,128)(2,1)S(1)}, bf16[912,512]{1,0:T(8,128)(2,1)S(1)}, u32[]{:S(2)}, u32[]{:S(2)}) collective-permute-start(bf16[912,512]{1,0:T(8,128)(2,1)S(1)} %get-tuple-element.25), channel_id=1, source_target_pairs={{0,1},{1,0},{2,3},{3,2},{4,5},{5,4},{6,7},{7,6},{8,9},{9,8},{10,11... | collective-permute-start | bytes 2801672 | tf_op jit(solution)/shard_map/ppermute | solution.py:352
  13.0 6.0 %collective-permute-start.1 = (bf16[896,512]{1,0:T(8,128)(2,1)S(1)}, bf16[896,512]{1,0:T(8,128)(2,1)S(1)}, u32[]{:S(2)}, u32[]{:S(2)}) collective-permute-start(bf16[896,512]{1,0:T(8,128)(2,1)S(1)} %project_rest.1.after), channel_id=1, source_target_pairs={{0,1},{1,0},{2,3},{3,2},{4,5},{5,4},{6,7},{7,6},{8,9},{9,8},{10,11... | collective-permute-start | bytes 2752520 | tf_op jit(solution)/shard_map/ppermute | solution.py:352
  13.1 9.9 %collective-permute-start.2 = (bf16[272,512]{1,0:T(8,128)(2,1)S(1)}, bf16[272,512]{1,0:T(8,128)(2,1)S(1)}, u32[]{:S(2)}, u32[]{:S(2)}) collective-permute-start(bf16[272,512]{1,0:T(8,128)(2,1)S(1)} %respond.2.after), channel_id=1, source_target_pairs={{0,2},{1,3},{2,0},{3,1},{4,6},{5,7},{6,4},{7,5},{8,10},{9,11},{10,... | collective-permute-start | bytes 835592 | tf_op jit(solution)/shard_map/ppermute | solution.py:352
  21.3 23.8 %copy-start.1 = (s32[2048]{0:T(1024)S(1)}, s32[2048]{0:T(1024)}, u32[]{:S(2)}) copy-start(s32[2048]{0:T(1024)} %param.15) | copy-start | bytes 24580
  23.1 4.5 %collective-permute-start.3 = (bf16[272,128]{1,0:T(8,128)(2,1)S(1)}, bf16[272,128]{1,0:T(8,128)(2,1)S(1)}, u32[]{:S(2)}, u32[]{:S(2)}) collective-permute-start(bf16[272,128]{1,0:T(8,128)(2,1)S(1)} %get-tuple-element.33), channel_id=1, source_target_pairs={{0,4},{1,5},{2,6},{3,7},{4,0},{5,1},{6,2},{7,3},{8,12},{9,13},{10,... | collective-permute-start | bytes 208904 | tf_op jit(solution)/shard_map/ppermute | solution.py:352
  25.0 6.9 %collective-permute-start.4 = (bf16[272,128]{1,0:T(8,128)(2,1)S(1)}, bf16[272,128]{1,0:T(8,128)(2,1)S(1)}, u32[]{:S(2)}, u32[]{:S(2)}) collective-permute-start(bf16[272,128]{1,0:T(8,128)(2,1)S(1)} %get-tuple-element.34), channel_id=1, source_target_pairs={{0,8},{1,9},{2,10},{3,11},{4,12},{5,13},{6,14},{7,15},{8,0},{9,1},... | collective-permute-start | bytes 208904 | tf_op jit(solution)/shard_map/ppermute | solution.py:352
  27.6 6.1 %collective-permute-start.5 = (bf16[272,128]{1,0:T(8,128)(2,1)S(1)}, bf16[272,128]{1,0:T(8,128)(2,1)S(1)}, u32[]{:S(2)}, u32[]{:S(2)}) collective-permute-start(bf16[272,128]{1,0:T(8,128)(2,1)S(1)} %get-tuple-element.35), channel_id=1, source_target_pairs={{0,12},{1,13},{2,14},{3,15},{4,8},{5,9},{6,10},{7,11},{8,4},{9,5},... | collective-permute-start | bytes 208904 | tf_op jit(solution)/shard_map/ppermute | solution.py:352
  33.7 6.2 %collective-permute-start.8 = (bf16[256,128]{1,0:T(8,128)(2,1)S(1)}, bf16[256,128]{1,0:T(8,128)(2,1)S(1)}, u32[]{:S(2)}, u32[]{:S(2)}) collective-permute-start(bf16[256,128]{1,0:T(8,128)(2,1)S(1)} %settle.1.refs_0_), channel_id=1, source_target_pairs={{0,12},{1,13},{2,14},{3,15},{4,8},{5,9},{6,10},{7,11},{8,4},{9,5},... | collective-permute-start | bytes 196616 | tf_op jit(solution)/shard_map/ppermute | solution.py:352
  35.2 6.0 %collective-permute-start.7 = (bf16[256,128]{1,0:T(8,128)(2,1)S(1)}, bf16[256,128]{1,0:T(8,128)(2,1)S(1)}, u32[]{:S(2)}, u32[]{:S(2)}) collective-permute-start(bf16[256,128]{1,0:T(8,128)(2,1)S(1)} %settle.1.refs_0_), channel_id=1, source_target_pairs={{0,8},{1,9},{2,10},{3,11},{4,12},{5,13},{6,14},{7,15},{8,0},{9,1},... | collective-permute-start | bytes 196616 | tf_op jit(solution)/shard_map/ppermute | solution.py:352
  35.3 6.0 %collective-permute-start.6 = (bf16[256,128]{1,0:T(8,128)(2,1)S(1)}, bf16[256,128]{1,0:T(8,128)(2,1)S(1)}, u32[]{:S(2)}, u32[]{:S(2)}) collective-permute-start(bf16[256,128]{1,0:T(8,128)(2,1)S(1)} %settle.1.refs_0_), channel_id=1, source_target_pairs={{0,4},{1,5},{2,6},{3,7},{4,0},{5,1},{6,2},{7,3},{8,12},{9,13},{10,... | collective-permute-start | bytes 196616 | tf_op jit(solution)/shard_map/ppermute | solution.py:352
  41.3 6.4 %collective-permute-start.9 = (bf16[256,512]{1,0:T(8,128)(2,1)S(1)}, bf16[256,512]{1,0:T(8,128)(2,1)S(1)}, u32[]{:S(2)}, u32[]{:S(2)}) collective-permute-start(bf16[256,512]{1,0:T(8,128)(2,1)S(1)} %join.2.after.refs_0_), channel_id=1, source_target_pairs={{0,2},{1,3},{2,0},{3,1},{4,6},{5,7},{6,4},{7,5},{8,10},{9,11},{10,... | collective-permute-start | bytes 786440 | tf_op jit(solution)/shard_map/ppermute | solution.py:352
  47.8 2.0 %collective-permute-start.10 = (bf16[256,1024]{1,0:T(8,128)(2,1)S(1)}, bf16[256,1024]{1,0:T(8,128)(2,1)S(1)}, u32[]{:S(2)}, u32[]{:S(2)}) collective-permute-start(bf16[256,1024]{1,0:T(8,128)(2,1)S(1)} %join.3.mine), channel_id=1, source_target_pairs={{0,1},{1,0},{2,3},{3,2},{4,5},{5,4},{6,7},{7,6},{8,9},{9,8},{10,11... | collective-permute-start | bytes 1572872 | tf_op jit(solution)/shard_map/ppermute | solution.py:352

commit v11 on v10

--- a/solution.py
+++ b/solution.py
@@ -246,6 +246,10 @@
         out[W + 2 : W + 4, :LANES] = other[hist : hist + 2, :LANES]
 
 
+def turns_of(core):
+    return 3 - 2 * core, 2, 1 + 2 * core
+
+
 def fold_kernel(place, own, got, coef, other, keep, known, first, second, third):
     z = place[0] >> 2
     size = keep.shape[1]
@@ -254,11 +258,11 @@
     known[0:2, :] = coef[...]
     known[2:4, :] = other[hist : hist + 2, :LANES]
     known[4:8, :] = got[W : W + 4, :LANES]
-    for d, out in enumerate((keep, first, second, third)):
+    for d, out in zip((0, *turns_of(place[0] & 1)), (keep, first, second, third)):
         where = block((z ^ d) * size, size)
         total = own[:, where] + got[:W, where].astype(F32)
         out[:W, :] = total.astype(out.dtype)
-        if d:
+        if out.shape[0] > W:
             out[W:, :] = known[...]
 
 
@@ -288,7 +292,7 @@
 def mixers_kernel(place, order, known, first, second, third, after, coef, held):
     me = place[0]
     held[...] = jnp.zeros(held.shape, F32)
-    for z, rows in enumerate((known, first, second, third)):
+    for z, rows in zip((0, *turns_of(me & 1)), (known, first, second, third)):
         top = rows.shape[0] - EXTRA
         for low in range(4):
             where = block((me ^ (4 * z + low)) * LANES, LANES)
@@ -348,8 +352,9 @@
         out[r : r + TILE, :] = total.astype(BF)
 
 
-def swap(x, devices, bits):
-    return lax.ppermute(x, "frdm", [(i, i ^ bits) for i in range(devices)])
+def swap(x, devices, bits, odd=None):
+    odd = bits if odd is None else odd
+    return lax.ppermute(x, "frdm", [(i, i ^ (odd if i & 1 else bits)) for i in range(devices)])
 
 
 def shards(devices, loads, shapes, mode_order, partner, taps, offsets, coef):
@@ -405,7 +410,8 @@
             fold_kernel, "fold", [array(W, size, dtype=F32), array(EXTRA, LANES)] + [array(W + EXTRA, size)] * 3,
             place, own, away, coef_near, got,
         )
-        parts = [swap(part, devices, 4 * d) for d, part in zip((1, 2, 3), parts)]
+        ways = zip(turns_of(0), turns_of(1))
+        parts = [swap(part, devices, 4 * even, 4 * odd) for part, (even, odd) in zip(parts, ways)]
         total = call(settle_kernel, "settle", [array(W, size)], keep, *parts, scalars=0)[0]
         spread = [swap(total, devices, 4 * d) for d in (1, 2, 3)]
         resp = join(total, *spread)

time: 53.4 us -> 53.3 us (level)
  transfers between devices with their start and end apart: 11 -> 11, of which waited for: 7 -> 7; matrix products, arithmetic and copies ran while one was open for 0% -> 0% of each run, Pallas kernels for 25% -> 26%
where the time goes in v11:
time: 53.3 us; the launch traced here: 53.2 us
  Pallas kernels  26.5 us (50%)
  starting transfers between devices  14.2 us (27%)
  waiting for transfers between devices  12.3 us (23%)
    pallas_call x14, Pallas kernels, call(): pl.pallas_call(kernel, in_specs=places, out_specs=[vmem] * len(out_shape)...  26.5 us
    ppermute x11, starting transfers between devices, swap(): lax.ppermute(x, 'frdm', [(i, i ^ (odd if i & 1 else bits)) for i in range...  14.2 us
    ppermute x11, waiting for transfers between devices, swap(): lax.ppermute(x, 'frdm', [(i, i ^ (odd if i & 1 else bits)) for i in range...  12.3 us
  transfers between devices with their start and end apart: 11, of which 7 were waited for; matrix products, arithmetic and copies ran while one was open for 0% of the time, Pallas kernels for 26%

profile of v11, /device:TPU:0, one launch (start us, length us, event | category | flops | bytes accessed | tf_op | source)
XLA Modules:
  0.0 53.2 jit_solution(12317679856923074699)
XLA Ops:
  0.0 0.0 copy-start
  0.0 5.7 %project.1 = (bf16[912,512]{1,0:T(8,128)(2,1)S(1)}, bf16[896,1024]{1,0:T(8,128)(2,1)S(1)}, bf16[1024,1024]{1,0:T(8,128)(2,1)S(1)}, bf16[528,2048]{1,0:T(8,128)(2,1)S(1)}, bf16[2,128]{1,0:T(2,128)(2,1)S(1)}) custom-call(s32[1]{0:T(128)} %bitcast.place, bf16[1024,896]{1,0:T(8,128)(2,1)} %loads_far.1, bf16[896,896]{1,0:T(8,128)(2,1)} %constant.14.clone.forward_far, ...), custom_call_target="tpu_custom_call" | custom-call | tf_op jit(solution)/shard_map/project/pallas_call | solution.py:69
  5.7 0.5 collective-permute-start
  6.2 0.0 copy-done
  6.2 3.3 %spectrum.1 = (f32[896,512]{1,0:T(8,128)S(1)}, bf16[1024,1024]{1,0:T(8,128)(2,1)S(1)}, bf16[896,1024]{1,0:T(8,128)(2,1)S(1)}, bf16[896,128]{1,0:T(8,128)(2,1)S(1...) custom-call(s32[1]{0:T(128)} %bitcast.place, bf16[528,2048]{1,0:T(8,128)(2,1)S(1)} %get-tuple-element.22.stack, ...), custom_call_target="tpu_custom_call" | custom-call | tf_op jit(solution)/shard_map/spectrum/pallas_call | solution.py:69
  9.5 0.0 collective-permute-done.other
  9.5 2.4 %respond.2.after = bf16[272,512]{1,0:T(8,128)(2,1)S(1)} custom-call(s32[1]{0:T(128)} %bitcast.place, bf16[896,1024]{1,0:T(8,128)(2,1)S(1)} %get-tuple-element.21.lft, bf16[1024,1024]{1,0:T(8,128)(2,1)S(1)} %get-tuple-element.23.shapes.near, bf16[912,512]{1,0:T(8,128)(2,1)S(1)} %collective-permute-done.other, f32[896,512]{1,0:T(8,128)S(1)} %get-tuple-element.26.spec, ...), custom_call_target="tpu_custom_call" | custom-call | tf_op jit(solution)/shard_map/respond/pallas_call | solution.py:69
  11.9 1.1 %project_rest.1.after = bf16[896,512]{1,0:T(8,128)(2,1)S(1)} custom-call(s32[1]{0:T(128)} %bitcast.place, bf16[896,1024]{1,0:T(8,128)(2,1)S(1)} %get-tuple-element.21.lft, bf16[1024,1024]{1,0:T(8,128)(2,1)S(1)} %get-tuple-element.24.shapes.far, bf16[272,512]{1,0:T(8,128)(2,1)S(1)} %respond.2.after), custom_call_target="tpu_custom_call" | custom-call | flops 3758096384 | tf_op jit(solution)/shard_map/project_rest/pallas_call | solution.py:69
  13.0 0.1 collective-permute-start.1
  13.1 3.0 %collective-permute-start.2 = (bf16[272,512]{1,0:T(8,128)(2,1)S(1)}, bf16[272,512]{1,0:T(8,128)(2,1)S(1)}, u32[]{:S(2)}, u32[]{:S(2)}) collective-permute-start(bf16[272,512]{1,0:T(8,128)(2,1)S(1)} %respond.2.after), channel_id=1, source_target_pairs={{0,2},{1,3},{2,0},{3,1},{4,6},{5,7},{6,4},{7,5},{8,10},{9,11},{10,... | collective-permute-start | bytes 835592 | tf_op jit(solution)/shard_map/ppermute | solution.py:357
  16.1 2.9 %spectrum_rest.1.spec = f32[896,512]{1,0:T(8,128)S(1)} custom-call(s32[1]{0:T(128)} %bitcast.place, bf16[528,2048]{1,0:T(8,128)(2,1)S(1)} %get-tuple-element.22.stack, s32[1,2048]{1,0:T(1,128)S(1)} %bitcast.6, bf16[896,1024]{1,0:T(8,128)(2,1)S(1)} %get-tuple-element.29.table, bf16[896,128]{1,0:T(8,128)(2,1)S(1)} %get-tuple-element.30.last, ...), custom_call_target="tpu_custom_call" | custom-call | tf_op jit(solution)/shard_map/spectrum_rest/pallas_call | solution.py:69
  19.0 0.0 collective-permute-done.1.other
  19.0 2.3 %respond.3.own = f32[256,512]{1,0:T(8,128)S(1)} custom-call(s32[1]{0:T(128)} %bitcast.place, bf16[896,1024]{1,0:T(8,128)(2,1)S(1)} %get-tuple-element.21.lft, bf16[1024,1024]{1,0:T(8,128)(2,1)S(1)} %get-tuple-element.23.shapes.near, bf16[896,512]{1,0:T(8,128)(2,1)S(1)} %collective-permute-done.1.other, f32[896,512]{1,0:T(8,128)S(1)} %spectrum_rest.1.spec, ...), custom_call_target="tpu_custom_call" | custom-call | tf_op jit(solution)/shard_map/respond/pallas_call | solution.py:69
  21.3 0.0 copy-start.1
  21.4 1.6 %collective-permute-done.2.got = bf16[272,512]{1,0:T(8,128)(2,1)S(1)} collective-permute-done((bf16[272,512]{1,0:T(8,128)(2,1)S(1)}, bf16[272,512]{1,0:T(8,128)(2,1)S(1)}, u32[]{:S(2)}, u32[]{:S(2)}) %collective-permute-start.2) | collective-permute-done | bytes 278560 | tf_op jit(solution)/shard_map/ppermute | solution.py:357
  23.0 0.1 fold.1
  23.1 3.9 %collective-permute-start.3 = (bf16[272,128]{1,0:T(8,128)(2,1)S(1)}, bf16[272,128]{1,0:T(8,128)(2,1)S(1)}, u32[]{:S(2)}, u32[]{:S(2)}) collective-permute-start(bf16[272,128]{1,0:T(8,128)(2,1)S(1)} %get-tuple-element.33), channel_id=1, source_target_pairs={{0,12},{1,5},{2,14},{3,7},{4,8},{5,1},{6,10},{7,3},{8,4},{9,13},{1... | collective-permute-start | bytes 208904 | tf_op jit(solution)/shard_map/ppermute | solution.py:357
  27.0 0.0 collective-permute-start.4
  27.0 0.6 %collective-permute-start.5 = (bf16[272,128]{1,0:T(8,128)(2,1)S(1)}, bf16[272,128]{1,0:T(8,128)(2,1)S(1)}, u32[]{:S(2)}, u32[]{:S(2)}) collective-permute-start(bf16[272,128]{1,0:T(8,128)(2,1)S(1)} %get-tuple-element.35), channel_id=1, source_target_pairs={{0,4},{1,13},{2,6},{3,15},{4,0},{5,9},{6,2},{7,11},{8,12},{9,5},{1... | collective-permute-start | bytes 208904 | tf_op jit(solution)/shard_map/ppermute | solution.py:357
  27.7 2.0 %collective-permute-done.3.first = bf16[272,128]{1,0:T(8,128)(2,1)S(1)} collective-permute-done((bf16[272,128]{1,0:T(8,128)(2,1)S(1)}, bf16[272,128]{1,0:T(8,128)(2,1)S(1)}, u32[]{:S(2)}, u32[]{:S(2)}) %collective-permute-start.3) | collective-permute-done | bytes 69664 | tf_op jit(solution)/shard_map/ppermute | solution.py:357
  29.6 3.8 %collective-permute-done.4.second = bf16[272,128]{1,0:T(8,128)(2,1)S(1)} collective-permute-done((bf16[272,128]{1,0:T(8,128)(2,1)S(1)}, bf16[272,128]{1,0:T(8,128)(2,1)S(1)}, u32[]{:S(2)}, u32[]{:S(2)}) %collective-permute-start.4) | collective-permute-done | bytes 69664 | tf_op jit(solution)/shard_map/ppermute | solution.py:357
  33.4 0.0 collective-permute-done.5.third
  33.5 2.5 %collective-permute-start.8 = (bf16[256,128]{1,0:T(8,128)(2,1)S(1)}, bf16[256,128]{1,0:T(8,128)(2,1)S(1)}, u32[]{:S(2)}, u32[]{:S(2)}) collective-permute-start(bf16[256,128]{1,0:T(8,128)(2,1)S(1)} %settle.1.refs_0_), channel_id=1, source_target_pairs={{0,12},{1,13},{2,14},{3,15},{4,8},{5,9},{6,10},{7,11},{8,4},{9,5},... | collective-permute-start | bytes 196616 | tf_op jit(solution)/shard_map/ppermute | solution.py:357
  36.0 0.0 collective-permute-start.7
  36.0 1.9 %collective-permute-start.6 = (bf16[256,128]{1,0:T(8,128)(2,1)S(1)}, bf16[256,128]{1,0:T(8,128)(2,1)S(1)}, u32[]{:S(2)}, u32[]{:S(2)}) collective-permute-start(bf16[256,128]{1,0:T(8,128)(2,1)S(1)} %settle.1.refs_0_), channel_id=1, source_target_pairs={{0,4},{1,5},{2,6},{3,7},{4,0},{5,1},{6,2},{7,3},{8,12},{9,13},{10,... | collective-permute-start | bytes 196616 | tf_op jit(solution)/shard_map/ppermute | solution.py:357
  37.9 1.9 %collective-permute-done.8.refs_3_ = bf16[256,128]{1,0:T(8,128)(2,1)S(1)} collective-permute-done((bf16[256,128]{1,0:T(8,128)(2,1)S(1)}, bf16[256,128]{1,0:T(8,128)(2,1)S(1)}, u32[]{:S(2)}, u32[]{:S(2)}) %collective-permute-start.8) | collective-permute-done | bytes 65568 | tf_op jit(solution)/shard_map/ppermute | solution.py:357
  39.8 1.4 %collective-permute-done.7.refs_2_ = bf16[256,128]{1,0:T(8,128)(2,1)S(1)} collective-permute-done((bf16[256,128]{1,0:T(8,128)(2,1)S(1)}, bf16[256,128]{1,0:T(8,128)(2,1)S(1)}, u32[]{:S(2)}, u32[]{:S(2)}) %collective-permute-start.7) | collective-permute-done | bytes 65568 | tf_op jit(solution)/shard_map/ppermute | solution.py:357
  41.2 0.0 collective-permute-done.6.refs_1_
  41.2 1.6 %collective-permute-start.9 = (bf16[256,512]{1,0:T(8,128)(2,1)S(1)}, bf16[256,512]{1,0:T(8,128)(2,1)S(1)}, u32[]{:S(2)}, u32[]{:S(2)}) collective-permute-start(bf16[256,512]{1,0:T(8,128)(2,1)S(1)} %join.2.after.refs_0_), channel_id=1, source_target_pairs={{0,2},{1,3},{2,0},{3,1},{4,6},{5,7},{6,4},{7,5},{8,10},{9,11},{10,... | collective-permute-start | bytes 786440 | tf_op jit(solution)/shard_map/ppermute | solution.py:357
  42.8 2.3 %mixers.1.after.coef = f32[8,2048]{1,0:T(8,128)S(1)} custom-call(s32[1]{0:T(128)} %bitcast.place, s32[1,2048]{1,0:T(1,128)S(1)} %bitcast.7, bf16[16,128]{1,0:T(8,128)(2,1)S(1)} %get-tuple-element.32.known, bf16[272,128]{1,0:T(8,128)(2,1)S(1)} %collective-permute-done.3.first, bf16[272,128]{1,0:T(8,128)(2,1)S(1)} %collective-permute-done.4.second, ...), custom_call_target="tpu_custom_call" | custom-call | tf_op jit(solution)/shard_map/mixers/pallas_call | solution.py:69
  45.1 0.0 copy-done.1
  45.1 1.6 %pick.1._ = bf16[2048,2048]{1,0:T(8,128)(2,1)S(1)} custom-call(s32[1]{0:T(128)} %bitcast.place, s32[1,2048]{1,0:T(1,128)S(1)} %bitcast.8, f32[8,2048]{1,0:T(8,128)S(1)} %mixers.1.after.coef), custom_call_target="tpu_custom_call" | custom-call | tf_op jit(solution)/shard_map/pick/pallas_call | solution.py:69
  46.7 1.0 %collective-permute-done.9.refs_1_ = bf16[256,512]{1,0:T(8,128)(2,1)S(1)} collective-permute-done((bf16[256,512]{1,0:T(8,128)(2,1)S(1)}, bf16[256,512]{1,0:T(8,128)(2,1)S(1)}, u32[]{:S(2)}, u32[]{:S(2)}) %collective-permute-start.9) | collective-permute-done | bytes 262176 | tf_op jit(solution)/shard_map/ppermute | solution.py:357
  47.7 0.1 collective-permute-start.10
  47.8 1.2 %mate.1.mates = f32[256,2048]{1,0:T(8,128)S(1)} custom-call(bf16[256,1024]{1,0:T(8,128)(2,1)S(1)} %join.3.mine, bf16[2048,2048]{1,0:T(8,128)(2,1)S(1)} %pick.1._), custom_call_target="tpu_custom_call" | custom-call | tf_op jit(solution)/shard_map/mate/pallas_call | solution.py:69
  49.1 0.6 %collective-permute-done.10.theirs = bf16[256,1024]{1,0:T(8,128)(2,1)S(1)} collective-permute-done((bf16[256,1024]{1,0:T(8,128)(2,1)S(1)}, bf16[256,1024]{1,0:T(8,128)(2,1)S(1)}, u32[]{:S(2)}, u32[]{:S(2)}) %collective-permute-start.10) | collective-permute-done | bytes 524320 | tf_op jit(solution)/shard_map/ppermute | solution.py:357
  49.7 3.5 %expand.1 = bf16[1024,256]{1,0:T(8,128)(2,1)} custom-call(s32[1]{0:T(128)} %bitcast.place, bf16[256,1024]{1,0:T(8,128)(2,1)S(1)} %join.3.mine, bf16[256,1024]{1,0:T(8,128)(2,1)S(1)} %collective-permute-done.10.theirs, f32[256,2048]{1,0:T(8,128)S(1)} %mate.1.mates, bf16[2048,2048]{1,0:T(8,128)(2,1)S(1)} %pick.1._, f32[8,2048]{1,0:T(8,128)S(1)} %mixers.1.after.coef, ...), custom_call_target="tpu_custom_call" | custom-call | tf_op jit(solution)/shard_map/expand/pallas_call | solution.py:69
  (3 shorter events, 0.1 us)
Async XLA Ops:
  0.0 6.2 %copy-start = (s32[2048]{0:T(1024)S(1)}, s32[2048]{0:T(1024)}, u32[]{:S(2)}) copy-start(s32[2048]{0:T(1024)} %param.14) | copy-start | bytes 24580
  5.7 3.8 %collective-permute-start = (bf16[912,512]{1,0:T(8,128)(2,1)S(1)}, bf16[912,512]{1,0:T(8,128)(2,1)S(1)}, u32[]{:S(2)}, u32[]{:S(2)}) collective-permute-start(bf16[912,512]{1,0:T(8,128)(2,1)S(1)} %get-tuple-element.25), channel_id=1, source_target_pairs={{0,1},{1,0},{2,3},{3,2},{4,5},{5,4},{6,7},{7,6},{8,9},{9,8},{10,11... | collective-permute-start | bytes 2801672 | tf_op jit(solution)/shard_map/ppermute | solution.py:357
  13.0 6.0 %collective-permute-start.1 = (bf16[896,512]{1,0:T(8,128)(2,1)S(1)}, bf16[896,512]{1,0:T(8,128)(2,1)S(1)}, u32[]{:S(2)}, u32[]{:S(2)}) collective-permute-start(bf16[896,512]{1,0:T(8,128)(2,1)S(1)} %project_rest.1.after), channel_id=1, source_target_pairs={{0,1},{1,0},{2,3},{3,2},{4,5},{5,4},{6,7},{7,6},{8,9},{9,8},{10,11... | collective-permute-start | bytes 2752520 | tf_op jit(solution)/shard_map/ppermute | solution.py:357
  13.1 9.9 %collective-permute-start.2 = (bf16[272,512]{1,0:T(8,128)(2,1)S(1)}, bf16[272,512]{1,0:T(8,128)(2,1)S(1)}, u32[]{:S(2)}, u32[]{:S(2)}) collective-permute-start(bf16[272,512]{1,0:T(8,128)(2,1)S(1)} %respond.2.after), channel_id=1, source_target_pairs={{0,2},{1,3},{2,0},{3,1},{4,6},{5,7},{6,4},{7,5},{8,10},{9,11},{10,... | collective-permute-start | bytes 835592 | tf_op jit(solution)/shard_map/ppermute | solution.py:357
  21.3 23.8 %copy-start.1 = (s32[2048]{0:T(1024)S(1)}, s32[2048]{0:T(1024)}, u32[]{:S(2)}) copy-start(s32[2048]{0:T(1024)} %param.15) | copy-start | bytes 24580
  23.1 6.5 %collective-permute-start.3 = (bf16[272,128]{1,0:T(8,128)(2,1)S(1)}, bf16[272,128]{1,0:T(8,128)(2,1)S(1)}, u32[]{:S(2)}, u32[]{:S(2)}) collective-permute-start(bf16[272,128]{1,0:T(8,128)(2,1)S(1)} %get-tuple-element.33), channel_id=1, source_target_pairs={{0,12},{1,5},{2,14},{3,7},{4,8},{5,1},{6,10},{7,3},{8,4},{9,13},{1... | collective-permute-start | bytes 208904 | tf_op jit(solution)/shard_map/ppermute | solution.py:357
  27.0 6.4 %collective-permute-start.4 = (bf16[272,128]{1,0:T(8,128)(2,1)S(1)}, bf16[272,128]{1,0:T(8,128)(2,1)S(1)}, u32[]{:S(2)}, u32[]{:S(2)}) collective-permute-start(bf16[272,128]{1,0:T(8,128)(2,1)S(1)} %get-tuple-element.34), channel_id=1, source_target_pairs={{0,8},{1,9},{2,10},{3,11},{4,12},{5,13},{6,14},{7,15},{8,0},{9,1},... | collective-permute-start | bytes 208904 | tf_op jit(solution)/shard_map/ppermute | solution.py:357
  27.0 6.4 %collective-permute-start.5 = (bf16[272,128]{1,0:T(8,128)(2,1)S(1)}, bf16[272,128]{1,0:T(8,128)(2,1)S(1)}, u32[]{:S(2)}, u32[]{:S(2)}) collective-permute-start(bf16[272,128]{1,0:T(8,128)(2,1)S(1)} %get-tuple-element.35), channel_id=1, source_target_pairs={{0,4},{1,13},{2,6},{3,15},{4,0},{5,9},{6,2},{7,11},{8,12},{9,5},{1... | collective-permute-start | bytes 208904 | tf_op jit(solution)/shard_map/ppermute | solution.py:357
  33.5 6.4 %collective-permute-start.8 = (bf16[256,128]{1,0:T(8,128)(2,1)S(1)}, bf16[256,128]{1,0:T(8,128)(2,1)S(1)}, u32[]{:S(2)}, u32[]{:S(2)}) collective-permute-start(bf16[256,128]{1,0:T(8,128)(2,1)S(1)} %settle.1.refs_0_), channel_id=1, source_target_pairs={{0,12},{1,13},{2,14},{3,15},{4,8},{5,9},{6,10},{7,11},{8,4},{9,5},... | collective-permute-start | bytes 196616 | tf_op jit(solution)/shard_map/ppermute | solution.py:357
  36.0 5.2 %collective-permute-start.7 = (bf16[256,128]{1,0:T(8,128)(2,1)S(1)}, bf16[256,128]{1,0:T(8,128)(2,1)S(1)}, u32[]{:S(2)}, u32[]{:S(2)}) collective-permute-start(bf16[256,128]{1,0:T(8,128)(2,1)S(1)} %settle.1.refs_0_), channel_id=1, source_target_pairs={{0,8},{1,9},{2,10},{3,11},{4,12},{5,13},{6,14},{7,15},{8,0},{9,1},... | collective-permute-start | bytes 196616 | tf_op jit(solution)/shard_map/ppermute | solution.py:357
  36.0 5.2 %collective-permute-start.6 = (bf16[256,128]{1,0:T(8,128)(2,1)S(1)}, bf16[256,128]{1,0:T(8,128)(2,1)S(1)}, u32[]{:S(2)}, u32[]{:S(2)}) collective-permute-start(bf16[256,128]{1,0:T(8,128)(2,1)S(1)} %settle.1.refs_0_), channel_id=1, source_target_pairs={{0,4},{1,5},{2,6},{3,7},{4,0},{5,1},{6,2},{7,3},{8,12},{9,13},{10,... | collective-permute-start | bytes 196616 | tf_op jit(solution)/shard_map/ppermute | solution.py:357
  41.2 6.4 %collective-permute-start.9 = (bf16[256,512]{1,0:T(8,128)(2,1)S(1)}, bf16[256,512]{1,0:T(8,128)(2,1)S(1)}, u32[]{:S(2)}, u32[]{:S(2)}) collective-permute-start(bf16[256,512]{1,0:T(8,128)(2,1)S(1)} %join.2.after.refs_0_), channel_id=1, source_target_pairs={{0,2},{1,3},{2,0},{3,1},{4,6},{5,7},{6,4},{7,5},{8,10},{9,11},{10,... | collective-permute-start | bytes 786440 | tf_op jit(solution)/shard_map/ppermute | solution.py:357
  47.7 2.0 %collective-permute-start.10 = (bf16[256,1024]{1,0:T(8,128)(2,1)S(1)}, bf16[256,1024]{1,0:T(8,128)(2,1)S(1)}, u32[]{:S(2)}, u32[]{:S(2)}) collective-permute-start(bf16[256,1024]{1,0:T(8,128)(2,1)S(1)} %join.3.mine), channel_id=1, source_target_pairs={{0,1},{1,0},{2,3},{3,2},{4,5},{5,4},{6,7},{7,6},{8,9},{9,8},{10,11... | collective-permute-start | bytes 1572872 | tf_op jit(solution)/shard_map/ppermute | solution.py:357

commit v12 on v11

--- a/solution.py
+++ b/solution.py
@@ -395,7 +395,7 @@
     sent = call(project_rest_kernel, "project_rest", [array(hist, quarter)], place, lft, far, away, products=4 * hist * rows * quarter)[0]
     rest = swap(sent, devices, 1)
     spec = call(
-        spectrum_rest_kernel, "spectrum_rest", [array(hist, quarter, dtype=F32)], place, stack, order, *held, sent
+        spectrum_rest_kernel, "spectrum_rest", [array(hist, quarter, dtype=F32)], place, stack, order, *held, away, products=10**10
     )[0]
     own = respond(0, rest, spec, array(W, quarter, dtype=F32))
 

time: 53.3 us -> 53.2 us (level)
  transfers between devices with their start and end apart: 11 -> 11, of which waited for: 7 -> 7; matrix products, arithmetic and copies ran while one was open for 0% -> 0% of each run, Pallas kernels for 26% -> 28%
where the time goes in v12:
time: 53.2 us; the launch traced here: 53.1 us
  Pallas kernels  26.6 us (50%)
  starting transfers between devices  14 us (26%)
  waiting for transfers between devices  12.3 us (23%)
    pallas_call x14, Pallas kernels, call(): pl.pallas_call(kernel, in_specs=places, out_specs=[vmem] * len(out_shape)...  26.6 us
    ppermute x11, starting transfers between devices, swap(): lax.ppermute(x, 'frdm', [(i, i ^ (odd if i & 1 else bits)) for i in range...  14 us
    ppermute x11, waiting for transfers between devices, swap(): lax.ppermute(x, 'frdm', [(i, i ^ (odd if i & 1 else bits)) for i in range...  12.3 us
  transfers between devices with their start and end apart: 11, of which 7 were waited for; matrix products, arithmetic and copies ran while one was open for 0% of the time, Pallas kernels for 28%

profile of v12, /device:TPU:0, one launch (start us, length us, event | category | flops | bytes accessed | tf_op | source)
XLA Modules:
  0.0 53.1 jit_solution(10711967576882154585)
XLA Ops:
  0.0 0.0 copy-start
  0.0 5.7 %project.1 = (bf16[912,512]{1,0:T(8,128)(2,1)S(1)}, bf16[896,1024]{1,0:T(8,128)(2,1)S(1)}, bf16[1024,1024]{1,0:T(8,128)(2,1)S(1)}, bf16[528,2048]{1,0:T(8,128)(2,1)S(1)}, bf16[2,128]{1,0:T(2,128)(2,1)S(1)}) custom-call(s32[1]{0:T(128)} %bitcast.place, bf16[1024,896]{1,0:T(8,128)(2,1)} %loads_far.1, bf16[896,896]{1,0:T(8,128)(2,1)} %constant.14.clone.forward_far, ...), custom_call_target="tpu_custom_call" | custom-call | tf_op jit(solution)/shard_map/project/pallas_call | solution.py:69
  5.7 0.5 collective-permute-start
  6.2 0.0 copy-done
  6.2 3.3 %spectrum.1 = (f32[896,512]{1,0:T(8,128)S(1)}, bf16[1024,1024]{1,0:T(8,128)(2,1)S(1)}, bf16[896,1024]{1,0:T(8,128)(2,1)S(1)}, bf16[896,128]{1,0:T(8,128)(2,1)S(1...) custom-call(s32[1]{0:T(128)} %bitcast.place, bf16[528,2048]{1,0:T(8,128)(2,1)S(1)} %get-tuple-element.22.stack, ...), custom_call_target="tpu_custom_call" | custom-call | tf_op jit(solution)/shard_map/spectrum/pallas_call | solution.py:69
  9.5 0.0 collective-permute-done.other
  9.5 2.4 %respond.2.after = bf16[272,512]{1,0:T(8,128)(2,1)S(1)} custom-call(s32[1]{0:T(128)} %bitcast.place, bf16[896,1024]{1,0:T(8,128)(2,1)S(1)} %get-tuple-element.21.lft, bf16[1024,1024]{1,0:T(8,128)(2,1)S(1)} %get-tuple-element.23.shapes.near, bf16[912,512]{1,0:T(8,128)(2,1)S(1)} %collective-permute-done.other, f32[896,512]{1,0:T(8,128)S(1)} %get-tuple-element.26.spec, ...), custom_call_target="tpu_custom_call" | custom-call | tf_op jit(solution)/shard_map/respond/pallas_call | solution.py:69
  11.9 2.6 %collective-permute-start.2 = (bf16[272,512]{1,0:T(8,128)(2,1)S(1)}, bf16[272,512]{1,0:T(8,128)(2,1)S(1)}, u32[]{:S(2)}, u32[]{:S(2)}) collective-permute-start(bf16[272,512]{1,0:T(8,128)(2,1)S(1)} %respond.2.after), channel_id=1, source_target_pairs={{0,2},{1,3},{2,0},{3,1},{4,6},{5,7},{6,4},{7,5},{8,10},{9,11},{10,... | collective-permute-start | bytes 835592 | tf_op jit(solution)/shard_map/ppermute | solution.py:357
  14.5 1.1 %project_rest.1 = bf16[896,512]{1,0:T(8,128)(2,1)S(1)} custom-call(s32[1]{0:T(128)} %bitcast.place, bf16[896,1024]{1,0:T(8,128)(2,1)S(1)} %get-tuple-element.21.lft, bf16[1024,1024]{1,0:T(8,128)(2,1)S(1)} %get-tuple-element.24.shapes.far, bf16[272,512]{1,0:T(8,128)(2,1)S(1)} %respond.2.after), custom_call_target="tpu_custom_call" | custom-call | flops 3758096384 | tf_op jit(solution)/shard_map/project_rest/pallas_call | solution.py:69
  15.6 0.3 collective-permute-start.1
  15.9 2.9 %spectrum_rest.1.spec = f32[896,512]{1,0:T(8,128)S(1)} custom-call(s32[1]{0:T(128)} %bitcast.place, bf16[528,2048]{1,0:T(8,128)(2,1)S(1)} %get-tuple-element.22.stack, s32[1,2048]{1,0:T(1,128)S(1)} %bitcast.6, bf16[896,1024]{1,0:T(8,128)(2,1)S(1)} %get-tuple-element.29.table, bf16[896,128]{1,0:T(8,128)(2,1)S(1)} %get-tuple-element.30.last, ...), custom_call_target="tpu_custom_call" | custom-call | flops 20000000000 | tf_op jit(solution)/shard_map/spectrum_rest/pallas_call | solution.py:69
  18.8 0.0 collective-permute-done.1.other
  18.8 2.4 %respond.3.own = f32[256,512]{1,0:T(8,128)S(1)} custom-call(s32[1]{0:T(128)} %bitcast.place, bf16[896,1024]{1,0:T(8,128)(2,1)S(1)} %get-tuple-element.21.lft, bf16[1024,1024]{1,0:T(8,128)(2,1)S(1)} %get-tuple-element.23.shapes.near, bf16[896,512]{1,0:T(8,128)(2,1)S(1)} %collective-permute-done.1.other, f32[896,512]{1,0:T(8,128)S(1)} %spectrum_rest.1.spec, ...), custom_call_target="tpu_custom_call" | custom-call | tf_op jit(solution)/shard_map/respond/pallas_call | solution.py:69
  21.2 0.0 copy-start.1
  21.2 0.6 %collective-permute-done.2.got = bf16[272,512]{1,0:T(8,128)(2,1)S(1)} collective-permute-done((bf16[272,512]{1,0:T(8,128)(2,1)S(1)}, bf16[272,512]{1,0:T(8,128)(2,1)S(1)}, u32[]{:S(2)}, u32[]{:S(2)}) %collective-permute-start.2) | collective-permute-done | bytes 278560 | tf_op jit(solution)/shard_map/ppermute | solution.py:357
  21.8 0.1 fold.1
  21.9 3.9 %collective-permute-start.3 = (bf16[272,128]{1,0:T(8,128)(2,1)S(1)}, bf16[272,128]{1,0:T(8,128)(2,1)S(1)}, u32[]{:S(2)}, u32[]{:S(2)}) collective-permute-start(bf16[272,128]{1,0:T(8,128)(2,1)S(1)} %get-tuple-element.33), channel_id=1, source_target_pairs={{0,12},{1,5},{2,14},{3,7},{4,8},{5,1},{6,10},{7,3},{8,4},{9,13},{1... | collective-permute-start | bytes 208904 | tf_op jit(solution)/shard_map/ppermute | solution.py:357
  25.8 0.0 collective-permute-start.4
  25.8 0.6 %collective-permute-start.5 = (bf16[272,128]{1,0:T(8,128)(2,1)S(1)}, bf16[272,128]{1,0:T(8,128)(2,1)S(1)}, u32[]{:S(2)}, u32[]{:S(2)}) collective-permute-start(bf16[272,128]{1,0:T(8,128)(2,1)S(1)} %get-tuple-element.35), channel_id=1, source_target_pairs={{0,4},{1,13},{2,6},{3,15},{4,0},{5,9},{6,2},{7,11},{8,12},{9,5},{1... | collective-permute-start | bytes 208904 | tf_op jit(solution)/shard_map/ppermute | solution.py:357
  26.5 2.4 %collective-permute-done.3.first = bf16[272,128]{1,0:T(8,128)(2,1)S(1)} collective-permute-done((bf16[272,128]{1,0:T(8,128)(2,1)S(1)}, bf16[272,128]{1,0:T(8,128)(2,1)S(1)}, u32[]{:S(2)}, u32[]{:S(2)}) %collective-permute-start.3) | collective-permute-done | bytes 69664 | tf_op jit(solution)/shard_map/ppermute | solution.py:357
  28.9 3.8 %collective-permute-done.4.second = bf16[272,128]{1,0:T(8,128)(2,1)S(1)} collective-permute-done((bf16[272,128]{1,0:T(8,128)(2,1)S(1)}, bf16[272,128]{1,0:T(8,128)(2,1)S(1)}, u32[]{:S(2)}, u32[]{:S(2)}) %collective-permute-start.4) | collective-permute-done | bytes 69664 | tf_op jit(solution)/shard_map/ppermute | solution.py:357
  32.7 0.0 collective-permute-done.5.third
  32.7 2.6 %collective-permute-start.8 = (bf16[256,128]{1,0:T(8,128)(2,1)S(1)}, bf16[256,128]{1,0:T(8,128)(2,1)S(1)}, u32[]{:S(2)}, u32[]{:S(2)}) collective-permute-start(bf16[256,128]{1,0:T(8,128)(2,1)S(1)} %settle.1.refs_0_), channel_id=1, source_target_pairs={{0,12},{1,13},{2,14},{3,15},{4,8},{5,9},{6,10},{7,11},{8,4},{9,5},... | collective-permute-start | bytes 196616 | tf_op jit(solution)/shard_map/ppermute | solution.py:357
  35.3 0.0 collective-permute-start.7
  35.3 1.9 %collective-permute-start.6 = (bf16[256,128]{1,0:T(8,128)(2,1)S(1)}, bf16[256,128]{1,0:T(8,128)(2,1)S(1)}, u32[]{:S(2)}, u32[]{:S(2)}) collective-permute-start(bf16[256,128]{1,0:T(8,128)(2,1)S(1)} %settle.1.refs_0_), channel_id=1, source_target_pairs={{0,4},{1,5},{2,6},{3,7},{4,0},{5,1},{6,2},{7,3},{8,12},{9,13},{10,... | collective-permute-start | bytes 196616 | tf_op jit(solution)/shard_map/ppermute | solution.py:357
  37.2 2.3 %collective-permute-done.8.refs_3_ = bf16[256,128]{1,0:T(8,128)(2,1)S(1)} collective-permute-done((bf16[256,128]{1,0:T(8,128)(2,1)S(1)}, bf16[256,128]{1,0:T(8,128)(2,1)S(1)}, u32[]{:S(2)}, u32[]{:S(2)}) %collective-permute-start.8) | collective-permute-done | bytes 65568 | tf_op jit(solution)/shard_map/ppermute | solution.py:357
  39.4 1.4 %collective-permute-done.7.refs_2_ = bf16[256,128]{1,0:T(8,128)(2,1)S(1)} collective-permute-done((bf16[256,128]{1,0:T(8,128)(2,1)S(1)}, bf16[256,128]{1,0:T(8,128)(2,1)S(1)}, u32[]{:S(2)}, u32[]{:S(2)}) %collective-permute-start.7) | collective-permute-done | bytes 65568 | tf_op jit(solution)/shard_map/ppermute | solution.py:357
  40.8 0.0 collective-permute-done.6.refs_1_
  40.9 1.6 %collective-permute-start.9 = (bf16[256,512]{1,0:T(8,128)(2,1)S(1)}, bf16[256,512]{1,0:T(8,128)(2,1)S(1)}, u32[]{:S(2)}, u32[]{:S(2)}) collective-permute-start(bf16[256,512]{1,0:T(8,128)(2,1)S(1)} %join.2.after.refs_0_), channel_id=1, source_target_pairs={{0,2},{1,3},{2,0},{3,1},{4,6},{5,7},{6,4},{7,5},{8,10},{9,11},{10,... | collective-permute-start | bytes 786440 | tf_op jit(solution)/shard_map/ppermute | solution.py:357
  42.5 2.3 %mixers.1.after.coef = f32[8,2048]{1,0:T(8,128)S(1)} custom-call(s32[1]{0:T(128)} %bitcast.place, s32[1,2048]{1,0:T(1,128)S(1)} %bitcast.7, bf16[16,128]{1,0:T(8,128)(2,1)S(1)} %get-tuple-element.32.known, bf16[272,128]{1,0:T(8,128)(2,1)S(1)} %collective-permute-done.3.first, bf16[272,128]{1,0:T(8,128)(2,1)S(1)} %collective-permute-done.4.second, ...), custom_call_target="tpu_custom_call" | custom-call | tf_op jit(solution)/shard_map/mixers/pallas_call | solution.py:69
  44.7 0.0 copy-done.1
  44.7 1.6 %pick.1._ = bf16[2048,2048]{1,0:T(8,128)(2,1)S(1)} custom-call(s32[1]{0:T(128)} %bitcast.place, s32[1,2048]{1,0:T(1,128)S(1)} %bitcast.8, f32[8,2048]{1,0:T(8,128)S(1)} %mixers.1.after.coef), custom_call_target="tpu_custom_call" | custom-call | tf_op jit(solution)/shard_map/pick/pallas_call | solution.py:69
  46.3 1.2 %collective-permute-done.9.refs_1_ = bf16[256,512]{1,0:T(8,128)(2,1)S(1)} collective-permute-done((bf16[256,512]{1,0:T(8,128)(2,1)S(1)}, bf16[256,512]{1,0:T(8,128)(2,1)S(1)}, u32[]{:S(2)}, u32[]{:S(2)}) %collective-permute-start.9) | collective-permute-done | bytes 262176 | tf_op jit(solution)/shard_map/ppermute | solution.py:357
  47.6 0.1 collective-permute-start.10
  47.7 1.2 %mate.1.mates = f32[256,2048]{1,0:T(8,128)S(1)} custom-call(bf16[256,1024]{1,0:T(8,128)(2,1)S(1)} %join.3.mine, bf16[2048,2048]{1,0:T(8,128)(2,1)S(1)} %pick.1._), custom_call_target="tpu_custom_call" | custom-call | tf_op jit(solution)/shard_map/mate/pallas_call | solution.py:69
  48.9 0.6 %collective-permute-done.10.theirs = bf16[256,1024]{1,0:T(8,128)(2,1)S(1)} collective-permute-done((bf16[256,1024]{1,0:T(8,128)(2,1)S(1)}, bf16[256,1024]{1,0:T(8,128)(2,1)S(1)}, u32[]{:S(2)}, u32[]{:S(2)}) %collective-permute-start.10) | collective-permute-done | bytes 524320 | tf_op jit(solution)/shard_map/ppermute | solution.py:357
  49.6 3.5 %expand.1 = bf16[1024,256]{1,0:T(8,128)(2,1)} custom-call(s32[1]{0:T(128)} %bitcast.place, bf16[256,1024]{1,0:T(8,128)(2,1)S(1)} %join.3.mine, bf16[256,1024]{1,0:T(8,128)(2,1)S(1)} %collective-permute-done.10.theirs, f32[256,2048]{1,0:T(8,128)S(1)} %mate.1.mates, bf16[2048,2048]{1,0:T(8,128)(2,1)S(1)} %pick.1._, f32[8,2048]{1,0:T(8,128)S(1)} %mixers.1.after.coef, ...), custom_call_target="tpu_custom_call" | custom-call | tf_op jit(solution)/shard_map/expand/pallas_call | solution.py:69
  (3 shorter events, 0.1 us)
Async XLA Ops:
  0.0 6.2 %copy-start = (s32[2048]{0:T(1024)S(1)}, s32[2048]{0:T(1024)}, u32[]{:S(2)}) copy-start(s32[2048]{0:T(1024)} %param.14) | copy-start | bytes 24580
  5.7 3.8 %collective-permute-start = (bf16[912,512]{1,0:T(8,128)(2,1)S(1)}, bf16[912,512]{1,0:T(8,128)(2,1)S(1)}, u32[]{:S(2)}, u32[]{:S(2)}) collective-permute-start(bf16[912,512]{1,0:T(8,128)(2,1)S(1)} %get-tuple-element.25), channel_id=1, source_target_pairs={{0,1},{1,0},{2,3},{3,2},{4,5},{5,4},{6,7},{7,6},{8,9},{9,8},{10,11... | collective-permute-start | bytes 2801672 | tf_op jit(solution)/shard_map/ppermute | solution.py:357
  11.9 9.9 %collective-permute-start.2 = (bf16[272,512]{1,0:T(8,128)(2,1)S(1)}, bf16[272,512]{1,0:T(8,128)(2,1)S(1)}, u32[]{:S(2)}, u32[]{:S(2)}) collective-permute-start(bf16[272,512]{1,0:T(8,128)(2,1)S(1)} %respond.2.after), channel_id=1, source_target_pairs={{0,2},{1,3},{2,0},{3,1},{4,6},{5,7},{6,4},{7,5},{8,10},{9,11},{10,... | collective-permute-start | bytes 835592 | tf_op jit(solution)/shard_map/ppermute | solution.py:357
  15.6 3.1 %collective-permute-start.1 = (bf16[896,512]{1,0:T(8,128)(2,1)S(1)}, bf16[896,512]{1,0:T(8,128)(2,1)S(1)}, u32[]{:S(2)}, u32[]{:S(2)}) collective-permute-start(bf16[896,512]{1,0:T(8,128)(2,1)S(1)} %project_rest.1), channel_id=1, source_target_pairs={{0,1},{1,0},{2,3},{3,2},{4,5},{5,4},{6,7},{7,6},{8,9},{9,8},{10,11... | collective-permute-start | bytes 2752520 | tf_op jit(solution)/shard_map/ppermute | solution.py:357
  21.2 23.5 %copy-start.1 = (s32[2048]{0:T(1024)S(1)}, s32[2048]{0:T(1024)}, u32[]{:S(2)}) copy-start(s32[2048]{0:T(1024)} %param.15) | copy-start | bytes 24580
  21.9 6.9 %collective-permute-start.3 = (bf16[272,128]{1,0:T(8,128)(2,1)S(1)}, bf16[272,128]{1,0:T(8,128)(2,1)S(1)}, u32[]{:S(2)}, u32[]{:S(2)}) collective-permute-start(bf16[272,128]{1,0:T(8,128)(2,1)S(1)} %get-tuple-element.33), channel_id=1, source_target_pairs={{0,12},{1,5},{2,14},{3,7},{4,8},{5,1},{6,10},{7,3},{8,4},{9,13},{1... | collective-permute-start | bytes 208904 | tf_op jit(solution)/shard_map/ppermute | solution.py:357
  25.8 6.8 %collective-permute-start.4 = (bf16[272,128]{1,0:T(8,128)(2,1)S(1)}, bf16[272,128]{1,0:T(8,128)(2,1)S(1)}, u32[]{:S(2)}, u32[]{:S(2)}) collective-permute-start(bf16[272,128]{1,0:T(8,128)(2,1)S(1)} %get-tuple-element.34), channel_id=1, source_target_pairs={{0,8},{1,9},{2,10},{3,11},{4,12},{5,13},{6,14},{7,15},{8,0},{9,1},... | collective-permute-start | bytes 208904 | tf_op jit(solution)/shard_map/ppermute | solution.py:357
  25.8 6.8 %collective-permute-start.5 = (bf16[272,128]{1,0:T(8,128)(2,1)S(1)}, bf16[272,128]{1,0:T(8,128)(2,1)S(1)}, u32[]{:S(2)}, u32[]{:S(2)}) collective-permute-start(bf16[272,128]{1,0:T(8,128)(2,1)S(1)} %get-tuple-element.35), channel_id=1, source_target_pairs={{0,4},{1,13},{2,6},{3,15},{4,0},{5,9},{6,2},{7,11},{8,12},{9,5},{1... | collective-permute-start | bytes 208904 | tf_op jit(solution)/shard_map/ppermute | solution.py:357
  32.7 6.7 %collective-permute-start.8 = (bf16[256,128]{1,0:T(8,128)(2,1)S(1)}, bf16[256,128]{1,0:T(8,128)(2,1)S(1)}, u32[]{:S(2)}, u32[]{:S(2)}) collective-permute-start(bf16[256,128]{1,0:T(8,128)(2,1)S(1)} %settle.1.refs_0_), channel_id=1, source_target_pairs={{0,12},{1,13},{2,14},{3,15},{4,8},{5,9},{6,10},{7,11},{8,4},{9,5},... | collective-permute-start | bytes 196616 | tf_op jit(solution)/shard_map/ppermute | solution.py:357
  35.3 5.6 %collective-permute-start.7 = (bf16[256,128]{1,0:T(8,128)(2,1)S(1)}, bf16[256,128]{1,0:T(8,128)(2,1)S(1)}, u32[]{:S(2)}, u32[]{:S(2)}) collective-permute-start(bf16[256,128]{1,0:T(8,128)(2,1)S(1)} %settle.1.refs_0_), channel_id=1, source_target_pairs={{0,8},{1,9},{2,10},{3,11},{4,12},{5,13},{6,14},{7,15},{8,0},{9,1},... | collective-permute-start | bytes 196616 | tf_op jit(solution)/shard_map/ppermute | solution.py:357
  35.3 5.6 %collective-permute-start.6 = (bf16[256,128]{1,0:T(8,128)(2,1)S(1)}, bf16[256,128]{1,0:T(8,128)(2,1)S(1)}, u32[]{:S(2)}, u32[]{:S(2)}) collective-permute-start(bf16[256,128]{1,0:T(8,128)(2,1)S(1)} %settle.1.refs_0_), channel_id=1, source_target_pairs={{0,4},{1,5},{2,6},{3,7},{4,0},{5,1},{6,2},{7,3},{8,12},{9,13},{10,... | collective-permute-start | bytes 196616 | tf_op jit(solution)/shard_map/ppermute | solution.py:357
  40.9 6.7 %collective-permute-start.9 = (bf16[256,512]{1,0:T(8,128)(2,1)S(1)}, bf16[256,512]{1,0:T(8,128)(2,1)S(1)}, u32[]{:S(2)}, u32[]{:S(2)}) collective-permute-start(bf16[256,512]{1,0:T(8,128)(2,1)S(1)} %join.2.after.refs_0_), channel_id=1, source_target_pairs={{0,2},{1,3},{2,0},{3,1},{4,6},{5,7},{6,4},{7,5},{8,10},{9,11},{10,... | collective-permute-start | bytes 786440 | tf_op jit(solution)/shard_map/ppermute | solution.py:357
  47.6 2.0 %collective-permute-start.10 = (bf16[256,1024]{1,0:T(8,128)(2,1)S(1)}, bf16[256,1024]{1,0:T(8,128)(2,1)S(1)}, u32[]{:S(2)}, u32[]{:S(2)}) collective-permute-start(bf16[256,1024]{1,0:T(8,128)(2,1)S(1)} %join.3.mine), channel_id=1, source_target_pairs={{0,1},{1,0},{2,3},{3,2},{4,5},{5,4},{6,7},{7,6},{8,9},{9,8},{10,11... | collective-permute-start | bytes 1572872 | tf_op jit(solution)/shard_map/ppermute | solution.py:357

commit v13 on v12

--- a/solution.py
+++ b/solution.py
@@ -107,7 +107,14 @@
     start, later = quarter_start(place, 1, 2 * half), quarter_start(place, 0, 2 * half)
     base = (1 - (place[0] & 1)) * half
     step = TILE
-    pairs = [(forward_far, forward), (loads_far, loads)]
+    top, left = slice(0, hist // 2), slice(0, step)
+    low, right = slice(hist // 2, hist), slice(step, rows)
+    pairs = [
+        (forward_far.at[top, :], forward.at[top, :]),
+        (loads_far.at[left, :], loads.at[left, :]),
+        (loads_far.at[right, :], loads.at[right, :]),
+        (forward_far.at[low, :], forward.at[low, :]),
+    ]
     first = len(pairs)
     pairs += [
         (coef_far, coef),
@@ -120,16 +127,15 @@
     for copy in copies[:first]:
         copy.start()
     copies[0].wait()
-    for copy in copies[1:first]:
-        copy.wait()
+    copies[1].wait()
+    lft[top, left] = dot(forward[top, :], loads[left, :], NT).astype(BF)
+    copies[2].wait()
     for copy in copies[first:]:
         copy.start()
-
-    @pl.loop(0, rows // step)
-    def _(j):
-        here = block(j * step, step)
-        lft[:, here] = dot(forward[...], loads[here, :], NT).astype(BF)
-
+    lft[top, right] = dot(forward[top, :], loads[right, :], NT).astype(BF)
+    copies[3].wait()
+    for part in (left, right):
+        lft[low, part] = dot(forward[low, :], loads[part, :], NT).astype(BF)
     for copy in copies[first : first + 3]:
         copy.wait()
     count = taps.shape[0] - 1
@@ -314,6 +320,12 @@
     mixers(order, mask_of(place, devices, order.shape[1]), held, coef)
 
 
+def line_kernel(place, total, first, second, third, out):
+    size = total.shape[1]
+    for d, part in zip((0, *turns_of(place[0] & 1)), (total, first, second, third)):
+        out[:, block(d * size, size)] = part[...]
+
+
 def join_kernel(*refs):
     *parts, out = refs
     start = 0
@@ -374,7 +386,7 @@
         place, loads, forward, shapes, taps, offsets, coef, far=range(1, 7),
         scratch=[
             pltpu.VMEM(loads.shape, BF), pltpu.VMEM(forward.shape, BF), pltpu.VMEM(taps.shape, F32),
-            pltpu.VMEM(offsets.shape, I32), pltpu.SemaphoreType.DMA((7,)),
+            pltpu.VMEM(offsets.shape, I32), pltpu.SemaphoreType.DMA((9,)),
         ],
         limit=24,
     )
@@ -413,8 +425,8 @@
         ways = zip(turns_of(0), turns_of(1))
         parts = [swap(part, devices, 4 * even, 4 * odd) for part, (even, odd) in zip(parts, ways)]
         total = call(settle_kernel, "settle", [array(W, size)], keep, *parts, scalars=0)[0]
-        spread = [swap(total, devices, 4 * d) for d in (1, 2, 3)]
-        resp = join(total, *spread)
+        spread = [swap(total, devices, 4 * even, 4 * odd) for even, odd in reversed(list(zip(turns_of(0), turns_of(1))))]
+        resp = call(line_kernel, "line", [array(W, quarter)], place, total, *reversed(spread))[0]
         mode_coef = call(
             mixers_kernel, "mixers", [array(8, modes, dtype=F32)],
             place, order, known, *parts, resp, scratch=[pltpu.VMEM((8, modes), F32)],

time: 53.2 us -> 53.8 us (1.011)
  waiting for transfers between devices: 12.3 us -> 13.2 us
    ppermute x11, waiting for transfers between devices: 12.3 us -> 13.2 us  [swap(): lax.ppermute(x, 'frdm', [(i, i ^ (odd if i & 1 else bits)) for i in range...]
  transfers between devices with their start and end apart: 11 -> 11, of which waited for: 7 -> 7; matrix products, arithmetic and copies ran while one was open for 0% -> 0% of each run, Pallas kernels for 28% -> 27%
where the time goes in v13:
time: 53.8 us; the launch traced here: 53.6 us
  Pallas kernels  26.2 us (49%)
  starting transfers between devices  14 us (26%)
  waiting for transfers between devices  13.2 us (25%)
    pallas_call x14, Pallas kernels, call(): pl.pallas_call(kernel, in_specs=places, out_specs=[vmem] * len(out_shape)...  26.2 us
    ppermute x11, starting transfers between devices, swap(): lax.ppermute(x, 'frdm', [(i, i ^ (odd if i & 1 else bits)) for i in range...  14 us
    ppermute x11, waiting for transfers between devices, swap(): lax.ppermute(x, 'frdm', [(i, i ^ (odd if i & 1 else bits)) for i in range...  13.2 us
  transfers between devices with their start and end apart: 11, of which 7 were waited for; matrix products, arithmetic and copies ran while one was open for 0% of the time, Pallas kernels for 27%

profile of v13, /device:TPU:0, one launch (start us, length us, event | category | flops | bytes accessed | tf_op | source)
XLA Modules:
  0.0 53.6 jit_solution(8147704201538596122)
XLA Ops:
  0.0 0.0 copy-start
  0.0 5.4 %project.1 = (bf16[912,512]{1,0:T(8,128)(2,1)S(1)}, bf16[896,1024]{1,0:T(8,128)(2,1)S(1)}, bf16[1024,1024]{1,0:T(8,128)(2,1)S(1)}, bf16[528,2048]{1,0:T(8,128)(2,1)S(1)}, bf16[2,128]{1,0:T(2,128)(2,1)S(1)}) custom-call(s32[1]{0:T(128)} %bitcast.place, bf16[1024,896]{1,0:T(8,128)(2,1)} %loads_far.1, bf16[896,896]{1,0:T(8,128)(2,1)} %constant.14.clone.forward_far, ...), custom_call_target="tpu_custom_call" | custom-call | tf_op jit(solution)/shard_map/project/pallas_call | solution.py:69
  5.4 0.5 collective-permute-start
  5.9 0.0 copy-done
  5.9 3.3 %spectrum.1 = (f32[896,512]{1,0:T(8,128)S(1)}, bf16[1024,1024]{1,0:T(8,128)(2,1)S(1)}, bf16[896,1024]{1,0:T(8,128)(2,1)S(1)}, bf16[896,128]{1,0:T(8,128)(2,1)S(1...) custom-call(s32[1]{0:T(128)} %bitcast.place, bf16[528,2048]{1,0:T(8,128)(2,1)S(1)} %get-tuple-element.22.stack, ...), custom_call_target="tpu_custom_call" | custom-call | tf_op jit(solution)/shard_map/spectrum/pallas_call | solution.py:69
  9.2 0.0 collective-permute-done.other
  9.2 2.4 %respond.2.after = bf16[272,512]{1,0:T(8,128)(2,1)S(1)} custom-call(s32[1]{0:T(128)} %bitcast.place, bf16[896,1024]{1,0:T(8,128)(2,1)S(1)} %get-tuple-element.21.lft, bf16[1024,1024]{1,0:T(8,128)(2,1)S(1)} %get-tuple-element.23.shapes.near, bf16[912,512]{1,0:T(8,128)(2,1)S(1)} %collective-permute-done.other, f32[896,512]{1,0:T(8,128)S(1)} %get-tuple-element.26.spec, ...), custom_call_target="tpu_custom_call" | custom-call | tf_op jit(solution)/shard_map/respond/pallas_call | solution.py:69
  11.6 2.6 %collective-permute-start.2 = (bf16[272,512]{1,0:T(8,128)(2,1)S(1)}, bf16[272,512]{1,0:T(8,128)(2,1)S(1)}, u32[]{:S(2)}, u32[]{:S(2)}) collective-permute-start(bf16[272,512]{1,0:T(8,128)(2,1)S(1)} %respond.2.after), channel_id=1, source_target_pairs={{0,2},{1,3},{2,0},{3,1},{4,6},{5,7},{6,4},{7,5},{8,10},{9,11},{10,... | collective-permute-start | bytes 835592 | tf_op jit(solution)/shard_map/ppermute | solution.py:369
  14.2 1.1 %project_rest.1 = bf16[896,512]{1,0:T(8,128)(2,1)S(1)} custom-call(s32[1]{0:T(128)} %bitcast.place, bf16[896,1024]{1,0:T(8,128)(2,1)S(1)} %get-tuple-element.21.lft, bf16[1024,1024]{1,0:T(8,128)(2,1)S(1)} %get-tuple-element.24.shapes.far, bf16[272,512]{1,0:T(8,128)(2,1)S(1)} %respond.2.after), custom_call_target="tpu_custom_call" | custom-call | flops 3758096384 | tf_op jit(solution)/shard_map/project_rest/pallas_call | solution.py:69
  15.3 0.3 collective-permute-start.1
  15.6 2.9 %spectrum_rest.1.spec = f32[896,512]{1,0:T(8,128)S(1)} custom-call(s32[1]{0:T(128)} %bitcast.place, bf16[528,2048]{1,0:T(8,128)(2,1)S(1)} %get-tuple-element.22.stack, s32[1,2048]{1,0:T(1,128)S(1)} %bitcast.6, bf16[896,1024]{1,0:T(8,128)(2,1)S(1)} %get-tuple-element.29.table, bf16[896,128]{1,0:T(8,128)(2,1)S(1)} %get-tuple-element.30.last, ...), custom_call_target="tpu_custom_call" | custom-call | flops 20000000000 | tf_op jit(solution)/shard_map/spectrum_rest/pallas_call | solution.py:69
  18.4 0.0 collective-permute-done.1.other
  18.5 2.4 %respond.3.own = f32[256,512]{1,0:T(8,128)S(1)} custom-call(s32[1]{0:T(128)} %bitcast.place, bf16[896,1024]{1,0:T(8,128)(2,1)S(1)} %get-tuple-element.21.lft, bf16[1024,1024]{1,0:T(8,128)(2,1)S(1)} %get-tuple-element.23.shapes.near, bf16[896,512]{1,0:T(8,128)(2,1)S(1)} %collective-permute-done.1.other, f32[896,512]{1,0:T(8,128)S(1)} %spectrum_rest.1.spec, ...), custom_call_target="tpu_custom_call" | custom-call | tf_op jit(solution)/shard_map/respond/pallas_call | solution.py:69
  20.8 0.0 copy-start.1
  20.9 0.6 %collective-permute-done.2.got = bf16[272,512]{1,0:T(8,128)(2,1)S(1)} collective-permute-done((bf16[272,512]{1,0:T(8,128)(2,1)S(1)}, bf16[272,512]{1,0:T(8,128)(2,1)S(1)}, u32[]{:S(2)}, u32[]{:S(2)}) %collective-permute-start.2) | collective-permute-done | bytes 278560 | tf_op jit(solution)/shard_map/ppermute | solution.py:369
  21.5 0.1 fold.1
  21.6 3.9 %collective-permute-start.3 = (bf16[272,128]{1,0:T(8,128)(2,1)S(1)}, bf16[272,128]{1,0:T(8,128)(2,1)S(1)}, u32[]{:S(2)}, u32[]{:S(2)}) collective-permute-start(bf16[272,128]{1,0:T(8,128)(2,1)S(1)} %get-tuple-element.33), channel_id=1, source_target_pairs={{0,12},{1,5},{2,14},{3,7},{4,8},{5,1},{6,10},{7,3},{8,4},{9,13},{1... | collective-permute-start | bytes 208904 | tf_op jit(solution)/shard_map/ppermute | solution.py:369
  25.5 0.0 collective-permute-start.4
  25.5 0.6 %collective-permute-start.5 = (bf16[272,128]{1,0:T(8,128)(2,1)S(1)}, bf16[272,128]{1,0:T(8,128)(2,1)S(1)}, u32[]{:S(2)}, u32[]{:S(2)}) collective-permute-start(bf16[272,128]{1,0:T(8,128)(2,1)S(1)} %get-tuple-element.35), channel_id=1, source_target_pairs={{0,4},{1,13},{2,6},{3,15},{4,0},{5,9},{6,2},{7,11},{8,12},{9,5},{1... | collective-permute-start | bytes 208904 | tf_op jit(solution)/shard_map/ppermute | solution.py:369
  26.1 2.4 %collective-permute-done.3.first = bf16[272,128]{1,0:T(8,128)(2,1)S(1)} collective-permute-done((bf16[272,128]{1,0:T(8,128)(2,1)S(1)}, bf16[272,128]{1,0:T(8,128)(2,1)S(1)}, u32[]{:S(2)}, u32[]{:S(2)}) %collective-permute-start.3) | collective-permute-done | bytes 69664 | tf_op jit(solution)/shard_map/ppermute | solution.py:369
  28.6 3.8 %collective-permute-done.4.second = bf16[272,128]{1,0:T(8,128)(2,1)S(1)} collective-permute-done((bf16[272,128]{1,0:T(8,128)(2,1)S(1)}, bf16[272,128]{1,0:T(8,128)(2,1)S(1)}, u32[]{:S(2)}, u32[]{:S(2)}) %collective-permute-start.4) | collective-permute-done | bytes 69664 | tf_op jit(solution)/shard_map/ppermute | solution.py:369
  32.4 0.0 collective-permute-done.5.third
  32.4 0.1 collective-permute-start.8
  32.5 3.0 %collective-permute-start.7 = (bf16[256,128]{1,0:T(8,128)(2,1)S(1)}, bf16[256,128]{1,0:T(8,128)(2,1)S(1)}, u32[]{:S(2)}, u32[]{:S(2)}) collective-permute-start(bf16[256,128]{1,0:T(8,128)(2,1)S(1)} %settle.1.total), channel_id=1, source_target_pairs={{0,8},{1,9},{2,10},{3,11},{4,12},{5,13},{6,14},{7,15},{8,0},{9,1},... | collective-permute-start | bytes 196616 | tf_op jit(solution)/shard_map/ppermute | solution.py:369
  35.5 1.3 %collective-permute-start.6 = (bf16[256,128]{1,0:T(8,128)(2,1)S(1)}, bf16[256,128]{1,0:T(8,128)(2,1)S(1)}, u32[]{:S(2)}, u32[]{:S(2)}) collective-permute-start(bf16[256,128]{1,0:T(8,128)(2,1)S(1)} %settle.1.total), channel_id=1, source_target_pairs={{0,12},{1,5},{2,14},{3,7},{4,8},{5,1},{6,10},{7,3},{8,4},{9,13},{1... | collective-permute-start | bytes 196616 | tf_op jit(solution)/shard_map/ppermute | solution.py:369
  36.8 1.8 %collective-permute-done.8.third = bf16[256,128]{1,0:T(8,128)(2,1)S(1)} collective-permute-done((bf16[256,128]{1,0:T(8,128)(2,1)S(1)}, bf16[256,128]{1,0:T(8,128)(2,1)S(1)}, u32[]{:S(2)}, u32[]{:S(2)}) %collective-permute-start.8) | collective-permute-done | bytes 65568 | tf_op jit(solution)/shard_map/ppermute | solution.py:369
  38.6 0.0 collective-permute-done.7.second
  38.6 3.0 %collective-permute-done.6.first = bf16[256,128]{1,0:T(8,128)(2,1)S(1)} collective-permute-done((bf16[256,128]{1,0:T(8,128)(2,1)S(1)}, bf16[256,128]{1,0:T(8,128)(2,1)S(1)}, u32[]{:S(2)}, u32[]{:S(2)}) %collective-permute-start.6) | collective-permute-done | bytes 65568 | tf_op jit(solution)/shard_map/ppermute | solution.py:369
  41.6 1.6 %collective-permute-start.9 = (bf16[256,512]{1,0:T(8,128)(2,1)S(1)}, bf16[256,512]{1,0:T(8,128)(2,1)S(1)}, u32[]{:S(2)}, u32[]{:S(2)}) collective-permute-start(bf16[256,512]{1,0:T(8,128)(2,1)S(1)} %line.1.after.refs_0_), channel_id=1, source_target_pairs={{0,2},{1,3},{2,0},{3,1},{4,6},{5,7},{6,4},{7,5},{8,10},{9,11},{10,... | collective-permute-start | bytes 786440 | tf_op jit(solution)/shard_map/ppermute | solution.py:369
  43.2 2.4 %mixers.1.after.coef = f32[8,2048]{1,0:T(8,128)S(1)} custom-call(s32[1]{0:T(128)} %bitcast.place, s32[1,2048]{1,0:T(1,128)S(1)} %bitcast.7, bf16[16,128]{1,0:T(8,128)(2,1)S(1)} %get-tuple-element.32.known, bf16[272,128]{1,0:T(8,128)(2,1)S(1)} %collective-permute-done.3.first, bf16[272,128]{1,0:T(8,128)(2,1)S(1)} %collective-permute-done.4.second, ...), custom_call_target="tpu_custom_call" | custom-call | tf_op jit(solution)/shard_map/mixers/pallas_call | solution.py:69
  45.6 0.0 copy-done.1
  45.6 1.4 %pick.1._ = bf16[2048,2048]{1,0:T(8,128)(2,1)S(1)} custom-call(s32[1]{0:T(128)} %bitcast.place, s32[1,2048]{1,0:T(1,128)S(1)} %bitcast.8, f32[8,2048]{1,0:T(8,128)S(1)} %mixers.1.after.coef), custom_call_target="tpu_custom_call" | custom-call | tf_op jit(solution)/shard_map/pick/pallas_call | solution.py:69
  47.0 1.0 %collective-permute-done.9.refs_1_ = bf16[256,512]{1,0:T(8,128)(2,1)S(1)} collective-permute-done((bf16[256,512]{1,0:T(8,128)(2,1)S(1)}, bf16[256,512]{1,0:T(8,128)(2,1)S(1)}, u32[]{:S(2)}, u32[]{:S(2)}) %collective-permute-start.9) | collective-permute-done | bytes 262176 | tf_op jit(solution)/shard_map/ppermute | solution.py:369
  48.1 0.1 collective-permute-start.10
  48.2 1.2 %mate.1.mates = f32[256,2048]{1,0:T(8,128)S(1)} custom-call(bf16[256,1024]{1,0:T(8,128)(2,1)S(1)} %join.1.mine, bf16[2048,2048]{1,0:T(8,128)(2,1)S(1)} %pick.1._), custom_call_target="tpu_custom_call" | custom-call | tf_op jit(solution)/shard_map/mate/pallas_call | solution.py:69
  49.4 0.6 %collective-permute-done.10.theirs = bf16[256,1024]{1,0:T(8,128)(2,1)S(1)} collective-permute-done((bf16[256,1024]{1,0:T(8,128)(2,1)S(1)}, bf16[256,1024]{1,0:T(8,128)(2,1)S(1)}, u32[]{:S(2)}, u32[]{:S(2)}) %collective-permute-start.10) | collective-permute-done | bytes 524320 | tf_op jit(solution)/shard_map/ppermute | solution.py:369
  50.1 3.5 %expand.1 = bf16[1024,256]{1,0:T(8,128)(2,1)} custom-call(s32[1]{0:T(128)} %bitcast.place, bf16[256,1024]{1,0:T(8,128)(2,1)S(1)} %join.1.mine, bf16[256,1024]{1,0:T(8,128)(2,1)S(1)} %collective-permute-done.10.theirs, f32[256,2048]{1,0:T(8,128)S(1)} %mate.1.mates, bf16[2048,2048]{1,0:T(8,128)(2,1)S(1)} %pick.1._, f32[8,2048]{1,0:T(8,128)S(1)} %mixers.1.after.coef, ...), custom_call_target="tpu_custom_call" | custom-call | tf_op jit(solution)/shard_map/expand/pallas_call | solution.py:69
  (3 shorter events, 0.1 us)
Async XLA Ops:
  0.0 5.9 %copy-start = (s32[2048]{0:T(1024)S(1)}, s32[2048]{0:T(1024)}, u32[]{:S(2)}) copy-start(s32[2048]{0:T(1024)} %param.14) | copy-start | bytes 24580
  5.4 3.8 %collective-permute-start = (bf16[912,512]{1,0:T(8,128)(2,1)S(1)}, bf16[912,512]{1,0:T(8,128)(2,1)S(1)}, u32[]{:S(2)}, u32[]{:S(2)}) collective-permute-start(bf16[912,512]{1,0:T(8,128)(2,1)S(1)} %get-tuple-element.25), channel_id=1, source_target_pairs={{0,1},{1,0},{2,3},{3,2},{4,5},{5,4},{6,7},{7,6},{8,9},{9,8},{10,11... | collective-permute-start | bytes 2801672 | tf_op jit(solution)/shard_map/ppermute | solution.py:369
  11.6 9.9 %collective-permute-start.2 = (bf16[272,512]{1,0:T(8,128)(2,1)S(1)}, bf16[272,512]{1,0:T(8,128)(2,1)S(1)}, u32[]{:S(2)}, u32[]{:S(2)}) collective-permute-start(bf16[272,512]{1,0:T(8,128)(2,1)S(1)} %respond.2.after), channel_id=1, source_target_pairs={{0,2},{1,3},{2,0},{3,1},{4,6},{5,7},{6,4},{7,5},{8,10},{9,11},{10,... | collective-permute-start | bytes 835592 | tf_op jit(solution)/shard_map/ppermute | solution.py:369
  15.3 3.2 %collective-permute-start.1 = (bf16[896,512]{1,0:T(8,128)(2,1)S(1)}, bf16[896,512]{1,0:T(8,128)(2,1)S(1)}, u32[]{:S(2)}, u32[]{:S(2)}) collective-permute-start(bf16[896,512]{1,0:T(8,128)(2,1)S(1)} %project_rest.1), channel_id=1, source_target_pairs={{0,1},{1,0},{2,3},{3,2},{4,5},{5,4},{6,7},{7,6},{8,9},{9,8},{10,11... | collective-permute-start | bytes 2752520 | tf_op jit(solution)/shard_map/ppermute | solution.py:369
  20.8 24.8 %copy-start.1 = (s32[2048]{0:T(1024)S(1)}, s32[2048]{0:T(1024)}, u32[]{:S(2)}) copy-start(s32[2048]{0:T(1024)} %param.15) | copy-start | bytes 24580
  21.6 7.0 %collective-permute-start.3 = (bf16[272,128]{1,0:T(8,128)(2,1)S(1)}, bf16[272,128]{1,0:T(8,128)(2,1)S(1)}, u32[]{:S(2)}, u32[]{:S(2)}) collective-permute-start(bf16[272,128]{1,0:T(8,128)(2,1)S(1)} %get-tuple-element.33), channel_id=1, source_target_pairs={{0,12},{1,5},{2,14},{3,7},{4,8},{5,1},{6,10},{7,3},{8,4},{9,13},{1... | collective-permute-start | bytes 208904 | tf_op jit(solution)/shard_map/ppermute | solution.py:369
  25.5 6.9 %collective-permute-start.4 = (bf16[272,128]{1,0:T(8,128)(2,1)S(1)}, bf16[272,128]{1,0:T(8,128)(2,1)S(1)}, u32[]{:S(2)}, u32[]{:S(2)}) collective-permute-start(bf16[272,128]{1,0:T(8,128)(2,1)S(1)} %get-tuple-element.34), channel_id=1, source_target_pairs={{0,8},{1,9},{2,10},{3,11},{4,12},{5,13},{6,14},{7,15},{8,0},{9,1},... | collective-permute-start | bytes 208904 | tf_op jit(solution)/shard_map/ppermute | solution.py:369
  25.5 6.9 %collective-permute-start.5 = (bf16[272,128]{1,0:T(8,128)(2,1)S(1)}, bf16[272,128]{1,0:T(8,128)(2,1)S(1)}, u32[]{:S(2)}, u32[]{:S(2)}) collective-permute-start(bf16[272,128]{1,0:T(8,128)(2,1)S(1)} %get-tuple-element.35), channel_id=1, source_target_pairs={{0,4},{1,13},{2,6},{3,15},{4,0},{5,9},{6,2},{7,11},{8,12},{9,5},{1... | collective-permute-start | bytes 208904 | tf_op jit(solution)/shard_map/ppermute | solution.py:369
  32.4 6.2 %collective-permute-start.8 = (bf16[256,128]{1,0:T(8,128)(2,1)S(1)}, bf16[256,128]{1,0:T(8,128)(2,1)S(1)}, u32[]{:S(2)}, u32[]{:S(2)}) collective-permute-start(bf16[256,128]{1,0:T(8,128)(2,1)S(1)} %settle.1.total), channel_id=1, source_target_pairs={{0,4},{1,13},{2,6},{3,15},{4,0},{5,9},{6,2},{7,11},{8,12},{9,5},{1... | collective-permute-start | bytes 196616 | tf_op jit(solution)/shard_map/ppermute | solution.py:369
  32.5 6.1 %collective-permute-start.7 = (bf16[256,128]{1,0:T(8,128)(2,1)S(1)}, bf16[256,128]{1,0:T(8,128)(2,1)S(1)}, u32[]{:S(2)}, u32[]{:S(2)}) collective-permute-start(bf16[256,128]{1,0:T(8,128)(2,1)S(1)} %settle.1.total), channel_id=1, source_target_pairs={{0,8},{1,9},{2,10},{3,11},{4,12},{5,13},{6,14},{7,15},{8,0},{9,1},... | collective-permute-start | bytes 196616 | tf_op jit(solution)/shard_map/ppermute | solution.py:369
  35.5 6.1 %collective-permute-start.6 = (bf16[256,128]{1,0:T(8,128)(2,1)S(1)}, bf16[256,128]{1,0:T(8,128)(2,1)S(1)}, u32[]{:S(2)}, u32[]{:S(2)}) collective-permute-start(bf16[256,128]{1,0:T(8,128)(2,1)S(1)} %settle.1.total), channel_id=1, source_target_pairs={{0,12},{1,5},{2,14},{3,7},{4,8},{5,1},{6,10},{7,3},{8,4},{9,13},{1... | collective-permute-start | bytes 196616 | tf_op jit(solution)/shard_map/ppermute | solution.py:369
  41.6 6.4 %collective-permute-start.9 = (bf16[256,512]{1,0:T(8,128)(2,1)S(1)}, bf16[256,512]{1,0:T(8,128)(2,1)S(1)}, u32[]{:S(2)}, u32[]{:S(2)}) collective-permute-start(bf16[256,512]{1,0:T(8,128)(2,1)S(1)} %line.1.after.refs_0_), channel_id=1, source_target_pairs={{0,2},{1,3},{2,0},{3,1},{4,6},{5,7},{6,4},{7,5},{8,10},{9,11},{10,... | collective-permute-start | bytes 786440 | tf_op jit(solution)/shard_map/ppermute | solution.py:369
  48.1 2.0 %collective-permute-start.10 = (bf16[256,1024]{1,0:T(8,128)(2,1)S(1)}, bf16[256,1024]{1,0:T(8,128)(2,1)S(1)}, u32[]{:S(2)}, u32[]{:S(2)}) collective-permute-start(bf16[256,1024]{1,0:T(8,128)(2,1)S(1)} %join.1.mine), channel_id=1, source_target_pairs={{0,1},{1,0},{2,3},{3,2},{4,5},{5,4},{6,7},{7,6},{8,9},{9,8},{10,11... | collective-permute-start | bytes 1572872 | tf_op jit(solution)/shard_map/ppermute | solution.py:369

commit v14 on v13

--- a/solution.py
+++ b/solution.py
@@ -320,7 +320,7 @@
     mixers(order, mask_of(place, devices, order.shape[1]), held, coef)
 
 
-def line_kernel(place, total, first, second, third, out):
+def line_kernel(place, total, third, second, first, out):
     size = total.shape[1]
     for d, part in zip((0, *turns_of(place[0] & 1)), (total, first, second, third)):
         out[:, block(d * size, size)] = part[...]
@@ -425,7 +425,7 @@
         ways = zip(turns_of(0), turns_of(1))
         parts = [swap(part, devices, 4 * even, 4 * odd) for part, (even, odd) in zip(parts, ways)]
         total = call(settle_kernel, "settle", [array(W, size)], keep, *parts, scalars=0)[0]
-        spread = [swap(total, devices, 4 * even, 4 * odd) for even, odd in reversed(list(zip(turns_of(0), turns_of(1))))]
+        spread = [swap(total, devices, 4 * even, 4 * odd) for even, odd in zip(turns_of(0), turns_of(1))]
         resp = call(line_kernel, "line", [array(W, quarter)], place, total, *reversed(spread))[0]
         mode_coef = call(
             mixers_kernel, "mixers", [array(8, modes, dtype=F32)],

time: 53.8 us -> 53.3 us (level)
  transfers between devices with their start and end apart: 11 -> 11, of which waited for: 7 -> 7; matrix products, arithmetic and copies ran while one was open for 0% -> 0% of each run, Pallas kernels for 27% -> 28%
where the time goes in v14:
time: 53.3 us; the launch traced here: 53.2 us
  Pallas kernels  26.2 us (49%)
  starting transfers between devices  14 us (26%)
  waiting for transfers between devices  12.8 us (24%)
    pallas_call x14, Pallas kernels, call(): pl.pallas_call(kernel, in_specs=places, out_specs=[vmem] * len(out_shape)...  26.2 us
    ppermute x11, starting transfers between devices, swap(): lax.ppermute(x, 'frdm', [(i, i ^ (odd if i & 1 else bits)) for i in range...  14 us
    ppermute x11, waiting for transfers between devices, swap(): lax.ppermute(x, 'frdm', [(i, i ^ (odd if i & 1 else bits)) for i in range...  12.8 us
  transfers between devices with their start and end apart: 11, of which 7 were waited for; matrix products, arithmetic and copies ran while one was open for 0% of the time, Pallas kernels for 28%

profile of v14, /device:TPU:0, one launch (start us, length us, event | category | flops | bytes accessed | tf_op | source)
XLA Modules:
  0.0 53.2 jit_solution(6052979185954998140)
XLA Ops:
  0.0 0.0 copy-start
  0.0 5.4 %project.1 = (bf16[912,512]{1,0:T(8,128)(2,1)S(1)}, bf16[896,1024]{1,0:T(8,128)(2,1)S(1)}, bf16[1024,1024]{1,0:T(8,128)(2,1)S(1)}, bf16[528,2048]{1,0:T(8,128)(2,1)S(1)}, bf16[2,128]{1,0:T(2,128)(2,1)S(1)}) custom-call(s32[1]{0:T(128)} %bitcast.place, bf16[1024,896]{1,0:T(8,128)(2,1)} %loads_far.1, bf16[896,896]{1,0:T(8,128)(2,1)} %constant.14.clone.forward_far, ...), custom_call_target="tpu_custom_call" | custom-call | tf_op jit(solution)/shard_map/project/pallas_call | solution.py:69
  5.4 0.5 collective-permute-start
  5.9 0.0 copy-done
  5.9 3.3 %spectrum.1 = (f32[896,512]{1,0:T(8,128)S(1)}, bf16[1024,1024]{1,0:T(8,128)(2,1)S(1)}, bf16[896,1024]{1,0:T(8,128)(2,1)S(1)}, bf16[896,128]{1,0:T(8,128)(2,1)S(1...) custom-call(s32[1]{0:T(128)} %bitcast.place, bf16[528,2048]{1,0:T(8,128)(2,1)S(1)} %get-tuple-element.22.stack, ...), custom_call_target="tpu_custom_call" | custom-call | tf_op jit(solution)/shard_map/spectrum/pallas_call | solution.py:69
  9.2 0.0 collective-permute-done.other
  9.2 2.4 %respond.2.after = bf16[272,512]{1,0:T(8,128)(2,1)S(1)} custom-call(s32[1]{0:T(128)} %bitcast.place, bf16[896,1024]{1,0:T(8,128)(2,1)S(1)} %get-tuple-element.21.lft, bf16[1024,1024]{1,0:T(8,128)(2,1)S(1)} %get-tuple-element.23.shapes.near, bf16[912,512]{1,0:T(8,128)(2,1)S(1)} %collective-permute-done.other, f32[896,512]{1,0:T(8,128)S(1)} %get-tuple-element.26.spec, ...), custom_call_target="tpu_custom_call" | custom-call | tf_op jit(solution)/shard_map/respond/pallas_call | solution.py:69
  11.6 2.6 %collective-permute-start.2 = (bf16[272,512]{1,0:T(8,128)(2,1)S(1)}, bf16[272,512]{1,0:T(8,128)(2,1)S(1)}, u32[]{:S(2)}, u32[]{:S(2)}) collective-permute-start(bf16[272,512]{1,0:T(8,128)(2,1)S(1)} %respond.2.after), channel_id=1, source_target_pairs={{0,2},{1,3},{2,0},{3,1},{4,6},{5,7},{6,4},{7,5},{8,10},{9,11},{10,... | collective-permute-start | bytes 835592 | tf_op jit(solution)/shard_map/ppermute | solution.py:369
  14.2 1.1 %project_rest.1 = bf16[896,512]{1,0:T(8,128)(2,1)S(1)} custom-call(s32[1]{0:T(128)} %bitcast.place, bf16[896,1024]{1,0:T(8,128)(2,1)S(1)} %get-tuple-element.21.lft, bf16[1024,1024]{1,0:T(8,128)(2,1)S(1)} %get-tuple-element.24.shapes.far, bf16[272,512]{1,0:T(8,128)(2,1)S(1)} %respond.2.after), custom_call_target="tpu_custom_call" | custom-call | flops 3758096384 | tf_op jit(solution)/shard_map/project_rest/pallas_call | solution.py:69
  15.3 0.3 collective-permute-start.1
  15.6 2.9 %spectrum_rest.1.spec = f32[896,512]{1,0:T(8,128)S(1)} custom-call(s32[1]{0:T(128)} %bitcast.place, bf16[528,2048]{1,0:T(8,128)(2,1)S(1)} %get-tuple-element.22.stack, s32[1,2048]{1,0:T(1,128)S(1)} %bitcast.6, bf16[896,1024]{1,0:T(8,128)(2,1)S(1)} %get-tuple-element.29.table, bf16[896,128]{1,0:T(8,128)(2,1)S(1)} %get-tuple-element.30.last, ...), custom_call_target="tpu_custom_call" | custom-call | flops 20000000000 | tf_op jit(solution)/shard_map/spectrum_rest/pallas_call | solution.py:69
  18.4 0.0 collective-permute-done.1.other
  18.5 2.4 %respond.3.own = f32[256,512]{1,0:T(8,128)S(1)} custom-call(s32[1]{0:T(128)} %bitcast.place, bf16[896,1024]{1,0:T(8,128)(2,1)S(1)} %get-tuple-element.21.lft, bf16[1024,1024]{1,0:T(8,128)(2,1)S(1)} %get-tuple-element.23.shapes.near, bf16[896,512]{1,0:T(8,128)(2,1)S(1)} %collective-permute-done.1.other, f32[896,512]{1,0:T(8,128)S(1)} %spectrum_rest.1.spec, ...), custom_call_target="tpu_custom_call" | custom-call | tf_op jit(solution)/shard_map/respond/pallas_call | solution.py:69
  20.8 0.0 copy-start.1
  20.9 0.6 %collective-permute-done.2.got = bf16[272,512]{1,0:T(8,128)(2,1)S(1)} collective-permute-done((bf16[272,512]{1,0:T(8,128)(2,1)S(1)}, bf16[272,512]{1,0:T(8,128)(2,1)S(1)}, u32[]{:S(2)}, u32[]{:S(2)}) %collective-permute-start.2) | collective-permute-done | bytes 278560 | tf_op jit(solution)/shard_map/ppermute | solution.py:369
  21.5 0.1 fold.1
  21.6 3.9 %collective-permute-start.3 = (bf16[272,128]{1,0:T(8,128)(2,1)S(1)}, bf16[272,128]{1,0:T(8,128)(2,1)S(1)}, u32[]{:S(2)}, u32[]{:S(2)}) collective-permute-start(bf16[272,128]{1,0:T(8,128)(2,1)S(1)} %get-tuple-element.33), channel_id=1, source_target_pairs={{0,12},{1,5},{2,14},{3,7},{4,8},{5,1},{6,10},{7,3},{8,4},{9,13},{1... | collective-permute-start | bytes 208904 | tf_op jit(solution)/shard_map/ppermute | solution.py:369
  25.5 0.0 collective-permute-start.4
  25.5 0.6 %collective-permute-start.5 = (bf16[272,128]{1,0:T(8,128)(2,1)S(1)}, bf16[272,128]{1,0:T(8,128)(2,1)S(1)}, u32[]{:S(2)}, u32[]{:S(2)}) collective-permute-start(bf16[272,128]{1,0:T(8,128)(2,1)S(1)} %get-tuple-element.35), channel_id=1, source_target_pairs={{0,4},{1,13},{2,6},{3,15},{4,0},{5,9},{6,2},{7,11},{8,12},{9,5},{1... | collective-permute-start | bytes 208904 | tf_op jit(solution)/shard_map/ppermute | solution.py:369
  26.1 2.4 %collective-permute-done.3.first = bf16[272,128]{1,0:T(8,128)(2,1)S(1)} collective-permute-done((bf16[272,128]{1,0:T(8,128)(2,1)S(1)}, bf16[272,128]{1,0:T(8,128)(2,1)S(1)}, u32[]{:S(2)}, u32[]{:S(2)}) %collective-permute-start.3) | collective-permute-done | bytes 69664 | tf_op jit(solution)/shard_map/ppermute | solution.py:369
  28.6 3.8 %collective-permute-done.4.second = bf16[272,128]{1,0:T(8,128)(2,1)S(1)} collective-permute-done((bf16[272,128]{1,0:T(8,128)(2,1)S(1)}, bf16[272,128]{1,0:T(8,128)(2,1)S(1)}, u32[]{:S(2)}, u32[]{:S(2)}) %collective-permute-start.4) | collective-permute-done | bytes 69664 | tf_op jit(solution)/shard_map/ppermute | solution.py:369
  32.4 0.0 collective-permute-done.5.third
  32.4 2.5 %collective-permute-start.8 = (bf16[256,128]{1,0:T(8,128)(2,1)S(1)}, bf16[256,128]{1,0:T(8,128)(2,1)S(1)}, u32[]{:S(2)}, u32[]{:S(2)}) collective-permute-start(bf16[256,128]{1,0:T(8,128)(2,1)S(1)} %settle.1.total), channel_id=1, source_target_pairs={{0,12},{1,5},{2,14},{3,7},{4,8},{5,1},{6,10},{7,3},{8,4},{9,13},{1... | collective-permute-start | bytes 196616 | tf_op jit(solution)/shard_map/ppermute | solution.py:369
  34.9 0.0 collective-permute-start.7
  34.9 1.9 %collective-permute-start.6 = (bf16[256,128]{1,0:T(8,128)(2,1)S(1)}, bf16[256,128]{1,0:T(8,128)(2,1)S(1)}, u32[]{:S(2)}, u32[]{:S(2)}) collective-permute-start(bf16[256,128]{1,0:T(8,128)(2,1)S(1)} %settle.1.total), channel_id=1, source_target_pairs={{0,4},{1,13},{2,6},{3,15},{4,0},{5,9},{6,2},{7,11},{8,12},{9,5},{1... | collective-permute-start | bytes 196616 | tf_op jit(solution)/shard_map/ppermute | solution.py:369
  36.8 2.4 %collective-permute-done.8.first = bf16[256,128]{1,0:T(8,128)(2,1)S(1)} collective-permute-done((bf16[256,128]{1,0:T(8,128)(2,1)S(1)}, bf16[256,128]{1,0:T(8,128)(2,1)S(1)}, u32[]{:S(2)}, u32[]{:S(2)}) %collective-permute-start.8) | collective-permute-done | bytes 65568 | tf_op jit(solution)/shard_map/ppermute | solution.py:369
  39.3 1.6 %collective-permute-done.7.second = bf16[256,128]{1,0:T(8,128)(2,1)S(1)} collective-permute-done((bf16[256,128]{1,0:T(8,128)(2,1)S(1)}, bf16[256,128]{1,0:T(8,128)(2,1)S(1)}, u32[]{:S(2)}, u32[]{:S(2)}) %collective-permute-start.7) | collective-permute-done | bytes 65568 | tf_op jit(solution)/shard_map/ppermute | solution.py:369
  40.9 0.0 collective-permute-done.6.third
  40.9 1.6 %collective-permute-start.9 = (bf16[256,512]{1,0:T(8,128)(2,1)S(1)}, bf16[256,512]{1,0:T(8,128)(2,1)S(1)}, u32[]{:S(2)}, u32[]{:S(2)}) collective-permute-start(bf16[256,512]{1,0:T(8,128)(2,1)S(1)} %line.1.after.refs_0_), channel_id=1, source_target_pairs={{0,2},{1,3},{2,0},{3,1},{4,6},{5,7},{6,4},{7,5},{8,10},{9,11},{10,... | collective-permute-start | bytes 786440 | tf_op jit(solution)/shard_map/ppermute | solution.py:369
  42.5 2.4 %mixers.1.after.coef = f32[8,2048]{1,0:T(8,128)S(1)} custom-call(s32[1]{0:T(128)} %bitcast.place, s32[1,2048]{1,0:T(1,128)S(1)} %bitcast.7, bf16[16,128]{1,0:T(8,128)(2,1)S(1)} %get-tuple-element.32.known, bf16[272,128]{1,0:T(8,128)(2,1)S(1)} %collective-permute-done.3.first, bf16[272,128]{1,0:T(8,128)(2,1)S(1)} %collective-permute-done.4.second, ...), custom_call_target="tpu_custom_call" | custom-call | tf_op jit(solution)/shard_map/mixers/pallas_call | solution.py:69
  44.9 0.0 copy-done.1
  45.0 1.4 %pick.1._ = bf16[2048,2048]{1,0:T(8,128)(2,1)S(1)} custom-call(s32[1]{0:T(128)} %bitcast.place, s32[1,2048]{1,0:T(1,128)S(1)} %bitcast.8, f32[8,2048]{1,0:T(8,128)S(1)} %mixers.1.after.coef), custom_call_target="tpu_custom_call" | custom-call | tf_op jit(solution)/shard_map/pick/pallas_call | solution.py:69
  46.4 1.2 %collective-permute-done.9.refs_1_ = bf16[256,512]{1,0:T(8,128)(2,1)S(1)} collective-permute-done((bf16[256,512]{1,0:T(8,128)(2,1)S(1)}, bf16[256,512]{1,0:T(8,128)(2,1)S(1)}, u32[]{:S(2)}, u32[]{:S(2)}) %collective-permute-start.9) | collective-permute-done | bytes 262176 | tf_op jit(solution)/shard_map/ppermute | solution.py:369
  47.6 0.1 collective-permute-start.10
  47.7 1.2 %mate.1.mates = f32[256,2048]{1,0:T(8,128)S(1)} custom-call(bf16[256,1024]{1,0:T(8,128)(2,1)S(1)} %join.1.mine, bf16[2048,2048]{1,0:T(8,128)(2,1)S(1)} %pick.1._), custom_call_target="tpu_custom_call" | custom-call | tf_op jit(solution)/shard_map/mate/pallas_call | solution.py:69
  49.0 0.6 %collective-permute-done.10.theirs = bf16[256,1024]{1,0:T(8,128)(2,1)S(1)} collective-permute-done((bf16[256,1024]{1,0:T(8,128)(2,1)S(1)}, bf16[256,1024]{1,0:T(8,128)(2,1)S(1)}, u32[]{:S(2)}, u32[]{:S(2)}) %collective-permute-start.10) | collective-permute-done | bytes 524320 | tf_op jit(solution)/shard_map/ppermute | solution.py:369
  49.6 3.5 %expand.1 = bf16[1024,256]{1,0:T(8,128)(2,1)} custom-call(s32[1]{0:T(128)} %bitcast.place, bf16[256,1024]{1,0:T(8,128)(2,1)S(1)} %join.1.mine, bf16[256,1024]{1,0:T(8,128)(2,1)S(1)} %collective-permute-done.10.theirs, f32[256,2048]{1,0:T(8,128)S(1)} %mate.1.mates, bf16[2048,2048]{1,0:T(8,128)(2,1)S(1)} %pick.1._, f32[8,2048]{1,0:T(8,128)S(1)} %mixers.1.after.coef, ...), custom_call_target="tpu_custom_call" | custom-call | tf_op jit(solution)/shard_map/expand/pallas_call | solution.py:69
  (3 shorter events, 0.1 us)
Async XLA Ops:
  0.0 5.9 %copy-start = (s32[2048]{0:T(1024)S(1)}, s32[2048]{0:T(1024)}, u32[]{:S(2)}) copy-start(s32[2048]{0:T(1024)} %param.14) | copy-start | bytes 24580
  5.4 3.8 %collective-permute-start = (bf16[912,512]{1,0:T(8,128)(2,1)S(1)}, bf16[912,512]{1,0:T(8,128)(2,1)S(1)}, u32[]{:S(2)}, u32[]{:S(2)}) collective-permute-start(bf16[912,512]{1,0:T(8,128)(2,1)S(1)} %get-tuple-element.25), channel_id=1, source_target_pairs={{0,1},{1,0},{2,3},{3,2},{4,5},{5,4},{6,7},{7,6},{8,9},{9,8},{10,11... | collective-permute-start | bytes 2801672 | tf_op jit(solution)/shard_map/ppermute | solution.py:369
  11.6 9.9 %collective-permute-start.2 = (bf16[272,512]{1,0:T(8,128)(2,1)S(1)}, bf16[272,512]{1,0:T(8,128)(2,1)S(1)}, u32[]{:S(2)}, u32[]{:S(2)}) collective-permute-start(bf16[272,512]{1,0:T(8,128)(2,1)S(1)} %respond.2.after), channel_id=1, source_target_pairs={{0,2},{1,3},{2,0},{3,1},{4,6},{5,7},{6,4},{7,5},{8,10},{9,11},{10,... | collective-permute-start | bytes 835592 | tf_op jit(solution)/shard_map/ppermute | solution.py:369
  15.3 3.2 %collective-permute-start.1 = (bf16[896,512]{1,0:T(8,128)(2,1)S(1)}, bf16[896,512]{1,0:T(8,128)(2,1)S(1)}, u32[]{:S(2)}, u32[]{:S(2)}) collective-permute-start(bf16[896,512]{1,0:T(8,128)(2,1)S(1)} %project_rest.1), channel_id=1, source_target_pairs={{0,1},{1,0},{2,3},{3,2},{4,5},{5,4},{6,7},{7,6},{8,9},{9,8},{10,11... | collective-permute-start | bytes 2752520 | tf_op jit(solution)/shard_map/ppermute | solution.py:369
  20.8 24.1 %copy-start.1 = (s32[2048]{0:T(1024)S(1)}, s32[2048]{0:T(1024)}, u32[]{:S(2)}) copy-start(s32[2048]{0:T(1024)} %param.15) | copy-start | bytes 24580
  21.6 7.0 %collective-permute-start.3 = (bf16[272,128]{1,0:T(8,128)(2,1)S(1)}, bf16[272,128]{1,0:T(8,128)(2,1)S(1)}, u32[]{:S(2)}, u32[]{:S(2)}) collective-permute-start(bf16[272,128]{1,0:T(8,128)(2,1)S(1)} %get-tuple-element.33), channel_id=1, source_target_pairs={{0,12},{1,5},{2,14},{3,7},{4,8},{5,1},{6,10},{7,3},{8,4},{9,13},{1... | collective-permute-start | bytes 208904 | tf_op jit(solution)/shard_map/ppermute | solution.py:369
  25.5 6.9 %collective-permute-start.4 = (bf16[272,128]{1,0:T(8,128)(2,1)S(1)}, bf16[272,128]{1,0:T(8,128)(2,1)S(1)}, u32[]{:S(2)}, u32[]{:S(2)}) collective-permute-start(bf16[272,128]{1,0:T(8,128)(2,1)S(1)} %get-tuple-element.34), channel_id=1, source_target_pairs={{0,8},{1,9},{2,10},{3,11},{4,12},{5,13},{6,14},{7,15},{8,0},{9,1},... | collective-permute-start | bytes 208904 | tf_op jit(solution)/shard_map/ppermute | solution.py:369
  25.5 6.9 %collective-permute-start.5 = (bf16[272,128]{1,0:T(8,128)(2,1)S(1)}, bf16[272,128]{1,0:T(8,128)(2,1)S(1)}, u32[]{:S(2)}, u32[]{:S(2)}) collective-permute-start(bf16[272,128]{1,0:T(8,128)(2,1)S(1)} %get-tuple-element.35), channel_id=1, source_target_pairs={{0,4},{1,13},{2,6},{3,15},{4,0},{5,9},{6,2},{7,11},{8,12},{9,5},{1... | collective-permute-start | bytes 208904 | tf_op jit(solution)/shard_map/ppermute | solution.py:369
  32.4 6.9 %collective-permute-start.8 = (bf16[256,128]{1,0:T(8,128)(2,1)S(1)}, bf16[256,128]{1,0:T(8,128)(2,1)S(1)}, u32[]{:S(2)}, u32[]{:S(2)}) collective-permute-start(bf16[256,128]{1,0:T(8,128)(2,1)S(1)} %settle.1.total), channel_id=1, source_target_pairs={{0,12},{1,5},{2,14},{3,7},{4,8},{5,1},{6,10},{7,3},{8,4},{9,13},{1... | collective-permute-start | bytes 196616 | tf_op jit(solution)/shard_map/ppermute | solution.py:369
  34.9 5.9 %collective-permute-start.7 = (bf16[256,128]{1,0:T(8,128)(2,1)S(1)}, bf16[256,128]{1,0:T(8,128)(2,1)S(1)}, u32[]{:S(2)}, u32[]{:S(2)}) collective-permute-start(bf16[256,128]{1,0:T(8,128)(2,1)S(1)} %settle.1.total), channel_id=1, source_target_pairs={{0,8},{1,9},{2,10},{3,11},{4,12},{5,13},{6,14},{7,15},{8,0},{9,1},... | collective-permute-start | bytes 196616 | tf_op jit(solution)/shard_map/ppermute | solution.py:369
  34.9 5.9 %collective-permute-start.6 = (bf16[256,128]{1,0:T(8,128)(2,1)S(1)}, bf16[256,128]{1,0:T(8,128)(2,1)S(1)}, u32[]{:S(2)}, u32[]{:S(2)}) collective-permute-start(bf16[256,128]{1,0:T(8,128)(2,1)S(1)} %settle.1.total), channel_id=1, source_target_pairs={{0,4},{1,13},{2,6},{3,15},{4,0},{5,9},{6,2},{7,11},{8,12},{9,5},{1... | collective-permute-start | bytes 196616 | tf_op jit(solution)/shard_map/ppermute | solution.py:369
  40.9 6.7 %collective-permute-start.9 = (bf16[256,512]{1,0:T(8,128)(2,1)S(1)}, bf16[256,512]{1,0:T(8,128)(2,1)S(1)}, u32[]{:S(2)}, u32[]{:S(2)}) collective-permute-start(bf16[256,512]{1,0:T(8,128)(2,1)S(1)} %line.1.after.refs_0_), channel_id=1, source_target_pairs={{0,2},{1,3},{2,0},{3,1},{4,6},{5,7},{6,4},{7,5},{8,10},{9,11},{10,... | collective-permute-start | bytes 786440 | tf_op jit(solution)/shard_map/ppermute | solution.py:369
  47.6 2.0 %collective-permute-start.10 = (bf16[256,1024]{1,0:T(8,128)(2,1)S(1)}, bf16[256,1024]{1,0:T(8,128)(2,1)S(1)}, u32[]{:S(2)}, u32[]{:S(2)}) collective-permute-start(bf16[256,1024]{1,0:T(8,128)(2,1)S(1)} %join.1.mine), channel_id=1, source_target_pairs={{0,1},{1,0},{2,3},{3,2},{4,5},{5,4},{6,7},{7,6},{8,9},{9,8},{10,11... | collective-permute-start | bytes 1572872 | tf_op jit(solution)/shard_map/ppermute | solution.py:369

commit v15 on v14

--- a/solution.py
+++ b/solution.py
@@ -320,12 +320,6 @@
     mixers(order, mask_of(place, devices, order.shape[1]), held, coef)
 
 
-def line_kernel(place, total, third, second, first, out):
-    size = total.shape[1]
-    for d, part in zip((0, *turns_of(place[0] & 1)), (total, first, second, third)):
-        out[:, block(d * size, size)] = part[...]
-
-
 def join_kernel(*refs):
     *parts, out = refs
     start = 0
@@ -425,8 +419,8 @@
         ways = zip(turns_of(0), turns_of(1))
         parts = [swap(part, devices, 4 * even, 4 * odd) for part, (even, odd) in zip(parts, ways)]
         total = call(settle_kernel, "settle", [array(W, size)], keep, *parts, scalars=0)[0]
-        spread = [swap(total, devices, 4 * even, 4 * odd) for even, odd in zip(turns_of(0), turns_of(1))]
-        resp = call(line_kernel, "line", [array(W, quarter)], place, total, *reversed(spread))[0]
+        spread = [swap(total, devices, 4 * d) for d in (1, 2, 3)]
+        resp = join(total, *spread)
         mode_coef = call(
             mixers_kernel, "mixers", [array(8, modes, dtype=F32)],
             place, order, known, *parts, resp, scratch=[pltpu.VMEM((8, modes), F32)],

time: 53.3 us -> 52.9 us (level)
  no operation moved by 1% of the time
where the time goes in v15:
time: 52.9 us; the launch traced here: 52.8 us
  Pallas kernels  26.2 us (50%)
  starting transfers between devices  14 us (26%)
  waiting for transfers between devices  12.4 us (23%)
    pallas_call x14, Pallas kernels, call(): pl.pallas_call(kernel, in_specs=places, out_specs=[vmem] * len(out_shape)...  26.2 us
    ppermute x11, starting transfers between devices, swap(): lax.ppermute(x, 'frdm', [(i, i ^ (odd if i & 1 else bits)) for i in range...  14 us
    ppermute x11, waiting for transfers between devices, swap(): lax.ppermute(x, 'frdm', [(i, i ^ (odd if i & 1 else bits)) for i in range...  12.4 us
  transfers between devices with their start and end apart: 11, of which 7 were waited for; matrix products, arithmetic and copies ran while one was open for 0% of the time, Pallas kernels for 28%

profile of v15, /device:TPU:0, one launch (start us, length us, event | category | flops | bytes accessed | tf_op | source)
XLA Modules:
  0.0 52.8 jit_solution(15888447522674582047)
XLA Ops:
  0.0 0.0 copy-start
  0.0 5.4 %project.1 = (bf16[912,512]{1,0:T(8,128)(2,1)S(1)}, bf16[896,1024]{1,0:T(8,128)(2,1)S(1)}, bf16[1024,1024]{1,0:T(8,128)(2,1)S(1)}, bf16[528,2048]{1,0:T(8,128)(2,1)S(1)}, bf16[2,128]{1,0:T(2,128)(2,1)S(1)}) custom-call(s32[1]{0:T(128)} %bitcast.place, bf16[1024,896]{1,0:T(8,128)(2,1)} %loads_far.1, bf16[896,896]{1,0:T(8,128)(2,1)} %constant.14.clone.forward_far, ...), custom_call_target="tpu_custom_call" | custom-call | tf_op jit(solution)/shard_map/project/pallas_call | solution.py:69
  5.4 0.5 collective-permute-start
  5.9 0.0 copy-done
  5.9 3.3 %spectrum.1 = (f32[896,512]{1,0:T(8,128)S(1)}, bf16[1024,1024]{1,0:T(8,128)(2,1)S(1)}, bf16[896,1024]{1,0:T(8,128)(2,1)S(1)}, bf16[896,128]{1,0:T(8,128)(2,1)S(1...) custom-call(s32[1]{0:T(128)} %bitcast.place, bf16[528,2048]{1,0:T(8,128)(2,1)S(1)} %get-tuple-element.22.stack, ...), custom_call_target="tpu_custom_call" | custom-call | tf_op jit(solution)/shard_map/spectrum/pallas_call | solution.py:69
  9.2 0.0 collective-permute-done.other
  9.2 2.4 %respond.2.after = bf16[272,512]{1,0:T(8,128)(2,1)S(1)} custom-call(s32[1]{0:T(128)} %bitcast.place, bf16[896,1024]{1,0:T(8,128)(2,1)S(1)} %get-tuple-element.21.lft, bf16[1024,1024]{1,0:T(8,128)(2,1)S(1)} %get-tuple-element.23.shapes.near, bf16[912,512]{1,0:T(8,128)(2,1)S(1)} %collective-permute-done.other, f32[896,512]{1,0:T(8,128)S(1)} %get-tuple-element.26.spec, ...), custom_call_target="tpu_custom_call" | custom-call | tf_op jit(solution)/shard_map/respond/pallas_call | solution.py:69
  11.6 2.6 %collective-permute-start.2 = (bf16[272,512]{1,0:T(8,128)(2,1)S(1)}, bf16[272,512]{1,0:T(8,128)(2,1)S(1)}, u32[]{:S(2)}, u32[]{:S(2)}) collective-permute-start(bf16[272,512]{1,0:T(8,128)(2,1)S(1)} %respond.2.after), channel_id=1, source_target_pairs={{0,2},{1,3},{2,0},{3,1},{4,6},{5,7},{6,4},{7,5},{8,10},{9,11},{10,... | collective-permute-start | bytes 835592 | tf_op jit(solution)/shard_map/ppermute | solution.py:363
  14.2 1.1 %project_rest.1 = bf16[896,512]{1,0:T(8,128)(2,1)S(1)} custom-call(s32[1]{0:T(128)} %bitcast.place, bf16[896,1024]{1,0:T(8,128)(2,1)S(1)} %get-tuple-element.21.lft, bf16[1024,1024]{1,0:T(8,128)(2,1)S(1)} %get-tuple-element.24.shapes.far, bf16[272,512]{1,0:T(8,128)(2,1)S(1)} %respond.2.after), custom_call_target="tpu_custom_call" | custom-call | flops 3758096384 | tf_op jit(solution)/shard_map/project_rest/pallas_call | solution.py:69
  15.3 0.3 collective-permute-start.1
  15.6 2.9 %spectrum_rest.1.spec = f32[896,512]{1,0:T(8,128)S(1)} custom-call(s32[1]{0:T(128)} %bitcast.place, bf16[528,2048]{1,0:T(8,128)(2,1)S(1)} %get-tuple-element.22.stack, s32[1,2048]{1,0:T(1,128)S(1)} %bitcast.6, bf16[896,1024]{1,0:T(8,128)(2,1)S(1)} %get-tuple-element.29.table, bf16[896,128]{1,0:T(8,128)(2,1)S(1)} %get-tuple-element.30.last, ...), custom_call_target="tpu_custom_call" | custom-call | flops 20000000000 | tf_op jit(solution)/shard_map/spectrum_rest/pallas_call | solution.py:69
  18.4 0.0 collective-permute-done.1.other
  18.5 2.4 %respond.3.own = f32[256,512]{1,0:T(8,128)S(1)} custom-call(s32[1]{0:T(128)} %bitcast.place, bf16[896,1024]{1,0:T(8,128)(2,1)S(1)} %get-tuple-element.21.lft, bf16[1024,1024]{1,0:T(8,128)(2,1)S(1)} %get-tuple-element.23.shapes.near, bf16[896,512]{1,0:T(8,128)(2,1)S(1)} %collective-permute-done.1.other, f32[896,512]{1,0:T(8,128)S(1)} %spectrum_rest.1.spec, ...), custom_call_target="tpu_custom_call" | custom-call | tf_op jit(solution)/shard_map/respond/pallas_call | solution.py:69
  20.8 0.0 copy-start.1
  20.9 0.6 %collective-permute-done.2.got = bf16[272,512]{1,0:T(8,128)(2,1)S(1)} collective-permute-done((bf16[272,512]{1,0:T(8,128)(2,1)S(1)}, bf16[272,512]{1,0:T(8,128)(2,1)S(1)}, u32[]{:S(2)}, u32[]{:S(2)}) %collective-permute-start.2) | collective-permute-done | bytes 278560 | tf_op jit(solution)/shard_map/ppermute | solution.py:363
  21.5 0.1 fold.1
  21.6 3.9 %collective-permute-start.3 = (bf16[272,128]{1,0:T(8,128)(2,1)S(1)}, bf16[272,128]{1,0:T(8,128)(2,1)S(1)}, u32[]{:S(2)}, u32[]{:S(2)}) collective-permute-start(bf16[272,128]{1,0:T(8,128)(2,1)S(1)} %get-tuple-element.33), channel_id=1, source_target_pairs={{0,12},{1,5},{2,14},{3,7},{4,8},{5,1},{6,10},{7,3},{8,4},{9,13},{1... | collective-permute-start | bytes 208904 | tf_op jit(solution)/shard_map/ppermute | solution.py:363
  25.5 0.0 collective-permute-start.4
  25.5 0.6 %collective-permute-start.5 = (bf16[272,128]{1,0:T(8,128)(2,1)S(1)}, bf16[272,128]{1,0:T(8,128)(2,1)S(1)}, u32[]{:S(2)}, u32[]{:S(2)}) collective-permute-start(bf16[272,128]{1,0:T(8,128)(2,1)S(1)} %get-tuple-element.35), channel_id=1, source_target_pairs={{0,4},{1,13},{2,6},{3,15},{4,0},{5,9},{6,2},{7,11},{8,12},{9,5},{1... | collective-permute-start | bytes 208904 | tf_op jit(solution)/shard_map/ppermute | solution.py:363
  26.1 2.4 %collective-permute-done.3.first = bf16[272,128]{1,0:T(8,128)(2,1)S(1)} collective-permute-done((bf16[272,128]{1,0:T(8,128)(2,1)S(1)}, bf16[272,128]{1,0:T(8,128)(2,1)S(1)}, u32[]{:S(2)}, u32[]{:S(2)}) %collective-permute-start.3) | collective-permute-done | bytes 69664 | tf_op jit(solution)/shard_map/ppermute | solution.py:363
  28.6 3.8 %collective-permute-done.4.second = bf16[272,128]{1,0:T(8,128)(2,1)S(1)} collective-permute-done((bf16[272,128]{1,0:T(8,128)(2,1)S(1)}, bf16[272,128]{1,0:T(8,128)(2,1)S(1)}, u32[]{:S(2)}, u32[]{:S(2)}) %collective-permute-start.4) | collective-permute-done | bytes 69664 | tf_op jit(solution)/shard_map/ppermute | solution.py:363
  32.4 0.0 collective-permute-done.5.third
  32.4 2.5 %collective-permute-start.8 = (bf16[256,128]{1,0:T(8,128)(2,1)S(1)}, bf16[256,128]{1,0:T(8,128)(2,1)S(1)}, u32[]{:S(2)}, u32[]{:S(2)}) collective-permute-start(bf16[256,128]{1,0:T(8,128)(2,1)S(1)} %settle.1.refs_0_), channel_id=1, source_target_pairs={{0,12},{1,13},{2,14},{3,15},{4,8},{5,9},{6,10},{7,11},{8,4},{9,5},... | collective-permute-start | bytes 196616 | tf_op jit(solution)/shard_map/ppermute | solution.py:363
  34.9 0.0 collective-permute-start.7
  34.9 1.9 %collective-permute-start.6 = (bf16[256,128]{1,0:T(8,128)(2,1)S(1)}, bf16[256,128]{1,0:T(8,128)(2,1)S(1)}, u32[]{:S(2)}, u32[]{:S(2)}) collective-permute-start(bf16[256,128]{1,0:T(8,128)(2,1)S(1)} %settle.1.refs_0_), channel_id=1, source_target_pairs={{0,4},{1,5},{2,6},{3,7},{4,0},{5,1},{6,2},{7,3},{8,12},{9,13},{10,... | collective-permute-start | bytes 196616 | tf_op jit(solution)/shard_map/ppermute | solution.py:363
  36.8 2.3 %collective-permute-done.8.refs_3_ = bf16[256,128]{1,0:T(8,128)(2,1)S(1)} collective-permute-done((bf16[256,128]{1,0:T(8,128)(2,1)S(1)}, bf16[256,128]{1,0:T(8,128)(2,1)S(1)}, u32[]{:S(2)}, u32[]{:S(2)}) %collective-permute-start.8) | collective-permute-done | bytes 65568 | tf_op jit(solution)/shard_map/ppermute | solution.py:363
  39.1 1.4 %collective-permute-done.7.refs_2_ = bf16[256,128]{1,0:T(8,128)(2,1)S(1)} collective-permute-done((bf16[256,128]{1,0:T(8,128)(2,1)S(1)}, bf16[256,128]{1,0:T(8,128)(2,1)S(1)}, u32[]{:S(2)}, u32[]{:S(2)}) %collective-permute-start.7) | collective-permute-done | bytes 65568 | tf_op jit(solution)/shard_map/ppermute | solution.py:363
  40.5 0.0 collective-permute-done.6.refs_1_
  40.5 1.6 %collective-permute-start.9 = (bf16[256,512]{1,0:T(8,128)(2,1)S(1)}, bf16[256,512]{1,0:T(8,128)(2,1)S(1)}, u32[]{:S(2)}, u32[]{:S(2)}) collective-permute-start(bf16[256,512]{1,0:T(8,128)(2,1)S(1)} %join.2.after.refs_0_), channel_id=1, source_target_pairs={{0,2},{1,3},{2,0},{3,1},{4,6},{5,7},{6,4},{7,5},{8,10},{9,11},{10,... | collective-permute-start | bytes 786440 | tf_op jit(solution)/shard_map/ppermute | solution.py:363
  42.1 2.4 %mixers.1.after.coef = f32[8,2048]{1,0:T(8,128)S(1)} custom-call(s32[1]{0:T(128)} %bitcast.place, s32[1,2048]{1,0:T(1,128)S(1)} %bitcast.7, bf16[16,128]{1,0:T(8,128)(2,1)S(1)} %get-tuple-element.32.known, bf16[272,128]{1,0:T(8,128)(2,1)S(1)} %collective-permute-done.3.first, bf16[272,128]{1,0:T(8,128)(2,1)S(1)} %collective-permute-done.4.second, ...), custom_call_target="tpu_custom_call" | custom-call | tf_op jit(solution)/shard_map/mixers/pallas_call | solution.py:69
  44.6 0.0 copy-done.1
  44.6 1.4 %pick.1._ = bf16[2048,2048]{1,0:T(8,128)(2,1)S(1)} custom-call(s32[1]{0:T(128)} %bitcast.place, s32[1,2048]{1,0:T(1,128)S(1)} %bitcast.8, f32[8,2048]{1,0:T(8,128)S(1)} %mixers.1.after.coef), custom_call_target="tpu_custom_call" | custom-call | tf_op jit(solution)/shard_map/pick/pallas_call | solution.py:69
  46.0 1.3 %collective-permute-done.9.refs_1_ = bf16[256,512]{1,0:T(8,128)(2,1)S(1)} collective-permute-done((bf16[256,512]{1,0:T(8,128)(2,1)S(1)}, bf16[256,512]{1,0:T(8,128)(2,1)S(1)}, u32[]{:S(2)}, u32[]{:S(2)}) %collective-permute-start.9) | collective-permute-done | bytes 262176 | tf_op jit(solution)/shard_map/ppermute | solution.py:363
  47.3 0.1 collective-permute-start.10
  47.3 1.2 %mate.1.mates = f32[256,2048]{1,0:T(8,128)S(1)} custom-call(bf16[256,1024]{1,0:T(8,128)(2,1)S(1)} %join.3.mine, bf16[2048,2048]{1,0:T(8,128)(2,1)S(1)} %pick.1._), custom_call_target="tpu_custom_call" | custom-call | tf_op jit(solution)/shard_map/mate/pallas_call | solution.py:69
  48.6 0.6 %collective-permute-done.10.theirs = bf16[256,1024]{1,0:T(8,128)(2,1)S(1)} collective-permute-done((bf16[256,1024]{1,0:T(8,128)(2,1)S(1)}, bf16[256,1024]{1,0:T(8,128)(2,1)S(1)}, u32[]{:S(2)}, u32[]{:S(2)}) %collective-permute-start.10) | collective-permute-done | bytes 524320 | tf_op jit(solution)/shard_map/ppermute | solution.py:363
  49.2 3.5 %expand.1 = bf16[1024,256]{1,0:T(8,128)(2,1)} custom-call(s32[1]{0:T(128)} %bitcast.place, bf16[256,1024]{1,0:T(8,128)(2,1)S(1)} %join.3.mine, bf16[256,1024]{1,0:T(8,128)(2,1)S(1)} %collective-permute-done.10.theirs, f32[256,2048]{1,0:T(8,128)S(1)} %mate.1.mates, bf16[2048,2048]{1,0:T(8,128)(2,1)S(1)} %pick.1._, f32[8,2048]{1,0:T(8,128)S(1)} %mixers.1.after.coef, ...), custom_call_target="tpu_custom_call" | custom-call | tf_op jit(solution)/shard_map/expand/pallas_call | solution.py:69
  (3 shorter events, 0.1 us)
Async XLA Ops:
  0.0 5.9 %copy-start = (s32[2048]{0:T(1024)S(1)}, s32[2048]{0:T(1024)}, u32[]{:S(2)}) copy-start(s32[2048]{0:T(1024)} %param.14) | copy-start | bytes 24580
  5.4 3.8 %collective-permute-start = (bf16[912,512]{1,0:T(8,128)(2,1)S(1)}, bf16[912,512]{1,0:T(8,128)(2,1)S(1)}, u32[]{:S(2)}, u32[]{:S(2)}) collective-permute-start(bf16[912,512]{1,0:T(8,128)(2,1)S(1)} %get-tuple-element.25), channel_id=1, source_target_pairs={{0,1},{1,0},{2,3},{3,2},{4,5},{5,4},{6,7},{7,6},{8,9},{9,8},{10,11... | collective-permute-start | bytes 2801672 | tf_op jit(solution)/shard_map/ppermute | solution.py:363
  11.6 9.9 %collective-permute-start.2 = (bf16[272,512]{1,0:T(8,128)(2,1)S(1)}, bf16[272,512]{1,0:T(8,128)(2,1)S(1)}, u32[]{:S(2)}, u32[]{:S(2)}) collective-permute-start(bf16[272,512]{1,0:T(8,128)(2,1)S(1)} %respond.2.after), channel_id=1, source_target_pairs={{0,2},{1,3},{2,0},{3,1},{4,6},{5,7},{6,4},{7,5},{8,10},{9,11},{10,... | collective-permute-start | bytes 835592 | tf_op jit(solution)/shard_map/ppermute | solution.py:363
  15.3 3.2 %collective-permute-start.1 = (bf16[896,512]{1,0:T(8,128)(2,1)S(1)}, bf16[896,512]{1,0:T(8,128)(2,1)S(1)}, u32[]{:S(2)}, u32[]{:S(2)}) collective-permute-start(bf16[896,512]{1,0:T(8,128)(2,1)S(1)} %project_rest.1), channel_id=1, source_target_pairs={{0,1},{1,0},{2,3},{3,2},{4,5},{5,4},{6,7},{7,6},{8,9},{9,8},{10,11... | collective-permute-start | bytes 2752520 | tf_op jit(solution)/shard_map/ppermute | solution.py:363
  20.8 23.7 %copy-start.1 = (s32[2048]{0:T(1024)S(1)}, s32[2048]{0:T(1024)}, u32[]{:S(2)}) copy-start(s32[2048]{0:T(1024)} %param.15) | copy-start | bytes 24580
  21.6 7.0 %collective-permute-start.3 = (bf16[272,128]{1,0:T(8,128)(2,1)S(1)}, bf16[272,128]{1,0:T(8,128)(2,1)S(1)}, u32[]{:S(2)}, u32[]{:S(2)}) collective-permute-start(bf16[272,128]{1,0:T(8,128)(2,1)S(1)} %get-tuple-element.33), channel_id=1, source_target_pairs={{0,12},{1,5},{2,14},{3,7},{4,8},{5,1},{6,10},{7,3},{8,4},{9,13},{1... | collective-permute-start | bytes 208904 | tf_op jit(solution)/shard_map/ppermute | solution.py:363
  25.5 6.9 %collective-permute-start.4 = (bf16[272,128]{1,0:T(8,128)(2,1)S(1)}, bf16[272,128]{1,0:T(8,128)(2,1)S(1)}, u32[]{:S(2)}, u32[]{:S(2)}) collective-permute-start(bf16[272,128]{1,0:T(8,128)(2,1)S(1)} %get-tuple-element.34), channel_id=1, source_target_pairs={{0,8},{1,9},{2,10},{3,11},{4,12},{5,13},{6,14},{7,15},{8,0},{9,1},... | collective-permute-start | bytes 208904 | tf_op jit(solution)/shard_map/ppermute | solution.py:363
  25.5 6.9 %collective-permute-start.5 = (bf16[272,128]{1,0:T(8,128)(2,1)S(1)}, bf16[272,128]{1,0:T(8,128)(2,1)S(1)}, u32[]{:S(2)}, u32[]{:S(2)}) collective-permute-start(bf16[272,128]{1,0:T(8,128)(2,1)S(1)} %get-tuple-element.35), channel_id=1, source_target_pairs={{0,4},{1,13},{2,6},{3,15},{4,0},{5,9},{6,2},{7,11},{8,12},{9,5},{1... | collective-permute-start | bytes 208904 | tf_op jit(solution)/shard_map/ppermute | solution.py:363
  32.4 6.7 %collective-permute-start.8 = (bf16[256,128]{1,0:T(8,128)(2,1)S(1)}, bf16[256,128]{1,0:T(8,128)(2,1)S(1)}, u32[]{:S(2)}, u32[]{:S(2)}) collective-permute-start(bf16[256,128]{1,0:T(8,128)(2,1)S(1)} %settle.1.refs_0_), channel_id=1, source_target_pairs={{0,12},{1,13},{2,14},{3,15},{4,8},{5,9},{6,10},{7,11},{8,4},{9,5},... | collective-permute-start | bytes 196616 | tf_op jit(solution)/shard_map/ppermute | solution.py:363
  34.9 5.6 %collective-permute-start.7 = (bf16[256,128]{1,0:T(8,128)(2,1)S(1)}, bf16[256,128]{1,0:T(8,128)(2,1)S(1)}, u32[]{:S(2)}, u32[]{:S(2)}) collective-permute-start(bf16[256,128]{1,0:T(8,128)(2,1)S(1)} %settle.1.refs_0_), channel_id=1, source_target_pairs={{0,8},{1,9},{2,10},{3,11},{4,12},{5,13},{6,14},{7,15},{8,0},{9,1},... | collective-permute-start | bytes 196616 | tf_op jit(solution)/shard_map/ppermute | solution.py:363
  34.9 5.6 %collective-permute-start.6 = (bf16[256,128]{1,0:T(8,128)(2,1)S(1)}, bf16[256,128]{1,0:T(8,128)(2,1)S(1)}, u32[]{:S(2)}, u32[]{:S(2)}) collective-permute-start(bf16[256,128]{1,0:T(8,128)(2,1)S(1)} %settle.1.refs_0_), channel_id=1, source_target_pairs={{0,4},{1,5},{2,6},{3,7},{4,0},{5,1},{6,2},{7,3},{8,12},{9,13},{10,... | collective-permute-start | bytes 196616 | tf_op jit(solution)/shard_map/ppermute | solution.py:363
  40.5 6.7 %collective-permute-start.9 = (bf16[256,512]{1,0:T(8,128)(2,1)S(1)}, bf16[256,512]{1,0:T(8,128)(2,1)S(1)}, u32[]{:S(2)}, u32[]{:S(2)}) collective-permute-start(bf16[256,512]{1,0:T(8,128)(2,1)S(1)} %join.2.after.refs_0_), channel_id=1, source_target_pairs={{0,2},{1,3},{2,0},{3,1},{4,6},{5,7},{6,4},{7,5},{8,10},{9,11},{10,... | collective-permute-start | bytes 786440 | tf_op jit(solution)/shard_map/ppermute | solution.py:363
  47.3 2.0 %collective-permute-start.10 = (bf16[256,1024]{1,0:T(8,128)(2,1)S(1)}, bf16[256,1024]{1,0:T(8,128)(2,1)S(1)}, u32[]{:S(2)}, u32[]{:S(2)}) collective-permute-start(bf16[256,1024]{1,0:T(8,128)(2,1)S(1)} %join.3.mine), channel_id=1, source_target_pairs={{0,1},{1,0},{2,3},{3,2},{4,5},{5,4},{6,7},{7,6},{8,9},{9,8},{10,11... | collective-permute-start | bytes 1572872 | tf_op jit(solution)/shard_map/ppermute | solution.py:363

commit v16 on v15

--- a/solution.py
+++ b/solution.py
@@ -253,7 +253,7 @@
 
 
 def turns_of(core):
-    return 3 - 2 * core, 2, 1 + 2 * core
+    return 1, 2, 3
 
 
 def fold_kernel(place, own, got, coef, other, keep, known, first, second, third):

time: 52.9 us -> 52.1 us (0.985)
  waiting for transfers between devices: 12.4 us -> 11.6 us
    ppermute x11, waiting for transfers between devices: 12.4 us -> 11.6 us  [swap(): lax.ppermute(x, 'frdm', [(i, i ^ (odd if i & 1 else bits)) for i in range...]
where the time goes in v16:
time: 52.1 us; the launch traced here: 52 us
  Pallas kernels  26.2 us (50%)
  starting transfers between devices  14 us (27%)
  waiting for transfers between devices  11.6 us (22%)
    pallas_call x14, Pallas kernels, call(): pl.pallas_call(kernel, in_specs=places, out_specs=[vmem] * len(out_shape)...  26.2 us
    ppermute x11, starting transfers between devices, swap(): lax.ppermute(x, 'frdm', [(i, i ^ (odd if i & 1 else bits)) for i in range...  14 us
    ppermute x11, waiting for transfers between devices, swap(): lax.ppermute(x, 'frdm', [(i, i ^ (odd if i & 1 else bits)) for i in range...  11.6 us
  transfers between devices with their start and end apart: 11, of which 7 were waited for; matrix products, arithmetic and copies ran while one was open for 0% of the time, Pallas kernels for 28%

profile of v16, /device:TPU:0, one launch (start us, length us, event | category | flops | bytes accessed | tf_op | source)
XLA Modules:
  0.0 52.0 jit_solution(17017641360723003468)
XLA Ops:
  0.0 0.0 copy-start
  0.0 5.4 %project.1 = (bf16[912,512]{1,0:T(8,128)(2,1)S(1)}, bf16[896,1024]{1,0:T(8,128)(2,1)S(1)}, bf16[1024,1024]{1,0:T(8,128)(2,1)S(1)}, bf16[528,2048]{1,0:T(8,128)(2,1)S(1)}, bf16[2,128]{1,0:T(2,128)(2,1)S(1)}) custom-call(s32[1]{0:T(128)} %bitcast.place, bf16[1024,896]{1,0:T(8,128)(2,1)} %loads_far.1, bf16[896,896]{1,0:T(8,128)(2,1)} %constant.14.clone.forward_far, ...), custom_call_target="tpu_custom_call" | custom-call | tf_op jit(solution)/shard_map/project/pallas_call | solution.py:69
  5.4 0.5 %collective-permute-start = (bf16[912,512]{1,0:T(8,128)(2,1)S(1)}, bf16[912,512]{1,0:T(8,128)(2,1)S(1)}, u32[]{:S(2)}, u32[]{:S(2)}) collective-permute-start(bf16[912,512]{1,0:T(8,128)(2,1)S(1)} %get-tuple-element.25), channel_id=1, source_target_pairs={{0,1},{1,0},{2,3},{3,2},{4,5},{5,4},{6,7},{7,6},{8,9},{9,8},{10,11... | collective-permute-start | bytes 2801672 | tf_op jit(solution)/shard_map/ppermute | solution.py:363
  5.9 0.0 copy-done
  5.9 3.3 %spectrum.1 = (f32[896,512]{1,0:T(8,128)S(1)}, bf16[1024,1024]{1,0:T(8,128)(2,1)S(1)}, bf16[896,1024]{1,0:T(8,128)(2,1)S(1)}, bf16[896,128]{1,0:T(8,128)(2,1)S(1...) custom-call(s32[1]{0:T(128)} %bitcast.place, bf16[528,2048]{1,0:T(8,128)(2,1)S(1)} %get-tuple-element.22.stack, ...), custom_call_target="tpu_custom_call" | custom-call | tf_op jit(solution)/shard_map/spectrum/pallas_call | solution.py:69
  9.2 0.0 collective-permute-done.other
  9.2 2.4 %respond.2.after = bf16[272,512]{1,0:T(8,128)(2,1)S(1)} custom-call(s32[1]{0:T(128)} %bitcast.place, bf16[896,1024]{1,0:T(8,128)(2,1)S(1)} %get-tuple-element.21.lft, bf16[1024,1024]{1,0:T(8,128)(2,1)S(1)} %get-tuple-element.23.shapes.near, bf16[912,512]{1,0:T(8,128)(2,1)S(1)} %collective-permute-done.other, f32[896,512]{1,0:T(8,128)S(1)} %get-tuple-element.26.spec, ...), custom_call_target="tpu_custom_call" | custom-call | tf_op jit(solution)/shard_map/respond/pallas_call | solution.py:69
  11.6 2.6 %collective-permute-start.2 = (bf16[272,512]{1,0:T(8,128)(2,1)S(1)}, bf16[272,512]{1,0:T(8,128)(2,1)S(1)}, u32[]{:S(2)}, u32[]{:S(2)}) collective-permute-start(bf16[272,512]{1,0:T(8,128)(2,1)S(1)} %respond.2.after), channel_id=1, source_target_pairs={{0,2},{1,3},{2,0},{3,1},{4,6},{5,7},{6,4},{7,5},{8,10},{9,11},{10,... | collective-permute-start | bytes 835592 | tf_op jit(solution)/shard_map/ppermute | solution.py:363
  14.2 1.1 %project_rest.1 = bf16[896,512]{1,0:T(8,128)(2,1)S(1)} custom-call(s32[1]{0:T(128)} %bitcast.place, bf16[896,1024]{1,0:T(8,128)(2,1)S(1)} %get-tuple-element.21.lft, bf16[1024,1024]{1,0:T(8,128)(2,1)S(1)} %get-tuple-element.24.shapes.far, bf16[272,512]{1,0:T(8,128)(2,1)S(1)} %respond.2.after), custom_call_target="tpu_custom_call" | custom-call | flops 3758096384 | tf_op jit(solution)/shard_map/project_rest/pallas_call | solution.py:69
  15.3 0.3 collective-permute-start.1
  15.6 2.9 %spectrum_rest.1.spec = f32[896,512]{1,0:T(8,128)S(1)} custom-call(s32[1]{0:T(128)} %bitcast.place, bf16[528,2048]{1,0:T(8,128)(2,1)S(1)} %get-tuple-element.22.stack, s32[1,2048]{1,0:T(1,128)S(1)} %bitcast.6, bf16[896,1024]{1,0:T(8,128)(2,1)S(1)} %get-tuple-element.29.table, bf16[896,128]{1,0:T(8,128)(2,1)S(1)} %get-tuple-element.30.last, ...), custom_call_target="tpu_custom_call" | custom-call | flops 20000000000 | tf_op jit(solution)/shard_map/spectrum_rest/pallas_call | solution.py:69
  18.4 0.0 collective-permute-done.1.other
  18.5 2.4 %respond.3.own = f32[256,512]{1,0:T(8,128)S(1)} custom-call(s32[1]{0:T(128)} %bitcast.place, bf16[896,1024]{1,0:T(8,128)(2,1)S(1)} %get-tuple-element.21.lft, bf16[1024,1024]{1,0:T(8,128)(2,1)S(1)} %get-tuple-element.23.shapes.near, bf16[896,512]{1,0:T(8,128)(2,1)S(1)} %collective-permute-done.1.other, f32[896,512]{1,0:T(8,128)S(1)} %spectrum_rest.1.spec, ...), custom_call_target="tpu_custom_call" | custom-call | tf_op jit(solution)/shard_map/respond/pallas_call | solution.py:69
  20.8 0.0 copy-start.1
  20.9 0.6 %collective-permute-done.2.got = bf16[272,512]{1,0:T(8,128)(2,1)S(1)} collective-permute-done((bf16[272,512]{1,0:T(8,128)(2,1)S(1)}, bf16[272,512]{1,0:T(8,128)(2,1)S(1)}, u32[]{:S(2)}, u32[]{:S(2)}) %collective-permute-start.2) | collective-permute-done | bytes 278560 | tf_op jit(solution)/shard_map/ppermute | solution.py:363
  21.5 0.1 fold.1
  21.6 1.9 %collective-permute-start.3 = (bf16[272,128]{1,0:T(8,128)(2,1)S(1)}, bf16[272,128]{1,0:T(8,128)(2,1)S(1)}, u32[]{:S(2)}, u32[]{:S(2)}) collective-permute-start(bf16[272,128]{1,0:T(8,128)(2,1)S(1)} %get-tuple-element.33), channel_id=1, source_target_pairs={{0,4},{1,5},{2,6},{3,7},{4,0},{5,1},{6,2},{7,3},{8,12},{9,13},{10,... | collective-permute-start | bytes 208904 | tf_op jit(solution)/shard_map/ppermute | solution.py:363
  23.5 2.6 %collective-permute-start.4 = (bf16[272,128]{1,0:T(8,128)(2,1)S(1)}, bf16[272,128]{1,0:T(8,128)(2,1)S(1)}, u32[]{:S(2)}, u32[]{:S(2)}) collective-permute-start(bf16[272,128]{1,0:T(8,128)(2,1)S(1)} %get-tuple-element.34), channel_id=1, source_target_pairs={{0,8},{1,9},{2,10},{3,11},{4,12},{5,13},{6,14},{7,15},{8,0},{9,1},... | collective-permute-start | bytes 208904 | tf_op jit(solution)/shard_map/ppermute | solution.py:363
  26.1 0.0 collective-permute-start.5
  26.1 0.0 collective-permute-done.3.first
  26.1 4.8 %collective-permute-done.4.second = bf16[272,128]{1,0:T(8,128)(2,1)S(1)} collective-permute-done((bf16[272,128]{1,0:T(8,128)(2,1)S(1)}, bf16[272,128]{1,0:T(8,128)(2,1)S(1)}, u32[]{:S(2)}, u32[]{:S(2)}) %collective-permute-start.4) | collective-permute-done | bytes 69664 | tf_op jit(solution)/shard_map/ppermute | solution.py:363
  30.9 1.4 %collective-permute-done.5.third = bf16[272,128]{1,0:T(8,128)(2,1)S(1)} collective-permute-done((bf16[272,128]{1,0:T(8,128)(2,1)S(1)}, bf16[272,128]{1,0:T(8,128)(2,1)S(1)}, u32[]{:S(2)}, u32[]{:S(2)}) %collective-permute-start.5) | collective-permute-done | bytes 69664 | tf_op jit(solution)/shard_map/ppermute | solution.py:363
  32.3 1.9 %collective-permute-start.8 = (bf16[256,128]{1,0:T(8,128)(2,1)S(1)}, bf16[256,128]{1,0:T(8,128)(2,1)S(1)}, u32[]{:S(2)}, u32[]{:S(2)}) collective-permute-start(bf16[256,128]{1,0:T(8,128)(2,1)S(1)} %settle.1.refs_0_), channel_id=1, source_target_pairs={{0,12},{1,13},{2,14},{3,15},{4,8},{5,9},{6,10},{7,11},{8,4},{9,5},... | collective-permute-start | bytes 196616 | tf_op jit(solution)/shard_map/ppermute | solution.py:363
  34.2 0.3 collective-permute-start.7
  34.5 2.3 %collective-permute-start.6 = (bf16[256,128]{1,0:T(8,128)(2,1)S(1)}, bf16[256,128]{1,0:T(8,128)(2,1)S(1)}, u32[]{:S(2)}, u32[]{:S(2)}) collective-permute-start(bf16[256,128]{1,0:T(8,128)(2,1)S(1)} %settle.1.refs_0_), channel_id=1, source_target_pairs={{0,4},{1,5},{2,6},{3,7},{4,0},{5,1},{6,2},{7,3},{8,12},{9,13},{10,... | collective-permute-start | bytes 196616 | tf_op jit(solution)/shard_map/ppermute | solution.py:363
  36.8 1.7 %collective-permute-done.8.refs_3_ = bf16[256,128]{1,0:T(8,128)(2,1)S(1)} collective-permute-done((bf16[256,128]{1,0:T(8,128)(2,1)S(1)}, bf16[256,128]{1,0:T(8,128)(2,1)S(1)}, u32[]{:S(2)}, u32[]{:S(2)}) %collective-permute-start.8) | collective-permute-done | bytes 65568 | tf_op jit(solution)/shard_map/ppermute | solution.py:363
  38.5 1.4 %collective-permute-done.7.refs_2_ = bf16[256,128]{1,0:T(8,128)(2,1)S(1)} collective-permute-done((bf16[256,128]{1,0:T(8,128)(2,1)S(1)}, bf16[256,128]{1,0:T(8,128)(2,1)S(1)}, u32[]{:S(2)}, u32[]{:S(2)}) %collective-permute-start.7) | collective-permute-done | bytes 65568 | tf_op jit(solution)/shard_map/ppermute | solution.py:363
  39.9 0.0 collective-permute-done.6.refs_1_
  40.0 1.6 %collective-permute-start.9 = (bf16[256,512]{1,0:T(8,128)(2,1)S(1)}, bf16[256,512]{1,0:T(8,128)(2,1)S(1)}, u32[]{:S(2)}, u32[]{:S(2)}) collective-permute-start(bf16[256,512]{1,0:T(8,128)(2,1)S(1)} %join.2.after.refs_0_), channel_id=1, source_target_pairs={{0,2},{1,3},{2,0},{3,1},{4,6},{5,7},{6,4},{7,5},{8,10},{9,11},{10,... | collective-permute-start | bytes 786440 | tf_op jit(solution)/shard_map/ppermute | solution.py:363
  41.5 2.4 %mixers.1.after.coef = f32[8,2048]{1,0:T(8,128)S(1)} custom-call(s32[1]{0:T(128)} %bitcast.place, s32[1,2048]{1,0:T(1,128)S(1)} %bitcast.7, bf16[16,128]{1,0:T(8,128)(2,1)S(1)} %get-tuple-element.32.known, bf16[272,128]{1,0:T(8,128)(2,1)S(1)} %collective-permute-done.3.first, bf16[272,128]{1,0:T(8,128)(2,1)S(1)} %collective-permute-done.4.second, ...), custom_call_target="tpu_custom_call" | custom-call | tf_op jit(solution)/shard_map/mixers/pallas_call | solution.py:69
  44.0 0.0 copy-done.1
  44.0 1.4 %pick.1._ = bf16[2048,2048]{1,0:T(8,128)(2,1)S(1)} custom-call(s32[1]{0:T(128)} %bitcast.place, s32[1,2048]{1,0:T(1,128)S(1)} %bitcast.8, f32[8,2048]{1,0:T(8,128)S(1)} %mixers.1.after.coef), custom_call_target="tpu_custom_call" | custom-call | tf_op jit(solution)/shard_map/pick/pallas_call | solution.py:69
  45.4 1.0 %collective-permute-done.9.refs_1_ = bf16[256,512]{1,0:T(8,128)(2,1)S(1)} collective-permute-done((bf16[256,512]{1,0:T(8,128)(2,1)S(1)}, bf16[256,512]{1,0:T(8,128)(2,1)S(1)}, u32[]{:S(2)}, u32[]{:S(2)}) %collective-permute-start.9) | collective-permute-done | bytes 262176 | tf_op jit(solution)/shard_map/ppermute | solution.py:363
  46.4 0.1 collective-permute-start.10
  46.5 1.2 %mate.1.mates = f32[256,2048]{1,0:T(8,128)S(1)} custom-call(bf16[256,1024]{1,0:T(8,128)(2,1)S(1)} %join.3.mine, bf16[2048,2048]{1,0:T(8,128)(2,1)S(1)} %pick.1._), custom_call_target="tpu_custom_call" | custom-call | tf_op jit(solution)/shard_map/mate/pallas_call | solution.py:69
  47.8 0.6 %collective-permute-done.10.theirs = bf16[256,1024]{1,0:T(8,128)(2,1)S(1)} collective-permute-done((bf16[256,1024]{1,0:T(8,128)(2,1)S(1)}, bf16[256,1024]{1,0:T(8,128)(2,1)S(1)}, u32[]{:S(2)}, u32[]{:S(2)}) %collective-permute-start.10) | collective-permute-done | bytes 524320 | tf_op jit(solution)/shard_map/ppermute | solution.py:363
  48.4 3.5 %expand.1 = bf16[1024,256]{1,0:T(8,128)(2,1)} custom-call(s32[1]{0:T(128)} %bitcast.place, bf16[256,1024]{1,0:T(8,128)(2,1)S(1)} %join.3.mine, bf16[256,1024]{1,0:T(8,128)(2,1)S(1)} %collective-permute-done.10.theirs, f32[256,2048]{1,0:T(8,128)S(1)} %mate.1.mates, bf16[2048,2048]{1,0:T(8,128)(2,1)S(1)} %pick.1._, f32[8,2048]{1,0:T(8,128)S(1)} %mixers.1.after.coef, ...), custom_call_target="tpu_custom_call" | custom-call | tf_op jit(solution)/shard_map/expand/pallas_call | solution.py:69
  (3 shorter events, 0.1 us)
Async XLA Ops:
  0.0 5.9 %copy-start = (s32[2048]{0:T(1024)S(1)}, s32[2048]{0:T(1024)}, u32[]{:S(2)}) copy-start(s32[2048]{0:T(1024)} %param.14) | copy-start | bytes 24580
  5.4 3.8 %collective-permute-start = (bf16[912,512]{1,0:T(8,128)(2,1)S(1)}, bf16[912,512]{1,0:T(8,128)(2,1)S(1)}, u32[]{:S(2)}, u32[]{:S(2)}) collective-permute-start(bf16[912,512]{1,0:T(8,128)(2,1)S(1)} %get-tuple-element.25), channel_id=1, source_target_pairs={{0,1},{1,0},{2,3},{3,2},{4,5},{5,4},{6,7},{7,6},{8,9},{9,8},{10,11... | collective-permute-start | bytes 2801672 | tf_op jit(solution)/shard_map/ppermute | solution.py:363
  11.6 9.9 %collective-permute-start.2 = (bf16[272,512]{1,0:T(8,128)(2,1)S(1)}, bf16[272,512]{1,0:T(8,128)(2,1)S(1)}, u32[]{:S(2)}, u32[]{:S(2)}) collective-permute-start(bf16[272,512]{1,0:T(8,128)(2,1)S(1)} %respond.2.after), channel_id=1, source_target_pairs={{0,2},{1,3},{2,0},{3,1},{4,6},{5,7},{6,4},{7,5},{8,10},{9,11},{10,... | collective-permute-start | bytes 835592 | tf_op jit(solution)/shard_map/ppermute | solution.py:363
  15.3 3.2 %collective-permute-start.1 = (bf16[896,512]{1,0:T(8,128)(2,1)S(1)}, bf16[896,512]{1,0:T(8,128)(2,1)S(1)}, u32[]{:S(2)}, u32[]{:S(2)}) collective-permute-start(bf16[896,512]{1,0:T(8,128)(2,1)S(1)} %project_rest.1), channel_id=1, source_target_pairs={{0,1},{1,0},{2,3},{3,2},{4,5},{5,4},{6,7},{7,6},{8,9},{9,8},{10,11... | collective-permute-start | bytes 2752520 | tf_op jit(solution)/shard_map/ppermute | solution.py:363
  20.8 23.1 %copy-start.1 = (s32[2048]{0:T(1024)S(1)}, s32[2048]{0:T(1024)}, u32[]{:S(2)}) copy-start(s32[2048]{0:T(1024)} %param.15) | copy-start | bytes 24580
  21.6 4.5 %collective-permute-start.3 = (bf16[272,128]{1,0:T(8,128)(2,1)S(1)}, bf16[272,128]{1,0:T(8,128)(2,1)S(1)}, u32[]{:S(2)}, u32[]{:S(2)}) collective-permute-start(bf16[272,128]{1,0:T(8,128)(2,1)S(1)} %get-tuple-element.33), channel_id=1, source_target_pairs={{0,4},{1,5},{2,6},{3,7},{4,0},{5,1},{6,2},{7,3},{8,12},{9,13},{10,... | collective-permute-start | bytes 208904 | tf_op jit(solution)/shard_map/ppermute | solution.py:363
  23.5 7.4 %collective-permute-start.4 = (bf16[272,128]{1,0:T(8,128)(2,1)S(1)}, bf16[272,128]{1,0:T(8,128)(2,1)S(1)}, u32[]{:S(2)}, u32[]{:S(2)}) collective-permute-start(bf16[272,128]{1,0:T(8,128)(2,1)S(1)} %get-tuple-element.34), channel_id=1, source_target_pairs={{0,8},{1,9},{2,10},{3,11},{4,12},{5,13},{6,14},{7,15},{8,0},{9,1},... | collective-permute-start | bytes 208904 | tf_op jit(solution)/shard_map/ppermute | solution.py:363
  26.1 6.2 %collective-permute-start.5 = (bf16[272,128]{1,0:T(8,128)(2,1)S(1)}, bf16[272,128]{1,0:T(8,128)(2,1)S(1)}, u32[]{:S(2)}, u32[]{:S(2)}) collective-permute-start(bf16[272,128]{1,0:T(8,128)(2,1)S(1)} %get-tuple-element.35), channel_id=1, source_target_pairs={{0,12},{1,13},{2,14},{3,15},{4,8},{5,9},{6,10},{7,11},{8,4},{9,5},... | collective-permute-start | bytes 208904 | tf_op jit(solution)/shard_map/ppermute | solution.py:363
  32.3 6.1 %collective-permute-start.8 = (bf16[256,128]{1,0:T(8,128)(2,1)S(1)}, bf16[256,128]{1,0:T(8,128)(2,1)S(1)}, u32[]{:S(2)}, u32[]{:S(2)}) collective-permute-start(bf16[256,128]{1,0:T(8,128)(2,1)S(1)} %settle.1.refs_0_), channel_id=1, source_target_pairs={{0,12},{1,13},{2,14},{3,15},{4,8},{5,9},{6,10},{7,11},{8,4},{9,5},... | collective-permute-start | bytes 196616 | tf_op jit(solution)/shard_map/ppermute | solution.py:363
  34.2 5.7 %collective-permute-start.7 = (bf16[256,128]{1,0:T(8,128)(2,1)S(1)}, bf16[256,128]{1,0:T(8,128)(2,1)S(1)}, u32[]{:S(2)}, u32[]{:S(2)}) collective-permute-start(bf16[256,128]{1,0:T(8,128)(2,1)S(1)} %settle.1.refs_0_), channel_id=1, source_target_pairs={{0,8},{1,9},{2,10},{3,11},{4,12},{5,13},{6,14},{7,15},{8,0},{9,1},... | collective-permute-start | bytes 196616 | tf_op jit(solution)/shard_map/ppermute | solution.py:363
  34.5 5.4 %collective-permute-start.6 = (bf16[256,128]{1,0:T(8,128)(2,1)S(1)}, bf16[256,128]{1,0:T(8,128)(2,1)S(1)}, u32[]{:S(2)}, u32[]{:S(2)}) collective-permute-start(bf16[256,128]{1,0:T(8,128)(2,1)S(1)} %settle.1.refs_0_), channel_id=1, source_target_pairs={{0,4},{1,5},{2,6},{3,7},{4,0},{5,1},{6,2},{7,3},{8,12},{9,13},{10,... | collective-permute-start | bytes 196616 | tf_op jit(solution)/shard_map/ppermute | solution.py:363
  40.0 6.4 %collective-permute-start.9 = (bf16[256,512]{1,0:T(8,128)(2,1)S(1)}, bf16[256,512]{1,0:T(8,128)(2,1)S(1)}, u32[]{:S(2)}, u32[]{:S(2)}) collective-permute-start(bf16[256,512]{1,0:T(8,128)(2,1)S(1)} %join.2.after.refs_0_), channel_id=1, source_target_pairs={{0,2},{1,3},{2,0},{3,1},{4,6},{5,7},{6,4},{7,5},{8,10},{9,11},{10,... | collective-permute-start | bytes 786440 | tf_op jit(solution)/shard_map/ppermute | solution.py:363
  46.4 2.0 %collective-permute-start.10 = (bf16[256,1024]{1,0:T(8,128)(2,1)S(1)}, bf16[256,1024]{1,0:T(8,128)(2,1)S(1)}, u32[]{:S(2)}, u32[]{:S(2)}) collective-permute-start(bf16[256,1024]{1,0:T(8,128)(2,1)S(1)} %join.3.mine), channel_id=1, source_target_pairs={{0,1},{1,0},{2,3},{3,2},{4,5},{5,4},{6,7},{7,6},{8,9},{9,8},{10,11... | collective-permute-start | bytes 1572872 | tf_op jit(solution)/shard_map/ppermute | solution.py:363

commit v17 on v16

--- a/solution.py
+++ b/solution.py
@@ -320,6 +320,10 @@
     mixers(order, mask_of(place, devices, order.shape[1]), held, coef)
 
 
+def line_kernel(total, third, second, first, out):
+    join_kernel(total, first, second, third, out)
+
+
 def join_kernel(*refs):
     *parts, out = refs
     start = 0
@@ -419,8 +423,8 @@
         ways = zip(turns_of(0), turns_of(1))
         parts = [swap(part, devices, 4 * even, 4 * odd) for part, (even, odd) in zip(parts, ways)]
         total = call(settle_kernel, "settle", [array(W, size)], keep, *parts, scalars=0)[0]
-        spread = [swap(total, devices, 4 * d) for d in (1, 2, 3)]
-        resp = join(total, *spread)
+        spread = [swap(total, devices, 4 * d) for d in (3, 2, 1)]
+        resp = call(line_kernel, "line", [array(W, quarter)], total, *spread, scalars=0)[0]
         mode_coef = call(
             mixers_kernel, "mixers", [array(8, modes, dtype=F32)],
             place, order, known, *parts, resp, scratch=[pltpu.VMEM((8, modes), F32)],

time: 52.1 us -> 53 us (1.017)
  waiting for transfers between devices: 11.6 us -> 12.5 us
    ppermute x11, waiting for transfers between devices: 11.6 us -> 12.5 us  [swap(): lax.ppermute(x, 'frdm', [(i, i ^ (odd if i & 1 else bits)) for i in range...]
where the time goes in v17:
time: 53 us; the launch traced here: 52.9 us
  Pallas kernels  26.2 us (49%)
  starting transfers between devices  14 us (26%)
  waiting for transfers between devices  12.5 us (24%)
    pallas_call x14, Pallas kernels, call(): pl.pallas_call(kernel, in_specs=places, out_specs=[vmem] * len(out_shape)...  26.2 us
    ppermute x11, starting transfers between devices, swap(): lax.ppermute(x, 'frdm', [(i, i ^ (odd if i & 1 else bits)) for i in range...  14 us
    ppermute x11, waiting for transfers between devices, swap(): lax.ppermute(x, 'frdm', [(i, i ^ (odd if i & 1 else bits)) for i in range...  12.5 us
  transfers between devices with their start and end apart: 11, of which 7 were waited for; matrix products, arithmetic and copies ran while one was open for 0% of the time, Pallas kernels for 28%

profile of v17, /device:TPU:0, one launch (start us, length us, event | category | flops | bytes accessed | tf_op | source)
XLA Modules:
  0.0 52.9 jit_solution(15625519531847549502)
XLA Ops:
  0.0 0.0 copy-start
  0.0 5.4 %project.1 = (bf16[912,512]{1,0:T(8,128)(2,1)S(1)}, bf16[896,1024]{1,0:T(8,128)(2,1)S(1)}, bf16[1024,1024]{1,0:T(8,128)(2,1)S(1)}, bf16[528,2048]{1,0:T(8,128)(2,1)S(1)}, bf16[2,128]{1,0:T(2,128)(2,1)S(1)}) custom-call(s32[1]{0:T(128)} %bitcast.place, bf16[1024,896]{1,0:T(8,128)(2,1)} %loads_far.1, bf16[896,896]{1,0:T(8,128)(2,1)} %constant.14.clone.forward_far, ...), custom_call_target="tpu_custom_call" | custom-call | tf_op jit(solution)/shard_map/project/pallas_call | solution.py:69
  5.4 0.5 collective-permute-start
  5.9 0.0 copy-done
  5.9 3.3 %spectrum.1 = (f32[896,512]{1,0:T(8,128)S(1)}, bf16[1024,1024]{1,0:T(8,128)(2,1)S(1)}, bf16[896,1024]{1,0:T(8,128)(2,1)S(1)}, bf16[896,128]{1,0:T(8,128)(2,1)S(1...) custom-call(s32[1]{0:T(128)} %bitcast.place, bf16[528,2048]{1,0:T(8,128)(2,1)S(1)} %get-tuple-element.22.stack, ...), custom_call_target="tpu_custom_call" | custom-call | tf_op jit(solution)/shard_map/spectrum/pallas_call | solution.py:69
  9.2 0.0 collective-permute-done.other
  9.2 2.4 %respond.2.after = bf16[272,512]{1,0:T(8,128)(2,1)S(1)} custom-call(s32[1]{0:T(128)} %bitcast.place, bf16[896,1024]{1,0:T(8,128)(2,1)S(1)} %get-tuple-element.21.lft, bf16[1024,1024]{1,0:T(8,128)(2,1)S(1)} %get-tuple-element.23.shapes.near, bf16[912,512]{1,0:T(8,128)(2,1)S(1)} %collective-permute-done.other, f32[896,512]{1,0:T(8,128)S(1)} %get-tuple-element.26.spec, ...), custom_call_target="tpu_custom_call" | custom-call | tf_op jit(solution)/shard_map/respond/pallas_call | solution.py:69
  11.6 2.6 %collective-permute-start.2 = (bf16[272,512]{1,0:T(8,128)(2,1)S(1)}, bf16[272,512]{1,0:T(8,128)(2,1)S(1)}, u32[]{:S(2)}, u32[]{:S(2)}) collective-permute-start(bf16[272,512]{1,0:T(8,128)(2,1)S(1)} %respond.2.after), channel_id=1, source_target_pairs={{0,2},{1,3},{2,0},{3,1},{4,6},{5,7},{6,4},{7,5},{8,10},{9,11},{10,... | collective-permute-start | bytes 835592 | tf_op jit(solution)/shard_map/ppermute | solution.py:367
  14.2 1.1 %project_rest.1 = bf16[896,512]{1,0:T(8,128)(2,1)S(1)} custom-call(s32[1]{0:T(128)} %bitcast.place, bf16[896,1024]{1,0:T(8,128)(2,1)S(1)} %get-tuple-element.21.lft, bf16[1024,1024]{1,0:T(8,128)(2,1)S(1)} %get-tuple-element.24.shapes.far, bf16[272,512]{1,0:T(8,128)(2,1)S(1)} %respond.2.after), custom_call_target="tpu_custom_call" | custom-call | flops 3758096384 | tf_op jit(solution)/shard_map/project_rest/pallas_call | solution.py:69
  15.3 0.3 collective-permute-start.1
  15.6 2.9 %spectrum_rest.1.spec = f32[896,512]{1,0:T(8,128)S(1)} custom-call(s32[1]{0:T(128)} %bitcast.place, bf16[528,2048]{1,0:T(8,128)(2,1)S(1)} %get-tuple-element.22.stack, s32[1,2048]{1,0:T(1,128)S(1)} %bitcast.6, bf16[896,1024]{1,0:T(8,128)(2,1)S(1)} %get-tuple-element.29.table, bf16[896,128]{1,0:T(8,128)(2,1)S(1)} %get-tuple-element.30.last, ...), custom_call_target="tpu_custom_call" | custom-call | flops 20000000000 | tf_op jit(solution)/shard_map/spectrum_rest/pallas_call | solution.py:69
  18.4 0.0 collective-permute-done.1.other
  18.5 2.4 %respond.3.own = f32[256,512]{1,0:T(8,128)S(1)} custom-call(s32[1]{0:T(128)} %bitcast.place, bf16[896,1024]{1,0:T(8,128)(2,1)S(1)} %get-tuple-element.21.lft, bf16[1024,1024]{1,0:T(8,128)(2,1)S(1)} %get-tuple-element.23.shapes.near, bf16[896,512]{1,0:T(8,128)(2,1)S(1)} %collective-permute-done.1.other, f32[896,512]{1,0:T(8,128)S(1)} %spectrum_rest.1.spec, ...), custom_call_target="tpu_custom_call" | custom-call | tf_op jit(solution)/shard_map/respond/pallas_call | solution.py:69
  20.8 0.0 copy-start.1
  20.9 0.6 %collective-permute-done.2.got = bf16[272,512]{1,0:T(8,128)(2,1)S(1)} collective-permute-done((bf16[272,512]{1,0:T(8,128)(2,1)S(1)}, bf16[272,512]{1,0:T(8,128)(2,1)S(1)}, u32[]{:S(2)}, u32[]{:S(2)}) %collective-permute-start.2) | collective-permute-done | bytes 278560 | tf_op jit(solution)/shard_map/ppermute | solution.py:367
  21.5 0.1 fold.1
  21.6 1.9 %collective-permute-start.3 = (bf16[272,128]{1,0:T(8,128)(2,1)S(1)}, bf16[272,128]{1,0:T(8,128)(2,1)S(1)}, u32[]{:S(2)}, u32[]{:S(2)}) collective-permute-start(bf16[272,128]{1,0:T(8,128)(2,1)S(1)} %get-tuple-element.33), channel_id=1, source_target_pairs={{0,4},{1,5},{2,6},{3,7},{4,0},{5,1},{6,2},{7,3},{8,12},{9,13},{10,... | collective-permute-start | bytes 208904 | tf_op jit(solution)/shard_map/ppermute | solution.py:367
  23.5 2.6 %collective-permute-start.4 = (bf16[272,128]{1,0:T(8,128)(2,1)S(1)}, bf16[272,128]{1,0:T(8,128)(2,1)S(1)}, u32[]{:S(2)}, u32[]{:S(2)}) collective-permute-start(bf16[272,128]{1,0:T(8,128)(2,1)S(1)} %get-tuple-element.34), channel_id=1, source_target_pairs={{0,8},{1,9},{2,10},{3,11},{4,12},{5,13},{6,14},{7,15},{8,0},{9,1},... | collective-permute-start | bytes 208904 | tf_op jit(solution)/shard_map/ppermute | solution.py:367
  26.1 0.0 collective-permute-start.5
  26.1 0.0 collective-permute-done.3.first
  26.1 4.8 %collective-permute-done.4.second = bf16[272,128]{1,0:T(8,128)(2,1)S(1)} collective-permute-done((bf16[272,128]{1,0:T(8,128)(2,1)S(1)}, bf16[272,128]{1,0:T(8,128)(2,1)S(1)}, u32[]{:S(2)}, u32[]{:S(2)}) %collective-permute-start.4) | collective-permute-done | bytes 69664 | tf_op jit(solution)/shard_map/ppermute | solution.py:367
  30.9 1.4 %collective-permute-done.5.third = bf16[272,128]{1,0:T(8,128)(2,1)S(1)} collective-permute-done((bf16[272,128]{1,0:T(8,128)(2,1)S(1)}, bf16[272,128]{1,0:T(8,128)(2,1)S(1)}, u32[]{:S(2)}, u32[]{:S(2)}) %collective-permute-start.5) | collective-permute-done | bytes 69664 | tf_op jit(solution)/shard_map/ppermute | solution.py:367
  32.3 0.7 %collective-permute-start.8 = (bf16[256,128]{1,0:T(8,128)(2,1)S(1)}, bf16[256,128]{1,0:T(8,128)(2,1)S(1)}, u32[]{:S(2)}, u32[]{:S(2)}) collective-permute-start(bf16[256,128]{1,0:T(8,128)(2,1)S(1)} %settle.1.total), channel_id=1, source_target_pairs={{0,4},{1,5},{2,6},{3,7},{4,0},{5,1},{6,2},{7,3},{8,12},{9,13},{10,... | collective-permute-start | bytes 196616 | tf_op jit(solution)/shard_map/ppermute | solution.py:367
  33.0 1.7 %collective-permute-start.7 = (bf16[256,128]{1,0:T(8,128)(2,1)S(1)}, bf16[256,128]{1,0:T(8,128)(2,1)S(1)}, u32[]{:S(2)}, u32[]{:S(2)}) collective-permute-start(bf16[256,128]{1,0:T(8,128)(2,1)S(1)} %settle.1.total), channel_id=1, source_target_pairs={{0,8},{1,9},{2,10},{3,11},{4,12},{5,13},{6,14},{7,15},{8,0},{9,1},... | collective-permute-start | bytes 196616 | tf_op jit(solution)/shard_map/ppermute | solution.py:367
  34.8 2.0 %collective-permute-start.6 = (bf16[256,128]{1,0:T(8,128)(2,1)S(1)}, bf16[256,128]{1,0:T(8,128)(2,1)S(1)}, u32[]{:S(2)}, u32[]{:S(2)}) collective-permute-start(bf16[256,128]{1,0:T(8,128)(2,1)S(1)} %settle.1.total), channel_id=1, source_target_pairs={{0,12},{1,13},{2,14},{3,15},{4,8},{5,9},{6,10},{7,11},{8,4},{9,5},... | collective-permute-start | bytes 196616 | tf_op jit(solution)/shard_map/ppermute | solution.py:367
  36.8 0.0 collective-permute-done.8.first
  36.8 2.4 %collective-permute-done.7.second = bf16[256,128]{1,0:T(8,128)(2,1)S(1)} collective-permute-done((bf16[256,128]{1,0:T(8,128)(2,1)S(1)}, bf16[256,128]{1,0:T(8,128)(2,1)S(1)}, u32[]{:S(2)}, u32[]{:S(2)}) %collective-permute-start.7) | collective-permute-done | bytes 65568 | tf_op jit(solution)/shard_map/ppermute | solution.py:367
  39.2 1.6 %collective-permute-done.6.third = bf16[256,128]{1,0:T(8,128)(2,1)S(1)} collective-permute-done((bf16[256,128]{1,0:T(8,128)(2,1)S(1)}, bf16[256,128]{1,0:T(8,128)(2,1)S(1)}, u32[]{:S(2)}, u32[]{:S(2)}) %collective-permute-start.6) | collective-permute-done | bytes 65568 | tf_op jit(solution)/shard_map/ppermute | solution.py:367
  40.9 1.6 %collective-permute-start.9 = (bf16[256,512]{1,0:T(8,128)(2,1)S(1)}, bf16[256,512]{1,0:T(8,128)(2,1)S(1)}, u32[]{:S(2)}, u32[]{:S(2)}) collective-permute-start(bf16[256,512]{1,0:T(8,128)(2,1)S(1)} %line.1.after.refs_0_), channel_id=1, source_target_pairs={{0,2},{1,3},{2,0},{3,1},{4,6},{5,7},{6,4},{7,5},{8,10},{9,11},{10,... | collective-permute-start | bytes 786440 | tf_op jit(solution)/shard_map/ppermute | solution.py:367
  42.4 2.4 %mixers.1.after.coef = f32[8,2048]{1,0:T(8,128)S(1)} custom-call(s32[1]{0:T(128)} %bitcast.place, s32[1,2048]{1,0:T(1,128)S(1)} %bitcast.7, bf16[16,128]{1,0:T(8,128)(2,1)S(1)} %get-tuple-element.32.known, bf16[272,128]{1,0:T(8,128)(2,1)S(1)} %collective-permute-done.3.first, bf16[272,128]{1,0:T(8,128)(2,1)S(1)} %collective-permute-done.4.second, ...), custom_call_target="tpu_custom_call" | custom-call | tf_op jit(solution)/shard_map/mixers/pallas_call | solution.py:69
  44.9 0.0 copy-done.1
  44.9 1.4 %pick.1._ = bf16[2048,2048]{1,0:T(8,128)(2,1)S(1)} custom-call(s32[1]{0:T(128)} %bitcast.place, s32[1,2048]{1,0:T(1,128)S(1)} %bitcast.8, f32[8,2048]{1,0:T(8,128)S(1)} %mixers.1.after.coef), custom_call_target="tpu_custom_call" | custom-call | tf_op jit(solution)/shard_map/pick/pallas_call | solution.py:69
  46.3 1.0 %collective-permute-done.9.refs_1_ = bf16[256,512]{1,0:T(8,128)(2,1)S(1)} collective-permute-done((bf16[256,512]{1,0:T(8,128)(2,1)S(1)}, bf16[256,512]{1,0:T(8,128)(2,1)S(1)}, u32[]{:S(2)}, u32[]{:S(2)}) %collective-permute-start.9) | collective-permute-done | bytes 262176 | tf_op jit(solution)/shard_map/ppermute | solution.py:367
  47.3 0.1 collective-permute-start.10
  47.4 1.2 %mate.1.mates = f32[256,2048]{1,0:T(8,128)S(1)} custom-call(bf16[256,1024]{1,0:T(8,128)(2,1)S(1)} %join.1.mine, bf16[2048,2048]{1,0:T(8,128)(2,1)S(1)} %pick.1._), custom_call_target="tpu_custom_call" | custom-call | tf_op jit(solution)/shard_map/mate/pallas_call | solution.py:69
  48.7 0.6 %collective-permute-done.10.theirs = bf16[256,1024]{1,0:T(8,128)(2,1)S(1)} collective-permute-done((bf16[256,1024]{1,0:T(8,128)(2,1)S(1)}, bf16[256,1024]{1,0:T(8,128)(2,1)S(1)}, u32[]{:S(2)}, u32[]{:S(2)}) %collective-permute-start.10) | collective-permute-done | bytes 524320 | tf_op jit(solution)/shard_map/ppermute | solution.py:367
  49.3 3.5 %expand.1 = bf16[1024,256]{1,0:T(8,128)(2,1)} custom-call(s32[1]{0:T(128)} %bitcast.place, bf16[256,1024]{1,0:T(8,128)(2,1)S(1)} %join.1.mine, bf16[256,1024]{1,0:T(8,128)(2,1)S(1)} %collective-permute-done.10.theirs, f32[256,2048]{1,0:T(8,128)S(1)} %mate.1.mates, bf16[2048,2048]{1,0:T(8,128)(2,1)S(1)} %pick.1._, f32[8,2048]{1,0:T(8,128)S(1)} %mixers.1.after.coef, ...), custom_call_target="tpu_custom_call" | custom-call | tf_op jit(solution)/shard_map/expand/pallas_call | solution.py:69
  (3 shorter events, 0.1 us)
Async XLA Ops:
  0.0 5.9 %copy-start = (s32[2048]{0:T(1024)S(1)}, s32[2048]{0:T(1024)}, u32[]{:S(2)}) copy-start(s32[2048]{0:T(1024)} %param.14) | copy-start | bytes 24580
  5.4 3.8 %collective-permute-start = (bf16[912,512]{1,0:T(8,128)(2,1)S(1)}, bf16[912,512]{1,0:T(8,128)(2,1)S(1)}, u32[]{:S(2)}, u32[]{:S(2)}) collective-permute-start(bf16[912,512]{1,0:T(8,128)(2,1)S(1)} %get-tuple-element.25), channel_id=1, source_target_pairs={{0,1},{1,0},{2,3},{3,2},{4,5},{5,4},{6,7},{7,6},{8,9},{9,8},{10,11... | collective-permute-start | bytes 2801672 | tf_op jit(solution)/shard_map/ppermute | solution.py:367
  11.6 9.9 %collective-permute-start.2 = (bf16[272,512]{1,0:T(8,128)(2,1)S(1)}, bf16[272,512]{1,0:T(8,128)(2,1)S(1)}, u32[]{:S(2)}, u32[]{:S(2)}) collective-permute-start(bf16[272,512]{1,0:T(8,128)(2,1)S(1)} %respond.2.after), channel_id=1, source_target_pairs={{0,2},{1,3},{2,0},{3,1},{4,6},{5,7},{6,4},{7,5},{8,10},{9,11},{10,... | collective-permute-start | bytes 835592 | tf_op jit(solution)/shard_map/ppermute | solution.py:367
  15.3 3.2 %collective-permute-start.1 = (bf16[896,512]{1,0:T(8,128)(2,1)S(1)}, bf16[896,512]{1,0:T(8,128)(2,1)S(1)}, u32[]{:S(2)}, u32[]{:S(2)}) collective-permute-start(bf16[896,512]{1,0:T(8,128)(2,1)S(1)} %project_rest.1), channel_id=1, source_target_pairs={{0,1},{1,0},{2,3},{3,2},{4,5},{5,4},{6,7},{7,6},{8,9},{9,8},{10,11... | collective-permute-start | bytes 2752520 | tf_op jit(solution)/shard_map/ppermute | solution.py:367
  20.8 24.0 %copy-start.1 = (s32[2048]{0:T(1024)S(1)}, s32[2048]{0:T(1024)}, u32[]{:S(2)}) copy-start(s32[2048]{0:T(1024)} %param.15) | copy-start | bytes 24580
  21.6 4.5 %collective-permute-start.3 = (bf16[272,128]{1,0:T(8,128)(2,1)S(1)}, bf16[272,128]{1,0:T(8,128)(2,1)S(1)}, u32[]{:S(2)}, u32[]{:S(2)}) collective-permute-start(bf16[272,128]{1,0:T(8,128)(2,1)S(1)} %get-tuple-element.33), channel_id=1, source_target_pairs={{0,4},{1,5},{2,6},{3,7},{4,0},{5,1},{6,2},{7,3},{8,12},{9,13},{10,... | collective-permute-start | bytes 208904 | tf_op jit(solution)/shard_map/ppermute | solution.py:367
  23.5 7.4 %collective-permute-start.4 = (bf16[272,128]{1,0:T(8,128)(2,1)S(1)}, bf16[272,128]{1,0:T(8,128)(2,1)S(1)}, u32[]{:S(2)}, u32[]{:S(2)}) collective-permute-start(bf16[272,128]{1,0:T(8,128)(2,1)S(1)} %get-tuple-element.34), channel_id=1, source_target_pairs={{0,8},{1,9},{2,10},{3,11},{4,12},{5,13},{6,14},{7,15},{8,0},{9,1},... | collective-permute-start | bytes 208904 | tf_op jit(solution)/shard_map/ppermute | solution.py:367
  26.1 6.2 %collective-permute-start.5 = (bf16[272,128]{1,0:T(8,128)(2,1)S(1)}, bf16[272,128]{1,0:T(8,128)(2,1)S(1)}, u32[]{:S(2)}, u32[]{:S(2)}) collective-permute-start(bf16[272,128]{1,0:T(8,128)(2,1)S(1)} %get-tuple-element.35), channel_id=1, source_target_pairs={{0,12},{1,13},{2,14},{3,15},{4,8},{5,9},{6,10},{7,11},{8,4},{9,5},... | collective-permute-start | bytes 208904 | tf_op jit(solution)/shard_map/ppermute | solution.py:367
  32.3 4.5 %collective-permute-start.8 = (bf16[256,128]{1,0:T(8,128)(2,1)S(1)}, bf16[256,128]{1,0:T(8,128)(2,1)S(1)}, u32[]{:S(2)}, u32[]{:S(2)}) collective-permute-start(bf16[256,128]{1,0:T(8,128)(2,1)S(1)} %settle.1.total), channel_id=1, source_target_pairs={{0,4},{1,5},{2,6},{3,7},{4,0},{5,1},{6,2},{7,3},{8,12},{9,13},{10,... | collective-permute-start | bytes 196616 | tf_op jit(solution)/shard_map/ppermute | solution.py:367
  33.0 6.2 %collective-permute-start.7 = (bf16[256,128]{1,0:T(8,128)(2,1)S(1)}, bf16[256,128]{1,0:T(8,128)(2,1)S(1)}, u32[]{:S(2)}, u32[]{:S(2)}) collective-permute-start(bf16[256,128]{1,0:T(8,128)(2,1)S(1)} %settle.1.total), channel_id=1, source_target_pairs={{0,8},{1,9},{2,10},{3,11},{4,12},{5,13},{6,14},{7,15},{8,0},{9,1},... | collective-permute-start | bytes 196616 | tf_op jit(solution)/shard_map/ppermute | solution.py:367
  34.8 6.1 %collective-permute-start.6 = (bf16[256,128]{1,0:T(8,128)(2,1)S(1)}, bf16[256,128]{1,0:T(8,128)(2,1)S(1)}, u32[]{:S(2)}, u32[]{:S(2)}) collective-permute-start(bf16[256,128]{1,0:T(8,128)(2,1)S(1)} %settle.1.total), channel_id=1, source_target_pairs={{0,12},{1,13},{2,14},{3,15},{4,8},{5,9},{6,10},{7,11},{8,4},{9,5},... | collective-permute-start | bytes 196616 | tf_op jit(solution)/shard_map/ppermute | solution.py:367
  40.9 6.4 %collective-permute-start.9 = (bf16[256,512]{1,0:T(8,128)(2,1)S(1)}, bf16[256,512]{1,0:T(8,128)(2,1)S(1)}, u32[]{:S(2)}, u32[]{:S(2)}) collective-permute-start(bf16[256,512]{1,0:T(8,128)(2,1)S(1)} %line.1.after.refs_0_), channel_id=1, source_target_pairs={{0,2},{1,3},{2,0},{3,1},{4,6},{5,7},{6,4},{7,5},{8,10},{9,11},{10,... | collective-permute-start | bytes 786440 | tf_op jit(solution)/shard_map/ppermute | solution.py:367
  47.3 2.0 %collective-permute-start.10 = (bf16[256,1024]{1,0:T(8,128)(2,1)S(1)}, bf16[256,1024]{1,0:T(8,128)(2,1)S(1)}, u32[]{:S(2)}, u32[]{:S(2)}) collective-permute-start(bf16[256,1024]{1,0:T(8,128)(2,1)S(1)} %join.1.mine), channel_id=1, source_target_pairs={{0,1},{1,0},{2,3},{3,2},{4,5},{5,4},{6,7},{7,6},{8,9},{9,8},{10,11... | collective-permute-start | bytes 1572872 | tf_op jit(solution)/shard_map/ppermute | solution.py:367
